TPU v7x, 256 devices: a whole 4x4x8 slice. The times are simulated.
256 devices in a mesh: dom: 32 (over y, z_hi, core), rep: 8 (over x, z_lo).
Axes of the slice: x: 4, y: 4, z: 8 (z_hi: 4, z_lo: 2; z = z_hi * 2 + z_lo), core: 2. Of those that a mesh axis runs over, the one named last changes fastest.
Arguments:
- features: bfloat16 [16384, 768], P('dom'), may hold values from -6 to 6
- tiles: bfloat16 [128, 32, 4, 128, 128], P('dom', 'rep'), may hold values from -0.046875 to 0.046875
- tile_cols: int32 [128, 32, 4], P('dom', 'rep'), may hold values from 0 to 3
- tile_mask: int32 [128, 32, 4], P('dom', 'rep'), may hold values from 0 to 1, as said below
- weight: bfloat16 [768, 768], replicated, may hold values from -0.21875 to 0.21875
- bias: float32 [768], replicated, may hold values from -3 to 3
- cotangent: bfloat16 [16384, 768], P(('dom', 'rep')), may hold values from -0.046875 to 0.046875
Outputs:
- output: bfloat16 [16384, 768], P(('dom', 'rep'))
- grad_weight: float32 [768, 768], replicated
- grad_bias: float32 [768], replicated
Inputs may be any that keep to these rules, and one draw needn't show every extreme that they name: `tile_mask`: for each row block and source, the live slots come first and slot 0 is always live.
All inputs are finite; a program needn't handle non-finite values.
Results may differ from a plain program's by a relative error of at most 0.02.
Values may be sent and summed in bfloat16 or wider, within the bound.
No kernel may reach another device: no remote copies, remote signals or barrier semaphores. Data moves between devices by JAX's collectives and lax.ppermute only.
A program may use at most 128 MiB of HBM per device.

v0:
```python
import jax
import jax.numpy as jnp
from jax import lax
from jax.sharding import PartitionSpec as P


def spread(value, axis, source):
    kept = jnp.where(lax.axis_index(axis) == source, value, 0).astype(value.dtype)
    return lax.psum(kept, axis)


def section_term(source, tiles, tile_cols, tile_mask, section):
    rblocks = tiles.shape[0]
    tile_side = tiles.shape[3]
    feat_width = source.shape[1]
    source_blocks = source.reshape(source.shape[0] // tile_side, tile_side, feat_width)
    columns = lax.dynamic_index_in_dim(tile_cols, section, 1, keepdims=False)
    live = lax.dynamic_index_in_dim(tile_mask, section, 1, keepdims=False)
    tile_set = lax.dynamic_index_in_dim(tiles, section, 1, keepdims=False)
    block_ids = jnp.arange(source_blocks.shape[0])
    selector = ((columns[:, :, None] == block_ids[None, None, :]) * live[:, :, None]).astype(
        jnp.bfloat16
    )
    picked = jnp.einsum(
        "bkc,cjd->bkjd", selector, source_blocks, preferred_element_type=jnp.float32
    ).astype(jnp.bfloat16)
    summed = jnp.einsum("bkij,bkjd->bid", tile_set, picked, preferred_element_type=jnp.float32)
    return summed.reshape(rblocks * tile_side, feat_width)


def on_device(features, tiles, tile_cols, tile_mask, weight, bias, cotangent):
    sections = tiles.shape[1]
    replica = lax.axis_index("rep")
    aggregate = jnp.zeros(features.shape, jnp.float32)
    for turn_index in range(sections):
        root_index = replica * sections + turn_index
        source = spread(features, "dom", root_index)
        aggregate = aggregate + section_term(source, tiles, tile_cols, tile_mask, turn_index)
    rows_sum = lax.psum_scatter(
        aggregate.astype(jnp.bfloat16), "rep", scatter_dimension=0, tiled=True
    )
    pre_act = jnp.dot(rows_sum, weight, preferred_element_type=jnp.float32) + bias
    sigmoid_pre = jax.nn.sigmoid(pre_act)
    output = (pre_act * sigmoid_pre).astype(jnp.bfloat16)
    grad_pre = cotangent.astype(jnp.float32) * sigmoid_pre * (1.0 + pre_act * (1.0 - sigmoid_pre))
    grad_low = grad_pre.astype(jnp.bfloat16)
    local_weight = jnp.einsum("nd,ne->de", rows_sum, grad_low, preferred_element_type=jnp.float32)
    local_bias = jnp.sum(grad_pre, axis=0)
    grad_weight, grad_bias = lax.psum((local_weight, local_bias), ("dom", "rep"))
    return (output, grad_weight, grad_bias)


def solution(mesh):
    placed = (
        P("dom", None),
        P("dom", "rep", None, None, None),
        P("dom", "rep", None),
        P("dom", "rep", None),
        P(),
        P(),
        P(("dom", "rep"), None),
    )
    return jax.shard_map(
        on_device,
        mesh=mesh,
        in_specs=placed,
        out_specs=(P(("dom", "rep"), None), P(), P()),
        check_vma=False,
    )
```

profile of v0, /device:TPU:1, one launch (start us, length us, event | category | flops | bytes accessed | tf_op | source)
XLA Modules:
  0.0 637.4 jit_solution(3435864758097265437)
XLA Ops:
  7.2 0.0 copy-start
  7.2 0.0 all-reduce.6.cloned.1.call-start
  7.2 3.0 broadcast_select_fusion
  10.2 0.0 all-reduce.6.cloned.1.call-update
  10.2 0.0 copy-start.1
  10.3 0.0 reduce-scatter.2.cloned.1.call-start
  10.3 0.6 copy-done.6
  10.9 0.0 copy-done.7
  10.9 298.9 %all-reduce.6.cloned.1.call-done = (bf16[4,128,768]{2,1,0:T(8,128)(2,1)}, bf16[4,128,768]{2,1,0:T(8,128)(2,1)}, bf16[4,128,768]{2,1,0:T(8,128)(2,1)}, bf16[4,128,768]{2,1,0:T(8,128)(2,1)}) async-done(((bf16[4,128,768]{2,1,0:T(8,128)(2,1)}, bf16[4,128,768]{2,1,0:T(8,128)(2,1)}, bf16[4,128,768]{2,1,0:T(8,128)(2,1)}, bf16[4,128,768]{2,1,0:T(8,128)(2,1)}), (bf16[4,128,768]{2,1,0:T(8,128)(2,1)}, ...) | async-done | bytes 3145744 | tf_op jit(solution)/shard_map/psum | solution.py:9
  309.9 2.5 fusion.9
  312.4 0.6 fusion.1
  313.0 0.5 copy-done.4
  313.5 1.4 fusion.7
  314.9 0.6 fusion.2
  315.5 0.5 copy-done.3
  316.0 1.4 fusion.11
  317.4 0.6 fusion
  318.0 0.5 copy-done.2
  318.5 1.4 fusion.5
  319.9 0.0 copy-start.5
  319.9 0.0 copy-start.8
  319.9 1.8 fusion.4
  321.7 0.0 reduce-scatter.2.cloned.1.call-update
  321.8 0.0 all-reduce.4.cloned.1.call-start
  321.8 36.4 %reduce-scatter.2.cloned.1.call-done = bf16[64,768]{1,0:T(8,128)(2,1)} async-done(((bf16[512,768]{1,0:T(8,128)(2,1)}), bf16[64,768]{1,0:T(8,128)(2,1)}) %reduce-scatter.2.cloned.1.call-update) | async-done | bytes 98320 | tf_op jit(solution)/shard_map/reduce_scatter | solution.py:39
  358.2 0.0 copy-done
  358.3 1.9 fusion.47
  360.2 2.8 fusion.21
  363.0 0.0 all-reduce.4.cloned.1.call-update
  363.0 79.2 %psum.47 = f32[768]{0:T(1024)} all-reduce(f32[768]{0:T(1024)S(1)} %get-tuple-element.11), channel_id=1, replica_groups=mesh['dom'=32,'rep'=8] {'dom','rep'}, use_global_device_ids=true, to_apply=%region_7.8 | all-reduce | flops 768 | bytes 6144 | tf_op jit(solution)/shard_map/psum | solution.py:49
  442.2 185.4 %all-reduce.4.cloned.1.call-done = f32[768,768]{1,0:T(8,128)} async-done(((f32[768,768]{1,0:T(8,128)}), f32[768,768]{1,0:T(8,128)}) %all-reduce.4.cloned.1.call-update) | async-done | bytes 2359312 | tf_op jit(solution)/shard_map/psum | solution.py:49
  627.6 3.2 copy.57
  (10 shorter events, 0.0 us)
Async XLA Ops:
  7.2 351.1 %copy-start = (bf16[768,768]{1,0:T(8,128)(2,1)S(1)}, bf16[768,768]{1,0:T(8,128)(2,1)}, u32[]{:S(2)}) copy-start(bf16[768,768]{1,0:T(8,128)(2,1)} %param.11) | copy-start | bytes 3538948
  7.2 302.7 %all-reduce.6.cloned.1.call-start = ((), (), s32[]{:S(2)}) async-start(), calls=%async_computation.3 | async-start | bytes 6291456 | tf_op jit(solution)/shard_map/psum | solution.py:9
  10.2 0.7 copy-start.6
  10.2 0.7 copy-start.7
  10.2 302.2 %copy-start.1 = (bf16[4,4,4,128,128]{4,3,2,1,0:T(8,128)(2,1)S(1)}, bf16[4,4,4,128,128]{4,3,2,1,0:T(8,128)(2,1)}, u32[]{:S(2)}) copy-start(bf16[4,4,4,128,128]{4,3,2,1,0:T(8,128)(2,1)} %param.8) | copy-start | bytes 6291460
  10.3 348.0 %reduce-scatter.2.cloned.1.call-start = ((), (), s32[]{:S(2)}) async-start(), calls=%async_computation.1 | async-start | bytes 884736 | tf_op jit(solution)/shard_map/reduce_scatter | solution.py:39
  312.4 1.1 copy-start.4
  314.9 1.1 copy-start.3
  317.4 1.1 copy-start.2
  319.9 38.3 %copy-start.5 = (bf16[64,768]{1,0:T(8,128)(2,1)S(1)}, bf16[64,768]{1,0:T(8,128)(2,1)}, u32[]{:S(2)}) copy-start(bf16[64,768]{1,0:T(8,128)(2,1)} %param.13) | copy-start | bytes 294916
  319.9 38.3 %copy-start.8 = (f32[768]{0:T(1024)S(1)}, f32[768]{0:T(1024)}, u32[]{:S(2)}) copy-start(f32[768]{0:T(1024)} %param.12) | copy-start | bytes 9220
  321.8 305.9 %all-reduce.4.cloned.1.call-start = ((), (), s32[]{:S(2)}) async-start(), calls=%async_computation.2 | async-start | bytes 4718592 | tf_op jit(solution)/shard_map/psum | solution.py:49
Sparse Core Ops, SparseCore 0:
  11.5 298.3 all-reduce.5
  321.9 36.3 reduce-scatter.1
  364.3 263.2 all-reduce.3
where the time goes:
time: 639 us; the launch traced here: 637 us
  waiting for transfers between devices  521 us (82%)
  blocking collectives  79.2 us (12%)
  matrix products  14.9 us (2%)
  between operations  13.9 us (2%)
    psum x1, waiting for transfers between devices, spread(): return lax.psum(kept, axis)  299 us
    psum x1, waiting for transfers between devices, on_device(): lax.psum((local_weight, local_bias), ('dom', 'rep'))  185 us
    psum x1, blocking collectives, on_device(): lax.psum((local_weight, local_bias), ('dom', 'rep'))  79.2 us
    reduce_scatter x1, waiting for transfers between devices, on_device(): lax.psum_scatter(aggregate.astype(jnp.bfloat16), 'rep', scatter_dimension...  36.4 us
  transfers between devices with their start and end apart: 3, of which 3 were waited for; matrix products, arithmetic and copies ran while one was open for 0% of the time, Pallas kernels for 0%

commit v1 on v0

v1 whole, which is shorter than its diff:
```python
import jax
import jax.numpy as jnp
import numpy as np
from jax import lax
from jax.experimental import pallas as pl
from jax.experimental.pallas import tpu as pltpu
from jax.sharding import Mesh, PartitionSpec as P

AXES = ("y", "zh", "core", "x", "zl")
SIZES = (4, 4, 2, 4, 2)
DOM = ("y", "zh", "core")
REP = ("x", "zl")
PLANE = ("x", "y")
ZAXIS = ("zh", "zl")
BF = jnp.bfloat16
F32 = jnp.float32
VMEM_LIMIT = 48 * 1024 * 1024


def vmem():
    return pl.BlockSpec(memory_space=pltpu.VMEM)


def smem():
    return pl.BlockSpec(memory_space=pltpu.SMEM)


def anyspace():
    return pl.BlockSpec(memory_space=pl.ANY)


def params():
    return pltpu.CompilerParams(vmem_limit_bytes=VMEM_LIMIT)


def shift(n, k):
    return [(i, (i + k) % n) for i in range(n)]


def first_hop():
    pairs = []
    for target in range(int(np.prod(SIZES))):
        y, zh, core, x, zl = (int(v) for v in np.unravel_index(target, SIZES))
        source = (x, 2 * zl + y // 2, y % 2, (x + zh) % 4, core)
        pairs.append((int(np.ravel_multi_index(source, SIZES)), target))
    return sorted(pairs)


def aggregate_kernel(place, cols, live, tiles, *rest):
    parts, out, feat, sems = rest[:8], rest[8], rest[9], rest[10]
    copies = [
        pltpu.make_async_copy(part, feat.at[pl.ds(i * 256, 256)], sems.at[i])
        for i, part in enumerate(parts)
    ]
    for copy in copies:
        copy.start()
    for copy in copies:
        copy.wait()
    y, core = place[0], place[1]
    for b in range(4):
        total = jnp.zeros((128, 768), F32)
        for s in range(4):
            back = lax.rem(y - s + 4, 4)
            for pair in range(2):
                lhs, rhs = [], []
                for k in (2 * pair, 2 * pair + 1):
                    c = cols[b, s, k]
                    half = c // 2
                    away = lax.rem(half + core, 2)
                    row = (2 * back + away) * 256 + lax.rem(c, 2) * 128
                    rhs.append(feat[pl.ds(pl.multiple_of(row, 128), 128), :])
                    tile = tiles[b, s, k]
                    lhs.append(jnp.where(live[b, s, k] != 0, tile, jnp.zeros_like(tile)))
                total = total + jnp.dot(
                    jnp.concatenate(lhs, axis=1),
                    jnp.concatenate(rhs, axis=0),
                    preferred_element_type=F32,
                )
        out[pl.ds(b * 128, 128), :] = total.astype(BF)


def layer_kernel(recv, weight, bias, cot, out, packed):
    total = recv[0].astype(F32)
    for r in range(1, 8):
        total = total + recv[r].astype(F32)
    mixed = total.astype(BF)
    pre = jnp.dot(mixed, weight[...], preferred_element_type=F32) + bias[...]
    sig = jax.nn.sigmoid(pre)
    out[...] = (pre * sig).astype(BF)
    grad = cot[...].astype(F32) * sig * (1.0 + pre * (1.0 - sig))
    low = grad.astype(BF).astype(F32)
    wide = mixed.astype(F32)
    for i in range(4):
        left = wide[:, i * 192 : (i + 1) * 192]
        for j in range(4):
            both = jnp.concatenate([left, low[:, j * 192 : (j + 1) * 192]], axis=1)
            packed[i * 4 + j] = both.astype(BF)


def with_bias(block, row):
    high = row.astype(BF).astype(F32)
    low = row - high
    at = lax.broadcasted_iota(jnp.int32, (16, 384), 0)
    extra = jnp.where(at == 0, high, jnp.where(at == 1, low, 0.0))
    return jnp.concatenate([block, extra], axis=0)


def block_kernel(place, recv, keep, send):
    data = recv[...]
    left = data[:, :192]
    right = data[:, 192:]
    block = lax.dot_general(left, right, (((0,), (0,)), ((), ())), preferred_element_type=F32)
    row = jnp.sum(right.astype(F32), axis=0, keepdims=True)
    row = jnp.concatenate([row, row], axis=1)
    halves = [
        with_bias(
            jnp.concatenate([block[h * 96 : h * 96 + 48], block[h * 96 + 48 : h * 96 + 96]], axis=1),
            row,
        )
        for h in range(2)
    ]
    core = place[1]
    keep[...] = jnp.where(core == 0, halves[0], halves[1])
    send[...] = jnp.where(core == 0, halves[1], halves[0]).astype(BF)


def resplit(total):
    row = total[48:49] + total[49:50]
    return with_bias(total[:48], row).astype(BF)


def pair_kernel(copies, keep, recv, out):
    value = resplit(keep[...] + recv[...].astype(F32))
    for i in range(copies):
        out[i] = value


def sum_kernel(copies, recv, out):
    total = recv[0].astype(F32)
    for r in range(1, 8):
        total = total + recv[r].astype(F32)
    value = resplit(total)
    for i in range(copies):
        out[i] = value


def final_kernel(place, own, other, grad, bias):
    core = place[1]
    for source, at in ((own, core), (other, 1 - core)):
        for i in range(4):
            pieces = [source[i * 4 + j].astype(F32) for j in range(4)]
            for h in range(2):
                rows = jnp.concatenate(
                    [piece[:48, h * 192 : (h + 1) * 192] for piece in pieces], axis=1
                )
                start = pl.multiple_of(i * 192 + at * 96 + h * 48, 16)
                grad[pl.ds(start, 48), :] = rows
    bias[...] = jnp.concatenate(
        [
            own[j, 48:64, :].astype(F32)[0:1, :192] + own[j, 48:64, :].astype(F32)[1:2, :192]
            for j in range(4)
        ],
        axis=1,
    )


def call(kernel, shapes, specs, out_specs, scratch=()):
    return pl.pallas_call(
        kernel,
        out_shape=shapes,
        in_specs=specs,
        out_specs=out_specs,
        scratch_shapes=scratch,
        compiler_params=params(),
    )


def struct(shape, dtype):
    return jax.ShapeDtypeStruct(shape, dtype)


def on_device(features, tiles, tile_cols, tile_mask, weight, bias, cotangent):
    place = jnp.stack([lax.axis_index("y"), lax.axis_index("core")]).astype(jnp.int32)
    with jax.named_scope("spread_features"):
        half = lax.dynamic_slice_in_dim(features, lax.axis_index("zl") * 256, 256, 0)
        own = lax.ppermute(half, AXES, first_hop())
        parts = [own] + [lax.ppermute(own, "y", shift(4, k)) for k in (1, 2, 3)]
        swapped = [lax.ppermute(part, "core", shift(2, 1)) for part in parts]
        blocks = [block for pair in zip(parts, swapped) for block in pair]
    with jax.named_scope("aggregate"):
        partial = call(
            aggregate_kernel,
            struct((512, 768), BF),
            [smem(), smem(), smem(), vmem()] + [anyspace()] * 8,
            vmem(),
            [pltpu.VMEM((2048, 768), BF), pltpu.SemaphoreType.DMA((8,))],
        )(place, tile_cols, tile_mask, tiles, *blocks)
    with jax.named_scope("sum_over_rep"):
        recv = lax.all_to_all(partial, REP, 0, 0, tiled=True).reshape(8, 64, 768)
    with jax.named_scope("layer"):
        output, packed = call(
            layer_kernel,
            (struct((64, 768), BF), struct((16, 64, 384), BF)),
            [vmem()] * 4,
            (vmem(), vmem()),
        )(recv, weight, bias.reshape(1, 768), cotangent)
    with jax.named_scope("exchange_rows"):
        rows = lax.all_to_all(packed.reshape(1024, 384), PLANE, 0, 0, tiled=True)
    with jax.named_scope("weight_block"):
        keep, send = call(
            block_kernel,
            (struct((64, 384), F32), struct((64, 384), BF)),
            [smem(), vmem()],
            (vmem(), vmem()),
        )(place, rows)
        other = lax.ppermute(send, "core", shift(2, 1))
        pair = call(
            lambda *refs: pair_kernel(8, *refs),
            struct((8, 64, 384), BF),
            [vmem()] * 2,
            vmem(),
        )(keep, other)
    with jax.named_scope("sum_over_z"):
        chain = lax.all_to_all(pair.reshape(512, 384), ZAXIS, 0, 0, tiled=True)
        whole = call(
            lambda *refs: sum_kernel(16, *refs),
            struct((16, 64, 384), BF),
            [vmem()],
            vmem(),
        )(chain.reshape(8, 64, 384))
    with jax.named_scope("gather_plane"):
        mine = lax.all_to_all(whole.reshape(1024, 384), PLANE, 0, 0, tiled=True)
        theirs = lax.ppermute(mine, "core", shift(2, 1))
    with jax.named_scope("finish"):
        grad_weight, grad_bias = call(
            final_kernel,
            (struct((768, 768), F32), struct((1, 768), F32)),
            [smem(), vmem(), vmem()],
            (vmem(), vmem()),
        )(place, mine.reshape(16, 64, 384), theirs.reshape(16, 64, 384))
    return output, grad_weight, grad_bias.reshape(768)


def solution(mesh):
    fine = Mesh(mesh.devices.reshape(SIZES), AXES)
    placed = (
        P(DOM, None),
        P(DOM, REP, None, None, None),
        P(DOM, REP, None),
        P(DOM, REP, None),
        P(),
        P(),
        P(DOM + REP, None),
    )
    return jax.shard_map(
        on_device,
        mesh=fine,
        in_specs=placed,
        out_specs=(P(DOM + REP, None), P(), P()),
        check_vma=False,
    )
```

time: 639 us -> 160 us (0.25)
  waiting for transfers between devices: 521 us -> 37.8 us
  starting transfers between devices: 0.12 us -> 57.5 us
  blocking collectives: 79.2 us -> 47.7 us
  matrix products: 14.9 us -> 0 us
  between operations: 13.9 us -> 0.73 us
  Pallas kernels: 0 us -> 9.87 us
    psum x2 -> x0, waiting for transfers between devices: 484 us -> none  [the longest x1 299 us: spread(): return lax.psum(kept, axis)]
    psum x1 -> x0, blocking collectives: 79.2 us -> none  [on_device(): lax.psum((local_weight, local_bias), ('dom', 'rep'))]
    ppermute x0 -> x10, starting transfers between devices: none -> 49.7 us  [the longest x3 29.4 us: on_device(): parts = [own] + [lax.ppermute(own, 'y', shift(4, k)) for k in (1, 2, 3)]]
    all_to_all x0 -> x3, blocking collectives: none -> 47.7 us  [the longest x1 18.2 us: on_device(): chain = lax.all_to_all(pair.reshape(512, 384), ZAXIS, 0, 0, tiled=True)]
    reduce_scatter x1 -> x0, waiting for transfers between devices: 36.4 us -> none  [on_device(): lax.psum_scatter(aggregate.astype(jnp.bfloat16), 'rep', scatter_dimension...]
    ppermute x0 -> x10, waiting for transfers between devices: none -> 25.8 us  [the longest x1 12.1 us: on_device(): own = lax.ppermute(half, AXES, first_hop())]
    dot_general x10 -> x0, matrix products: 14.9 us -> none  [the longest x4 6.58 us: section_term(): jnp.einsum('bkc,cjd->bkjd', selector, source_blocks, preferred_element_ty...]
    all_to_all x0 -> x1, waiting for transfers between devices: none -> 12 us  [on_device(): recv = lax.all_to_all(partial, REP, 0, 0, tiled=True).reshape(8, 64, 768)]
  transfers between devices with their start and end apart: 3 -> 11, of which waited for: 3 -> 7; matrix products, arithmetic and copies ran while one was open for 0% -> 0% of each run, Pallas kernels for 0% -> 0%
where the time goes in v1:
time: 160 us; the launch traced here: 159 us
  starting transfers between devices  57.5 us (36%)
  blocking collectives  47.7 us (30%)
  waiting for transfers between devices  37.8 us (24%)
  Pallas kernels  9.87 us (6%)
  local copies, waits for them, and re-layouts  5.04 us (3%)
    ppermute x3, starting transfers between devices, on_device(): parts = [own] + [lax.ppermute(own, 'y', shift(4, k)) for k in (1, 2, 3)]  29.4 us
    all_to_all x1, blocking collectives, on_device(): chain = lax.all_to_all(pair.reshape(512, 384), ZAXIS, 0, 0, tiled=True)  18.2 us
    all_to_all x1, blocking collectives, on_device(): mine = lax.all_to_all(whole.reshape(1024, 384), PLANE, 0, 0, tiled=True)  14.9 us
    all_to_all x1, blocking collectives, on_device(): rows = lax.all_to_all(packed.reshape(1024, 384), PLANE, 0, 0, tiled=True)  14.6 us
    ppermute x1, waiting for transfers between devices, on_device(): own = lax.ppermute(half, AXES, first_hop())  12.1 us
    all_to_all x1, waiting for transfers between devices, on_device(): recv = lax.all_to_all(partial, REP, 0, 0, tiled=True).reshape(8, 64, 768)  12 us
    ppermute x3, waiting for transfers between devices, on_device(): parts = [own] + [lax.ppermute(own, 'y', shift(4, k)) for k in (1, 2, 3)]  9.49 us
    ppermute x4, starting transfers between devices, on_device(): swapped = [lax.ppermute(part, 'core', shift(2, 1)) for part in parts]  8.99 us
  transfers between devices with their start and end apart: 11, of which 7 were waited for; matrix products, arithmetic and copies ran while one was open for 0% of the time, Pallas kernels for 0%

profile of v1, /device:TPU:1, one launch (start us, length us, event | category | flops | bytes accessed | tf_op | source)
XLA Modules:
  0.0 159.3 jit_solution(5761449445189798406)
XLA Ops:
  0.6 1.1 copy-done
  1.8 4.6 %collective-permute-start = (bf16[256,768]{1,0:T(8,128)(2,1)S(1)}, bf16[256,768]{1,0:T(8,128)(2,1)S(1)}, u32[]{:S(2)}, u32[]{:S(2)}) collective-permute-start(bf16[256,768]{1,0:T(8,128)(2,1)S(1)} %constant_dynamic-slice_fusion), channel_id=1, source_target_pairs={{0,0},{1,8},{2,16},{3,24},{4,32},{5,40},{6,48},{7,56},{8,64},{9,72... | collective-permute-start | bytes 1179656 | tf_op jit(solution)/shard_map/spread_features/ppermute | solution.py:186
  6.4 12.1 %collective-permute-done.rest_0_ = bf16[256,768]{1,0:T(8,128)(2,1)S(1)} collective-permute-done((bf16[256,768]{1,0:T(8,128)(2,1)S(1)}, bf16[256,768]{1,0:T(8,128)(2,1)S(1)}, u32[]{:S(2)}, u32[]{:S(2)}) %collective-permute-start) | collective-permute-done | bytes 393248 | tf_op jit(solution)/shard_map/spread_features/ppermute | solution.py:186
  18.5 19.8 %collective-permute-start.6 = (bf16[256,768]{1,0:T(8,128)(2,1)S(1)}, bf16[256,768]{1,0:T(8,128)(2,1)S(1)}, u32[]{:S(2)}, u32[]{:S(2)}) collective-permute-start(bf16[256,768]{1,0:T(8,128)(2,1)S(1)} %collective-permute-done.rest_0_), channel_id=1, source_target_pairs={{0,192},{64,0},{128,64},{192,128},{1,193},{65,1},{129,65},{193,129... | collective-permute-start | bytes 1179656 | tf_op jit(solution)/shard_map/spread_features/ppermute | solution.py:187
  38.3 9.6 %collective-permute-start.4 = (bf16[256,768]{1,0:T(8,128)(2,1)S(1)}, bf16[256,768]{1,0:T(8,128)(2,1)S(1)}, u32[]{:S(2)}, u32[]{:S(2)}) collective-permute-start(bf16[256,768]{1,0:T(8,128)(2,1)S(1)} %collective-permute-done.rest_0_), channel_id=1, source_target_pairs={{0,128},{64,192},{128,0},{192,64},{1,129},{65,193},{129,1},{193,65... | collective-permute-start | bytes 1179656 | tf_op jit(solution)/shard_map/spread_features/ppermute | solution.py:187
  47.9 1.8 %collective-permute-start.1 = (bf16[256,768]{1,0:T(8,128)(2,1)S(1)}, bf16[256,768]{1,0:T(8,128)(2,1)S(1)}, u32[]{:S(2)}, u32[]{:S(2)}) collective-permute-start(bf16[256,768]{1,0:T(8,128)(2,1)S(1)} %collective-permute-done.rest_0_), channel_id=1, source_target_pairs={{0,8},{8,0},{1,9},{9,1},{2,10},{10,2},{3,11},{11,3},{4,12},{12,4},... | collective-permute-start | bytes 1179656 | tf_op jit(solution)/shard_map/spread_features/ppermute | solution.py:188
  49.7 4.8 %collective-permute-done.6.rest_6_ = bf16[256,768]{1,0:T(8,128)(2,1)S(1)} collective-permute-done((bf16[256,768]{1,0:T(8,128)(2,1)S(1)}, bf16[256,768]{1,0:T(8,128)(2,1)S(1)}, u32[]{:S(2)}, u32[]{:S(2)}) %collective-permute-start.6) | collective-permute-done | bytes 393248 | tf_op jit(solution)/shard_map/spread_features/ppermute | solution.py:187
  54.4 3.1 %collective-permute-start.7 = (bf16[256,768]{1,0:T(8,128)(2,1)S(1)}, bf16[256,768]{1,0:T(8,128)(2,1)S(1)}, u32[]{:S(2)}, u32[]{:S(2)}) collective-permute-start(bf16[256,768]{1,0:T(8,128)(2,1)S(1)} %collective-permute-done.6.rest_6_), channel_id=1, source_target_pairs={{0,8},{8,0},{1,9},{9,1},{2,10},{10,2},{3,11},{11,3},{4,12},{12,4},... | collective-permute-start | bytes 1179656 | tf_op jit(solution)/shard_map/spread_features/ppermute | solution.py:188
  57.5 3.6 %collective-permute-start.5 = (bf16[256,768]{1,0:T(8,128)(2,1)S(1)}, bf16[256,768]{1,0:T(8,128)(2,1)S(1)}, u32[]{:S(2)}, u32[]{:S(2)}) collective-permute-start(bf16[256,768]{1,0:T(8,128)(2,1)S(1)} %collective-permute-done.4.rest_4_), channel_id=1, source_target_pairs={{0,8},{8,0},{1,9},{9,1},{2,10},{10,2},{3,11},{11,3},{4,12},{12,4},... | collective-permute-start | bytes 1179656 | tf_op jit(solution)/shard_map/spread_features/ppermute | solution.py:188
  61.2 4.7 %collective-permute-done.2.rest_2_ = bf16[256,768]{1,0:T(8,128)(2,1)S(1)} collective-permute-done((bf16[256,768]{1,0:T(8,128)(2,1)S(1)}, bf16[256,768]{1,0:T(8,128)(2,1)S(1)}, u32[]{:S(2)}, u32[]{:S(2)}) %collective-permute-start.2) | collective-permute-done | bytes 393248 | tf_op jit(solution)/shard_map/spread_features/ppermute | solution.py:187
  65.9 0.5 collective-permute-start.3
  66.4 0.1 pad_add_fusion.place
  66.5 1.4 collective-permute-done.3.rest_3_
  67.9 1.6 copy-done.1
  69.5 0.7 copy-done.4
  70.2 0.7 copy-done.5
  70.9 5.2 %aggregate.1 = bf16[512,768]{1,0:T(8,128)(2,1)} custom-call(s32[2]{0:T(128)S(1)} %pad_add_fusion.place, s32[4,4,4]{2,1,0:T(4,128)S(1)} %copy-done.4, s32[4,4,4]{2,1,0:T(4,128)S(1)} %copy-done.5, bf16[4,4,4,128,128]{4,3,2,1,0:T(8,128)(2,1)S(1)} %copy-done.1, bf16[256,768]{1,0:T(8,128)(2,1)S(1)} %collective-permute-done.rest_0_, ...), custom_call_target="tpu_custom_call" | custom-call | tf_op jit(solution)/shard_map/aggregate/pallas_call | solution.py:191
  76.1 7.7 %all-to-all-start = ((bf16[8,64,768]{2,1,0:T(8,128)(2,1)}), bf16[8,64,768]{2,1,0:T(8,128)(2,1)S(1)}, u32[]{:S(2)}, u32[]{:S(2)}) async-start(bf16[8,64,768]{2,1,0:T(8,128)(2,1)} %bitcast.2), calls=%async_computation | async-start | bytes 1572864 | tf_op jit(solution)/shard_map/sum_over_rep/all_to_all | solution.py:199
  83.8 12.0 %all-to-all-done.recv = bf16[8,64,768]{2,1,0:T(8,128)(2,1)S(1)} async-done(((bf16[8,64,768]{2,1,0:T(8,128)(2,1)}), bf16[8,64,768]{2,1,0:T(8,128)(2,1)S(1)}, u32[]{:S(2)}, u32[]{:S(2)}) %all-to-all-start) | async-done | bytes 786464 | tf_op jit(solution)/shard_map/sum_over_rep/all_to_all | solution.py:199
  95.8 0.9 copy-done.3
  96.7 1.0 layer.1
  97.8 14.6 %all_to_all.32 = bf16[16,64,384]{2,1,0:T(8,128)(2,1)S(1)} all-to-all(bf16[16,64,384]{2,1,0:T(8,128)(2,1)S(1)} %get-tuple-element.10), channel_id=1, replica_groups=mesh['y'=4,'zh'=4,'core'=2,'x'=4,'zl'=2] {'x','y'}, dimensions={0} | all-to-all | bytes 1572864 | tf_op jit(solution)/shard_map/exchange_rows/all_to_all | solution.py:208
  112.4 1.3 weight_block.2
  113.6 3.4 %collective-permute-start.8 = (bf16[64,384]{1,0:T(8,128)(2,1)S(1)}, bf16[64,384]{1,0:T(8,128)(2,1)S(1)}, u32[]{:S(2)}, u32[]{:S(2)}) collective-permute-start(bf16[64,384]{1,0:T(8,128)(2,1)S(1)} %get-tuple-element.12), channel_id=1, source_target_pairs={{0,8},{8,0},{1,9},{9,1},{2,10},{10,2},{3,11},{11,3},{4,12},{12,4},... | collective-permute-start | bytes 147464 | tf_op jit(solution)/shard_map/weight_block/ppermute | solution.py:216
  117.1 0.9 collective-permute-done.8.refs_1_
  118.0 18.2 %all_to_all.33.refs_0_ = bf16[8,64,384]{2,1,0:T(8,128)(2,1)S(1)} all-to-all(bf16[8,64,384]{2,1,0:T(8,128)(2,1)S(1)} %weight_block.3), channel_id=1, replica_groups=mesh['y'=4,'zh'=4,'core'=2,'x'=4,'zl'=2] {'zh','zl'}, dimensions={0} | all-to-all | bytes 786432 | tf_op jit(solution)/shard_map/sum_over_z/all_to_all | solution.py:224
  136.2 0.1 sum_over_z.1
  136.3 14.9 %all_to_all.34.own = bf16[16,64,384]{2,1,0:T(8,128)(2,1)S(1)} all-to-all(bf16[16,64,384]{2,1,0:T(8,128)(2,1)S(1)} %sum_over_z.1), channel_id=1, replica_groups=mesh['y'=4,'zh'=4,'core'=2,'x'=4,'zl'=2] {'x','y'}, dimensions={0} | all-to-all | bytes 1572864 | tf_op jit(solution)/shard_map/gather_plane/all_to_all | solution.py:232
  151.2 3.3 %collective-permute-start.9 = (bf16[1024,384]{1,0:T(8,128)(2,1)S(1)}, bf16[1024,384]{1,0:T(8,128)(2,1)S(1)}, u32[]{:S(2)}, u32[]{:S(2)}) collective-permute-start(bf16[1024,384]{1,0:T(8,128)(2,1)S(1)} %bitcast.6), channel_id=1, source_target_pairs={{0,8},{8,0},{1,9},{9,1},{2,10},{10,2},{3,11},{11,3},{4,12},{12,4},... | collective-permute-start | bytes 2359304 | tf_op jit(solution)/shard_map/gather_plane/ppermute | solution.py:233
  154.6 1.9 %collective-permute-done.9 = bf16[1024,384]{1,0:T(8,128)(2,1)S(1)} collective-permute-done((bf16[1024,384]{1,0:T(8,128)(2,1)S(1)}, bf16[1024,384]{1,0:T(8,128)(2,1)S(1)}, u32[]{:S(2)}, u32[]{:S(2)}) %collective-permute-start.9) | collective-permute-done | bytes 786464 | tf_op jit(solution)/shard_map/gather_plane/ppermute | solution.py:233
  156.5 2.3 %finish.1 = (f32[768,768]{1,0:T(8,128)}, f32[1,768]{1,0:T(1,128)S(1)}) custom-call(s32[2]{0:T(128)S(1)} %pad_add_fusion.place, bf16[16,64,384]{2,1,0:T(8,128)(2,1)S(1)} %all_to_all.34.own, bf16[16,64,384]{2,1,0:T(8,128)(2,1)S(1)} %bitcast.8), custom_call_target="tpu_custom_call" | custom-call | tf_op jit(solution)/shard_map/finish/pallas_call | solution.py:235
  158.7 0.6 reduce
  (17 shorter events, 0.1 us)
Async XLA Ops:
  0.6 1.1 copy-start
  1.8 16.7 %collective-permute-start = (bf16[256,768]{1,0:T(8,128)(2,1)S(1)}, bf16[256,768]{1,0:T(8,128)(2,1)S(1)}, u32[]{:S(2)}, u32[]{:S(2)}) collective-permute-start(bf16[256,768]{1,0:T(8,128)(2,1)S(1)} %constant_dynamic-slice_fusion), channel_id=1, source_target_pairs={{0,0},{1,8},{2,16},{3,24},{4,32},{5,40},{6,48},{7,56},{8,64},{9,72... | collective-permute-start | bytes 1179656 | tf_op jit(solution)/shard_map/spread_features/ppermute | solution.py:186
  18.5 35.9 %collective-permute-start.6 = (bf16[256,768]{1,0:T(8,128)(2,1)S(1)}, bf16[256,768]{1,0:T(8,128)(2,1)S(1)}, u32[]{:S(2)}, u32[]{:S(2)}) collective-permute-start(bf16[256,768]{1,0:T(8,128)(2,1)S(1)} %collective-permute-done.rest_0_), channel_id=1, source_target_pairs={{0,192},{64,0},{128,64},{192,128},{1,193},{65,1},{129,65},{193,129... | collective-permute-start | bytes 1179656 | tf_op jit(solution)/shard_map/spread_features/ppermute | solution.py:187
  38.3 19.2 %collective-permute-start.4 = (bf16[256,768]{1,0:T(8,128)(2,1)S(1)}, bf16[256,768]{1,0:T(8,128)(2,1)S(1)}, u32[]{:S(2)}, u32[]{:S(2)}) collective-permute-start(bf16[256,768]{1,0:T(8,128)(2,1)S(1)} %collective-permute-done.rest_0_), channel_id=1, source_target_pairs={{0,128},{64,192},{128,0},{192,64},{1,129},{65,193},{129,1},{193,65... | collective-permute-start | bytes 1179656 | tf_op jit(solution)/shard_map/spread_features/ppermute | solution.py:187
  47.9 18.0 %collective-permute-start.2 = (bf16[256,768]{1,0:T(8,128)(2,1)S(1)}, bf16[256,768]{1,0:T(8,128)(2,1)S(1)}, u32[]{:S(2)}, u32[]{:S(2)}) collective-permute-start(bf16[256,768]{1,0:T(8,128)(2,1)S(1)} %collective-permute-done.rest_0_), channel_id=1, source_target_pairs={{0,64},{64,128},{128,192},{192,0},{1,65},{65,129},{129,193},{193,1... | collective-permute-start | bytes 1179656 | tf_op jit(solution)/shard_map/spread_features/ppermute | solution.py:187
  47.9 18.6 %collective-permute-start.1 = (bf16[256,768]{1,0:T(8,128)(2,1)S(1)}, bf16[256,768]{1,0:T(8,128)(2,1)S(1)}, u32[]{:S(2)}, u32[]{:S(2)}) collective-permute-start(bf16[256,768]{1,0:T(8,128)(2,1)S(1)} %collective-permute-done.rest_0_), channel_id=1, source_target_pairs={{0,8},{8,0},{1,9},{9,1},{2,10},{10,2},{3,11},{11,3},{4,12},{12,4},... | collective-permute-start | bytes 1179656 | tf_op jit(solution)/shard_map/spread_features/ppermute | solution.py:188
  54.4 12.0 %collective-permute-start.7 = (bf16[256,768]{1,0:T(8,128)(2,1)S(1)}, bf16[256,768]{1,0:T(8,128)(2,1)S(1)}, u32[]{:S(2)}, u32[]{:S(2)}) collective-permute-start(bf16[256,768]{1,0:T(8,128)(2,1)S(1)} %collective-permute-done.6.rest_6_), channel_id=1, source_target_pairs={{0,8},{8,0},{1,9},{9,1},{2,10},{10,2},{3,11},{11,3},{4,12},{12,4},... | collective-permute-start | bytes 1179656 | tf_op jit(solution)/shard_map/spread_features/ppermute | solution.py:188
  57.5 9.0 %collective-permute-start.5 = (bf16[256,768]{1,0:T(8,128)(2,1)S(1)}, bf16[256,768]{1,0:T(8,128)(2,1)S(1)}, u32[]{:S(2)}, u32[]{:S(2)}) collective-permute-start(bf16[256,768]{1,0:T(8,128)(2,1)S(1)} %collective-permute-done.4.rest_4_), channel_id=1, source_target_pairs={{0,8},{8,0},{1,9},{9,1},{2,10},{10,2},{3,11},{11,3},{4,12},{12,4},... | collective-permute-start | bytes 1179656 | tf_op jit(solution)/shard_map/spread_features/ppermute | solution.py:188
  65.9 2.0 %collective-permute-start.3 = (bf16[256,768]{1,0:T(8,128)(2,1)S(1)}, bf16[256,768]{1,0:T(8,128)(2,1)}, u32[]{:S(2)}, u32[]{:S(2)}) collective-permute-start(bf16[256,768]{1,0:T(8,128)(2,1)S(1)} %collective-permute-done.2.rest_2_), channel_id=1, source_target_pairs={{0,8},{8,0},{1,9},{9,1},{2,10},{10,2},{3,11},{11,3},{4,12},{12,4},... | collective-permute-start | bytes 1179656 | tf_op jit(solution)/shard_map/spread_features/ppermute | solution.py:188
  66.4 17.4 %copy-start.6 = (f32[768]{0:T(1024)S(1)}, f32[768]{0:T(1024)}, u32[]{:S(2)}) copy-start(f32[768]{0:T(1024)} %param.12) | copy-start | bytes 9220
  67.9 1.6 copy-start.1
  69.5 0.7 copy-start.4
  70.2 0.7 copy-start.5
  76.0 19.8 %copy-start.2 = (bf16[768,768]{1,0:T(8,128)(2,1)S(1)}, bf16[768,768]{1,0:T(8,128)(2,1)}, u32[]{:S(2)}) copy-start(bf16[768,768]{1,0:T(8,128)(2,1)} %weight.1) | copy-start | bytes 3538948
  76.1 19.8 %all-to-all-start = ((bf16[8,64,768]{2,1,0:T(8,128)(2,1)}), bf16[8,64,768]{2,1,0:T(8,128)(2,1)S(1)}, u32[]{:S(2)}, u32[]{:S(2)}) async-start(bf16[8,64,768]{2,1,0:T(8,128)(2,1)} %bitcast.2), calls=%async_computation | async-start | bytes 1572864 | tf_op jit(solution)/shard_map/sum_over_rep/all_to_all | solution.py:199
  95.8 0.9 copy-start.3
  113.6 4.3 %collective-permute-start.8 = (bf16[64,384]{1,0:T(8,128)(2,1)S(1)}, bf16[64,384]{1,0:T(8,128)(2,1)S(1)}, u32[]{:S(2)}, u32[]{:S(2)}) collective-permute-start(bf16[64,384]{1,0:T(8,128)(2,1)S(1)} %get-tuple-element.12), channel_id=1, source_target_pairs={{0,8},{8,0},{1,9},{9,1},{2,10},{10,2},{3,11},{11,3},{4,12},{12,4},... | collective-permute-start | bytes 147464 | tf_op jit(solution)/shard_map/weight_block/ppermute | solution.py:216
  151.2 5.3 %collective-permute-start.9 = (bf16[1024,384]{1,0:T(8,128)(2,1)S(1)}, bf16[1024,384]{1,0:T(8,128)(2,1)S(1)}, u32[]{:S(2)}, u32[]{:S(2)}) collective-permute-start(bf16[1024,384]{1,0:T(8,128)(2,1)S(1)} %bitcast.6), channel_id=1, source_target_pairs={{0,8},{8,0},{1,9},{9,1},{2,10},{10,2},{3,11},{11,3},{4,12},{12,4},... | collective-permute-start | bytes 2359304 | tf_op jit(solution)/shard_map/gather_plane/ppermute | solution.py:233

commit v2 on v1

--- a/solution.py
+++ b/solution.py
@@ -14,6 +14,7 @@
 ZAXIS = ("zh", "zl")
 BF = jnp.bfloat16
 F32 = jnp.float32
+BACK = (0, 1, 3, 2)
 VMEM_LIMIT = 48 * 1024 * 1024
 
 
@@ -37,46 +38,62 @@
     return [(i, (i + k) % n) for i in range(n)]
 
 
+ROUTES = (
+    (20, 7, 27, 6, 10, 28, 15, 2, 26, 14, 13, 19, 11, 25, 31, 18, 29, 16, 30, 12, 22, 1, 8, 5, 9, 3, 0, 17, 4, 23, 24, 21),
+    (5, 8, 0, 1, 16, 31, 25, 28, 24, 29, 30, 12, 27, 15, 6, 17, 18, 23, 26, 21, 9, 20, 19, 10, 3, 14, 11, 22, 2, 4, 7, 13),
+)
+
+
 def first_hop():
-    pairs = []
-    for target in range(int(np.prod(SIZES))):
-        y, zh, core, x, zl = (int(v) for v in np.unravel_index(target, SIZES))
-        source = (x, 2 * zl + y // 2, y % 2, (x + zh) % 4, core)
-        pairs.append((int(np.ravel_multi_index(source, SIZES)), target))
-    return sorted(pairs)
-
-
-def aggregate_kernel(place, cols, live, tiles, *rest):
-    parts, out, feat, sems = rest[:8], rest[8], rest[9], rest[10]
-    copies = [
-        pltpu.make_async_copy(part, feat.at[pl.ds(i * 256, 256)], sems.at[i])
-        for i, part in enumerate(parts)
-    ]
-    for copy in copies:
-        copy.start()
-    for copy in copies:
-        copy.wait()
-    y, core = place[0], place[1]
+    pairs, sends = [], np.zeros(SIZES, np.int32)
+    piece = np.zeros(SIZES, np.int32)
+    count = {}
+    for zl in range(2):
+        for at, pick in enumerate(ROUTES[zl]):
+            v, zh, core = np.unravel_index(at, (4, 4, 2))
+            u, a, b, zz = np.unravel_index(pick, (4, 2, 2, 2))
+            for x in range(4):
+                target = ((x + v) % 4, zh, core, x, zl)
+                source = (x, 2 * zl + a, b, (x + u) % 4, zz)
+                key = (x, zh, zl, 2 * a + b)
+                half = count.get(key, 0)
+                count[key] = half + 1
+                piece[target] = 2 * (2 * a + b) + half
+                sends[source] = half
+                pairs.append((int(np.ravel_multi_index(source, SIZES)), int(np.ravel_multi_index(target, SIZES))))
+    slots = np.zeros(SIZES + (8,), np.int32)
+    for at in np.ndindex(*SIZES):
+        y, zh, core, x, zl = at
+        for i, back in enumerate(BACK):
+            for c in range(2):
+                slots[at + (piece[(y - back) % 4, zh, (core + c) % 2, x, zl],)] = 2 * i + c
+    return sorted(pairs), sends.reshape(-1), slots.reshape(-1, 8)
+
+
+def spread_kernel(slots, cols, live, tiles, out):
     for b in range(4):
-        total = jnp.zeros((128, 768), F32)
         for s in range(4):
-            back = lax.rem(y - s + 4, 4)
-            for pair in range(2):
-                lhs, rhs = [], []
-                for k in (2 * pair, 2 * pair + 1):
-                    c = cols[b, s, k]
-                    half = c // 2
-                    away = lax.rem(half + core, 2)
-                    row = (2 * back + away) * 256 + lax.rem(c, 2) * 128
-                    rhs.append(feat[pl.ds(pl.multiple_of(row, 128), 128), :])
-                    tile = tiles[b, s, k]
-                    lhs.append(jnp.where(live[b, s, k] != 0, tile, jnp.zeros_like(tile)))
-                total = total + jnp.dot(
-                    jnp.concatenate(lhs, axis=1),
-                    jnp.concatenate(rhs, axis=0),
-                    preferred_element_type=F32,
-                )
-        out[pl.ds(b * 128, 128), :] = total.astype(BF)
+            picks = [jnp.where(live[b, s, k] != 0, cols[b, s, k], -1) for k in range(4)]
+            parts = [tiles[b, s, k].astype(F32) for k in range(4)]
+            for c in range(4):
+                total = jnp.zeros((128, 128), F32)
+                for pick, part in zip(picks, parts):
+                    total = total + jnp.where(pick == c, part, 0.0)
+                slot = slots[2 * s + c // 2]
+                out[slot, pl.ds(b * 128, 128), pl.ds((c % 2) * 128, 128)] = total.astype(BF)
+
+
+def first_terms_kernel(mix, one, two, out):
+    out[...] = jnp.dot(mix[0], one[...], preferred_element_type=F32)
+    out[...] += jnp.dot(mix[1], two[...], preferred_element_type=F32)
+
+
+def rest_kernel(mix, begun, *rest):
+    parts, out, total = rest[:6], rest[6], rest[7]
+    total[...] = begun[...]
+    for i, part in enumerate(parts):
+        total[...] += jnp.dot(mix[2 + i], part[...], preferred_element_type=F32)
+    out[...] = total[...].astype(BF)
 
 
 def layer_kernel(recv, weight, bias, cot, out, packed):
@@ -100,7 +117,7 @@
 def with_bias(block, row):
     high = row.astype(BF).astype(F32)
     low = row - high
-    at = lax.broadcasted_iota(jnp.int32, (16, 384), 0)
+    at = lax.broadcasted_iota(jnp.int32, (8, 384), 0)
     extra = jnp.where(at == 0, high, jnp.where(at == 1, low, 0.0))
     return jnp.concatenate([block, extra], axis=0)
 
@@ -155,13 +172,8 @@
                 )
                 start = pl.multiple_of(i * 192 + at * 96 + h * 48, 16)
                 grad[pl.ds(start, 48), :] = rows
-    bias[...] = jnp.concatenate(
-        [
-            own[j, 48:64, :].astype(F32)[0:1, :192] + own[j, 48:64, :].astype(F32)[1:2, :192]
-            for j in range(4)
-        ],
-        axis=1,
-    )
+    rows = [own[j].astype(F32) for j in range(4)]
+    bias[...] = jnp.concatenate([row[48:49, :192] + row[49:50, :192] for row in rows], axis=1)
 
 
 def call(kernel, shapes, specs, out_specs, scratch=()):
@@ -181,20 +193,39 @@
 
 def on_device(features, tiles, tile_cols, tile_mask, weight, bias, cotangent):
     place = jnp.stack([lax.axis_index("y"), lax.axis_index("core")]).astype(jnp.int32)
+    pairs, sends, slots = first_hop()
+    me = lax.axis_index(AXES)
     with jax.named_scope("spread_features"):
-        half = lax.dynamic_slice_in_dim(features, lax.axis_index("zl") * 256, 256, 0)
-        own = lax.ppermute(half, AXES, first_hop())
-        parts = [own] + [lax.ppermute(own, "y", shift(4, k)) for k in (1, 2, 3)]
+        start = lax.dynamic_index_in_dim(jnp.asarray(sends * 256), me, 0, keepdims=False)
+        half = lax.dynamic_slice_in_dim(features, start, 256, 0)
+        own = lax.ppermute(half, AXES, pairs)
+    with jax.named_scope("spread_tiles"):
+        mix = call(
+            spread_kernel,
+            struct((8, 512, 256), BF),
+            [smem(), smem(), smem(), vmem()],
+            vmem(),
+        )(lax.dynamic_index_in_dim(jnp.asarray(slots), me, 0, keepdims=False), tile_cols, tile_mask, tiles)
+    own, mix = lax.optimization_barrier((own, mix))
+    with jax.named_scope("spread_features"):
+        parts = [lax.ppermute(own, "y", shift(4, back)) for back in BACK[1:]]
+        own_swapped = lax.ppermute(own, "core", shift(2, 1))
+    with jax.named_scope("aggregate"):
+        begun = call(first_terms_kernel, struct((512, 768), F32), [vmem()] * 3, vmem())(
+            mix, own, own_swapped
+        )
+    parts[0], begun = lax.optimization_barrier((parts[0], begun))
+    with jax.named_scope("spread_features"):
         swapped = [lax.ppermute(part, "core", shift(2, 1)) for part in parts]
         blocks = [block for pair in zip(parts, swapped) for block in pair]
     with jax.named_scope("aggregate"):
         partial = call(
-            aggregate_kernel,
+            rest_kernel,
             struct((512, 768), BF),
-            [smem(), smem(), smem(), vmem()] + [anyspace()] * 8,
-            vmem(),
-            [pltpu.VMEM((2048, 768), BF), pltpu.SemaphoreType.DMA((8,))],
-        )(place, tile_cols, tile_mask, tiles, *blocks)
+            [vmem()] * 8,
+            vmem(),
+            [pltpu.VMEM((512, 768), F32)],
+        )(mix, begun, *blocks)
     with jax.named_scope("sum_over_rep"):
         recv = lax.all_to_all(partial, REP, 0, 0, tiled=True).reshape(8, 64, 768)
     with jax.named_scope("layer"):
@@ -209,27 +240,27 @@
     with jax.named_scope("weight_block"):
         keep, send = call(
             block_kernel,
-            (struct((64, 384), F32), struct((64, 384), BF)),
+            (struct((56, 384), F32), struct((56, 384), BF)),
             [smem(), vmem()],
             (vmem(), vmem()),
         )(place, rows)
         other = lax.ppermute(send, "core", shift(2, 1))
         pair = call(
             lambda *refs: pair_kernel(8, *refs),
-            struct((8, 64, 384), BF),
+            struct((8, 56, 384), BF),
             [vmem()] * 2,
             vmem(),
         )(keep, other)
     with jax.named_scope("sum_over_z"):
-        chain = lax.all_to_all(pair.reshape(512, 384), ZAXIS, 0, 0, tiled=True)
+        chain = lax.all_to_all(pair.reshape(448, 384), ZAXIS, 0, 0, tiled=True)
         whole = call(
             lambda *refs: sum_kernel(16, *refs),
-            struct((16, 64, 384), BF),
+            struct((16, 56, 384), BF),
             [vmem()],
             vmem(),
-        )(chain.reshape(8, 64, 384))
+        )(chain.reshape(8, 56, 384))
     with jax.named_scope("gather_plane"):
-        mine = lax.all_to_all(whole.reshape(1024, 384), PLANE, 0, 0, tiled=True)
+        mine = lax.all_to_all(whole.reshape(896, 384), PLANE, 0, 0, tiled=True)
         theirs = lax.ppermute(mine, "core", shift(2, 1))
     with jax.named_scope("finish"):
         grad_weight, grad_bias = call(
@@ -237,7 +268,7 @@
             (struct((768, 768), F32), struct((1, 768), F32)),
             [smem(), vmem(), vmem()],
             (vmem(), vmem()),
-        )(place, mine.reshape(16, 64, 384), theirs.reshape(16, 64, 384))
+        )(place, mine.reshape(16, 56, 384), theirs.reshape(16, 56, 384))
     return output, grad_weight, grad_bias.reshape(768)
 
 

time: 160 us -> 143 us (0.89)
  blocking collectives: 47.7 us -> 34.2 us
  starting transfers between devices: 57.5 us -> 46.8 us
  waiting for transfers between devices: 37.8 us -> 41.9 us
  between operations: 0.73 us -> 2.72 us
  Pallas kernels: 9.87 us -> 11.5 us
    all_to_all x3 -> x2, blocking collectives: 47.7 us -> 34.2 us  [the longest x1 20.5 us: on_device(): chain = lax.all_to_all(pair.reshape(448, 384), ZAXIS, 0, 0, tiled=True)]
    all_to_all x0 -> x1, waiting for transfers between devices: none -> 12.4 us  [on_device(): rows = lax.all_to_all(packed.reshape(1024, 384), PLANE, 0, 0, tiled=True)]
    ppermute x4 -> x5, waiting for transfers between devices: 21.6 us -> 13.5 us  [the longest x3 13.5 us: on_device(): parts = [lax.ppermute(own, 'y', shift(4, back)) for back in BACK[1:]]]
    ppermute x4 -> x3, starting transfers between devices: 8.99 us -> 2.92 us  [on_device(): swapped = [lax.ppermute(part, 'core', shift(2, 1)) for part in parts]]
    ppermute x4 -> x5, starting transfers between devices: 34 us -> 28.3 us  [the longest x3 15 us: on_device(): parts = [lax.ppermute(own, 'y', shift(4, back)) for back in BACK[1:]]]
    all_to_all x0 -> x1, starting transfers between devices: none -> 4.09 us  [on_device(): rows = lax.all_to_all(packed.reshape(1024, 384), PLANE, 0, 0, tiled=True)]
    all_to_all x1, starting transfers between devices: 7.75 us -> 5.39 us  [on_device(): recv = lax.all_to_all(partial, REP, 0, 0, tiled=True).reshape(8, 64, 768)]
    unnamed x14 -> x16, local copies, waits for them, and re-layouts: 5.01 us -> 3.02 us
  transfers between devices with their start and end apart: 11 -> 12, of which waited for: 7 -> 8; matrix products, arithmetic and copies ran while one was open for 0% -> 1% of each run, Pallas kernels for 0% -> 2%
where the time goes in v2:
time: 143 us
  starting transfers between devices  46.8 us (33%)
  waiting for transfers between devices  41.9 us (29%)
  blocking collectives  34.2 us (24%)
  Pallas kernels  11.5 us (8%)
  local copies, waits for them, and re-layouts  5.09 us (4%)
  between operations  2.72 us (2%)
    all_to_all x1, blocking collectives, on_device(): chain = lax.all_to_all(pair.reshape(448, 384), ZAXIS, 0, 0, tiled=True)  20.5 us
    ppermute x3, starting transfers between devices, on_device(): parts = [lax.ppermute(own, 'y', shift(4, back)) for back in BACK[1:]]  15 us
    all_to_all x1, blocking collectives, on_device(): mine = lax.all_to_all(whole.reshape(896, 384), PLANE, 0, 0, tiled=True)  13.8 us
    ppermute x3, waiting for transfers between devices, on_device(): parts = [lax.ppermute(own, 'y', shift(4, back)) for back in BACK[1:]]  13.5 us
    all_to_all x1, waiting for transfers between devices, on_device(): rows = lax.all_to_all(packed.reshape(1024, 384), PLANE, 0, 0, tiled=True)  12.4 us
    all_to_all x1, waiting for transfers between devices, on_device(): recv = lax.all_to_all(partial, REP, 0, 0, tiled=True).reshape(8, 64, 768)  12 us
    ppermute x1, starting transfers between devices, on_device(): own = lax.ppermute(half, AXES, pairs)  8.76 us
    all_to_all x1, starting transfers between devices, on_device(): recv = lax.all_to_all(partial, REP, 0, 0, tiled=True).reshape(8, 64, 768)  5.39 us
  transfers between devices with their start and end apart: 12, of which 8 were waited for; matrix products, arithmetic and copies ran while one was open for 1% of the time, Pallas kernels for 2%

profile of v2, /device:TPU:1, one launch (start us, length us, event | category | flops | bytes accessed | tf_op | source)
XLA Modules:
  0.0 142.9 jit_solution(17412866335990097271)
XLA Ops:
  0.7 1.3 dynamic_slice.11
  4.0 8.8 %collective-permute-start = (bf16[256,768]{1,0:T(8,128)(2,1)S(1)}, bf16[256,768]{1,0:T(8,128)(2,1)S(1)}, u32[]{:S(2)}, u32[]{:S(2)}) collective-permute-start(bf16[256,768]{1,0:T(8,128)(2,1)S(1)} %constant_dynamic-slice_fusion), channel_id=1, source_target_pairs={{0,208},{1,168},{2,176},{3,192},{4,136},{5,216},{6,240},{7,104},{8... | collective-permute-start | bytes 1179656 | tf_op jit(solution)/shard_map/spread_features/ppermute | solution.py:201
  12.8 0.7 dynamic-slice_bitcast_fusion.slots
  13.5 1.6 %copy-done.2 = bf16[4,4,4,128,128]{4,3,2,1,0:T(8,128)(2,1)S(1)} copy-done((bf16[4,4,4,128,128]{4,3,2,1,0:T(8,128)(2,1)S(1)}, bf16[4,4,4,128,128]{4,3,2,1,0:T(8,128)(2,1)}, u32[]{:S(2)}) %copy-start.2) | copy-done | bytes 2097176
  15.1 0.7 copy-done.5
  15.7 0.7 copy-done.6
  16.4 2.1 %spread_tiles.1.mix = bf16[8,512,256]{2,1,0:T(8,128)(2,1)S(1)} custom-call(s32[8]{0:T(128)S(1)} %dynamic-slice_bitcast_fusion.slots, s32[4,4,4]{2,1,0:T(4,128)S(1)} %copy-done.5, s32[4,4,4]{2,1,0:T(4,128)S(1)} %copy-done.6, bf16[4,4,4,128,128]{4,3,2,1,0:T(8,128)(2,1)S(1)} %copy-done.2), custom_call_target="tpu_custom_call" | custom-call | tf_op jit(solution)/shard_map/spread_tiles/pallas_call | solution.py:203
  18.6 4.5 %collective-permute-start.2 = (bf16[256,768]{1,0:T(8,128)(2,1)S(1)}, bf16[256,768]{1,0:T(8,128)(2,1)S(1)}, u32[]{:S(2)}, u32[]{:S(2)}) collective-permute-start(bf16[256,768]{1,0:T(8,128)(2,1)S(1)} %collective-permute-done.one), channel_id=1, source_target_pairs={{0,8},{8,0},{1,9},{9,1},{2,10},{10,2},{3,11},{11,3},{4,12},{12,4},... | collective-permute-start | bytes 1179656 | tf_op jit(solution)/shard_map/spread_features/ppermute | solution.py:212
  23.1 5.5 %collective-permute-start.1 = (bf16[256,768]{1,0:T(8,128)(2,1)S(1)}, bf16[256,768]{1,0:T(8,128)(2,1)S(1)}, u32[]{:S(2)}, u32[]{:S(2)}) collective-permute-start(bf16[256,768]{1,0:T(8,128)(2,1)S(1)} %collective-permute-done.one), channel_id=1, source_target_pairs={{0,64},{64,128},{128,192},{192,0},{1,65},{65,129},{129,193},{193,1... | collective-permute-start | bytes 1179656 | tf_op jit(solution)/shard_map/spread_features/ppermute | solution.py:211
  28.6 9.5 %collective-permute-start.6 = (bf16[256,768]{1,0:T(8,128)(2,1)S(1)}, bf16[256,768]{1,0:T(8,128)(2,1)S(1)}, u32[]{:S(2)}, u32[]{:S(2)}) collective-permute-start(bf16[256,768]{1,0:T(8,128)(2,1)S(1)} %collective-permute-done.one), channel_id=1, source_target_pairs={{0,128},{64,192},{128,0},{192,64},{1,129},{65,193},{129,1},{193,65... | collective-permute-start | bytes 1179656 | tf_op jit(solution)/shard_map/spread_features/ppermute | solution.py:211
  38.7 1.0 collective-permute-done.1.rest_0_
  39.8 1.2 collective-permute-start.3
  40.9 4.7 %collective-permute-done.4.rest_2_ = bf16[256,768]{1,0:T(8,128)(2,1)S(1)} collective-permute-done((bf16[256,768]{1,0:T(8,128)(2,1)S(1)}, bf16[256,768]{1,0:T(8,128)(2,1)S(1)}, u32[]{:S(2)}, u32[]{:S(2)}) %collective-permute-start.4) | collective-permute-done | bytes 393248 | tf_op jit(solution)/shard_map/spread_features/ppermute | solution.py:211
  45.6 1.2 collective-permute-start.5
  46.8 7.8 %collective-permute-done.6.rest_4_ = bf16[256,768]{1,0:T(8,128)(2,1)S(1)} collective-permute-done((bf16[256,768]{1,0:T(8,128)(2,1)S(1)}, bf16[256,768]{1,0:T(8,128)(2,1)S(1)}, u32[]{:S(2)}, u32[]{:S(2)}) %collective-permute-start.6) | collective-permute-done | bytes 393248 | tf_op jit(solution)/shard_map/spread_features/ppermute | solution.py:211
  54.6 0.6 collective-permute-start.7
  55.1 1.3 collective-permute-done.7.rest_5_
  56.5 3.9 %aggregate.3 = bf16[512,768]{1,0:T(8,128)(2,1)} custom-call(bf16[8,512,256]{2,1,0:T(8,128)(2,1)} %copy-done.1, f32[512,768]{1,0:T(8,128)S(1)} %aggregate.2.begun, bf16[256,768]{1,0:T(8,128)(2,1)S(1)} %collective-permute-done.1.rest_0_, bf16[256,768]{1,0:T(8,128)(2,1)S(1)} %collective-permute-done.3.rest_1_, ...), custom_call_target="tpu_custom_call" | custom-call | tf_op jit(solution)/shard_map/aggregate/pallas_call | solution.py:222
  60.4 5.4 %all-to-all-start = ((bf16[8,64,768]{2,1,0:T(8,128)(2,1)}), bf16[8,64,768]{2,1,0:T(8,128)(2,1)S(1)}, u32[]{:S(2)}, u32[]{:S(2)}) async-start(bf16[8,64,768]{2,1,0:T(8,128)(2,1)} %bitcast.2), calls=%async_computation | async-start | bytes 1572864 | tf_op jit(solution)/shard_map/sum_over_rep/all_to_all | solution.py:230
  65.8 12.0 %all-to-all-done.recv = bf16[8,64,768]{2,1,0:T(8,128)(2,1)S(1)} async-done(((bf16[8,64,768]{2,1,0:T(8,128)(2,1)}), bf16[8,64,768]{2,1,0:T(8,128)(2,1)S(1)}, u32[]{:S(2)}, u32[]{:S(2)}) %all-to-all-start) | async-done | bytes 786464 | tf_op jit(solution)/shard_map/sum_over_rep/all_to_all | solution.py:230
  77.8 1.4 layer.1
  79.1 4.1 %all-to-all-start.1 = ((bf16[16,64,384]{2,1,0:T(8,128)(2,1)}), bf16[16,64,384]{2,1,0:T(8,128)(2,1)S(1)}, u32[]{:S(2)}, u32[]{:S(2)}) async-start(bf16[16,64,384]{2,1,0:T(8,128)(2,1)} %get-tuple-element.18), calls=%async_computation.1 | async-start | bytes 1572864 | tf_op jit(solution)/shard_map/exchange_rows/all_to_all | solution.py:239
  83.3 12.4 %all-to-all-done.1 = bf16[16,64,384]{2,1,0:T(8,128)(2,1)S(1)} async-done(((bf16[16,64,384]{2,1,0:T(8,128)(2,1)}), bf16[16,64,384]{2,1,0:T(8,128)(2,1)S(1)}, u32[]{:S(2)}, u32[]{:S(2)}) %all-to-all-start.1) | async-done | bytes 786464 | tf_op jit(solution)/shard_map/exchange_rows/all_to_all | solution.py:239
  95.7 1.3 weight_block.2
  96.9 2.9 %collective-permute-start.8 = (bf16[56,384]{1,0:T(8,128)(2,1)S(1)}, bf16[56,384]{1,0:T(8,128)(2,1)S(1)}, u32[]{:S(2)}, u32[]{:S(2)}) collective-permute-start(bf16[56,384]{1,0:T(8,128)(2,1)S(1)} %get-tuple-element.20), channel_id=1, source_target_pairs={{0,8},{8,0},{1,9},{9,1},{2,10},{10,2},{3,11},{11,3},{4,12},{12,4},... | collective-permute-start | bytes 129032 | tf_op jit(solution)/shard_map/weight_block/ppermute | solution.py:247
  99.8 0.9 collective-permute-done.8.refs_1_
  100.8 20.5 %all_to_all.32.refs_0_ = bf16[8,56,384]{2,1,0:T(8,128)(2,1)S(1)} all-to-all(bf16[8,56,384]{2,1,0:T(8,128)(2,1)S(1)} %weight_block.3), channel_id=1, replica_groups=mesh['y'=4,'zh'=4,'core'=2,'x'=4,'zl'=2] {'zh','zl'}, dimensions={0} | all-to-all | bytes 688128 | tf_op jit(solution)/shard_map/sum_over_z/all_to_all | solution.py:255
  121.3 13.8 %all_to_all.33.own = bf16[16,56,384]{2,1,0:T(8,128)(2,1)S(1)} all-to-all(bf16[16,56,384]{2,1,0:T(8,128)(2,1)S(1)} %sum_over_z.1), channel_id=1, replica_groups=mesh['y'=4,'zh'=4,'core'=2,'x'=4,'zl'=2] {'x','y'}, dimensions={0} | all-to-all | bytes 1376256 | tf_op jit(solution)/shard_map/gather_plane/all_to_all | solution.py:263
  135.1 3.2 %collective-permute-start.9 = (bf16[896,384]{1,0:T(8,128)(2,1)S(1)}, bf16[896,384]{1,0:T(8,128)(2,1)S(1)}, u32[]{:S(2)}, u32[]{:S(2)}) collective-permute-start(bf16[896,384]{1,0:T(8,128)(2,1)S(1)} %bitcast.10), channel_id=1, source_target_pairs={{0,8},{8,0},{1,9},{9,1},{2,10},{10,2},{3,11},{11,3},{4,12},{12,4},... | collective-permute-start | bytes 2064392 | tf_op jit(solution)/shard_map/gather_plane/ppermute | solution.py:264
  138.3 1.8 %collective-permute-done.9 = bf16[896,384]{1,0:T(8,128)(2,1)S(1)} collective-permute-done((bf16[896,384]{1,0:T(8,128)(2,1)S(1)}, bf16[896,384]{1,0:T(8,128)(2,1)S(1)}, u32[]{:S(2)}, u32[]{:S(2)}) %collective-permute-start.9) | collective-permute-done | bytes 688160 | tf_op jit(solution)/shard_map/gather_plane/ppermute | solution.py:264
  140.0 2.3 %finish.1 = (f32[768,768]{1,0:T(8,128)}, f32[1,768]{1,0:T(1,128)S(1)}) custom-call(s32[2]{0:T(128)S(1)} %pad_add_fusion.place, bf16[16,56,384]{2,1,0:T(8,128)(2,1)S(1)} %all_to_all.33.own, bf16[16,56,384]{2,1,0:T(8,128)(2,1)S(1)} %bitcast.11), custom_call_target="tpu_custom_call" | custom-call | tf_op jit(solution)/shard_map/finish/pallas_call | solution.py:266
  142.3 0.6 reduce
  (24 shorter events, 0.8 us)
Async XLA Ops:
  0.6 3.3 %copy-start = (bf16[512,768]{1,0:T(8,128)(2,1)S(1)}, bf16[512,768]{1,0:T(8,128)(2,1)}, u32[]{:S(2)}) copy-start(bf16[512,768]{1,0:T(8,128)(2,1)} %param.9) | copy-start | bytes 2359300
  4.0 14.6 %collective-permute-start = (bf16[256,768]{1,0:T(8,128)(2,1)S(1)}, bf16[256,768]{1,0:T(8,128)(2,1)S(1)}, u32[]{:S(2)}, u32[]{:S(2)}) collective-permute-start(bf16[256,768]{1,0:T(8,128)(2,1)S(1)} %constant_dynamic-slice_fusion), channel_id=1, source_target_pairs={{0,208},{1,168},{2,176},{3,192},{4,136},{5,216},{6,240},{7,104},{8... | collective-permute-start | bytes 1179656 | tf_op jit(solution)/shard_map/spread_features/ppermute | solution.py:201
  13.5 1.6 %copy-start.2 = (bf16[4,4,4,128,128]{4,3,2,1,0:T(8,128)(2,1)S(1)}, bf16[4,4,4,128,128]{4,3,2,1,0:T(8,128)(2,1)}, u32[]{:S(2)}) copy-start(bf16[4,4,4,128,128]{4,3,2,1,0:T(8,128)(2,1)} %tiles.1) | copy-start | bytes 6291460
  15.0 0.7 copy-start.5
  15.7 0.7 copy-start.6
  18.5 20.1 %copy-start.1 = (bf16[8,512,256]{2,1,0:T(8,128)(2,1)}, bf16[8,512,256]{2,1,0:T(8,128)(2,1)S(1)}, u32[]{:S(2)}) copy-start(bf16[8,512,256]{2,1,0:T(8,128)(2,1)S(1)} %spread_tiles.1.mix) | copy-start | bytes 6291460
  18.6 19.5 %collective-permute-start.2 = (bf16[256,768]{1,0:T(8,128)(2,1)S(1)}, bf16[256,768]{1,0:T(8,128)(2,1)S(1)}, u32[]{:S(2)}, u32[]{:S(2)}) collective-permute-start(bf16[256,768]{1,0:T(8,128)(2,1)S(1)} %collective-permute-done.one), channel_id=1, source_target_pairs={{0,8},{8,0},{1,9},{9,1},{2,10},{10,2},{3,11},{11,3},{4,12},{12,4},... | collective-permute-start | bytes 1179656 | tf_op jit(solution)/shard_map/spread_features/ppermute | solution.py:212
  23.1 16.6 %collective-permute-start.1 = (bf16[256,768]{1,0:T(8,128)(2,1)S(1)}, bf16[256,768]{1,0:T(8,128)(2,1)S(1)}, u32[]{:S(2)}, u32[]{:S(2)}) collective-permute-start(bf16[256,768]{1,0:T(8,128)(2,1)S(1)} %collective-permute-done.one), channel_id=1, source_target_pairs={{0,64},{64,128},{128,192},{192,0},{1,65},{65,129},{129,193},{193,1... | collective-permute-start | bytes 1179656 | tf_op jit(solution)/shard_map/spread_features/ppermute | solution.py:211
  28.6 17.0 %collective-permute-start.4 = (bf16[256,768]{1,0:T(8,128)(2,1)S(1)}, bf16[256,768]{1,0:T(8,128)(2,1)S(1)}, u32[]{:S(2)}, u32[]{:S(2)}) collective-permute-start(bf16[256,768]{1,0:T(8,128)(2,1)S(1)} %collective-permute-done.one), channel_id=1, source_target_pairs={{0,192},{64,0},{128,64},{192,128},{1,193},{65,1},{129,65},{193,129... | collective-permute-start | bytes 1179656 | tf_op jit(solution)/shard_map/spread_features/ppermute | solution.py:211
  28.6 25.9 %collective-permute-start.6 = (bf16[256,768]{1,0:T(8,128)(2,1)S(1)}, bf16[256,768]{1,0:T(8,128)(2,1)S(1)}, u32[]{:S(2)}, u32[]{:S(2)}) collective-permute-start(bf16[256,768]{1,0:T(8,128)(2,1)S(1)} %collective-permute-done.one), channel_id=1, source_target_pairs={{0,128},{64,192},{128,0},{192,64},{1,129},{65,193},{129,1},{193,65... | collective-permute-start | bytes 1179656 | tf_op jit(solution)/shard_map/spread_features/ppermute | solution.py:211
  38.7 27.1 %copy-start.7 = (f32[768]{0:T(1024)S(1)}, f32[768]{0:T(1024)}, u32[]{:S(2)}) copy-start(f32[768]{0:T(1024)} %param.14) | copy-start | bytes 9220
  38.7 39.1 %copy-start.4 = (bf16[64,768]{1,0:T(8,128)(2,1)S(1)}, bf16[64,768]{1,0:T(8,128)(2,1)}, u32[]{:S(2)}) copy-start(bf16[64,768]{1,0:T(8,128)(2,1)} %cot.1) | copy-start | bytes 294916
  39.8 15.4 %collective-permute-start.3 = (bf16[256,768]{1,0:T(8,128)(2,1)S(1)}, bf16[256,768]{1,0:T(8,128)(2,1)S(1)}, u32[]{:S(2)}, u32[]{:S(2)}) collective-permute-start(bf16[256,768]{1,0:T(8,128)(2,1)S(1)} %collective-permute-done.1.rest_0_), channel_id=1, source_target_pairs={{0,8},{8,0},{1,9},{9,1},{2,10},{10,2},{3,11},{11,3},{4,12},{12,4},... | collective-permute-start | bytes 1179656 | tf_op jit(solution)/shard_map/spread_features/ppermute | solution.py:219
  45.6 9.5 %collective-permute-start.5 = (bf16[256,768]{1,0:T(8,128)(2,1)S(1)}, bf16[256,768]{1,0:T(8,128)(2,1)S(1)}, u32[]{:S(2)}, u32[]{:S(2)}) collective-permute-start(bf16[256,768]{1,0:T(8,128)(2,1)S(1)} %collective-permute-done.4.rest_2_), channel_id=1, source_target_pairs={{0,8},{8,0},{1,9},{9,1},{2,10},{10,2},{3,11},{11,3},{4,12},{12,4},... | collective-permute-start | bytes 1179656 | tf_op jit(solution)/shard_map/spread_features/ppermute | solution.py:219
  54.6 1.9 %collective-permute-start.7 = (bf16[256,768]{1,0:T(8,128)(2,1)S(1)}, bf16[256,768]{1,0:T(8,128)(2,1)S(1)}, u32[]{:S(2)}, u32[]{:S(2)}) collective-permute-start(bf16[256,768]{1,0:T(8,128)(2,1)S(1)} %collective-permute-done.6.rest_4_), channel_id=1, source_target_pairs={{0,8},{8,0},{1,9},{9,1},{2,10},{10,2},{3,11},{11,3},{4,12},{12,4},... | collective-permute-start | bytes 1179656 | tf_op jit(solution)/shard_map/spread_features/ppermute | solution.py:219
  60.4 17.4 %copy-start.3 = (bf16[768,768]{1,0:T(8,128)(2,1)S(1)}, bf16[768,768]{1,0:T(8,128)(2,1)}, u32[]{:S(2)}) copy-start(bf16[768,768]{1,0:T(8,128)(2,1)} %weight.1) | copy-start | bytes 3538948
  60.4 17.4 %all-to-all-start = ((bf16[8,64,768]{2,1,0:T(8,128)(2,1)}), bf16[8,64,768]{2,1,0:T(8,128)(2,1)S(1)}, u32[]{:S(2)}, u32[]{:S(2)}) async-start(bf16[8,64,768]{2,1,0:T(8,128)(2,1)} %bitcast.2), calls=%async_computation | async-start | bytes 1572864 | tf_op jit(solution)/shard_map/sum_over_rep/all_to_all | solution.py:230
  79.1 16.5 %all-to-all-start.1 = ((bf16[16,64,384]{2,1,0:T(8,128)(2,1)}), bf16[16,64,384]{2,1,0:T(8,128)(2,1)S(1)}, u32[]{:S(2)}, u32[]{:S(2)}) async-start(bf16[16,64,384]{2,1,0:T(8,128)(2,1)} %get-tuple-element.18), calls=%async_computation.1 | async-start | bytes 1572864 | tf_op jit(solution)/shard_map/exchange_rows/all_to_all | solution.py:239
  96.9 3.8 %collective-permute-start.8 = (bf16[56,384]{1,0:T(8,128)(2,1)S(1)}, bf16[56,384]{1,0:T(8,128)(2,1)S(1)}, u32[]{:S(2)}, u32[]{:S(2)}) collective-permute-start(bf16[56,384]{1,0:T(8,128)(2,1)S(1)} %get-tuple-element.20), channel_id=1, source_target_pairs={{0,8},{8,0},{1,9},{9,1},{2,10},{10,2},{3,11},{11,3},{4,12},{12,4},... | collective-permute-start | bytes 129032 | tf_op jit(solution)/shard_map/weight_block/ppermute | solution.py:247
  135.1 5.0 %collective-permute-start.9 = (bf16[896,384]{1,0:T(8,128)(2,1)S(1)}, bf16[896,384]{1,0:T(8,128)(2,1)S(1)}, u32[]{:S(2)}, u32[]{:S(2)}) collective-permute-start(bf16[896,384]{1,0:T(8,128)(2,1)S(1)} %bitcast.10), channel_id=1, source_target_pairs={{0,8},{8,0},{1,9},{9,1},{2,10},{10,2},{3,11},{11,3},{4,12},{12,4},... | collective-permute-start | bytes 2064392 | tf_op jit(solution)/shard_map/gather_plane/ppermute | solution.py:264

commit v3 on v1

v3 whole, which is shorter than its diff:
```python
import jax
import jax.numpy as jnp
import numpy as np
from jax import lax
from jax.experimental import pallas as pl
from jax.experimental.pallas import tpu as pltpu
from jax.sharding import Mesh, PartitionSpec as P

AXES = ("y", "zh", "core", "x", "zl")
SIZES = (4, 4, 2, 4, 2)
DOM = ("y", "zh", "core")
REP = ("x", "zl")
PLANE = ("x", "y")
ZAXIS = ("zh", "zl")
BF = jnp.bfloat16
F32 = jnp.float32
BACK = (0, 1, 3, 2)
VMEM_LIMIT = 32 * 1024 * 1024

TURN = (((0, 1), (2, 1), (0, 3), (2, 3)), ((2, 3), (2, 3), (0, 1), (0, 1)))
OFFSET = (
    ((2, 1, 0, 3), (2, 3, 1, 0), (0, 3, 2, 1), (3, 1, 0, 2), (1, 0, 3, 2), (1, 2, 3, 0), (0, 2, 1, 3), (3, 0, 2, 1)),
    ((0, 2, 1, 3), (1, 2, 3, 0), (1, 3, 2, 0), (3, 0, 1, 2), (3, 2, 0, 1), (2, 0, 3, 1), (0, 1, 3, 2), (2, 0, 3, 1)),
)


def first_hop():
    pairs = []
    for target in np.ndindex(*SIZES):
        y, zh, core, x, zl = target
        s = (y - x + TURN[zl][zh][core]) % 4
        source = (x, 2 * zl + s // 2, s % 2, (x + OFFSET[zl][2 * s + core][zh]) % 4, core)
        pairs.append((int(np.ravel_multi_index(source, SIZES)), int(np.ravel_multi_index(target, SIZES))))
    return sorted(pairs)


def shift(n, k):
    return [(i, (i + k) % n) for i in range(n)]


def vmem():
    return pl.BlockSpec(memory_space=pltpu.VMEM)


def smem():
    return pl.BlockSpec(memory_space=pltpu.SMEM)


def hbm():
    return pl.BlockSpec(memory_space=pltpu.HBM)


def anyspace():
    return pl.BlockSpec(memory_space=pl.ANY)


def struct(shape, dtype):
    return jax.ShapeDtypeStruct(shape, dtype)


def call(kernel, shapes, specs, out_specs, scratch=(), aliases=None, flops=0):
    return pl.pallas_call(
        kernel,
        out_shape=shapes,
        in_specs=specs,
        out_specs=out_specs,
        scratch_shapes=scratch,
        input_output_aliases=aliases or {},
        compiler_params=pltpu.CompilerParams(vmem_limit_bytes=VMEM_LIMIT),
        cost_estimate=pl.CostEstimate(flops=flops, bytes_accessed=1 << 20, transcendentals=0),
    )


def pick_kernel(features, out, sem):
    start = pl.multiple_of(lax.axis_index("zl") * 384, 384)
    copy = pltpu.make_async_copy(features.at[:, pl.ds(start, 384)], out, sem)
    copy.start()
    copy.wait()


def spread_kernel(picks, other_picks, tiles, other_tiles, out):
    for d, (pick, tile) in enumerate(((picks, tiles), (other_picks, other_tiles))):
        for b in range(4):
            for s in range(4):
                parts = [tile[b, s, k].astype(F32) for k in range(4)]
                for c in range(4):
                    total = jnp.zeros((128, 128), F32)
                    for k in range(4):
                        total = total + jnp.where(pick[b, s, k] == c, parts[k], 0.0)
                    out[d, s, b * 128 : (b + 1) * 128, c * 128 : (c + 1) * 128] = total.astype(BF)


def source_of(back):
    zl, zh, core = lax.axis_index("zl"), lax.axis_index("zh"), lax.axis_index("core")
    turn = jnp.int32(0)
    for i in range(2):
        for j in range(4):
            for k in range(2):
                here = jnp.logical_and(jnp.logical_and(zl == i, zh == j), core == k)
                turn = jnp.where(here, TURN[i][j][k], turn)
    return lax.rem(lax.axis_index("y") - lax.axis_index("x") + turn + 8 - back, 4)


def first_kernel(mix, part, out):
    s = source_of(0)
    for d in range(2):
        out[d] = jnp.dot(mix[d, s], part[...], preferred_element_type=F32)


def next_kernel(back, mix, part, begun, out):
    s = source_of(back)
    for d in range(2):
        out[d] = begun[d] + jnp.dot(mix[d, s], part[...], preferred_element_type=F32)


def last_kernel(back, mix, part, begun, out):
    s = source_of(back)
    core = lax.axis_index("core")
    for d, at in enumerate((core, 1 - core)):
        total = (begun[d] + jnp.dot(mix[d, s], part[...], preferred_element_type=F32)).astype(BF)
        for r in range(8):
            out[r, at] = total[r * 64 : (r + 1) * 64]


def rows_kernel(recv, keep, send):
    total = recv[0].astype(F32)
    for r in range(1, 8):
        total = total + recv[r].astype(F32)
    mixed = total.astype(BF)
    first = lax.axis_index("core") == 0
    keep[...] = jnp.where(first, mixed[0], mixed[1])
    send[...] = jnp.where(first, mixed[1], mixed[0])


def layer_kernel(keep, recv, weight, bias, cot, out, packed):
    first = lax.axis_index("core") == 0
    left = jnp.where(first, keep[...], recv[...])
    right = jnp.where(first, recv[...], keep[...])
    mixed = jnp.concatenate([left, right], axis=1)
    pre = jnp.dot(mixed, weight[...], preferred_element_type=F32) + bias[...]
    sig = jax.nn.sigmoid(pre)
    out[...] = (pre * sig).astype(BF)
    grad = cot[...].astype(F32) * sig * (1.0 + pre * (1.0 - sig))
    low = grad.astype(BF).astype(F32)
    wide = mixed.astype(F32)
    for i in range(4):
        part = wide[:, i * 192 : (i + 1) * 192]
        for j in range(4):
            both = jnp.concatenate([part, low[:, j * 192 : (j + 1) * 192]], axis=1)
            packed[i * 4 + j] = both.astype(BF)


def with_bias(block, row):
    high = row.astype(BF).astype(F32)
    low = row - high
    at = lax.broadcasted_iota(jnp.int32, (8, 384), 0)
    extra = jnp.where(at == 0, high, jnp.where(at == 1, low, 0.0))
    return jnp.concatenate([block, extra], axis=0)


def block_kernel(recv, keep, send):
    data = recv[...]
    left = data[:, :192]
    right = data[:, 192:]
    block = lax.dot_general(left, right, (((0,), (0,)), ((), ())), preferred_element_type=F32)
    row = jnp.sum(right.astype(F32), axis=0, keepdims=True)
    row = jnp.concatenate([row, row], axis=1)
    halves = [
        with_bias(
            jnp.concatenate([block[h * 96 : h * 96 + 48], block[h * 96 + 48 : h * 96 + 96]], axis=1),
            row,
        )
        for h in range(2)
    ]
    first = lax.axis_index("core") == 0
    keep[...] = jnp.where(first, halves[0], halves[1])
    send[...] = jnp.where(first, halves[1], halves[0]).astype(BF)


def resplit(total):
    row = total[48:49] + total[49:50]
    return with_bias(total[:48], row).astype(BF)


def pair_kernel(copies, keep, recv, out):
    value = resplit(keep[...] + recv[...].astype(F32))
    for i in range(copies):
        out[i] = value


def sum_kernel(copies, recv, out):
    total = recv[0].astype(F32)
    for r in range(1, 8):
        total = total + recv[r].astype(F32)
    value = resplit(total)
    for i in range(copies):
        out[i] = value


def write_rows(source, at, grad, rows, sems):
    copies = []
    for i in range(4):
        pieces = [source[i * 4 + j].astype(F32) for j in range(4)]
        for h in range(2):
            rows[i, h * 48 : (h + 1) * 48] = jnp.concatenate(
                [piece[:48, h * 192 : (h + 1) * 192] for piece in pieces], axis=1
            )
        start = pl.multiple_of(i * 192 + at * 96, 32)
        copies.append(pltpu.make_async_copy(rows.at[i], grad.at[pl.ds(start, 96)], sems.at[i]))
        copies[-1].start()
    return copies


def own_half_kernel(own, grad, bias, rows, sems):
    copies = write_rows(own, lax.axis_index("core"), grad, rows, sems)
    parts = [own[j].astype(F32) for j in range(4)]
    bias[...] = jnp.concatenate([part[48:49, :192] + part[49:50, :192] for part in parts], axis=1)
    for copy in copies:
        copy.wait()


def other_half_kernel(other, begun, grad, rows, sems):
    del begun
    for copy in write_rows(other, 1 - lax.axis_index("core"), grad, rows, sems):
        copy.wait()


def on_device(features, tiles, tile_cols, tile_mask, weight, bias, cotangent):
    picks = jnp.where(tile_mask != 0, tile_cols, -1)
    with jax.named_scope("spread_features"):
        half = call(pick_kernel, struct((512, 384), BF), [hbm()], vmem(), [pltpu.SemaphoreType.DMA])(features)
        half, tiles, picks = lax.optimization_barrier((half, tiles, picks))
        own = lax.ppermute(half, AXES, first_hop())
    with jax.named_scope("spread_tiles"):
        other_tiles = lax.ppermute(tiles, "core", shift(2, 1))
        other_picks = lax.ppermute(picks, "core", shift(2, 1))
        mix = call(spread_kernel, struct((2, 4, 512, 512), BF), [smem(), smem(), vmem(), vmem()], vmem())(
            picks, other_picks, tiles, other_tiles
        )
    own, mix = lax.optimization_barrier((own, mix))
    with jax.named_scope("spread_features"):
        parts = [lax.ppermute(own, "y", shift(4, back)) for back in BACK[1:]]
    with jax.named_scope("aggregate"):
        flops = 4 * 512 * 512 * 384
        begun = call(first_kernel, struct((2, 512, 384), F32), [vmem()] * 2, vmem(), flops=flops)(mix, own)
        for back, part in zip(BACK[1:3], parts[:2]):
            begun = call(
                lambda *refs, back=back: next_kernel(back, *refs),
                struct((2, 512, 384), F32),
                [vmem()] * 3,
                vmem(),
                aliases={2: 0},
                flops=flops,
            )(mix, part, begun)
        partial = call(
            lambda *refs: last_kernel(BACK[3], *refs),
            struct((8, 2, 64, 384), BF),
            [vmem()] * 3,
            vmem(),
            flops=flops,
        )(mix, parts[2], begun)
    with jax.named_scope("sum_over_rep"):
        recv = lax.all_to_all(partial, REP, 0, 0, tiled=True)
        keep, send = call(
            rows_kernel, (struct((64, 384), BF), struct((64, 384), BF)), [vmem()], (vmem(), vmem())
        )(recv)
        theirs = lax.ppermute(send, "core", shift(2, 1))
    with jax.named_scope("layer"):
        output, packed = call(
            layer_kernel,
            (struct((64, 768), BF), struct((16, 64, 384), BF)),
            [vmem()] * 5,
            (vmem(), vmem()),
        )(keep, theirs, weight, bias.reshape(1, 768), cotangent)
    with jax.named_scope("exchange_rows"):
        rows = lax.all_to_all(packed.reshape(1024, 384), PLANE, 0, 0, tiled=True)
    with jax.named_scope("weight_block"):
        keep, send = call(
            block_kernel, (struct((56, 384), F32), struct((56, 384), BF)), [vmem()], (vmem(), vmem())
        )(rows)
        other = lax.ppermute(send, "core", shift(2, 1))
        pair = call(lambda *refs: pair_kernel(8, *refs), struct((8, 56, 384), BF), [vmem()] * 2, vmem())(
            keep, other
        )
    with jax.named_scope("sum_over_z"):
        chain = lax.all_to_all(pair.reshape(448, 384), ZAXIS, 0, 0, tiled=True)
        whole = call(lambda *refs: sum_kernel(16, *refs), struct((16, 56, 384), BF), [vmem()], vmem())(
            chain.reshape(8, 56, 384)
        )
    with jax.named_scope("gather_plane"):
        mine = lax.all_to_all(whole.reshape(896, 384), PLANE, 0, 0, tiled=True)
        theirs = lax.ppermute(mine, "core", shift(2, 1))
    with jax.named_scope("finish"):
        scratch = [pltpu.VMEM((4, 96, 768), F32), pltpu.SemaphoreType.DMA((4,))]
        grad, grad_bias = call(
            own_half_kernel,
            (struct((768, 768), F32), struct((1, 768), F32)),
            [vmem()],
            (anyspace(), vmem()),
            scratch,
        )(mine.reshape(16, 56, 384))
        grad_weight = call(
            other_half_kernel,
            struct((768, 768), F32),
            [vmem(), anyspace()],
            anyspace(),
            scratch,
            aliases={1: 0},
        )(theirs.reshape(16, 56, 384), grad)
    return output, grad_weight, grad_bias.reshape(768)


def solution(mesh):
    fine = Mesh(mesh.devices.reshape(SIZES), AXES)
    placed = (
        P(DOM, None),
        P(DOM, REP, None, None, None),
        P(DOM, REP, None),
        P(DOM, REP, None),
        P(),
        P(),
        P(DOM + REP, None),
    )
    return jax.shard_map(
        on_device,
        mesh=fine,
        in_specs=placed,
        out_specs=(P(DOM + REP, None), P(), P()),
        check_vma=False,
    )
```

time: 160 us -> 135 us (0.84)
  starting transfers between devices: 57.5 us -> 21.3 us
  blocking collectives: 47.7 us -> 69.4 us
  waiting for transfers between devices: 37.8 us -> 28.7 us
  local copies, waits for them, and re-layouts: 5.04 us -> 2.74 us
    ppermute x7 -> x6, starting transfers between devices: 38.4 us -> 14.3 us  [the longest x1 5.53 us: on_device(): other_picks = lax.ppermute(picks, 'core', shift(2, 1))]
    all_to_all x2 -> x3, blocking collectives: 33.1 us -> 52.3 us  [the longest x1 21.8 us: on_device(): chain = lax.all_to_all(pair.reshape(448, 384), ZAXIS, 0, 0, tiled=True)]
    all_to_all x1 -> x0, waiting for transfers between devices: 12 us -> none  [on_device(): recv = lax.all_to_all(partial, REP, 0, 0, tiled=True).reshape(8, 64, 768)]
    all_to_all x1 -> x0, starting transfers between devices: 7.75 us -> none  [on_device(): recv = lax.all_to_all(partial, REP, 0, 0, tiled=True).reshape(8, 64, 768)]
    ppermute x7 -> x6, waiting for transfers between devices: 10.9 us -> 18 us  [the longest x3 16.3 us: on_device(): parts = [lax.ppermute(own, 'y', shift(4, back)) for back in BACK[1:]]]
    ppermute x1, starting transfers between devices: 4.59 us -> 1.91 us  [on_device(): own = lax.ppermute(half, AXES, first_hop())]
    all_to_all x1, blocking collectives: 14.6 us -> 17.1 us  [on_device(): rows = lax.all_to_all(packed.reshape(1024, 384), PLANE, 0, 0, tiled=True)]
    unnamed x14 -> x10, local copies, waits for them, and re-layouts: 5.01 us -> 2.74 us
  transfers between devices with their start and end apart: 11 -> 9, of which waited for: 7 -> 5; matrix products, arithmetic and copies ran while one was open for 0% -> 0% of each run, Pallas kernels for 0% -> 5%
where the time goes in v3:
time: 135 us
  blocking collectives  69.4 us (51%)
  waiting for transfers between devices  28.7 us (21%)
  starting transfers between devices  21.3 us (16%)
  Pallas kernels  10.7 us (8%)
  local copies, waits for them, and re-layouts  2.74 us (2%)
    all_to_all x1, blocking collectives, on_device(): chain = lax.all_to_all(pair.reshape(448, 384), ZAXIS, 0, 0, tiled=True)  21.8 us
    all_to_all x1, blocking collectives, on_device(): rows = lax.all_to_all(packed.reshape(1024, 384), PLANE, 0, 0, tiled=True)  17.1 us
    all_to_all x1, blocking collectives, on_device(): recv = lax.all_to_all(partial, REP, 0, 0, tiled=True)  16.6 us
    ppermute x3, waiting for transfers between devices, on_device(): parts = [lax.ppermute(own, 'y', shift(4, back)) for back in BACK[1:]]  16.3 us
    all_to_all x1, blocking collectives, on_device(): mine = lax.all_to_all(whole.reshape(896, 384), PLANE, 0, 0, tiled=True)  14 us
    ppermute x1, waiting for transfers between devices, on_device(): own = lax.ppermute(half, AXES, first_hop())  9.88 us
    ppermute x1, starting transfers between devices, on_device(): other_picks = lax.ppermute(picks, 'core', shift(2, 1))  5.53 us
    pallas_call x1, Pallas kernels, on_device(): call(spread_kernel, struct((2, 4, 512, 512), BF), [smem(), smem(), vmem()...  3.36 us
  transfers between devices with their start and end apart: 9, of which 5 were waited for; matrix products, arithmetic and copies ran while one was open for 0% of the time, Pallas kernels for 5%

profile of v3, /device:TPU:1, one launch (start us, length us, event | category | flops | bytes accessed | tf_op | source)
XLA Modules:
  0.0 134.9 jit_solution(1137236722938434684)
XLA Ops:
  0.6 1.1 copy-done.2
  1.8 0.1 spread_features.1
  1.8 0.7 compare_select_fusion.picks
  2.5 3.2 %collective-permute-start.2 = (bf16[4,4,4,128,128]{4,3,2,1,0:T(8,128)(2,1)}, bf16[4,4,4,128,128]{4,3,2,1,0:T(8,128)(2,1)S(1)}, u32[]{:S(2)}, u32[]{:S(2)}) collective-permute-start(bf16[4,4,4,128,128]{4,3,2,1,0:T(8,128)(2,1)} %tiles), channel_id=1, source_target_pairs={{0,8},{8,0},{1,9},{9,1},{2,10},{10,2},{3,11},{11,3},{4,12},{12,4},... | collective-permute-start | bytes 6291464 | tf_op jit(solution)/shard_map/spread_tiles/ppermute | solution.py:235
  5.8 1.9 %collective-permute-start = (bf16[512,384]{1,0:T(8,128)(2,1)S(1)}, bf16[512,384]{1,0:T(8,128)(2,1)S(1)}, u32[]{:S(2)}, u32[]{:S(2)}) collective-permute-start(bf16[512,384]{1,0:T(8,128)(2,1)S(1)} %spread_features.1), channel_id=1, source_target_pairs={{0,32},{1,120},{2,144},{3,104},{4,0},{5,200},{6,176},{7,216},{8,64... | collective-permute-start | bytes 1179656 | tf_op jit(solution)/shard_map/spread_features/ppermute | solution.py:233
  7.7 5.5 %collective-permute-start.1 = (s32[4,4,4]{2,1,0:T(4,128)S(1)}, s32[4,4,4]{2,1,0:T(4,128)S(1)}, u32[]{:S(2)}, u32[]{:S(2)}) collective-permute-start(s32[4,4,4]{2,1,0:T(4,128)S(1)} %compare_select_fusion.picks), channel_id=1, source_target_pairs={{0,8},{8,0},{1,9},{9,1},{2,10},{10,2},{3,11},{11,3},{4,12},{12,4},... | collective-permute-start | bytes 776 | tf_op jit(solution)/shard_map/spread_tiles/ppermute | solution.py:236
  13.2 0.8 collective-permute-done.1.other_picks
  14.1 1.6 %copy-done = bf16[4,4,4,128,128]{4,3,2,1,0:T(8,128)(2,1)S(1)} copy-done((bf16[4,4,4,128,128]{4,3,2,1,0:T(8,128)(2,1)S(1)}, bf16[4,4,4,128,128]{4,3,2,1,0:T(8,128)(2,1)}, u32[]{:S(2)}) %copy-start) | copy-done | bytes 2097176
  15.7 3.4 %spread_tiles.1.mix.refs_0_ = bf16[2,4,512,512]{3,2,1,0:T(8,128)(2,1)S(1)} custom-call(s32[4,4,4]{2,1,0:T(4,128)S(1)} %compare_select_fusion.picks, s32[4,4,4]{2,1,0:T(4,128)S(1)} %collective-permute-done.1.other_picks, bf16[4,4,4,128,128]{4,3,2,1,0:T(8,128)(2,1)S(1)} %copy-done, bf16[4,4,4,128,128]{4,3,2,1,0:T(8,128)(2,1)S(1)} %collective-permute-done.2.other_tiles), custom_call_target="tpu_custom_call" | custom-call | bytes 1048576 | tf_op jit(solution)/shard_map/spread_tiles/pallas_call | solution.py:237
  19.0 9.9 %collective-permute-done.part = bf16[512,384]{1,0:T(8,128)(2,1)S(1)} collective-permute-done((bf16[512,384]{1,0:T(8,128)(2,1)S(1)}, bf16[512,384]{1,0:T(8,128)(2,1)S(1)}, u32[]{:S(2)}, u32[]{:S(2)}) %collective-permute-start) | collective-permute-done | bytes 393248 | tf_op jit(solution)/shard_map/spread_features/ppermute | solution.py:233
  28.9 2.7 %collective-permute-start.4 = (bf16[512,384]{1,0:T(8,128)(2,1)S(1)}, bf16[512,384]{1,0:T(8,128)(2,1)S(1)}, u32[]{:S(2)}, u32[]{:S(2)}) collective-permute-start(bf16[512,384]{1,0:T(8,128)(2,1)S(1)} %collective-permute-done.part), channel_id=1, source_target_pairs={{0,192},{64,0},{128,64},{192,128},{1,193},{65,1},{129,65},{193,129... | collective-permute-start | bytes 1179656 | tf_op jit(solution)/shard_map/spread_features/ppermute | solution.py:242
  31.6 0.7 aggregate.4.refs_2_
  32.3 16.2 %collective-permute-done.5.refs_1_ = bf16[512,384]{1,0:T(8,128)(2,1)S(1)} collective-permute-done((bf16[512,384]{1,0:T(8,128)(2,1)S(1)}, bf16[512,384]{1,0:T(8,128)(2,1)S(1)}, u32[]{:S(2)}, u32[]{:S(2)}) %collective-permute-start.5) | collective-permute-done | bytes 393248 | tf_op jit(solution)/shard_map/spread_features/ppermute | solution.py:242
  48.5 0.8 aggregate.5.refs_2_
  49.4 0.8 aggregate.6.refs_2_
  50.2 0.7 aggregate.7
  50.9 16.6 %all_to_all.28.recv = bf16[8,2,64,384]{3,2,1,0:T(8,128)(2,1)S(1)} all-to-all(bf16[8,2,64,384]{3,2,1,0:T(8,128)(2,1)S(1)} %aggregate.7), channel_id=1, replica_groups=mesh['y'=4,'zh'=4,'core'=2,'x'=4,'zl'=2] {'x','zl'}, dimensions={0} | all-to-all | bytes 1572864 | tf_op jit(solution)/shard_map/sum_over_rep/all_to_all | solution.py:263
  67.5 0.1 sum_over_rep.1
  67.6 2.9 %collective-permute-start.6 = (bf16[64,384]{1,0:T(8,128)(2,1)S(1)}, bf16[64,384]{1,0:T(8,128)(2,1)S(1)}, u32[]{:S(2)}, u32[]{:S(2)}) collective-permute-start(bf16[64,384]{1,0:T(8,128)(2,1)S(1)} %get-tuple-element.22), channel_id=1, source_target_pairs={{0,8},{8,0},{1,9},{9,1},{2,10},{10,2},{3,11},{11,3},{4,12},{12,4},... | collective-permute-start | bytes 147464 | tf_op jit(solution)/shard_map/sum_over_rep/ppermute | solution.py:267
  70.5 0.9 collective-permute-done.6.recv
  71.4 1.0 layer.1
  72.4 17.1 %all_to_all.29 = bf16[16,64,384]{2,1,0:T(8,128)(2,1)S(1)} all-to-all(bf16[16,64,384]{2,1,0:T(8,128)(2,1)S(1)} %get-tuple-element.24), channel_id=1, replica_groups=mesh['y'=4,'zh'=4,'core'=2,'x'=4,'zl'=2] {'x','y'}, dimensions={0} | all-to-all | bytes 1572864 | tf_op jit(solution)/shard_map/exchange_rows/all_to_all | solution.py:276
  89.5 0.7 weight_block.2
  90.2 1.9 %collective-permute-start.7 = (bf16[56,384]{1,0:T(8,128)(2,1)S(1)}, bf16[56,384]{1,0:T(8,128)(2,1)S(1)}, u32[]{:S(2)}, u32[]{:S(2)}) collective-permute-start(bf16[56,384]{1,0:T(8,128)(2,1)S(1)} %get-tuple-element.26), channel_id=1, source_target_pairs={{0,8},{8,0},{1,9},{9,1},{2,10},{10,2},{3,11},{11,3},{4,12},{12,4},... | collective-permute-start | bytes 129032 | tf_op jit(solution)/shard_map/weight_block/ppermute | solution.py:281
  92.1 0.9 collective-permute-done.7.refs_1_
  93.0 21.8 %all_to_all.30.refs_0_ = bf16[8,56,384]{2,1,0:T(8,128)(2,1)S(1)} all-to-all(bf16[8,56,384]{2,1,0:T(8,128)(2,1)S(1)} %weight_block.3), channel_id=1, replica_groups=mesh['y'=4,'zh'=4,'core'=2,'x'=4,'zl'=2] {'zh','zl'}, dimensions={0} | all-to-all | bytes 688128 | tf_op jit(solution)/shard_map/sum_over_z/all_to_all | solution.py:286
  114.8 0.1 sum_over_z.1
  114.9 14.0 %all_to_all.31.own = bf16[16,56,384]{2,1,0:T(8,128)(2,1)S(1)} all-to-all(bf16[16,56,384]{2,1,0:T(8,128)(2,1)S(1)} %sum_over_z.1), channel_id=1, replica_groups=mesh['y'=4,'zh'=4,'core'=2,'x'=4,'zl'=2] {'x','y'}, dimensions={0} | all-to-all | bytes 1376256 | tf_op jit(solution)/shard_map/gather_plane/all_to_all | solution.py:291
  128.8 3.2 %collective-permute-start.8 = (bf16[896,384]{1,0:T(8,128)(2,1)S(1)}, bf16[896,384]{1,0:T(8,128)(2,1)S(1)}, u32[]{:S(2)}, u32[]{:S(2)}) collective-permute-start(bf16[896,384]{1,0:T(8,128)(2,1)S(1)} %bitcast.4), channel_id=1, source_target_pairs={{0,8},{8,0},{1,9},{9,1},{2,10},{10,2},{3,11},{11,3},{4,12},{12,4},... | collective-permute-start | bytes 2064392 | tf_op jit(solution)/shard_map/gather_plane/ppermute | solution.py:292
  132.0 1.1 finish.2
  133.2 0.6 reduce
  133.8 1.1 finish.3
  (16 shorter events, 0.1 us)
Async XLA Ops:
  0.6 1.1 copy-start.2
  2.5 11.5 %collective-permute-start.2 = (bf16[4,4,4,128,128]{4,3,2,1,0:T(8,128)(2,1)}, bf16[4,4,4,128,128]{4,3,2,1,0:T(8,128)(2,1)S(1)}, u32[]{:S(2)}, u32[]{:S(2)}) collective-permute-start(bf16[4,4,4,128,128]{4,3,2,1,0:T(8,128)(2,1)} %tiles), channel_id=1, source_target_pairs={{0,8},{8,0},{1,9},{9,1},{2,10},{10,2},{3,11},{11,3},{4,12},{12,4},... | collective-permute-start | bytes 6291464 | tf_op jit(solution)/shard_map/spread_tiles/ppermute | solution.py:235
  5.8 23.1 %collective-permute-start = (bf16[512,384]{1,0:T(8,128)(2,1)S(1)}, bf16[512,384]{1,0:T(8,128)(2,1)S(1)}, u32[]{:S(2)}, u32[]{:S(2)}) collective-permute-start(bf16[512,384]{1,0:T(8,128)(2,1)S(1)} %spread_features.1), channel_id=1, source_target_pairs={{0,32},{1,120},{2,144},{3,104},{4,0},{5,200},{6,176},{7,216},{8,64... | collective-permute-start | bytes 1179656 | tf_op jit(solution)/shard_map/spread_features/ppermute | solution.py:233
  7.7 6.4 %collective-permute-start.1 = (s32[4,4,4]{2,1,0:T(4,128)S(1)}, s32[4,4,4]{2,1,0:T(4,128)S(1)}, u32[]{:S(2)}, u32[]{:S(2)}) collective-permute-start(s32[4,4,4]{2,1,0:T(4,128)S(1)} %compare_select_fusion.picks), channel_id=1, source_target_pairs={{0,8},{8,0},{1,9},{9,1},{2,10},{10,2},{3,11},{11,3},{4,12},{12,4},... | collective-permute-start | bytes 776 | tf_op jit(solution)/shard_map/spread_tiles/ppermute | solution.py:236
  14.1 1.6 %copy-start = (bf16[4,4,4,128,128]{4,3,2,1,0:T(8,128)(2,1)S(1)}, bf16[4,4,4,128,128]{4,3,2,1,0:T(8,128)(2,1)}, u32[]{:S(2)}) copy-start(bf16[4,4,4,128,128]{4,3,2,1,0:T(8,128)(2,1)} %tiles) | copy-start | bytes 6291460
  28.9 19.6 %collective-permute-start.5 = (bf16[512,384]{1,0:T(8,128)(2,1)S(1)}, bf16[512,384]{1,0:T(8,128)(2,1)S(1)}, u32[]{:S(2)}, u32[]{:S(2)}) collective-permute-start(bf16[512,384]{1,0:T(8,128)(2,1)S(1)} %collective-permute-done.part), channel_id=1, source_target_pairs={{0,64},{64,128},{128,192},{192,0},{1,65},{65,129},{129,193},{193,1... | collective-permute-start | bytes 1179656 | tf_op jit(solution)/shard_map/spread_features/ppermute | solution.py:242
  28.9 20.4 %collective-permute-start.4 = (bf16[512,384]{1,0:T(8,128)(2,1)S(1)}, bf16[512,384]{1,0:T(8,128)(2,1)S(1)}, u32[]{:S(2)}, u32[]{:S(2)}) collective-permute-start(bf16[512,384]{1,0:T(8,128)(2,1)S(1)} %collective-permute-done.part), channel_id=1, source_target_pairs={{0,192},{64,0},{128,64},{192,128},{1,193},{65,1},{129,65},{193,129... | collective-permute-start | bytes 1179656 | tf_op jit(solution)/shard_map/spread_features/ppermute | solution.py:242
  31.6 18.6 %collective-permute-start.3 = (bf16[512,384]{1,0:T(8,128)(2,1)S(1)}, bf16[512,384]{1,0:T(8,128)(2,1)S(1)}, u32[]{:S(2)}, u32[]{:S(2)}) collective-permute-start(bf16[512,384]{1,0:T(8,128)(2,1)S(1)} %collective-permute-done.part), channel_id=1, source_target_pairs={{0,128},{64,192},{128,0},{192,64},{1,129},{65,193},{129,1},{193,65... | collective-permute-start | bytes 1179656 | tf_op jit(solution)/shard_map/spread_features/ppermute | solution.py:242
  50.9 19.6 %copy-start.4 = (f32[768]{0:T(1024)S(1)}, f32[768]{0:T(1024)}, u32[]{:S(2)}) copy-start(f32[768]{0:T(1024)} %param.12) | copy-start | bytes 9220
  50.9 20.5 %copy-start.1 = (bf16[768,768]{1,0:T(8,128)(2,1)S(1)}, bf16[768,768]{1,0:T(8,128)(2,1)}, u32[]{:S(2)}) copy-start(bf16[768,768]{1,0:T(8,128)(2,1)} %weight.1) | copy-start | bytes 3538948
  50.9 20.5 %copy-start.3 = (bf16[64,768]{1,0:T(8,128)(2,1)S(1)}, bf16[64,768]{1,0:T(8,128)(2,1)}, u32[]{:S(2)}) copy-start(bf16[64,768]{1,0:T(8,128)(2,1)} %cot.1) | copy-start | bytes 294916
  67.6 3.8 %collective-permute-start.6 = (bf16[64,384]{1,0:T(8,128)(2,1)S(1)}, bf16[64,384]{1,0:T(8,128)(2,1)S(1)}, u32[]{:S(2)}, u32[]{:S(2)}) collective-permute-start(bf16[64,384]{1,0:T(8,128)(2,1)S(1)} %get-tuple-element.22), channel_id=1, source_target_pairs={{0,8},{8,0},{1,9},{9,1},{2,10},{10,2},{3,11},{11,3},{4,12},{12,4},... | collective-permute-start | bytes 147464 | tf_op jit(solution)/shard_map/sum_over_rep/ppermute | solution.py:267
  90.2 2.7 %collective-permute-start.7 = (bf16[56,384]{1,0:T(8,128)(2,1)S(1)}, bf16[56,384]{1,0:T(8,128)(2,1)S(1)}, u32[]{:S(2)}, u32[]{:S(2)}) collective-permute-start(bf16[56,384]{1,0:T(8,128)(2,1)S(1)} %get-tuple-element.26), channel_id=1, source_target_pairs={{0,8},{8,0},{1,9},{9,1},{2,10},{10,2},{3,11},{11,3},{4,12},{12,4},... | collective-permute-start | bytes 129032 | tf_op jit(solution)/shard_map/weight_block/ppermute | solution.py:281
  128.8 5.0 %collective-permute-start.8 = (bf16[896,384]{1,0:T(8,128)(2,1)S(1)}, bf16[896,384]{1,0:T(8,128)(2,1)S(1)}, u32[]{:S(2)}, u32[]{:S(2)}) collective-permute-start(bf16[896,384]{1,0:T(8,128)(2,1)S(1)} %bitcast.4), channel_id=1, source_target_pairs={{0,8},{8,0},{1,9},{9,1},{2,10},{10,2},{3,11},{11,3},{4,12},{12,4},... | collective-permute-start | bytes 2064392 | tf_op jit(solution)/shard_map/gather_plane/ppermute | solution.py:292

commit v4 on v3

--- a/solution.py
+++ b/solution.py
@@ -11,16 +11,15 @@
 DOM = ("y", "zh", "core")
 REP = ("x", "zl")
 PLANE = ("x", "y")
-ZAXIS = ("zh", "zl")
 BF = jnp.bfloat16
 F32 = jnp.float32
-BACK = (0, 1, 3, 2)
+BACK = (2, 1, 3)
 VMEM_LIMIT = 32 * 1024 * 1024
 
-TURN = (((0, 1), (2, 1), (0, 3), (2, 3)), ((2, 3), (2, 3), (0, 1), (0, 1)))
+TURN = (((3, 3), (0, 1), (1, 2), (2, 0)), ((2, 0), (3, 3), (1, 2), (0, 1)))
 OFFSET = (
-    ((2, 1, 0, 3), (2, 3, 1, 0), (0, 3, 2, 1), (3, 1, 0, 2), (1, 0, 3, 2), (1, 2, 3, 0), (0, 2, 1, 3), (3, 0, 2, 1)),
-    ((0, 2, 1, 3), (1, 2, 3, 0), (1, 3, 2, 0), (3, 0, 1, 2), (3, 2, 0, 1), (2, 0, 3, 1), (0, 1, 3, 2), (2, 0, 3, 1)),
+    ((1, 2, 3, 0), (2, 1, 0, 3), (2, 0, 1, 3), (3, 2, 0, 1), (2, 3, 1, 0), (0, 1, 2, 3), (0, 2, 3, 1), (1, 0, 2, 3)),
+    ((0, 2, 1, 3), (0, 2, 3, 1), (3, 2, 1, 0), (3, 1, 2, 0), (2, 0, 1, 3), (1, 0, 3, 2), (0, 1, 3, 2), (2, 3, 0, 1)),
 )
 
 
@@ -71,22 +70,28 @@
     )
 
 
-def pick_kernel(features, out, sem):
+def pick_kernel(features, one, two, sems):
     start = pl.multiple_of(lax.axis_index("zl") * 384, 384)
-    copy = pltpu.make_async_copy(features.at[:, pl.ds(start, 384)], out, sem)
-    copy.start()
-    copy.wait()
-
-
-def spread_kernel(picks, other_picks, tiles, other_tiles, out):
-    for d, (pick, tile) in enumerate(((picks, tiles), (other_picks, other_tiles))):
+    copies = [
+        pltpu.make_async_copy(features.at[pl.ds(i * 256, 256), pl.ds(start, 384)], out, sems.at[i])
+        for i, out in enumerate((one, two))
+    ]
+    for copy in copies:
+        copy.start()
+    for copy in copies:
+        copy.wait()
+
+
+def spread_kernel(cols, live, other_cols, other_live, tiles, other_tiles, out):
+    for d, (col, on, tile) in enumerate(((cols, live, tiles), (other_cols, other_live, other_tiles))):
         for b in range(4):
             for s in range(4):
+                picks = [jnp.where(on[b, s, k] != 0, col[b, s, k], -1) for k in range(4)]
                 parts = [tile[b, s, k].astype(F32) for k in range(4)]
                 for c in range(4):
                     total = jnp.zeros((128, 128), F32)
-                    for k in range(4):
-                        total = total + jnp.where(pick[b, s, k] == c, parts[k], 0.0)
+                    for pick, part in zip(picks, parts):
+                        total = total + jnp.where(pick == c, part, 0.0)
                     out[d, s, b * 128 : (b + 1) * 128, c * 128 : (c + 1) * 128] = total.astype(BF)
 
 
@@ -101,42 +106,41 @@
     return lax.rem(lax.axis_index("y") - lax.axis_index("x") + turn + 8 - back, 4)
 
 
-def first_kernel(mix, part, out):
-    s = source_of(0)
+def terms(d, mix, keys, parts):
+    total = None
+    for (back, half), part in zip(keys, parts):
+        left = mix[d, source_of(back), :, half * 256 : (half + 1) * 256]
+        term = jnp.dot(left, part[...], preferred_element_type=F32)
+        total = term if total is None else total + term
+    return total
+
+
+def first_kernel(keys, mix, *refs):
     for d in range(2):
-        out[d] = jnp.dot(mix[d, s], part[...], preferred_element_type=F32)
-
-
-def next_kernel(back, mix, part, begun, out):
-    s = source_of(back)
+        refs[-1][d] = terms(d, mix, keys, refs[:-1])
+
+
+def next_kernel(keys, mix, begun, *refs):
     for d in range(2):
-        out[d] = begun[d] + jnp.dot(mix[d, s], part[...], preferred_element_type=F32)
-
-
-def last_kernel(back, mix, part, begun, out):
-    s = source_of(back)
+        refs[-1][d] = begun[d] + terms(d, mix, keys, refs[:-1])
+
+
+def last_kernel(keys, mix, begun, *refs):
     core = lax.axis_index("core")
     for d, at in enumerate((core, 1 - core)):
-        total = (begun[d] + jnp.dot(mix[d, s], part[...], preferred_element_type=F32)).astype(BF)
+        total = (begun[d] + terms(d, mix, keys, refs[:-1])).astype(BF)
         for r in range(8):
-            out[r, at] = total[r * 64 : (r + 1) * 64]
-
-
-def rows_kernel(recv, keep, send):
-    total = recv[0].astype(F32)
-    for r in range(1, 8):
-        total = total + recv[r].astype(F32)
-    mixed = total.astype(BF)
-    first = lax.axis_index("core") == 0
-    keep[...] = jnp.where(first, mixed[0], mixed[1])
-    send[...] = jnp.where(first, mixed[1], mixed[0])
-
-
-def layer_kernel(keep, recv, weight, bias, cot, out, packed):
-    first = lax.axis_index("core") == 0
-    left = jnp.where(first, keep[...], recv[...])
-    right = jnp.where(first, recv[...], keep[...])
-    mixed = jnp.concatenate([left, right], axis=1)
+            refs[-1][at, r] = total[r * 64 : (r + 1) * 64]
+
+
+def layer_kernel(recv, weight, bias, cot, out, packed):
+    halves = []
+    for c in range(2):
+        total = recv[8 * c].astype(F32)
+        for r in range(1, 8):
+            total = total + recv[8 * c + r].astype(F32)
+        halves.append(total.astype(BF))
+    mixed = jnp.concatenate(halves, axis=1)
     pre = jnp.dot(mixed, weight[...], preferred_element_type=F32) + bias[...]
     sig = jax.nn.sigmoid(pre)
     out[...] = (pre * sig).astype(BF)
@@ -182,17 +186,14 @@
     return with_bias(total[:48], row).astype(BF)
 
 
-def pair_kernel(copies, keep, recv, out):
-    value = resplit(keep[...] + recv[...].astype(F32))
-    for i in range(copies):
-        out[i] = value
-
-
-def sum_kernel(copies, recv, out):
-    total = recv[0].astype(F32)
-    for r in range(1, 8):
-        total = total + recv[r].astype(F32)
-    value = resplit(total)
+def pair_kernel(keep, recv, out):
+    out[...] = resplit(keep[...].astype(F32) + recv[...].astype(F32))
+
+
+def sum_kernel(copies, own, across, back, ahead, out):
+    one = own[...].astype(F32) + across[...].astype(F32)
+    two = back[...].astype(F32) + ahead[...].astype(F32)
+    value = resplit(one + two)
     for i in range(copies):
         out[i] = value
 
@@ -225,53 +226,59 @@
         copy.wait()
 
 
+def product(kernel, keys, mix, parts, begun=None):
+    last = kernel is last_kernel
+    extra = [] if begun is None else [begun]
+    return call(
+        lambda *refs: kernel(keys, *refs),
+        struct((2, 8, 64, 384), BF) if last else struct((2, 512, 384), F32),
+        [vmem()] * (1 + len(extra) + len(parts)),
+        vmem(),
+        aliases={1: 0} if extra and not last else None,
+        flops=4 * 512 * 256 * 384 * len(parts),
+    )(mix, *extra, *parts)
+
+
 def on_device(features, tiles, tile_cols, tile_mask, weight, bias, cotangent):
-    picks = jnp.where(tile_mask != 0, tile_cols, -1)
     with jax.named_scope("spread_features"):
-        half = call(pick_kernel, struct((512, 384), BF), [hbm()], vmem(), [pltpu.SemaphoreType.DMA])(features)
-        half, tiles, picks = lax.optimization_barrier((half, tiles, picks))
-        own = lax.ppermute(half, AXES, first_hop())
+        halves = call(
+            pick_kernel,
+            (struct((256, 384), BF), struct((256, 384), BF)),
+            [hbm()],
+            (vmem(), vmem()),
+            [pltpu.SemaphoreType.DMA((2,))],
+        )(features)
+        *halves, tiles = lax.optimization_barrier((*halves, tiles))
+        own = [lax.ppermute(half, AXES, first_hop()) for half in halves]
     with jax.named_scope("spread_tiles"):
-        other_tiles = lax.ppermute(tiles, "core", shift(2, 1))
-        other_picks = lax.ppermute(picks, "core", shift(2, 1))
-        mix = call(spread_kernel, struct((2, 4, 512, 512), BF), [smem(), smem(), vmem(), vmem()], vmem())(
-            picks, other_picks, tiles, other_tiles
-        )
-    own, mix = lax.optimization_barrier((own, mix))
+        there = [lax.ppermute(value, "core", shift(2, 1)) for value in (tiles, tile_cols, tile_mask)]
+        own[0], *there = lax.optimization_barrier((own[0], *there))
+        mix = call(
+            spread_kernel,
+            struct((2, 4, 512, 512), BF),
+            [smem(), smem(), smem(), smem(), vmem(), vmem()],
+            vmem(),
+        )(tile_cols, tile_mask, *there[1:], tiles, there[0])
     with jax.named_scope("spread_features"):
-        parts = [lax.ppermute(own, "y", shift(4, back)) for back in BACK[1:]]
+        early = [lax.ppermute(own[0], "y", shift(4, back)) for back in BACK]
+    own[1], mix = lax.optimization_barrier((own[1], mix))
+    with jax.named_scope("spread_features"):
+        late = [lax.ppermute(own[1], "y", shift(4, back)) for back in BACK]
     with jax.named_scope("aggregate"):
-        flops = 4 * 512 * 512 * 384
-        begun = call(first_kernel, struct((2, 512, 384), F32), [vmem()] * 2, vmem(), flops=flops)(mix, own)
-        for back, part in zip(BACK[1:3], parts[:2]):
-            begun = call(
-                lambda *refs, back=back: next_kernel(back, *refs),
-                struct((2, 512, 384), F32),
-                [vmem()] * 3,
-                vmem(),
-                aliases={2: 0},
-                flops=flops,
-            )(mix, part, begun)
-        partial = call(
-            lambda *refs: last_kernel(BACK[3], *refs),
-            struct((8, 2, 64, 384), BF),
-            [vmem()] * 3,
-            vmem(),
-            flops=flops,
-        )(mix, parts[2], begun)
+        begun = product(first_kernel, [(0, 0), (0, 1)], mix, own)
+        begun = product(next_kernel, [(back, 0) for back in BACK], mix, early, begun)
+        begun = product(next_kernel, [(BACK[0], 1)], mix, late[:1], begun)
+        begun = product(next_kernel, [(BACK[1], 1)], mix, late[1:2], begun)
+        partial = product(last_kernel, [(BACK[2], 1)], mix, late[2:], begun)
     with jax.named_scope("sum_over_rep"):
-        recv = lax.all_to_all(partial, REP, 0, 0, tiled=True)
-        keep, send = call(
-            rows_kernel, (struct((64, 384), BF), struct((64, 384), BF)), [vmem()], (vmem(), vmem())
-        )(recv)
-        theirs = lax.ppermute(send, "core", shift(2, 1))
+        recv = lax.all_to_all(partial.reshape(1024, 384), ("core",) + REP, 0, 0, tiled=True)
     with jax.named_scope("layer"):
         output, packed = call(
             layer_kernel,
             (struct((64, 768), BF), struct((16, 64, 384), BF)),
-            [vmem()] * 5,
+            [vmem()] * 4,
             (vmem(), vmem()),
-        )(keep, theirs, weight, bias.reshape(1, 768), cotangent)
+        )(recv.reshape(16, 64, 384), weight, bias.reshape(1, 768), cotangent)
     with jax.named_scope("exchange_rows"):
         rows = lax.all_to_all(packed.reshape(1024, 384), PLANE, 0, 0, tiled=True)
     with jax.named_scope("weight_block"):
@@ -279,13 +286,13 @@
             block_kernel, (struct((56, 384), F32), struct((56, 384), BF)), [vmem()], (vmem(), vmem())
         )(rows)
         other = lax.ppermute(send, "core", shift(2, 1))
-        pair = call(lambda *refs: pair_kernel(8, *refs), struct((8, 56, 384), BF), [vmem()] * 2, vmem())(
-            keep, other
-        )
+        pair = call(pair_kernel, struct((56, 384), BF), [vmem()] * 2, vmem())(keep, other)
     with jax.named_scope("sum_over_z"):
-        chain = lax.all_to_all(pair.reshape(448, 384), ZAXIS, 0, 0, tiled=True)
-        whole = call(lambda *refs: sum_kernel(16, *refs), struct((16, 56, 384), BF), [vmem()], vmem())(
-            chain.reshape(8, 56, 384)
+        beside = lax.ppermute(pair, "zl", shift(2, 1))
+        pair = call(pair_kernel, struct((56, 384), BF), [vmem()] * 2, vmem())(pair, beside)
+        chain = [lax.ppermute(pair, "zh", shift(4, back)) for back in BACK]
+        whole = call(lambda *refs: sum_kernel(16, *refs), struct((16, 56, 384), BF), [vmem()] * 4, vmem())(
+            pair, *chain
         )
     with jax.named_scope("gather_plane"):
         mine = lax.all_to_all(whole.reshape(896, 384), PLANE, 0, 0, tiled=True)

time: 135 us -> 125 us (0.926)
  blocking collectives: 69.4 us -> 30.9 us
  starting transfers between devices: 21.3 us -> 53.5 us
  waiting for transfers between devices: 28.7 us -> 22.4 us
  local copies, waits for them, and re-layouts: 2.74 us -> 4.13 us
    all_to_all x2 -> x0, blocking collectives: 38.4 us -> none  [the longest x1 21.8 us: on_device(): chain = lax.all_to_all(pair.reshape(448, 384), ZAXIS, 0, 0, tiled=True)]
    ppermute x7 -> x15, starting transfers between devices: 16.2 us -> 36.1 us  [the longest x3 11.5 us: on_device(): early = [lax.ppermute(own[0], 'y', shift(4, back)) for back in BACK]]
    ppermute x7 -> x15, waiting for transfers between devices: 27.8 us -> 9.33 us  [the longest x3 3.92 us: on_device(): chain = [lax.ppermute(pair, 'zh', shift(4, back)) for back in BACK]]
    all_to_all x0 -> x1, waiting for transfers between devices: none -> 12.2 us  [on_device(): lax.all_to_all(partial.reshape(1024, 384), ('core',) + REP, 0, 0, tiled=T...]
    all_to_all x0 -> x1, starting transfers between devices: none -> 11.4 us  [on_device(): lax.all_to_all(partial.reshape(1024, 384), ('core',) + REP, 0, 0, tiled=T...]
    unnamed x10 -> x14, local copies, waits for them, and re-layouts: 2.74 us -> 4.13 us
    pallas_call x8 -> x9, Pallas kernels: 6.57 us -> 7.73 us  [the longest x5 3.99 us: product(): call(lambda *refs: kernel(keys, *refs), struct((2, 8, 64, 384), BF) if la...]
  transfers between devices with their start and end apart: 9 -> 18, of which waited for: 5 -> 9; matrix products, arithmetic and copies ran while one was open for 0% -> 0% of each run, Pallas kernels for 5% -> 6%
where the time goes in v4:
time: 125 us; the launch traced here: 124 us
  starting transfers between devices  53.5 us (43%)
  blocking collectives  30.9 us (25%)
  waiting for transfers between devices  22.4 us (18%)
  Pallas kernels  11.8 us (9%)
  local copies, waits for them, and re-layouts  4.13 us (3%)
    all_to_all x1, blocking collectives, on_device(): rows = lax.all_to_all(packed.reshape(1024, 384), PLANE, 0, 0, tiled=True)  17.1 us
    all_to_all x1, blocking collectives, on_device(): mine = lax.all_to_all(whole.reshape(896, 384), PLANE, 0, 0, tiled=True)  13.8 us
    all_to_all x1, waiting for transfers between devices, on_device(): lax.all_to_all(partial.reshape(1024, 384), ('core',) + REP, 0, 0, tiled=T...  12.2 us
    ppermute x3, starting transfers between devices, on_device(): early = [lax.ppermute(own[0], 'y', shift(4, back)) for back in BACK]  11.5 us
    all_to_all x1, starting transfers between devices, on_device(): lax.all_to_all(partial.reshape(1024, 384), ('core',) + REP, 0, 0, tiled=T...  11.4 us
    ppermute x3, starting transfers between devices, on_device(): chain = [lax.ppermute(pair, 'zh', shift(4, back)) for back in BACK]  7.34 us
    ppermute x3, starting transfers between devices, on_device(): lax.ppermute(value, 'core', shift(2, 1))  6.8 us
    ppermute x2, starting transfers between devices, on_device(): own = [lax.ppermute(half, AXES, first_hop()) for half in halves]  5.48 us
  transfers between devices with their start and end apart: 18, of which 9 were waited for; matrix products, arithmetic and copies ran while one was open for 0% of the time, Pallas kernels for 6%

profile of v4, /device:TPU:1, one launch (start us, length us, event | category | flops | bytes accessed | tf_op | source)
XLA Modules:
  0.0 124.3 jit_solution(3354104735107380000)
XLA Ops:
  0.6 1.1 copy-done.2
  1.8 3.3 %collective-permute-start.2 = (bf16[4,4,4,128,128]{4,3,2,1,0:T(8,128)(2,1)}, bf16[4,4,4,128,128]{4,3,2,1,0:T(8,128)(2,1)S(1)}, u32[]{:S(2)}, u32[]{:S(2)}) collective-permute-start(bf16[4,4,4,128,128]{4,3,2,1,0:T(8,128)(2,1)} %tiles), channel_id=1, source_target_pairs={{0,8},{8,0},{1,9},{9,1},{2,10},{10,2},{3,11},{11,3},{4,12},{12,4},... | collective-permute-start | bytes 6291464 | tf_op jit(solution)/shard_map/spread_tiles/ppermute | solution.py:254
  5.2 2.3 %collective-permute-start.1 = (bf16[256,384]{1,0:T(8,128)(2,1)S(1)}, bf16[256,384]{1,0:T(8,128)(2,1)S(1)}, u32[]{:S(2)}, u32[]{:S(2)}) collective-permute-start(bf16[256,384]{1,0:T(8,128)(2,1)S(1)} %get-tuple-element.23), channel_id=1, source_target_pairs={{0,176},{1,168},{2,64},{3,216},{4,16},{5,72},{6,224},{7,56},{8,80}... | collective-permute-start | bytes 589832 | tf_op jit(solution)/shard_map/spread_features/ppermute | solution.py:252
  7.4 3.2 %collective-permute-start = (bf16[256,384]{1,0:T(8,128)(2,1)S(1)}, bf16[256,384]{1,0:T(8,128)(2,1)S(1)}, u32[]{:S(2)}, u32[]{:S(2)}) collective-permute-start(bf16[256,384]{1,0:T(8,128)(2,1)S(1)} %get-tuple-element.22), channel_id=1, source_target_pairs={{0,176},{1,168},{2,64},{3,216},{4,16},{5,72},{6,224},{7,56},{8,80}... | collective-permute-start | bytes 589832 | tf_op jit(solution)/shard_map/spread_features/ppermute | solution.py:252
  10.6 3.5 %collective-permute-start.3 = (s32[4,4,4]{2,1,0:T(4,128)}, s32[4,4,4]{2,1,0:T(4,128)S(1)}, u32[]{:S(2)}, u32[]{:S(2)}) collective-permute-start(s32[4,4,4]{2,1,0:T(4,128)} %cols.1), channel_id=1, source_target_pairs={{0,8},{8,0},{1,9},{9,1},{2,10},{10,2},{3,11},{11,3},{4,12},{12,4},... | collective-permute-start | bytes 776 | tf_op jit(solution)/shard_map/spread_tiles/ppermute | solution.py:254
  14.1 1.0 collective-permute-done.3.other_cols
  15.5 8.9 %collective-permute-start.5 = (bf16[256,384]{1,0:T(8,128)(2,1)S(1)}, bf16[256,384]{1,0:T(8,128)(2,1)S(1)}, u32[]{:S(2)}, u32[]{:S(2)}) collective-permute-start(bf16[256,384]{1,0:T(8,128)(2,1)S(1)} %collective-permute-done.1.refs_1_), channel_id=1, source_target_pairs={{0,128},{64,192},{128,0},{192,64},{1,129},{65,193},{129,1},{193,65... | collective-permute-start | bytes 589832 | tf_op jit(solution)/shard_map/spread_features/ppermute | solution.py:263
  24.4 2.1 %collective-permute-start.6 = (bf16[256,384]{1,0:T(8,128)(2,1)S(1)}, bf16[256,384]{1,0:T(8,128)(2,1)S(1)}, u32[]{:S(2)}, u32[]{:S(2)}) collective-permute-start(bf16[256,384]{1,0:T(8,128)(2,1)S(1)} %collective-permute-done.1.refs_1_), channel_id=1, source_target_pairs={{0,64},{64,128},{128,192},{192,0},{1,65},{65,129},{129,193},{193,1... | collective-permute-start | bytes 589832 | tf_op jit(solution)/shard_map/spread_features/ppermute | solution.py:263
  27.0 1.6 %copy-done = bf16[4,4,4,128,128]{4,3,2,1,0:T(8,128)(2,1)S(1)} copy-done((bf16[4,4,4,128,128]{4,3,2,1,0:T(8,128)(2,1)S(1)}, bf16[4,4,4,128,128]{4,3,2,1,0:T(8,128)(2,1)}, u32[]{:S(2)}) %copy-start) | copy-done | bytes 2097176
  30.0 3.6 %spread_tiles.1.refs_0_ = bf16[2,4,512,512]{3,2,1,0:T(8,128)(2,1)S(1)} custom-call(s32[4,4,4]{2,1,0:T(4,128)S(1)} %copy-done.4, s32[4,4,4]{2,1,0:T(4,128)S(1)} %copy-done.5, s32[4,4,4]{2,1,0:T(4,128)S(1)} %collective-permute-done.3.other_cols, s32[4,4,4]{2,1,0:T(4,128)S(1)} %collective-permute-done.4.other_live, bf16[4,4,4,128,128]{4,3,2,1,0:T(8,128)(2,1)S(1)} %copy-done, ...), custom_call_target="tpu_custom_call" | custom-call | bytes 1048576 | tf_op jit(solution)/shard_map/spread_tiles/pallas_call | solution.py:256
  33.7 1.3 %collective-permute-start.8 = (bf16[256,384]{1,0:T(8,128)(2,1)S(1)}, bf16[256,384]{1,0:T(8,128)(2,1)S(1)}, u32[]{:S(2)}, u32[]{:S(2)}) collective-permute-start(bf16[256,384]{1,0:T(8,128)(2,1)S(1)} %collective-permute-done.refs_2_), channel_id=1, source_target_pairs={{0,128},{64,192},{128,0},{192,64},{1,129},{65,193},{129,1},{193,65... | collective-permute-start | bytes 589832 | tf_op jit(solution)/shard_map/spread_features/ppermute | solution.py:266
  35.0 2.7 %collective-permute-start.10 = (bf16[256,384]{1,0:T(8,128)(2,1)S(1)}, bf16[256,384]{1,0:T(8,128)(2,1)S(1)}, u32[]{:S(2)}, u32[]{:S(2)}) collective-permute-start(bf16[256,384]{1,0:T(8,128)(2,1)S(1)} %collective-permute-done.refs_2_), channel_id=1, source_target_pairs={{0,192},{64,0},{128,64},{192,128},{1,193},{65,1},{129,65},{193,129... | collective-permute-start | bytes 589832 | tf_op jit(solution)/shard_map/spread_features/ppermute | solution.py:266
  38.4 1.1 aggregate.6.refs_1_
  40.3 1.6 %collective-permute-done.9.refs_2_ = bf16[256,384]{1,0:T(8,128)(2,1)S(1)} collective-permute-done((bf16[256,384]{1,0:T(8,128)(2,1)S(1)}, bf16[256,384]{1,0:T(8,128)(2,1)S(1)}, u32[]{:S(2)}, u32[]{:S(2)}) %collective-permute-start.9) | collective-permute-done | bytes 196640 | tf_op jit(solution)/shard_map/spread_features/ppermute | solution.py:266
  42.4 1.3 %aggregate.9 = bf16[2,8,64,384]{3,2,1,0:T(8,128)(2,1)} custom-call(bf16[2,4,512,512]{3,2,1,0:T(8,128)(2,1)S(1)} %spread_tiles.1.refs_0_, f32[2,512,384]{2,1,0:T(8,128)S(1)} %aggregate.8.refs_1_, bf16[256,384]{1,0:T(8,128)(2,1)S(1)} %collective-permute-done.10.refs_2_), custom_call_target="tpu_custom_call" | custom-call | flops 201326592 | bytes 1048576 | tf_op jit(solution)/shard_map/aggregate/pallas_call | solution.py:232
  43.7 11.4 %all-to-all-start = ((bf16[16,64,384]{2,1,0:T(8,128)(2,1)}), bf16[16,64,384]{2,1,0:T(8,128)(2,1)S(1)}, u32[]{:S(2)}, u32[]{:S(2)}) async-start(bf16[16,64,384]{2,1,0:T(8,128)(2,1)} %bitcast), calls=%async_computation | async-start | bytes 1572864 | tf_op jit(solution)/shard_map/sum_over_rep/all_to_all | solution.py:274
  55.1 12.2 %all-to-all-done.recv = bf16[16,64,384]{2,1,0:T(8,128)(2,1)S(1)} async-done(((bf16[16,64,384]{2,1,0:T(8,128)(2,1)}), bf16[16,64,384]{2,1,0:T(8,128)(2,1)S(1)}, u32[]{:S(2)}, u32[]{:S(2)}) %all-to-all-start) | async-done | bytes 786464 | tf_op jit(solution)/shard_map/sum_over_rep/all_to_all | solution.py:274
  67.3 1.0 layer.1
  68.3 17.1 %all_to_all.26 = bf16[16,64,384]{2,1,0:T(8,128)(2,1)S(1)} all-to-all(bf16[16,64,384]{2,1,0:T(8,128)(2,1)S(1)} %get-tuple-element.32), channel_id=1, replica_groups=mesh['y'=4,'zh'=4,'core'=2,'x'=4,'zl'=2] {'x','y'}, dimensions={0} | all-to-all | bytes 1572864 | tf_op jit(solution)/shard_map/exchange_rows/all_to_all | solution.py:283
  86.1 2.7 %collective-permute-start.11 = (bf16[56,384]{1,0:T(8,128)(2,1)S(1)}, bf16[56,384]{1,0:T(8,128)(2,1)S(1)}, u32[]{:S(2)}, u32[]{:S(2)}) collective-permute-start(bf16[56,384]{1,0:T(8,128)(2,1)S(1)} %get-tuple-element.34), channel_id=1, source_target_pairs={{0,8},{8,0},{1,9},{9,1},{2,10},{10,2},{3,11},{11,3},{4,12},{12,4},... | collective-permute-start | bytes 129032 | tf_op jit(solution)/shard_map/weight_block/ppermute | solution.py:288
  88.8 0.9 collective-permute-done.11.recv
  89.7 0.9 collective-permute-start.12
  90.7 2.0 %collective-permute-done.12.recv = bf16[56,384]{1,0:T(8,128)(2,1)S(1)} collective-permute-done((bf16[56,384]{1,0:T(8,128)(2,1)S(1)}, bf16[56,384]{1,0:T(8,128)(2,1)S(1)}, u32[]{:S(2)}, u32[]{:S(2)}) %collective-permute-start.12) | collective-permute-done | bytes 43040 | tf_op jit(solution)/shard_map/sum_over_z/ppermute | solution.py:291
  92.7 3.2 %collective-permute-start.13 = (bf16[56,384]{1,0:T(8,128)(2,1)S(1)}, bf16[56,384]{1,0:T(8,128)(2,1)S(1)}, u32[]{:S(2)}, u32[]{:S(2)}) collective-permute-start(bf16[56,384]{1,0:T(8,128)(2,1)S(1)} %sum_over_z.2.refs_0_), channel_id=1, source_target_pairs={{0,32},{16,48},{32,0},{48,16},{1,33},{17,49},{33,1},{49,17},{2,34}... | collective-permute-start | bytes 129032 | tf_op jit(solution)/shard_map/sum_over_z/ppermute | solution.py:293
  95.9 3.1 %collective-permute-start.14 = (bf16[56,384]{1,0:T(8,128)(2,1)S(1)}, bf16[56,384]{1,0:T(8,128)(2,1)S(1)}, u32[]{:S(2)}, u32[]{:S(2)}) collective-permute-start(bf16[56,384]{1,0:T(8,128)(2,1)S(1)} %sum_over_z.2.refs_0_), channel_id=1, source_target_pairs={{0,16},{16,32},{32,48},{48,0},{1,17},{17,33},{33,49},{49,1},{2,18}... | collective-permute-start | bytes 129032 | tf_op jit(solution)/shard_map/sum_over_z/ppermute | solution.py:293
  99.0 1.1 collective-permute-start.15
  100.1 2.4 %collective-permute-done.14.refs_2_ = bf16[56,384]{1,0:T(8,128)(2,1)S(1)} collective-permute-done((bf16[56,384]{1,0:T(8,128)(2,1)S(1)}, bf16[56,384]{1,0:T(8,128)(2,1)S(1)}, u32[]{:S(2)}, u32[]{:S(2)}) %collective-permute-start.14) | collective-permute-done | bytes 43040 | tf_op jit(solution)/shard_map/sum_over_z/ppermute | solution.py:293
  102.5 1.5 %collective-permute-done.15.refs_3_ = bf16[56,384]{1,0:T(8,128)(2,1)S(1)} collective-permute-done((bf16[56,384]{1,0:T(8,128)(2,1)S(1)}, bf16[56,384]{1,0:T(8,128)(2,1)S(1)}, u32[]{:S(2)}, u32[]{:S(2)}) %collective-permute-start.15) | collective-permute-done | bytes 43040 | tf_op jit(solution)/shard_map/sum_over_z/ppermute | solution.py:293
  104.0 13.8 %all_to_all.27.own = bf16[16,56,384]{2,1,0:T(8,128)(2,1)S(1)} all-to-all(bf16[16,56,384]{2,1,0:T(8,128)(2,1)S(1)} %sum_over_z.3), channel_id=1, replica_groups=mesh['y'=4,'zh'=4,'core'=2,'x'=4,'zl'=2] {'x','y'}, dimensions={0} | all-to-all | bytes 1376256 | tf_op jit(solution)/shard_map/gather_plane/all_to_all | solution.py:298
  117.8 3.4 %collective-permute-start.16 = (bf16[896,384]{1,0:T(8,128)(2,1)S(1)}, bf16[896,384]{1,0:T(8,128)(2,1)S(1)}, u32[]{:S(2)}, u32[]{:S(2)}) collective-permute-start(bf16[896,384]{1,0:T(8,128)(2,1)S(1)} %bitcast.5), channel_id=1, source_target_pairs={{0,8},{8,0},{1,9},{9,1},{2,10},{10,2},{3,11},{11,3},{4,12},{12,4},... | collective-permute-start | bytes 2064392 | tf_op jit(solution)/shard_map/gather_plane/ppermute | solution.py:299
  121.3 1.1 finish.2
  123.0 1.1 finish.3
  (36 shorter events, 5.9 us)
Async XLA Ops:
  0.6 1.1 copy-start.2
  1.8 13.7 %collective-permute-start.2 = (bf16[4,4,4,128,128]{4,3,2,1,0:T(8,128)(2,1)}, bf16[4,4,4,128,128]{4,3,2,1,0:T(8,128)(2,1)S(1)}, u32[]{:S(2)}, u32[]{:S(2)}) collective-permute-start(bf16[4,4,4,128,128]{4,3,2,1,0:T(8,128)(2,1)} %tiles), channel_id=1, source_target_pairs={{0,8},{8,0},{1,9},{9,1},{2,10},{10,2},{3,11},{11,3},{4,12},{12,4},... | collective-permute-start | bytes 6291464 | tf_op jit(solution)/shard_map/spread_tiles/ppermute | solution.py:254
  5.2 10.3 %collective-permute-start.1 = (bf16[256,384]{1,0:T(8,128)(2,1)S(1)}, bf16[256,384]{1,0:T(8,128)(2,1)S(1)}, u32[]{:S(2)}, u32[]{:S(2)}) collective-permute-start(bf16[256,384]{1,0:T(8,128)(2,1)S(1)} %get-tuple-element.23), channel_id=1, source_target_pairs={{0,176},{1,168},{2,64},{3,216},{4,16},{5,72},{6,224},{7,56},{8,80}... | collective-permute-start | bytes 589832 | tf_op jit(solution)/shard_map/spread_features/ppermute | solution.py:252
  7.4 26.3 %collective-permute-start = (bf16[256,384]{1,0:T(8,128)(2,1)S(1)}, bf16[256,384]{1,0:T(8,128)(2,1)S(1)}, u32[]{:S(2)}, u32[]{:S(2)}) collective-permute-start(bf16[256,384]{1,0:T(8,128)(2,1)S(1)} %get-tuple-element.22), channel_id=1, source_target_pairs={{0,176},{1,168},{2,64},{3,216},{4,16},{5,72},{6,224},{7,56},{8,80}... | collective-permute-start | bytes 589832 | tf_op jit(solution)/shard_map/spread_features/ppermute | solution.py:252
  10.6 4.5 %collective-permute-start.3 = (s32[4,4,4]{2,1,0:T(4,128)}, s32[4,4,4]{2,1,0:T(4,128)S(1)}, u32[]{:S(2)}, u32[]{:S(2)}) collective-permute-start(s32[4,4,4]{2,1,0:T(4,128)} %cols.1), channel_id=1, source_target_pairs={{0,8},{8,0},{1,9},{9,1},{2,10},{10,2},{3,11},{11,3},{4,12},{12,4},... | collective-permute-start | bytes 776 | tf_op jit(solution)/shard_map/spread_tiles/ppermute | solution.py:254
  14.1 1.4 %collective-permute-start.4 = (s32[4,4,4]{2,1,0:T(4,128)}, s32[4,4,4]{2,1,0:T(4,128)S(1)}, u32[]{:S(2)}, u32[]{:S(2)}) collective-permute-start(s32[4,4,4]{2,1,0:T(4,128)} %live.1), channel_id=1, source_target_pairs={{0,8},{8,0},{1,9},{9,1},{2,10},{10,2},{3,11},{11,3},{4,12},{12,4},... | collective-permute-start | bytes 776 | tf_op jit(solution)/shard_map/spread_tiles/ppermute | solution.py:254
  15.5 19.5 %collective-permute-start.5 = (bf16[256,384]{1,0:T(8,128)(2,1)S(1)}, bf16[256,384]{1,0:T(8,128)(2,1)S(1)}, u32[]{:S(2)}, u32[]{:S(2)}) collective-permute-start(bf16[256,384]{1,0:T(8,128)(2,1)S(1)} %collective-permute-done.1.refs_1_), channel_id=1, source_target_pairs={{0,128},{64,192},{128,0},{192,64},{1,129},{65,193},{129,1},{193,65... | collective-permute-start | bytes 589832 | tf_op jit(solution)/shard_map/spread_features/ppermute | solution.py:263
  24.4 14.0 %collective-permute-start.6 = (bf16[256,384]{1,0:T(8,128)(2,1)S(1)}, bf16[256,384]{1,0:T(8,128)(2,1)S(1)}, u32[]{:S(2)}, u32[]{:S(2)}) collective-permute-start(bf16[256,384]{1,0:T(8,128)(2,1)S(1)} %collective-permute-done.1.refs_1_), channel_id=1, source_target_pairs={{0,64},{64,128},{128,192},{192,0},{1,65},{65,129},{129,193},{193,1... | collective-permute-start | bytes 589832 | tf_op jit(solution)/shard_map/spread_features/ppermute | solution.py:263
  26.5 11.9 %collective-permute-start.7 = (bf16[256,384]{1,0:T(8,128)(2,1)S(1)}, bf16[256,384]{1,0:T(8,128)(2,1)S(1)}, u32[]{:S(2)}, u32[]{:S(2)}) collective-permute-start(bf16[256,384]{1,0:T(8,128)(2,1)S(1)} %collective-permute-done.1.refs_1_), channel_id=1, source_target_pairs={{0,192},{64,0},{128,64},{192,128},{1,193},{65,1},{129,65},{193,129... | collective-permute-start | bytes 589832 | tf_op jit(solution)/shard_map/spread_features/ppermute | solution.py:263
  27.0 1.6 %copy-start = (bf16[4,4,4,128,128]{4,3,2,1,0:T(8,128)(2,1)S(1)}, bf16[4,4,4,128,128]{4,3,2,1,0:T(8,128)(2,1)}, u32[]{:S(2)}) copy-start(bf16[4,4,4,128,128]{4,3,2,1,0:T(8,128)(2,1)} %tiles) | copy-start | bytes 6291460
  28.6 0.7 copy-start.4
  29.3 0.7 copy-start.5
  33.7 6.2 %collective-permute-start.8 = (bf16[256,384]{1,0:T(8,128)(2,1)S(1)}, bf16[256,384]{1,0:T(8,128)(2,1)S(1)}, u32[]{:S(2)}, u32[]{:S(2)}) collective-permute-start(bf16[256,384]{1,0:T(8,128)(2,1)S(1)} %collective-permute-done.refs_2_), channel_id=1, source_target_pairs={{0,128},{64,192},{128,0},{192,64},{1,129},{65,193},{129,1},{193,65... | collective-permute-start | bytes 589832 | tf_op jit(solution)/shard_map/spread_features/ppermute | solution.py:266
  35.0 6.9 %collective-permute-start.9 = (bf16[256,384]{1,0:T(8,128)(2,1)S(1)}, bf16[256,384]{1,0:T(8,128)(2,1)S(1)}, u32[]{:S(2)}, u32[]{:S(2)}) collective-permute-start(bf16[256,384]{1,0:T(8,128)(2,1)S(1)} %collective-permute-done.refs_2_), channel_id=1, source_target_pairs={{0,64},{64,128},{128,192},{192,0},{1,65},{65,129},{129,193},{193,1... | collective-permute-start | bytes 589832 | tf_op jit(solution)/shard_map/spread_features/ppermute | solution.py:266
  35.0 7.4 %collective-permute-start.10 = (bf16[256,384]{1,0:T(8,128)(2,1)S(1)}, bf16[256,384]{1,0:T(8,128)(2,1)S(1)}, u32[]{:S(2)}, u32[]{:S(2)}) collective-permute-start(bf16[256,384]{1,0:T(8,128)(2,1)S(1)} %collective-permute-done.refs_2_), channel_id=1, source_target_pairs={{0,192},{64,0},{128,64},{192,128},{1,193},{65,1},{129,65},{193,129... | collective-permute-start | bytes 589832 | tf_op jit(solution)/shard_map/spread_features/ppermute | solution.py:266
  42.3 12.7 %copy-start.6 = (f32[768]{0:T(1024)S(1)}, f32[768]{0:T(1024)}, u32[]{:S(2)}) copy-start(f32[768]{0:T(1024)} %param.12) | copy-start | bytes 9220
  42.4 24.9 %copy-start.3 = (bf16[64,768]{1,0:T(8,128)(2,1)S(1)}, bf16[64,768]{1,0:T(8,128)(2,1)}, u32[]{:S(2)}) copy-start(bf16[64,768]{1,0:T(8,128)(2,1)} %cot.1) | copy-start | bytes 294916
  43.7 23.5 %copy-start.1 = (bf16[768,768]{1,0:T(8,128)(2,1)S(1)}, bf16[768,768]{1,0:T(8,128)(2,1)}, u32[]{:S(2)}) copy-start(bf16[768,768]{1,0:T(8,128)(2,1)} %weight.1) | copy-start | bytes 3538948
  43.7 23.5 %all-to-all-start = ((bf16[16,64,384]{2,1,0:T(8,128)(2,1)}), bf16[16,64,384]{2,1,0:T(8,128)(2,1)S(1)}, u32[]{:S(2)}, u32[]{:S(2)}) async-start(bf16[16,64,384]{2,1,0:T(8,128)(2,1)} %bitcast), calls=%async_computation | async-start | bytes 1572864 | tf_op jit(solution)/shard_map/sum_over_rep/all_to_all | solution.py:274
  86.1 3.6 %collective-permute-start.11 = (bf16[56,384]{1,0:T(8,128)(2,1)S(1)}, bf16[56,384]{1,0:T(8,128)(2,1)S(1)}, u32[]{:S(2)}, u32[]{:S(2)}) collective-permute-start(bf16[56,384]{1,0:T(8,128)(2,1)S(1)} %get-tuple-element.34), channel_id=1, source_target_pairs={{0,8},{8,0},{1,9},{9,1},{2,10},{10,2},{3,11},{11,3},{4,12},{12,4},... | collective-permute-start | bytes 129032 | tf_op jit(solution)/shard_map/weight_block/ppermute | solution.py:288
  89.7 3.0 %collective-permute-start.12 = (bf16[56,384]{1,0:T(8,128)(2,1)S(1)}, bf16[56,384]{1,0:T(8,128)(2,1)S(1)}, u32[]{:S(2)}, u32[]{:S(2)}) collective-permute-start(bf16[56,384]{1,0:T(8,128)(2,1)S(1)} %weight_block.3.keep), channel_id=1, source_target_pairs={{0,1},{1,0},{2,3},{3,2},{4,5},{5,4},{6,7},{7,6},{8,9},{9,8},{10,11... | collective-permute-start | bytes 129032 | tf_op jit(solution)/shard_map/sum_over_z/ppermute | solution.py:291
  92.7 7.3 %collective-permute-start.13 = (bf16[56,384]{1,0:T(8,128)(2,1)S(1)}, bf16[56,384]{1,0:T(8,128)(2,1)S(1)}, u32[]{:S(2)}, u32[]{:S(2)}) collective-permute-start(bf16[56,384]{1,0:T(8,128)(2,1)S(1)} %sum_over_z.2.refs_0_), channel_id=1, source_target_pairs={{0,32},{16,48},{32,0},{48,16},{1,33},{17,49},{33,1},{49,17},{2,34}... | collective-permute-start | bytes 129032 | tf_op jit(solution)/shard_map/sum_over_z/ppermute | solution.py:293
  95.9 6.6 %collective-permute-start.14 = (bf16[56,384]{1,0:T(8,128)(2,1)S(1)}, bf16[56,384]{1,0:T(8,128)(2,1)S(1)}, u32[]{:S(2)}, u32[]{:S(2)}) collective-permute-start(bf16[56,384]{1,0:T(8,128)(2,1)S(1)} %sum_over_z.2.refs_0_), channel_id=1, source_target_pairs={{0,16},{16,32},{32,48},{48,0},{1,17},{17,33},{33,49},{49,1},{2,18}... | collective-permute-start | bytes 129032 | tf_op jit(solution)/shard_map/sum_over_z/ppermute | solution.py:293
  99.0 5.0 %collective-permute-start.15 = (bf16[56,384]{1,0:T(8,128)(2,1)S(1)}, bf16[56,384]{1,0:T(8,128)(2,1)S(1)}, u32[]{:S(2)}, u32[]{:S(2)}) collective-permute-start(bf16[56,384]{1,0:T(8,128)(2,1)S(1)} %sum_over_z.2.refs_0_), channel_id=1, source_target_pairs={{0,48},{16,0},{32,16},{48,32},{1,49},{17,1},{33,17},{49,33},{2,50}... | collective-permute-start | bytes 129032 | tf_op jit(solution)/shard_map/sum_over_z/ppermute | solution.py:293
  117.8 5.2 %collective-permute-start.16 = (bf16[896,384]{1,0:T(8,128)(2,1)S(1)}, bf16[896,384]{1,0:T(8,128)(2,1)S(1)}, u32[]{:S(2)}, u32[]{:S(2)}) collective-permute-start(bf16[896,384]{1,0:T(8,128)(2,1)S(1)} %bitcast.5), channel_id=1, source_target_pairs={{0,8},{8,0},{1,9},{9,1},{2,10},{10,2},{3,11},{11,3},{4,12},{12,4},... | collective-permute-start | bytes 2064392 | tf_op jit(solution)/shard_map/gather_plane/ppermute | solution.py:299

commit v5 on v4

--- a/solution.py
+++ b/solution.py
@@ -173,12 +173,12 @@
         with_bias(
             jnp.concatenate([block[h * 96 : h * 96 + 48], block[h * 96 + 48 : h * 96 + 96]], axis=1),
             row,
-        )
+        ).astype(BF)
         for h in range(2)
     ]
     first = lax.axis_index("core") == 0
     keep[...] = jnp.where(first, halves[0], halves[1])
-    send[...] = jnp.where(first, halves[1], halves[0]).astype(BF)
+    send[...] = jnp.where(first, halves[1], halves[0])
 
 
 def resplit(total):
@@ -186,16 +186,14 @@
     return with_bias(total[:48], row).astype(BF)
 
 
-def pair_kernel(keep, recv, out):
-    out[...] = resplit(keep[...].astype(F32) + recv[...].astype(F32))
-
-
-def sum_kernel(copies, own, across, back, ahead, out):
-    one = own[...].astype(F32) + across[...].astype(F32)
-    two = back[...].astype(F32) + ahead[...].astype(F32)
-    value = resplit(one + two)
-    for i in range(copies):
-        out[i] = value
+def four_kernel(copies, one, two, three, four, out):
+    total = (one[...].astype(F32) + two[...].astype(F32)) + (three[...].astype(F32) + four[...].astype(F32))
+    value = resplit(total)
+    if copies is None:
+        out[...] = value
+    else:
+        for i in range(copies):
+            out[i] = value
 
 
 def write_rows(source, at, grad, rows, sems):
@@ -252,16 +250,15 @@
         own = [lax.ppermute(half, AXES, first_hop()) for half in halves]
     with jax.named_scope("spread_tiles"):
         there = [lax.ppermute(value, "core", shift(2, 1)) for value in (tiles, tile_cols, tile_mask)]
-        own[0], *there = lax.optimization_barrier((own[0], *there))
         mix = call(
             spread_kernel,
             struct((2, 4, 512, 512), BF),
             [smem(), smem(), smem(), smem(), vmem(), vmem()],
             vmem(),
         )(tile_cols, tile_mask, *there[1:], tiles, there[0])
+    own[0], mix = lax.optimization_barrier((own[0], mix))
     with jax.named_scope("spread_features"):
         early = [lax.ppermute(own[0], "y", shift(4, back)) for back in BACK]
-    own[1], mix = lax.optimization_barrier((own[1], mix))
     with jax.named_scope("spread_features"):
         late = [lax.ppermute(own[1], "y", shift(4, back)) for back in BACK]
     with jax.named_scope("aggregate"):
@@ -283,17 +280,19 @@
         rows = lax.all_to_all(packed.reshape(1024, 384), PLANE, 0, 0, tiled=True)
     with jax.named_scope("weight_block"):
         keep, send = call(
-            block_kernel, (struct((56, 384), F32), struct((56, 384), BF)), [vmem()], (vmem(), vmem())
+            block_kernel, (struct((56, 384), BF), struct((56, 384), BF)), [vmem()], (vmem(), vmem())
         )(rows)
+        beside = lax.ppermute(keep, "zl", shift(2, 1))
+        across = lax.ppermute(send, ("core", "zl"), [(0, 3), (1, 2), (2, 1), (3, 0)])
         other = lax.ppermute(send, "core", shift(2, 1))
-        pair = call(pair_kernel, struct((56, 384), BF), [vmem()] * 2, vmem())(keep, other)
+        pair = call(
+            lambda *refs: four_kernel(None, *refs), struct((56, 384), BF), [vmem()] * 4, vmem()
+        )(keep, other, beside, across)
     with jax.named_scope("sum_over_z"):
-        beside = lax.ppermute(pair, "zl", shift(2, 1))
-        pair = call(pair_kernel, struct((56, 384), BF), [vmem()] * 2, vmem())(pair, beside)
         chain = [lax.ppermute(pair, "zh", shift(4, back)) for back in BACK]
-        whole = call(lambda *refs: sum_kernel(16, *refs), struct((16, 56, 384), BF), [vmem()] * 4, vmem())(
-            pair, *chain
-        )
+        whole = call(
+            lambda *refs: four_kernel(16, *refs), struct((16, 56, 384), BF), [vmem()] * 4, vmem()
+        )(pair, *chain)
     with jax.named_scope("gather_plane"):
         mine = lax.all_to_all(whole.reshape(896, 384), PLANE, 0, 0, tiled=True)
         theirs = lax.ppermute(mine, "core", shift(2, 1))

time: 125 us -> 123 us (0.984)
  starting transfers between devices: 53.5 us -> 49 us
  waiting for transfers between devices: 22.4 us -> 26.8 us
  blocking collectives: 30.9 us -> 29.1 us
    ppermute x3, starting transfers between devices: 11.5 us -> 6.22 us  [on_device(): early = [lax.ppermute(own[0], 'y', shift(4, back)) for back in BACK]]
    ppermute x3, waiting for transfers between devices: 1.99 us -> 5.9 us  [on_device(): late = [lax.ppermute(own[1], 'y', shift(4, back)) for back in BACK]]
    all_to_all x1, blocking collectives: 17.1 us -> 15.2 us  [on_device(): rows = lax.all_to_all(packed.reshape(1024, 384), PLANE, 0, 0, tiled=True)]
    ppermute x3, waiting for transfers between devices: 0.01 us -> 1.54 us  [on_device(): early = [lax.ppermute(own[0], 'y', shift(4, back)) for back in BACK]]
    ppermute x1 -> x2, waiting for transfers between devices: 2.03 us -> 2.94 us  [the longest x1 1.78 us: on_device(): lax.ppermute(send, ('core', 'zl'), [(0, 3), (1, 2), (2, 1), (3, 0)])]
  transfers between devices with their start and end apart: 18 -> 19, of which waited for: 9 -> 10; matrix products, arithmetic and copies ran while one was open for 0% -> 0% of each run, Pallas kernels for 6% -> 6%
where the time goes in v5:
time: 123 us; the launch traced here: 122 us
  starting transfers between devices  49 us (40%)
  blocking collectives  29.1 us (24%)
  waiting for transfers between devices  26.8 us (22%)
  Pallas kernels  11.8 us (10%)
  local copies, waits for them, and re-layouts  4.13 us (3%)
    all_to_all x1, blocking collectives, on_device(): rows = lax.all_to_all(packed.reshape(1024, 384), PLANE, 0, 0, tiled=True)  15.2 us
    all_to_all x1, blocking collectives, on_device(): mine = lax.all_to_all(whole.reshape(896, 384), PLANE, 0, 0, tiled=True)  13.9 us
    all_to_all x1, waiting for transfers between devices, on_device(): lax.all_to_all(partial.reshape(1024, 384), ('core',) + REP, 0, 0, tiled=T...  12.2 us
    all_to_all x1, starting transfers between devices, on_device(): lax.all_to_all(partial.reshape(1024, 384), ('core',) + REP, 0, 0, tiled=T...  10.2 us
    ppermute x3, starting transfers between devices, on_device(): chain = [lax.ppermute(pair, 'zh', shift(4, back)) for back in BACK]  7.95 us
    ppermute x3, starting transfers between devices, on_device(): lax.ppermute(value, 'core', shift(2, 1))  6.8 us
    ppermute x3, starting transfers between devices, on_device(): early = [lax.ppermute(own[0], 'y', shift(4, back)) for back in BACK]  6.22 us
    ppermute x3, waiting for transfers between devices, on_device(): late = [lax.ppermute(own[1], 'y', shift(4, back)) for back in BACK]  5.9 us
  transfers between devices with their start and end apart: 19, of which 10 were waited for; matrix products, arithmetic and copies ran while one was open for 0% of the time, Pallas kernels for 6%

profile of v5, /device:TPU:1, one launch (start us, length us, event | category | flops | bytes accessed | tf_op | source)
XLA Modules:
  0.0 122.3 jit_solution(7768348301382301604)
XLA Ops:
  0.6 1.1 copy-done.2
  1.8 3.3 %collective-permute-start.3 = (bf16[4,4,4,128,128]{4,3,2,1,0:T(8,128)(2,1)}, bf16[4,4,4,128,128]{4,3,2,1,0:T(8,128)(2,1)S(1)}, u32[]{:S(2)}, u32[]{:S(2)}) collective-permute-start(bf16[4,4,4,128,128]{4,3,2,1,0:T(8,128)(2,1)} %tiles), channel_id=1, source_target_pairs={{0,8},{8,0},{1,9},{9,1},{2,10},{10,2},{3,11},{11,3},{4,12},{12,4},... | collective-permute-start | bytes 6291464 | tf_op jit(solution)/shard_map/spread_tiles/ppermute | solution.py:252
  5.2 2.3 %collective-permute-start = (bf16[256,384]{1,0:T(8,128)(2,1)S(1)}, bf16[256,384]{1,0:T(8,128)(2,1)S(1)}, u32[]{:S(2)}, u32[]{:S(2)}) collective-permute-start(bf16[256,384]{1,0:T(8,128)(2,1)S(1)} %get-tuple-element.18), channel_id=1, source_target_pairs={{0,176},{1,168},{2,64},{3,216},{4,16},{5,72},{6,224},{7,56},{8,80}... | collective-permute-start | bytes 589832 | tf_op jit(solution)/shard_map/spread_features/ppermute | solution.py:250
  7.4 3.2 %collective-permute-start.4 = (bf16[256,384]{1,0:T(8,128)(2,1)S(1)}, bf16[256,384]{1,0:T(8,128)(2,1)S(1)}, u32[]{:S(2)}, u32[]{:S(2)}) collective-permute-start(bf16[256,384]{1,0:T(8,128)(2,1)S(1)} %get-tuple-element.22), channel_id=1, source_target_pairs={{0,176},{1,168},{2,64},{3,216},{4,16},{5,72},{6,224},{7,56},{8,80}... | collective-permute-start | bytes 589832 | tf_op jit(solution)/shard_map/spread_features/ppermute | solution.py:250
  10.6 3.5 %collective-permute-start.1 = (s32[4,4,4]{2,1,0:T(4,128)}, s32[4,4,4]{2,1,0:T(4,128)S(1)}, u32[]{:S(2)}, u32[]{:S(2)}) collective-permute-start(s32[4,4,4]{2,1,0:T(4,128)} %cols.1), channel_id=1, source_target_pairs={{0,8},{8,0},{1,9},{9,1},{2,10},{10,2},{3,11},{11,3},{4,12},{12,4},... | collective-permute-start | bytes 776 | tf_op jit(solution)/shard_map/spread_tiles/ppermute | solution.py:252
  15.5 1.6 %copy-done = bf16[4,4,4,128,128]{4,3,2,1,0:T(8,128)(2,1)S(1)} copy-done((bf16[4,4,4,128,128]{4,3,2,1,0:T(8,128)(2,1)S(1)}, bf16[4,4,4,128,128]{4,3,2,1,0:T(8,128)(2,1)}, u32[]{:S(2)}) %copy-start) | copy-done | bytes 2097176
  18.5 3.6 %spread_tiles.1.refs_0_ = bf16[2,4,512,512]{3,2,1,0:T(8,128)(2,1)S(1)} custom-call(s32[4,4,4]{2,1,0:T(4,128)S(1)} %copy-done.4, s32[4,4,4]{2,1,0:T(4,128)S(1)} %copy-done.5, s32[4,4,4]{2,1,0:T(4,128)S(1)} %collective-permute-done.1.other_cols, s32[4,4,4]{2,1,0:T(4,128)S(1)} %collective-permute-done.2.other_live, bf16[4,4,4,128,128]{4,3,2,1,0:T(8,128)(2,1)S(1)} %copy-done, ...), custom_call_target="tpu_custom_call" | custom-call | bytes 1048576 | tf_op jit(solution)/shard_map/spread_tiles/pallas_call | solution.py:253
  22.1 3.5 %collective-permute-start.5 = (bf16[256,384]{1,0:T(8,128)(2,1)S(1)}, bf16[256,384]{1,0:T(8,128)(2,1)S(1)}, u32[]{:S(2)}, u32[]{:S(2)}) collective-permute-start(bf16[256,384]{1,0:T(8,128)(2,1)S(1)} %collective-permute-done.refs_1_), channel_id=1, source_target_pairs={{0,128},{64,192},{128,0},{192,64},{1,129},{65,193},{129,1},{193,65... | collective-permute-start | bytes 589832 | tf_op jit(solution)/shard_map/spread_features/ppermute | solution.py:261
  25.7 1.2 %collective-permute-start.6 = (bf16[256,384]{1,0:T(8,128)(2,1)S(1)}, bf16[256,384]{1,0:T(8,128)(2,1)S(1)}, u32[]{:S(2)}, u32[]{:S(2)}) collective-permute-start(bf16[256,384]{1,0:T(8,128)(2,1)S(1)} %collective-permute-done.refs_1_), channel_id=1, source_target_pairs={{0,64},{64,128},{128,192},{192,0},{1,65},{65,129},{129,193},{193,1... | collective-permute-start | bytes 589832 | tf_op jit(solution)/shard_map/spread_features/ppermute | solution.py:261
  26.9 1.4 %collective-permute-start.7 = (bf16[256,384]{1,0:T(8,128)(2,1)S(1)}, bf16[256,384]{1,0:T(8,128)(2,1)S(1)}, u32[]{:S(2)}, u32[]{:S(2)}) collective-permute-start(bf16[256,384]{1,0:T(8,128)(2,1)S(1)} %collective-permute-done.refs_1_), channel_id=1, source_target_pairs={{0,192},{64,0},{128,64},{192,128},{1,193},{65,1},{129,65},{193,129... | collective-permute-start | bytes 589832 | tf_op jit(solution)/shard_map/spread_features/ppermute | solution.py:261
  28.7 4.3 %collective-permute-start.9 = (bf16[256,384]{1,0:T(8,128)(2,1)S(1)}, bf16[256,384]{1,0:T(8,128)(2,1)S(1)}, u32[]{:S(2)}, u32[]{:S(2)}) collective-permute-start(bf16[256,384]{1,0:T(8,128)(2,1)S(1)} %collective-permute-done.4.refs_2_), channel_id=1, source_target_pairs={{0,64},{64,128},{128,192},{192,0},{1,65},{65,129},{129,193},{193,1... | collective-permute-start | bytes 589832 | tf_op jit(solution)/shard_map/spread_features/ppermute | solution.py:263
  33.7 1.5 %collective-permute-done.6.refs_3_ = bf16[256,384]{1,0:T(8,128)(2,1)S(1)} collective-permute-done((bf16[256,384]{1,0:T(8,128)(2,1)S(1)}, bf16[256,384]{1,0:T(8,128)(2,1)S(1)}, u32[]{:S(2)}, u32[]{:S(2)}) %collective-permute-start.6) | collective-permute-done | bytes 196640 | tf_op jit(solution)/shard_map/spread_features/ppermute | solution.py:261
  35.2 1.1 aggregate.6.refs_1_
  37.6 5.1 %collective-permute-done.9.refs_2_ = bf16[256,384]{1,0:T(8,128)(2,1)S(1)} collective-permute-done((bf16[256,384]{1,0:T(8,128)(2,1)S(1)}, bf16[256,384]{1,0:T(8,128)(2,1)S(1)}, u32[]{:S(2)}, u32[]{:S(2)}) %collective-permute-start.9) | collective-permute-done | bytes 196640 | tf_op jit(solution)/shard_map/spread_features/ppermute | solution.py:263
  43.1 1.3 %aggregate.9 = bf16[2,8,64,384]{3,2,1,0:T(8,128)(2,1)} custom-call(bf16[2,4,512,512]{3,2,1,0:T(8,128)(2,1)S(1)} %spread_tiles.1.refs_0_, f32[2,512,384]{2,1,0:T(8,128)S(1)} %aggregate.8.refs_1_, bf16[256,384]{1,0:T(8,128)(2,1)S(1)} %collective-permute-done.10.refs_2_), custom_call_target="tpu_custom_call" | custom-call | flops 201326592 | bytes 1048576 | tf_op jit(solution)/shard_map/aggregate/pallas_call | solution.py:230
  44.5 10.2 %all-to-all-start = ((bf16[16,64,384]{2,1,0:T(8,128)(2,1)}), bf16[16,64,384]{2,1,0:T(8,128)(2,1)S(1)}, u32[]{:S(2)}, u32[]{:S(2)}) async-start(bf16[16,64,384]{2,1,0:T(8,128)(2,1)} %bitcast), calls=%async_computation | async-start | bytes 1572864 | tf_op jit(solution)/shard_map/sum_over_rep/all_to_all | solution.py:271
  54.6 12.2 %all-to-all-done.recv = bf16[16,64,384]{2,1,0:T(8,128)(2,1)S(1)} async-done(((bf16[16,64,384]{2,1,0:T(8,128)(2,1)}), bf16[16,64,384]{2,1,0:T(8,128)(2,1)S(1)}, u32[]{:S(2)}, u32[]{:S(2)}) %all-to-all-start) | async-done | bytes 786464 | tf_op jit(solution)/shard_map/sum_over_rep/all_to_all | solution.py:271
  66.8 1.0 layer.1
  67.9 15.2 %all_to_all.26 = bf16[16,64,384]{2,1,0:T(8,128)(2,1)S(1)} all-to-all(bf16[16,64,384]{2,1,0:T(8,128)(2,1)S(1)} %get-tuple-element.24), channel_id=1, replica_groups=mesh['y'=4,'zh'=4,'core'=2,'x'=4,'zl'=2] {'x','y'}, dimensions={0} | all-to-all | bytes 1572864 | tf_op jit(solution)/shard_map/exchange_rows/all_to_all | solution.py:280
  83.8 2.7 %collective-permute-start.11 = (bf16[56,384]{1,0:T(8,128)(2,1)S(1)}, bf16[56,384]{1,0:T(8,128)(2,1)S(1)}, u32[]{:S(2)}, u32[]{:S(2)}) collective-permute-start(bf16[56,384]{1,0:T(8,128)(2,1)S(1)} %get-tuple-element.26), channel_id=1, source_target_pairs={{0,8},{8,0},{1,9},{9,1},{2,10},{10,2},{3,11},{11,3},{4,12},{12,4},... | collective-permute-start | bytes 129032 | tf_op jit(solution)/shard_map/weight_block/ppermute | solution.py:287
  86.5 1.1 collective-permute-start.12
  88.2 1.2 collective-permute-done.12.refs_2_
  89.4 1.8 %collective-permute-done.13.refs_3_ = bf16[56,384]{1,0:T(8,128)(2,1)S(1)} collective-permute-done((bf16[56,384]{1,0:T(8,128)(2,1)S(1)}, bf16[56,384]{1,0:T(8,128)(2,1)S(1)}, u32[]{:S(2)}, u32[]{:S(2)}) %collective-permute-start.13) | collective-permute-done | bytes 43040 | tf_op jit(solution)/shard_map/weight_block/ppermute | solution.py:286
  91.2 4.4 %collective-permute-start.14 = (bf16[56,384]{1,0:T(8,128)(2,1)S(1)}, bf16[56,384]{1,0:T(8,128)(2,1)S(1)}, u32[]{:S(2)}, u32[]{:S(2)}) collective-permute-start(bf16[56,384]{1,0:T(8,128)(2,1)S(1)} %weight_block.3.refs_0_), channel_id=1, source_target_pairs={{0,32},{16,48},{32,0},{48,16},{1,33},{17,49},{33,1},{49,17},{2,34}... | collective-permute-start | bytes 129032 | tf_op jit(solution)/shard_map/sum_over_z/ppermute | solution.py:292
  95.6 2.3 %collective-permute-start.15 = (bf16[56,384]{1,0:T(8,128)(2,1)S(1)}, bf16[56,384]{1,0:T(8,128)(2,1)S(1)}, u32[]{:S(2)}, u32[]{:S(2)}) collective-permute-start(bf16[56,384]{1,0:T(8,128)(2,1)S(1)} %weight_block.3.refs_0_), channel_id=1, source_target_pairs={{0,16},{16,32},{32,48},{48,0},{1,17},{17,33},{33,49},{49,1},{2,18}... | collective-permute-start | bytes 129032 | tf_op jit(solution)/shard_map/sum_over_z/ppermute | solution.py:292
  97.9 1.2 %collective-permute-start.16 = (bf16[56,384]{1,0:T(8,128)(2,1)S(1)}, bf16[56,384]{1,0:T(8,128)(2,1)S(1)}, u32[]{:S(2)}, u32[]{:S(2)}) collective-permute-start(bf16[56,384]{1,0:T(8,128)(2,1)S(1)} %weight_block.3.refs_0_), channel_id=1, source_target_pairs={{0,48},{16,0},{32,16},{48,32},{1,49},{17,1},{33,17},{49,33},{2,50}... | collective-permute-start | bytes 129032 | tf_op jit(solution)/shard_map/sum_over_z/ppermute | solution.py:292
  99.1 1.7 %collective-permute-done.15.refs_2_ = bf16[56,384]{1,0:T(8,128)(2,1)S(1)} collective-permute-done((bf16[56,384]{1,0:T(8,128)(2,1)S(1)}, bf16[56,384]{1,0:T(8,128)(2,1)S(1)}, u32[]{:S(2)}, u32[]{:S(2)}) %collective-permute-start.15) | collective-permute-done | bytes 43040 | tf_op jit(solution)/shard_map/sum_over_z/ppermute | solution.py:292
  100.8 1.1 collective-permute-done.16.refs_3_
  102.0 13.9 %all_to_all.27.own = bf16[16,56,384]{2,1,0:T(8,128)(2,1)S(1)} all-to-all(bf16[16,56,384]{2,1,0:T(8,128)(2,1)S(1)} %sum_over_z.1), channel_id=1, replica_groups=mesh['y'=4,'zh'=4,'core'=2,'x'=4,'zl'=2] {'x','y'}, dimensions={0} | all-to-all | bytes 1376256 | tf_op jit(solution)/shard_map/gather_plane/all_to_all | solution.py:297
  115.9 3.3 %collective-permute-start.17 = (bf16[896,384]{1,0:T(8,128)(2,1)S(1)}, bf16[896,384]{1,0:T(8,128)(2,1)S(1)}, u32[]{:S(2)}, u32[]{:S(2)}) collective-permute-start(bf16[896,384]{1,0:T(8,128)(2,1)S(1)} %bitcast.5), channel_id=1, source_target_pairs={{0,8},{8,0},{1,9},{9,1},{2,10},{10,2},{3,11},{11,3},{4,12},{12,4},... | collective-permute-start | bytes 2064392 | tf_op jit(solution)/shard_map/gather_plane/ppermute | solution.py:298
  119.2 1.1 finish.2
  121.0 1.1 finish.3
  (37 shorter events, 7.8 us)
Async XLA Ops:
  0.6 1.1 copy-start.2
  1.8 13.7 %collective-permute-start.3 = (bf16[4,4,4,128,128]{4,3,2,1,0:T(8,128)(2,1)}, bf16[4,4,4,128,128]{4,3,2,1,0:T(8,128)(2,1)S(1)}, u32[]{:S(2)}, u32[]{:S(2)}) collective-permute-start(bf16[4,4,4,128,128]{4,3,2,1,0:T(8,128)(2,1)} %tiles), channel_id=1, source_target_pairs={{0,8},{8,0},{1,9},{9,1},{2,10},{10,2},{3,11},{11,3},{4,12},{12,4},... | collective-permute-start | bytes 6291464 | tf_op jit(solution)/shard_map/spread_tiles/ppermute | solution.py:252
  5.2 17.0 %collective-permute-start = (bf16[256,384]{1,0:T(8,128)(2,1)S(1)}, bf16[256,384]{1,0:T(8,128)(2,1)S(1)}, u32[]{:S(2)}, u32[]{:S(2)}) collective-permute-start(bf16[256,384]{1,0:T(8,128)(2,1)S(1)} %get-tuple-element.18), channel_id=1, source_target_pairs={{0,176},{1,168},{2,64},{3,216},{4,16},{5,72},{6,224},{7,56},{8,80}... | collective-permute-start | bytes 589832 | tf_op jit(solution)/shard_map/spread_features/ppermute | solution.py:250
  7.4 20.9 %collective-permute-start.4 = (bf16[256,384]{1,0:T(8,128)(2,1)S(1)}, bf16[256,384]{1,0:T(8,128)(2,1)S(1)}, u32[]{:S(2)}, u32[]{:S(2)}) collective-permute-start(bf16[256,384]{1,0:T(8,128)(2,1)S(1)} %get-tuple-element.22), channel_id=1, source_target_pairs={{0,176},{1,168},{2,64},{3,216},{4,16},{5,72},{6,224},{7,56},{8,80}... | collective-permute-start | bytes 589832 | tf_op jit(solution)/shard_map/spread_features/ppermute | solution.py:250
  10.6 4.5 %collective-permute-start.1 = (s32[4,4,4]{2,1,0:T(4,128)}, s32[4,4,4]{2,1,0:T(4,128)S(1)}, u32[]{:S(2)}, u32[]{:S(2)}) collective-permute-start(s32[4,4,4]{2,1,0:T(4,128)} %cols.1), channel_id=1, source_target_pairs={{0,8},{8,0},{1,9},{9,1},{2,10},{10,2},{3,11},{11,3},{4,12},{12,4},... | collective-permute-start | bytes 776 | tf_op jit(solution)/shard_map/spread_tiles/ppermute | solution.py:252
  14.1 1.4 %collective-permute-start.2 = (s32[4,4,4]{2,1,0:T(4,128)}, s32[4,4,4]{2,1,0:T(4,128)S(1)}, u32[]{:S(2)}, u32[]{:S(2)}) collective-permute-start(s32[4,4,4]{2,1,0:T(4,128)} %live.1), channel_id=1, source_target_pairs={{0,8},{8,0},{1,9},{9,1},{2,10},{10,2},{3,11},{11,3},{4,12},{12,4},... | collective-permute-start | bytes 776 | tf_op jit(solution)/shard_map/spread_tiles/ppermute | solution.py:252
  15.5 1.6 %copy-start = (bf16[4,4,4,128,128]{4,3,2,1,0:T(8,128)(2,1)S(1)}, bf16[4,4,4,128,128]{4,3,2,1,0:T(8,128)(2,1)}, u32[]{:S(2)}) copy-start(bf16[4,4,4,128,128]{4,3,2,1,0:T(8,128)(2,1)} %tiles) | copy-start | bytes 6291460
  17.1 0.7 copy-start.4
  17.8 0.7 copy-start.5
  22.1 10.8 %collective-permute-start.5 = (bf16[256,384]{1,0:T(8,128)(2,1)S(1)}, bf16[256,384]{1,0:T(8,128)(2,1)S(1)}, u32[]{:S(2)}, u32[]{:S(2)}) collective-permute-start(bf16[256,384]{1,0:T(8,128)(2,1)S(1)} %collective-permute-done.refs_1_), channel_id=1, source_target_pairs={{0,128},{64,192},{128,0},{192,64},{1,129},{65,193},{129,1},{193,65... | collective-permute-start | bytes 589832 | tf_op jit(solution)/shard_map/spread_features/ppermute | solution.py:261
  25.7 9.6 %collective-permute-start.6 = (bf16[256,384]{1,0:T(8,128)(2,1)S(1)}, bf16[256,384]{1,0:T(8,128)(2,1)S(1)}, u32[]{:S(2)}, u32[]{:S(2)}) collective-permute-start(bf16[256,384]{1,0:T(8,128)(2,1)S(1)} %collective-permute-done.refs_1_), channel_id=1, source_target_pairs={{0,64},{64,128},{128,192},{192,0},{1,65},{65,129},{129,193},{193,1... | collective-permute-start | bytes 589832 | tf_op jit(solution)/shard_map/spread_features/ppermute | solution.py:261
  26.9 8.3 %collective-permute-start.7 = (bf16[256,384]{1,0:T(8,128)(2,1)S(1)}, bf16[256,384]{1,0:T(8,128)(2,1)S(1)}, u32[]{:S(2)}, u32[]{:S(2)}) collective-permute-start(bf16[256,384]{1,0:T(8,128)(2,1)S(1)} %collective-permute-done.refs_1_), channel_id=1, source_target_pairs={{0,192},{64,0},{128,64},{192,128},{1,193},{65,1},{129,65},{193,129... | collective-permute-start | bytes 589832 | tf_op jit(solution)/shard_map/spread_features/ppermute | solution.py:261
  28.4 8.8 %collective-permute-start.8 = (bf16[256,384]{1,0:T(8,128)(2,1)S(1)}, bf16[256,384]{1,0:T(8,128)(2,1)S(1)}, u32[]{:S(2)}, u32[]{:S(2)}) collective-permute-start(bf16[256,384]{1,0:T(8,128)(2,1)S(1)} %collective-permute-done.4.refs_2_), channel_id=1, source_target_pairs={{0,128},{64,192},{128,0},{192,64},{1,129},{65,193},{129,1},{193,65... | collective-permute-start | bytes 589832 | tf_op jit(solution)/shard_map/spread_features/ppermute | solution.py:263
  28.7 13.9 %collective-permute-start.9 = (bf16[256,384]{1,0:T(8,128)(2,1)S(1)}, bf16[256,384]{1,0:T(8,128)(2,1)S(1)}, u32[]{:S(2)}, u32[]{:S(2)}) collective-permute-start(bf16[256,384]{1,0:T(8,128)(2,1)S(1)} %collective-permute-done.4.refs_2_), channel_id=1, source_target_pairs={{0,64},{64,128},{128,192},{192,0},{1,65},{65,129},{129,193},{193,1... | collective-permute-start | bytes 589832 | tf_op jit(solution)/shard_map/spread_features/ppermute | solution.py:263
  33.0 10.2 %collective-permute-start.10 = (bf16[256,384]{1,0:T(8,128)(2,1)S(1)}, bf16[256,384]{1,0:T(8,128)(2,1)S(1)}, u32[]{:S(2)}, u32[]{:S(2)}) collective-permute-start(bf16[256,384]{1,0:T(8,128)(2,1)S(1)} %collective-permute-done.4.refs_2_), channel_id=1, source_target_pairs={{0,192},{64,0},{128,64},{192,128},{1,193},{65,1},{129,65},{193,129... | collective-permute-start | bytes 589832 | tf_op jit(solution)/shard_map/spread_features/ppermute | solution.py:263
  43.1 11.5 %copy-start.6 = (f32[768]{0:T(1024)S(1)}, f32[768]{0:T(1024)}, u32[]{:S(2)}) copy-start(f32[768]{0:T(1024)} %param.12) | copy-start | bytes 9220
  43.1 23.7 %copy-start.3 = (bf16[64,768]{1,0:T(8,128)(2,1)S(1)}, bf16[64,768]{1,0:T(8,128)(2,1)}, u32[]{:S(2)}) copy-start(bf16[64,768]{1,0:T(8,128)(2,1)} %cot.1) | copy-start | bytes 294916
  44.5 22.3 %copy-start.1 = (bf16[768,768]{1,0:T(8,128)(2,1)S(1)}, bf16[768,768]{1,0:T(8,128)(2,1)}, u32[]{:S(2)}) copy-start(bf16[768,768]{1,0:T(8,128)(2,1)} %weight.1) | copy-start | bytes 3538948
  44.5 22.3 %all-to-all-start = ((bf16[16,64,384]{2,1,0:T(8,128)(2,1)}), bf16[16,64,384]{2,1,0:T(8,128)(2,1)S(1)}, u32[]{:S(2)}, u32[]{:S(2)}) async-start(bf16[16,64,384]{2,1,0:T(8,128)(2,1)} %bitcast), calls=%async_computation | async-start | bytes 1572864 | tf_op jit(solution)/shard_map/sum_over_rep/all_to_all | solution.py:271
  83.8 4.4 %collective-permute-start.11 = (bf16[56,384]{1,0:T(8,128)(2,1)S(1)}, bf16[56,384]{1,0:T(8,128)(2,1)S(1)}, u32[]{:S(2)}, u32[]{:S(2)}) collective-permute-start(bf16[56,384]{1,0:T(8,128)(2,1)S(1)} %get-tuple-element.26), channel_id=1, source_target_pairs={{0,8},{8,0},{1,9},{9,1},{2,10},{10,2},{3,11},{11,3},{4,12},{12,4},... | collective-permute-start | bytes 129032 | tf_op jit(solution)/shard_map/weight_block/ppermute | solution.py:287
  86.5 2.9 %collective-permute-start.12 = (bf16[56,384]{1,0:T(8,128)(2,1)S(1)}, bf16[56,384]{1,0:T(8,128)(2,1)S(1)}, u32[]{:S(2)}, u32[]{:S(2)}) collective-permute-start(bf16[56,384]{1,0:T(8,128)(2,1)S(1)} %get-tuple-element.25.refs_0_), channel_id=1, source_target_pairs={{0,1},{1,0},{2,3},{3,2},{4,5},{5,4},{6,7},{7,6},{8,9},{9,8},{10,11... | collective-permute-start | bytes 129032 | tf_op jit(solution)/shard_map/weight_block/ppermute | solution.py:285
  87.6 3.6 %collective-permute-start.13 = (bf16[56,384]{1,0:T(8,128)(2,1)S(1)}, bf16[56,384]{1,0:T(8,128)(2,1)S(1)}, u32[]{:S(2)}, u32[]{:S(2)}) collective-permute-start(bf16[56,384]{1,0:T(8,128)(2,1)S(1)} %get-tuple-element.26), channel_id=1, source_target_pairs={{0,9},{1,8},{8,1},{9,0},{2,11},{3,10},{10,3},{11,2},{4,13},{5,12},... | collective-permute-start | bytes 129032 | tf_op jit(solution)/shard_map/weight_block/ppermute | solution.py:286
  91.2 8.0 %collective-permute-start.14 = (bf16[56,384]{1,0:T(8,128)(2,1)S(1)}, bf16[56,384]{1,0:T(8,128)(2,1)S(1)}, u32[]{:S(2)}, u32[]{:S(2)}) collective-permute-start(bf16[56,384]{1,0:T(8,128)(2,1)S(1)} %weight_block.3.refs_0_), channel_id=1, source_target_pairs={{0,32},{16,48},{32,0},{48,16},{1,33},{17,49},{33,1},{49,17},{2,34}... | collective-permute-start | bytes 129032 | tf_op jit(solution)/shard_map/sum_over_z/ppermute | solution.py:292
  95.6 5.3 %collective-permute-start.15 = (bf16[56,384]{1,0:T(8,128)(2,1)S(1)}, bf16[56,384]{1,0:T(8,128)(2,1)S(1)}, u32[]{:S(2)}, u32[]{:S(2)}) collective-permute-start(bf16[56,384]{1,0:T(8,128)(2,1)S(1)} %weight_block.3.refs_0_), channel_id=1, source_target_pairs={{0,16},{16,32},{32,48},{48,0},{1,17},{17,33},{33,49},{49,1},{2,18}... | collective-permute-start | bytes 129032 | tf_op jit(solution)/shard_map/sum_over_z/ppermute | solution.py:292
  97.9 4.1 %collective-permute-start.16 = (bf16[56,384]{1,0:T(8,128)(2,1)S(1)}, bf16[56,384]{1,0:T(8,128)(2,1)S(1)}, u32[]{:S(2)}, u32[]{:S(2)}) collective-permute-start(bf16[56,384]{1,0:T(8,128)(2,1)S(1)} %weight_block.3.refs_0_), channel_id=1, source_target_pairs={{0,48},{16,0},{32,16},{48,32},{1,49},{17,1},{33,17},{49,33},{2,50}... | collective-permute-start | bytes 129032 | tf_op jit(solution)/shard_map/sum_over_z/ppermute | solution.py:292
  115.9 5.1 %collective-permute-start.17 = (bf16[896,384]{1,0:T(8,128)(2,1)S(1)}, bf16[896,384]{1,0:T(8,128)(2,1)S(1)}, u32[]{:S(2)}, u32[]{:S(2)}) collective-permute-start(bf16[896,384]{1,0:T(8,128)(2,1)S(1)} %bitcast.5), channel_id=1, source_target_pairs={{0,8},{8,0},{1,9},{9,1},{2,10},{10,2},{3,11},{11,3},{4,12},{12,4},... | collective-permute-start | bytes 2064392 | tf_op jit(solution)/shard_map/gather_plane/ppermute | solution.py:298

commit v6 on v5

--- a/solution.py
+++ b/solution.py
@@ -57,7 +57,7 @@
     return jax.ShapeDtypeStruct(shape, dtype)
 
 
-def call(kernel, shapes, specs, out_specs, scratch=(), aliases=None, flops=0):
+def call(kernel, shapes, specs, out_specs, scratch=(), aliases=None, flops=0, limit=VMEM_LIMIT):
     return pl.pallas_call(
         kernel,
         out_shape=shapes,
@@ -65,7 +65,7 @@
         out_specs=out_specs,
         scratch_shapes=scratch,
         input_output_aliases=aliases or {},
-        compiler_params=pltpu.CompilerParams(vmem_limit_bytes=VMEM_LIMIT),
+        compiler_params=pltpu.CompilerParams(vmem_limit_bytes=limit),
         cost_estimate=pl.CostEstimate(flops=flops, bytes_accessed=1 << 20, transcendentals=0),
     )
 
@@ -128,9 +128,7 @@
 def last_kernel(keys, mix, begun, *refs):
     core = lax.axis_index("core")
     for d, at in enumerate((core, 1 - core)):
-        total = (begun[d] + terms(d, mix, keys, refs[:-1])).astype(BF)
-        for r in range(8):
-            refs[-1][at, r] = total[r * 64 : (r + 1) * 64]
+        refs[-1][at] = (begun[d] + terms(d, mix, keys, refs[:-1])).astype(BF)
 
 
 def layer_kernel(recv, weight, bias, cot, out, packed):
@@ -229,7 +227,7 @@
     extra = [] if begun is None else [begun]
     return call(
         lambda *refs: kernel(keys, *refs),
-        struct((2, 8, 64, 384), BF) if last else struct((2, 512, 384), F32),
+        struct((2, 512, 384), BF) if last else struct((2, 512, 384), F32),
         [vmem()] * (1 + len(extra) + len(parts)),
         vmem(),
         aliases={1: 0} if extra and not last else None,
@@ -245,6 +243,7 @@
             [hbm()],
             (vmem(), vmem()),
             [pltpu.SemaphoreType.DMA((2,))],
+            limit=60 * 1024 * 1024,
         )(features)
         *halves, tiles = lax.optimization_barrier((*halves, tiles))
         own = [lax.ppermute(half, AXES, first_hop()) for half in halves]

time: 123 us -> 123 us (level)
  Pallas kernels: 11.8 us -> 13.5 us
    pallas_call x1, Pallas kernels: 0.06 us -> 1.78 us  [on_device(): call(pick_kernel, (struct((256, 384), BF), struct((256, 384), BF)), [hbm(...]
    unnamed x14 -> x12, local copies, waits for them, and re-layouts: 4.13 us -> 3 us
where the time goes in v6:
time: 123 us
  starting transfers between devices  49.4 us (40%)
  blocking collectives  29.1 us (24%)
  waiting for transfers between devices  26.5 us (22%)
  Pallas kernels  13.5 us (11%)
  local copies, waits for them, and re-layouts  3.01 us (2%)
    all_to_all x1, blocking collectives, on_device(): rows = lax.all_to_all(packed.reshape(1024, 384), PLANE, 0, 0, tiled=True)  15.3 us
    all_to_all x1, blocking collectives, on_device(): mine = lax.all_to_all(whole.reshape(896, 384), PLANE, 0, 0, tiled=True)  13.9 us
    all_to_all x1, waiting for transfers between devices, on_device(): lax.all_to_all(partial.reshape(1024, 384), ('core',) + REP, 0, 0, tiled=T...  12.2 us
    all_to_all x1, starting transfers between devices, on_device(): lax.all_to_all(partial.reshape(1024, 384), ('core',) + REP, 0, 0, tiled=T...  10.3 us
    ppermute x3, starting transfers between devices, on_device(): chain = [lax.ppermute(pair, 'zh', shift(4, back)) for back in BACK]  8 us
    ppermute x3, starting transfers between devices, on_device(): lax.ppermute(value, 'core', shift(2, 1))  6.8 us
    ppermute x3, starting transfers between devices, on_device(): early = [lax.ppermute(own[0], 'y', shift(4, back)) for back in BACK]  6.22 us
    ppermute x3, waiting for transfers between devices, on_device(): late = [lax.ppermute(own[1], 'y', shift(4, back)) for back in BACK]  5.73 us
  transfers between devices with their start and end apart: 19, of which 10 were waited for; matrix products, arithmetic and copies ran while one was open for 0% of the time, Pallas kernels for 6%

profile of v6, /device:TPU:1, one launch (start us, length us, event | category | flops | bytes accessed | tf_op | source)
XLA Modules:
  0.0 123.1 jit_solution(12279458502687696882)
XLA Ops:
  0.6 1.8 %spread_features.1 = (bf16[256,384]{1,0:T(8,128)(2,1)}, bf16[256,384]{1,0:T(8,128)(2,1)}) custom-call(bf16[512,768]{1,0:T(8,128)(2,1)} %features.1), custom_call_target="tpu_custom_call" | custom-call | bytes 1048576 | tf_op jit(solution)/shard_map/spread_features/pallas_call | solution.py:240
  2.4 3.3 %collective-permute-start.3 = (bf16[4,4,4,128,128]{4,3,2,1,0:T(8,128)(2,1)}, bf16[4,4,4,128,128]{4,3,2,1,0:T(8,128)(2,1)S(1)}, u32[]{:S(2)}, u32[]{:S(2)}) collective-permute-start(bf16[4,4,4,128,128]{4,3,2,1,0:T(8,128)(2,1)} %tiles), channel_id=1, source_target_pairs={{0,8},{8,0},{1,9},{9,1},{2,10},{10,2},{3,11},{11,3},{4,12},{12,4},... | collective-permute-start | bytes 6291464 | tf_op jit(solution)/shard_map/spread_tiles/ppermute | solution.py:251
  5.7 2.3 %collective-permute-start = (bf16[256,384]{1,0:T(8,128)(2,1)}, bf16[256,384]{1,0:T(8,128)(2,1)S(1)}, u32[]{:S(2)}, u32[]{:S(2)}) collective-permute-start(bf16[256,384]{1,0:T(8,128)(2,1)} %get-tuple-element.18), channel_id=1, source_target_pairs={{0,176},{1,168},{2,64},{3,216},{4,16},{5,72},{6,224},{7,56},{8,80}... | collective-permute-start | bytes 589832 | tf_op jit(solution)/shard_map/spread_features/ppermute | solution.py:249
  8.0 3.2 %collective-permute-start.4 = (bf16[256,384]{1,0:T(8,128)(2,1)}, bf16[256,384]{1,0:T(8,128)(2,1)S(1)}, u32[]{:S(2)}, u32[]{:S(2)}) collective-permute-start(bf16[256,384]{1,0:T(8,128)(2,1)} %get-tuple-element.22), channel_id=1, source_target_pairs={{0,176},{1,168},{2,64},{3,216},{4,16},{5,72},{6,224},{7,56},{8,80}... | collective-permute-start | bytes 589832 | tf_op jit(solution)/shard_map/spread_features/ppermute | solution.py:249
  11.2 3.5 %collective-permute-start.1 = (s32[4,4,4]{2,1,0:T(4,128)}, s32[4,4,4]{2,1,0:T(4,128)S(1)}, u32[]{:S(2)}, u32[]{:S(2)}) collective-permute-start(s32[4,4,4]{2,1,0:T(4,128)} %cols.1), channel_id=1, source_target_pairs={{0,8},{8,0},{1,9},{9,1},{2,10},{10,2},{3,11},{11,3},{4,12},{12,4},... | collective-permute-start | bytes 776 | tf_op jit(solution)/shard_map/spread_tiles/ppermute | solution.py:251
  16.1 1.6 %copy-done = bf16[4,4,4,128,128]{4,3,2,1,0:T(8,128)(2,1)S(1)} copy-done((bf16[4,4,4,128,128]{4,3,2,1,0:T(8,128)(2,1)S(1)}, bf16[4,4,4,128,128]{4,3,2,1,0:T(8,128)(2,1)}, u32[]{:S(2)}) %copy-start) | copy-done | bytes 2097176
  19.1 3.6 %spread_tiles.1.refs_0_ = bf16[2,4,512,512]{3,2,1,0:T(8,128)(2,1)S(1)} custom-call(s32[4,4,4]{2,1,0:T(4,128)S(1)} %copy-done.3, s32[4,4,4]{2,1,0:T(4,128)S(1)} %copy-done.4, s32[4,4,4]{2,1,0:T(4,128)S(1)} %collective-permute-done.1.other_cols, s32[4,4,4]{2,1,0:T(4,128)S(1)} %collective-permute-done.2.other_live, bf16[4,4,4,128,128]{4,3,2,1,0:T(8,128)(2,1)S(1)} %copy-done, ...), custom_call_target="tpu_custom_call" | custom-call | bytes 1048576 | tf_op jit(solution)/shard_map/spread_tiles/pallas_call | solution.py:252
  22.7 3.5 %collective-permute-start.5 = (bf16[256,384]{1,0:T(8,128)(2,1)S(1)}, bf16[256,384]{1,0:T(8,128)(2,1)S(1)}, u32[]{:S(2)}, u32[]{:S(2)}) collective-permute-start(bf16[256,384]{1,0:T(8,128)(2,1)S(1)} %collective-permute-done.refs_1_), channel_id=1, source_target_pairs={{0,128},{64,192},{128,0},{192,64},{1,129},{65,193},{129,1},{193,65... | collective-permute-start | bytes 589832 | tf_op jit(solution)/shard_map/spread_features/ppermute | solution.py:260
  26.3 1.2 %collective-permute-start.6 = (bf16[256,384]{1,0:T(8,128)(2,1)S(1)}, bf16[256,384]{1,0:T(8,128)(2,1)S(1)}, u32[]{:S(2)}, u32[]{:S(2)}) collective-permute-start(bf16[256,384]{1,0:T(8,128)(2,1)S(1)} %collective-permute-done.refs_1_), channel_id=1, source_target_pairs={{0,64},{64,128},{128,192},{192,0},{1,65},{65,129},{129,193},{193,1... | collective-permute-start | bytes 589832 | tf_op jit(solution)/shard_map/spread_features/ppermute | solution.py:260
  27.5 1.4 %collective-permute-start.7 = (bf16[256,384]{1,0:T(8,128)(2,1)S(1)}, bf16[256,384]{1,0:T(8,128)(2,1)S(1)}, u32[]{:S(2)}, u32[]{:S(2)}) collective-permute-start(bf16[256,384]{1,0:T(8,128)(2,1)S(1)} %collective-permute-done.refs_1_), channel_id=1, source_target_pairs={{0,192},{64,0},{128,64},{192,128},{1,193},{65,1},{129,65},{193,129... | collective-permute-start | bytes 589832 | tf_op jit(solution)/shard_map/spread_features/ppermute | solution.py:260
  29.3 4.5 %collective-permute-start.9 = (bf16[256,384]{1,0:T(8,128)(2,1)S(1)}, bf16[256,384]{1,0:T(8,128)(2,1)S(1)}, u32[]{:S(2)}, u32[]{:S(2)}) collective-permute-start(bf16[256,384]{1,0:T(8,128)(2,1)S(1)} %collective-permute-done.4.refs_2_), channel_id=1, source_target_pairs={{0,64},{64,128},{128,192},{192,0},{1,65},{65,129},{129,193},{193,1... | collective-permute-start | bytes 589832 | tf_op jit(solution)/shard_map/spread_features/ppermute | solution.py:262
  34.6 1.5 %collective-permute-done.6.refs_3_ = bf16[256,384]{1,0:T(8,128)(2,1)S(1)} collective-permute-done((bf16[256,384]{1,0:T(8,128)(2,1)S(1)}, bf16[256,384]{1,0:T(8,128)(2,1)S(1)}, u32[]{:S(2)}, u32[]{:S(2)}) %collective-permute-start.6) | collective-permute-done | bytes 196640 | tf_op jit(solution)/shard_map/spread_features/ppermute | solution.py:260
  36.0 1.1 aggregate.6.refs_1_
  38.1 5.2 %collective-permute-done.9.refs_2_ = bf16[256,384]{1,0:T(8,128)(2,1)S(1)} collective-permute-done((bf16[256,384]{1,0:T(8,128)(2,1)S(1)}, bf16[256,384]{1,0:T(8,128)(2,1)S(1)}, u32[]{:S(2)}, u32[]{:S(2)}) %collective-permute-start.9) | collective-permute-done | bytes 196640 | tf_op jit(solution)/shard_map/spread_features/ppermute | solution.py:262
  43.8 1.3 %aggregate.9 = bf16[2,512,384]{2,1,0:T(8,128)(2,1)} custom-call(bf16[2,4,512,512]{3,2,1,0:T(8,128)(2,1)S(1)} %spread_tiles.1.refs_0_, f32[2,512,384]{2,1,0:T(8,128)S(1)} %aggregate.8.refs_1_, bf16[256,384]{1,0:T(8,128)(2,1)S(1)} %collective-permute-done.10.refs_2_), custom_call_target="tpu_custom_call" | custom-call | flops 201326592 | bytes 1048576 | tf_op jit(solution)/shard_map/aggregate/pallas_call | solution.py:228
  45.1 10.3 %all-to-all-start = ((bf16[16,64,384]{2,1,0:T(8,128)(2,1)}), bf16[16,64,384]{2,1,0:T(8,128)(2,1)S(1)}, u32[]{:S(2)}, u32[]{:S(2)}) async-start(bf16[16,64,384]{2,1,0:T(8,128)(2,1)} %bitcast), calls=%async_computation | async-start | bytes 1572864 | tf_op jit(solution)/shard_map/sum_over_rep/all_to_all | solution.py:270
  55.4 12.2 %all-to-all-done.recv = bf16[16,64,384]{2,1,0:T(8,128)(2,1)S(1)} async-done(((bf16[16,64,384]{2,1,0:T(8,128)(2,1)}), bf16[16,64,384]{2,1,0:T(8,128)(2,1)S(1)}, u32[]{:S(2)}, u32[]{:S(2)}) %all-to-all-start) | async-done | bytes 786464 | tf_op jit(solution)/shard_map/sum_over_rep/all_to_all | solution.py:270
  67.6 1.0 layer.1
  68.6 15.3 %all_to_all.26 = bf16[16,64,384]{2,1,0:T(8,128)(2,1)S(1)} all-to-all(bf16[16,64,384]{2,1,0:T(8,128)(2,1)S(1)} %get-tuple-element.24), channel_id=1, replica_groups=mesh['y'=4,'zh'=4,'core'=2,'x'=4,'zl'=2] {'x','y'}, dimensions={0} | all-to-all | bytes 1572864 | tf_op jit(solution)/shard_map/exchange_rows/all_to_all | solution.py:279
  84.6 2.7 %collective-permute-start.11 = (bf16[56,384]{1,0:T(8,128)(2,1)S(1)}, bf16[56,384]{1,0:T(8,128)(2,1)S(1)}, u32[]{:S(2)}, u32[]{:S(2)}) collective-permute-start(bf16[56,384]{1,0:T(8,128)(2,1)S(1)} %get-tuple-element.26), channel_id=1, source_target_pairs={{0,8},{8,0},{1,9},{9,1},{2,10},{10,2},{3,11},{11,3},{4,12},{12,4},... | collective-permute-start | bytes 129032 | tf_op jit(solution)/shard_map/weight_block/ppermute | solution.py:286
  87.3 1.0 collective-permute-start.12
  89.0 1.2 collective-permute-done.12.refs_2_
  90.2 1.7 %collective-permute-done.13.refs_3_ = bf16[56,384]{1,0:T(8,128)(2,1)S(1)} collective-permute-done((bf16[56,384]{1,0:T(8,128)(2,1)S(1)}, bf16[56,384]{1,0:T(8,128)(2,1)S(1)}, u32[]{:S(2)}, u32[]{:S(2)}) %collective-permute-start.13) | collective-permute-done | bytes 43040 | tf_op jit(solution)/shard_map/weight_block/ppermute | solution.py:285
  91.9 4.4 %collective-permute-start.14 = (bf16[56,384]{1,0:T(8,128)(2,1)S(1)}, bf16[56,384]{1,0:T(8,128)(2,1)S(1)}, u32[]{:S(2)}, u32[]{:S(2)}) collective-permute-start(bf16[56,384]{1,0:T(8,128)(2,1)S(1)} %weight_block.3.refs_0_), channel_id=1, source_target_pairs={{0,32},{16,48},{32,0},{48,16},{1,33},{17,49},{33,1},{49,17},{2,34}... | collective-permute-start | bytes 129032 | tf_op jit(solution)/shard_map/sum_over_z/ppermute | solution.py:291
  96.4 2.3 %collective-permute-start.15 = (bf16[56,384]{1,0:T(8,128)(2,1)S(1)}, bf16[56,384]{1,0:T(8,128)(2,1)S(1)}, u32[]{:S(2)}, u32[]{:S(2)}) collective-permute-start(bf16[56,384]{1,0:T(8,128)(2,1)S(1)} %weight_block.3.refs_0_), channel_id=1, source_target_pairs={{0,16},{16,32},{32,48},{48,0},{1,17},{17,33},{33,49},{49,1},{2,18}... | collective-permute-start | bytes 129032 | tf_op jit(solution)/shard_map/sum_over_z/ppermute | solution.py:291
  98.7 1.2 %collective-permute-start.16 = (bf16[56,384]{1,0:T(8,128)(2,1)S(1)}, bf16[56,384]{1,0:T(8,128)(2,1)S(1)}, u32[]{:S(2)}, u32[]{:S(2)}) collective-permute-start(bf16[56,384]{1,0:T(8,128)(2,1)S(1)} %weight_block.3.refs_0_), channel_id=1, source_target_pairs={{0,48},{16,0},{32,16},{48,32},{1,49},{17,1},{33,17},{49,33},{2,50}... | collective-permute-start | bytes 129032 | tf_op jit(solution)/shard_map/sum_over_z/ppermute | solution.py:291
  99.9 1.7 %collective-permute-done.15.refs_2_ = bf16[56,384]{1,0:T(8,128)(2,1)S(1)} collective-permute-done((bf16[56,384]{1,0:T(8,128)(2,1)S(1)}, bf16[56,384]{1,0:T(8,128)(2,1)S(1)}, u32[]{:S(2)}, u32[]{:S(2)}) %collective-permute-start.15) | collective-permute-done | bytes 43040 | tf_op jit(solution)/shard_map/sum_over_z/ppermute | solution.py:291
  101.6 1.1 collective-permute-done.16.refs_3_
  102.8 13.9 %all_to_all.27.own = bf16[16,56,384]{2,1,0:T(8,128)(2,1)S(1)} all-to-all(bf16[16,56,384]{2,1,0:T(8,128)(2,1)S(1)} %sum_over_z.1), channel_id=1, replica_groups=mesh['y'=4,'zh'=4,'core'=2,'x'=4,'zl'=2] {'x','y'}, dimensions={0} | all-to-all | bytes 1376256 | tf_op jit(solution)/shard_map/gather_plane/all_to_all | solution.py:296
  116.7 3.3 %collective-permute-start.17 = (bf16[896,384]{1,0:T(8,128)(2,1)S(1)}, bf16[896,384]{1,0:T(8,128)(2,1)S(1)}, u32[]{:S(2)}, u32[]{:S(2)}) collective-permute-start(bf16[896,384]{1,0:T(8,128)(2,1)S(1)} %bitcast.5), channel_id=1, source_target_pairs={{0,8},{8,0},{1,9},{9,1},{2,10},{10,2},{3,11},{11,3},{4,12},{12,4},... | collective-permute-start | bytes 2064392 | tf_op jit(solution)/shard_map/gather_plane/ppermute | solution.py:297
  120.0 1.1 finish.2
  121.8 1.1 finish.3
  (35 shorter events, 7.4 us)
Async XLA Ops:
  2.4 13.7 %collective-permute-start.3 = (bf16[4,4,4,128,128]{4,3,2,1,0:T(8,128)(2,1)}, bf16[4,4,4,128,128]{4,3,2,1,0:T(8,128)(2,1)S(1)}, u32[]{:S(2)}, u32[]{:S(2)}) collective-permute-start(bf16[4,4,4,128,128]{4,3,2,1,0:T(8,128)(2,1)} %tiles), channel_id=1, source_target_pairs={{0,8},{8,0},{1,9},{9,1},{2,10},{10,2},{3,11},{11,3},{4,12},{12,4},... | collective-permute-start | bytes 6291464 | tf_op jit(solution)/shard_map/spread_tiles/ppermute | solution.py:251
  5.7 17.0 %collective-permute-start = (bf16[256,384]{1,0:T(8,128)(2,1)}, bf16[256,384]{1,0:T(8,128)(2,1)S(1)}, u32[]{:S(2)}, u32[]{:S(2)}) collective-permute-start(bf16[256,384]{1,0:T(8,128)(2,1)} %get-tuple-element.18), channel_id=1, source_target_pairs={{0,176},{1,168},{2,64},{3,216},{4,16},{5,72},{6,224},{7,56},{8,80}... | collective-permute-start | bytes 589832 | tf_op jit(solution)/shard_map/spread_features/ppermute | solution.py:249
  8.0 20.9 %collective-permute-start.4 = (bf16[256,384]{1,0:T(8,128)(2,1)}, bf16[256,384]{1,0:T(8,128)(2,1)S(1)}, u32[]{:S(2)}, u32[]{:S(2)}) collective-permute-start(bf16[256,384]{1,0:T(8,128)(2,1)} %get-tuple-element.22), channel_id=1, source_target_pairs={{0,176},{1,168},{2,64},{3,216},{4,16},{5,72},{6,224},{7,56},{8,80}... | collective-permute-start | bytes 589832 | tf_op jit(solution)/shard_map/spread_features/ppermute | solution.py:249
  11.2 4.5 %collective-permute-start.1 = (s32[4,4,4]{2,1,0:T(4,128)}, s32[4,4,4]{2,1,0:T(4,128)S(1)}, u32[]{:S(2)}, u32[]{:S(2)}) collective-permute-start(s32[4,4,4]{2,1,0:T(4,128)} %cols.1), channel_id=1, source_target_pairs={{0,8},{8,0},{1,9},{9,1},{2,10},{10,2},{3,11},{11,3},{4,12},{12,4},... | collective-permute-start | bytes 776 | tf_op jit(solution)/shard_map/spread_tiles/ppermute | solution.py:251
  14.7 1.4 %collective-permute-start.2 = (s32[4,4,4]{2,1,0:T(4,128)}, s32[4,4,4]{2,1,0:T(4,128)S(1)}, u32[]{:S(2)}, u32[]{:S(2)}) collective-permute-start(s32[4,4,4]{2,1,0:T(4,128)} %live.1), channel_id=1, source_target_pairs={{0,8},{8,0},{1,9},{9,1},{2,10},{10,2},{3,11},{11,3},{4,12},{12,4},... | collective-permute-start | bytes 776 | tf_op jit(solution)/shard_map/spread_tiles/ppermute | solution.py:251
  16.1 1.6 %copy-start = (bf16[4,4,4,128,128]{4,3,2,1,0:T(8,128)(2,1)S(1)}, bf16[4,4,4,128,128]{4,3,2,1,0:T(8,128)(2,1)}, u32[]{:S(2)}) copy-start(bf16[4,4,4,128,128]{4,3,2,1,0:T(8,128)(2,1)} %tiles) | copy-start | bytes 6291460
  17.7 0.7 copy-start.3
  18.4 0.7 copy-start.4
  22.7 11.1 %collective-permute-start.5 = (bf16[256,384]{1,0:T(8,128)(2,1)S(1)}, bf16[256,384]{1,0:T(8,128)(2,1)S(1)}, u32[]{:S(2)}, u32[]{:S(2)}) collective-permute-start(bf16[256,384]{1,0:T(8,128)(2,1)S(1)} %collective-permute-done.refs_1_), channel_id=1, source_target_pairs={{0,128},{64,192},{128,0},{192,64},{1,129},{65,193},{129,1},{193,65... | collective-permute-start | bytes 589832 | tf_op jit(solution)/shard_map/spread_features/ppermute | solution.py:260
  26.3 9.8 %collective-permute-start.6 = (bf16[256,384]{1,0:T(8,128)(2,1)S(1)}, bf16[256,384]{1,0:T(8,128)(2,1)S(1)}, u32[]{:S(2)}, u32[]{:S(2)}) collective-permute-start(bf16[256,384]{1,0:T(8,128)(2,1)S(1)} %collective-permute-done.refs_1_), channel_id=1, source_target_pairs={{0,64},{64,128},{128,192},{192,0},{1,65},{65,129},{129,193},{193,1... | collective-permute-start | bytes 589832 | tf_op jit(solution)/shard_map/spread_features/ppermute | solution.py:260
  27.5 8.5 %collective-permute-start.7 = (bf16[256,384]{1,0:T(8,128)(2,1)S(1)}, bf16[256,384]{1,0:T(8,128)(2,1)S(1)}, u32[]{:S(2)}, u32[]{:S(2)}) collective-permute-start(bf16[256,384]{1,0:T(8,128)(2,1)S(1)} %collective-permute-done.refs_1_), channel_id=1, source_target_pairs={{0,192},{64,0},{128,64},{192,128},{1,193},{65,1},{129,65},{193,129... | collective-permute-start | bytes 589832 | tf_op jit(solution)/shard_map/spread_features/ppermute | solution.py:260
  28.9 8.7 %collective-permute-start.8 = (bf16[256,384]{1,0:T(8,128)(2,1)S(1)}, bf16[256,384]{1,0:T(8,128)(2,1)S(1)}, u32[]{:S(2)}, u32[]{:S(2)}) collective-permute-start(bf16[256,384]{1,0:T(8,128)(2,1)S(1)} %collective-permute-done.4.refs_2_), channel_id=1, source_target_pairs={{0,128},{64,192},{128,0},{192,64},{1,129},{65,193},{129,1},{193,65... | collective-permute-start | bytes 589832 | tf_op jit(solution)/shard_map/spread_features/ppermute | solution.py:262
  29.3 14.0 %collective-permute-start.9 = (bf16[256,384]{1,0:T(8,128)(2,1)S(1)}, bf16[256,384]{1,0:T(8,128)(2,1)S(1)}, u32[]{:S(2)}, u32[]{:S(2)}) collective-permute-start(bf16[256,384]{1,0:T(8,128)(2,1)S(1)} %collective-permute-done.4.refs_2_), channel_id=1, source_target_pairs={{0,64},{64,128},{128,192},{192,0},{1,65},{65,129},{129,193},{193,1... | collective-permute-start | bytes 589832 | tf_op jit(solution)/shard_map/spread_features/ppermute | solution.py:262
  33.9 9.9 %collective-permute-start.10 = (bf16[256,384]{1,0:T(8,128)(2,1)S(1)}, bf16[256,384]{1,0:T(8,128)(2,1)S(1)}, u32[]{:S(2)}, u32[]{:S(2)}) collective-permute-start(bf16[256,384]{1,0:T(8,128)(2,1)S(1)} %collective-permute-done.4.refs_2_), channel_id=1, source_target_pairs={{0,192},{64,0},{128,64},{192,128},{1,193},{65,1},{129,65},{193,129... | collective-permute-start | bytes 589832 | tf_op jit(solution)/shard_map/spread_features/ppermute | solution.py:262
  43.7 11.6 %copy-start.5 = (f32[768]{0:T(1024)S(1)}, f32[768]{0:T(1024)}, u32[]{:S(2)}) copy-start(f32[768]{0:T(1024)} %param.12) | copy-start | bytes 9220
  43.7 23.8 %copy-start.2 = (bf16[64,768]{1,0:T(8,128)(2,1)S(1)}, bf16[64,768]{1,0:T(8,128)(2,1)}, u32[]{:S(2)}) copy-start(bf16[64,768]{1,0:T(8,128)(2,1)} %cot.1) | copy-start | bytes 294916
  45.1 22.5 %copy-start.1 = (bf16[768,768]{1,0:T(8,128)(2,1)S(1)}, bf16[768,768]{1,0:T(8,128)(2,1)}, u32[]{:S(2)}) copy-start(bf16[768,768]{1,0:T(8,128)(2,1)} %weight.1) | copy-start | bytes 3538948
  45.1 22.5 %all-to-all-start = ((bf16[16,64,384]{2,1,0:T(8,128)(2,1)}), bf16[16,64,384]{2,1,0:T(8,128)(2,1)S(1)}, u32[]{:S(2)}, u32[]{:S(2)}) async-start(bf16[16,64,384]{2,1,0:T(8,128)(2,1)} %bitcast), calls=%async_computation | async-start | bytes 1572864 | tf_op jit(solution)/shard_map/sum_over_rep/all_to_all | solution.py:270
  84.6 4.4 %collective-permute-start.11 = (bf16[56,384]{1,0:T(8,128)(2,1)S(1)}, bf16[56,384]{1,0:T(8,128)(2,1)S(1)}, u32[]{:S(2)}, u32[]{:S(2)}) collective-permute-start(bf16[56,384]{1,0:T(8,128)(2,1)S(1)} %get-tuple-element.26), channel_id=1, source_target_pairs={{0,8},{8,0},{1,9},{9,1},{2,10},{10,2},{3,11},{11,3},{4,12},{12,4},... | collective-permute-start | bytes 129032 | tf_op jit(solution)/shard_map/weight_block/ppermute | solution.py:286
  87.3 2.9 %collective-permute-start.12 = (bf16[56,384]{1,0:T(8,128)(2,1)S(1)}, bf16[56,384]{1,0:T(8,128)(2,1)S(1)}, u32[]{:S(2)}, u32[]{:S(2)}) collective-permute-start(bf16[56,384]{1,0:T(8,128)(2,1)S(1)} %get-tuple-element.25.refs_0_), channel_id=1, source_target_pairs={{0,1},{1,0},{2,3},{3,2},{4,5},{5,4},{6,7},{7,6},{8,9},{9,8},{10,11... | collective-permute-start | bytes 129032 | tf_op jit(solution)/shard_map/weight_block/ppermute | solution.py:284
  88.3 3.6 %collective-permute-start.13 = (bf16[56,384]{1,0:T(8,128)(2,1)S(1)}, bf16[56,384]{1,0:T(8,128)(2,1)S(1)}, u32[]{:S(2)}, u32[]{:S(2)}) collective-permute-start(bf16[56,384]{1,0:T(8,128)(2,1)S(1)} %get-tuple-element.26), channel_id=1, source_target_pairs={{0,9},{1,8},{8,1},{9,0},{2,11},{3,10},{10,3},{11,2},{4,13},{5,12},... | collective-permute-start | bytes 129032 | tf_op jit(solution)/shard_map/weight_block/ppermute | solution.py:285
  91.9 8.0 %collective-permute-start.14 = (bf16[56,384]{1,0:T(8,128)(2,1)S(1)}, bf16[56,384]{1,0:T(8,128)(2,1)S(1)}, u32[]{:S(2)}, u32[]{:S(2)}) collective-permute-start(bf16[56,384]{1,0:T(8,128)(2,1)S(1)} %weight_block.3.refs_0_), channel_id=1, source_target_pairs={{0,32},{16,48},{32,0},{48,16},{1,33},{17,49},{33,1},{49,17},{2,34}... | collective-permute-start | bytes 129032 | tf_op jit(solution)/shard_map/sum_over_z/ppermute | solution.py:291
  96.4 5.3 %collective-permute-start.15 = (bf16[56,384]{1,0:T(8,128)(2,1)S(1)}, bf16[56,384]{1,0:T(8,128)(2,1)S(1)}, u32[]{:S(2)}, u32[]{:S(2)}) collective-permute-start(bf16[56,384]{1,0:T(8,128)(2,1)S(1)} %weight_block.3.refs_0_), channel_id=1, source_target_pairs={{0,16},{16,32},{32,48},{48,0},{1,17},{17,33},{33,49},{49,1},{2,18}... | collective-permute-start | bytes 129032 | tf_op jit(solution)/shard_map/sum_over_z/ppermute | solution.py:291
  98.7 4.1 %collective-permute-start.16 = (bf16[56,384]{1,0:T(8,128)(2,1)S(1)}, bf16[56,384]{1,0:T(8,128)(2,1)S(1)}, u32[]{:S(2)}, u32[]{:S(2)}) collective-permute-start(bf16[56,384]{1,0:T(8,128)(2,1)S(1)} %weight_block.3.refs_0_), channel_id=1, source_target_pairs={{0,48},{16,0},{32,16},{48,32},{1,49},{17,1},{33,17},{49,33},{2,50}... | collective-permute-start | bytes 129032 | tf_op jit(solution)/shard_map/sum_over_z/ppermute | solution.py:291
  116.7 5.1 %collective-permute-start.17 = (bf16[896,384]{1,0:T(8,128)(2,1)S(1)}, bf16[896,384]{1,0:T(8,128)(2,1)S(1)}, u32[]{:S(2)}, u32[]{:S(2)}) collective-permute-start(bf16[896,384]{1,0:T(8,128)(2,1)S(1)} %bitcast.5), channel_id=1, source_target_pairs={{0,8},{8,0},{1,9},{9,1},{2,10},{10,2},{3,11},{11,3},{4,12},{12,4},... | collective-permute-start | bytes 2064392 | tf_op jit(solution)/shard_map/gather_plane/ppermute | solution.py:297

commit v7 on v5

--- a/solution.py
+++ b/solution.py
@@ -16,10 +16,10 @@
 BACK = (2, 1, 3)
 VMEM_LIMIT = 32 * 1024 * 1024
 
-TURN = (((3, 3), (0, 1), (1, 2), (2, 0)), ((2, 0), (3, 3), (1, 2), (0, 1)))
+TURN = (((1, 3), (3, 1), (1, 3), (3, 1)), ((2, 0), (0, 2), (2, 0), (0, 2)))
 OFFSET = (
-    ((1, 2, 3, 0), (2, 1, 0, 3), (2, 0, 1, 3), (3, 2, 0, 1), (2, 3, 1, 0), (0, 1, 2, 3), (0, 2, 3, 1), (1, 0, 2, 3)),
-    ((0, 2, 1, 3), (0, 2, 3, 1), (3, 2, 1, 0), (3, 1, 2, 0), (2, 0, 1, 3), (1, 0, 3, 2), (0, 1, 3, 2), (2, 3, 0, 1)),
+    ((2, 3, 0, 1), (2, 1, 0, 3), (2, 1, 3, 0), (1, 3, 0, 2), (1, 0, 2, 3), (0, 2, 3, 1), (0, 2, 1, 3), (3, 1, 2, 0)),
+    ((0, 2, 3, 1), (3, 1, 2, 0), (3, 2, 1, 0), (0, 3, 1, 2), (2, 0, 1, 3), (2, 3, 0, 1), (1, 0, 2, 3), (1, 0, 3, 2)),
 )
 
 
@@ -224,6 +224,10 @@
         copy.wait()
 
 
+def neighbours(piece, step):
+    return [lax.ppermute(piece, "zh", shift(4, step))] + [lax.ppermute(piece, "y", shift(4, k)) for k in BACK[1:]]
+
+
 def product(kernel, keys, mix, parts, begun=None):
     last = kernel is last_kernel
     extra = [] if begun is None else [begun]
@@ -256,11 +260,11 @@
             [smem(), smem(), smem(), smem(), vmem(), vmem()],
             vmem(),
         )(tile_cols, tile_mask, *there[1:], tiles, there[0])
-    own[0], mix = lax.optimization_barrier((own[0], mix))
+    own[0], mix, bias = lax.optimization_barrier((own[0], mix, bias.reshape(1, 768)))
     with jax.named_scope("spread_features"):
-        early = [lax.ppermute(own[0], "y", shift(4, back)) for back in BACK]
+        early = neighbours(own[0], 3)
     with jax.named_scope("spread_features"):
-        late = [lax.ppermute(own[1], "y", shift(4, back)) for back in BACK]
+        late = neighbours(own[1], 1)
     with jax.named_scope("aggregate"):
         begun = product(first_kernel, [(0, 0), (0, 1)], mix, own)
         begun = product(next_kernel, [(back, 0) for back in BACK], mix, early, begun)
@@ -275,7 +279,7 @@
             (struct((64, 768), BF), struct((16, 64, 384), BF)),
             [vmem()] * 4,
             (vmem(), vmem()),
-        )(recv.reshape(16, 64, 384), weight, bias.reshape(1, 768), cotangent)
+        )(recv.reshape(16, 64, 384), weight, bias, cotangent)
     with jax.named_scope("exchange_rows"):
         rows = lax.all_to_all(packed.reshape(1024, 384), PLANE, 0, 0, tiled=True)
     with jax.named_scope("weight_block"):

time: 123 us -> 126 us (1.024)
  blocking collectives: 29.1 us -> 56.4 us
  starting transfers between devices: 49 us -> 34.2 us
  waiting for transfers between devices: 26.8 us -> 18 us
    all_to_all x0 -> x1, blocking collectives: none -> 23.8 us  [on_device(): lax.all_to_all(partial.reshape(1024, 384), ('core',) + REP, 0, 0, tiled=T...]
    all_to_all x1 -> x0, waiting for transfers between devices: 12.2 us -> none  [on_device(): lax.all_to_all(partial.reshape(1024, 384), ('core',) + REP, 0, 0, tiled=T...]
    all_to_all x1 -> x0, starting transfers between devices: 10.2 us -> none  [on_device(): lax.all_to_all(partial.reshape(1024, 384), ('core',) + REP, 0, 0, tiled=T...]
    ppermute x3, starting transfers between devices: 7.95 us -> 3.75 us  [on_device(): chain = [lax.ppermute(pair, 'zh', shift(4, back)) for back in BACK]]
    ppermute x2, starting transfers between devices: 5.48 us -> 8.55 us  [on_device(): own = [lax.ppermute(half, AXES, first_hop()) for half in halves]]
    ppermute x3, waiting for transfers between devices: 2.82 us -> 5.76 us  [on_device(): chain = [lax.ppermute(pair, 'zh', shift(4, back)) for back in BACK]]
    all_to_all x1, blocking collectives: 15.2 us -> 17.6 us  [on_device(): rows = lax.all_to_all(packed.reshape(1024, 384), PLANE, 0, 0, tiled=True)]
    ppermute x6, starting transfers between devices: 10.8 us -> 8.5 us  [the longest x4 6.05 us: neighbours(): lax.ppermute(piece, 'y', shift(4, k))]
  transfers between devices with their start and end apart: 19 -> 18, of which waited for: 10 -> 8; matrix products, arithmetic and copies ran while one was open for 0% -> 1% of each run, Pallas kernels for 6% -> 6%
where the time goes in v7:
time: 126 us
  blocking collectives  56.4 us (45%)
  starting transfers between devices  34.2 us (27%)
  waiting for transfers between devices  18 us (14%)
  Pallas kernels  10.9 us (9%)
  local copies, waits for them, and re-layouts  4.81 us (4%)
    all_to_all x1, blocking collectives, on_device(): lax.all_to_all(partial.reshape(1024, 384), ('core',) + REP, 0, 0, tiled=T...  23.8 us
    all_to_all x1, blocking collectives, on_device(): rows = lax.all_to_all(packed.reshape(1024, 384), PLANE, 0, 0, tiled=True)  17.6 us
    all_to_all x1, blocking collectives, on_device(): mine = lax.all_to_all(whole.reshape(896, 384), PLANE, 0, 0, tiled=True)  15.1 us
    ppermute x2, starting transfers between devices, on_device(): own = [lax.ppermute(half, AXES, first_hop()) for half in halves]  8.55 us
    ppermute x3, starting transfers between devices, on_device(): lax.ppermute(value, 'core', shift(2, 1))  6.91 us
    ppermute x4, starting transfers between devices, neighbours(): lax.ppermute(piece, 'y', shift(4, k))  6.05 us
    ppermute x3, waiting for transfers between devices, on_device(): chain = [lax.ppermute(pair, 'zh', shift(4, back)) for back in BACK]  5.76 us
    ppermute x2, waiting for transfers between devices, neighbours(): lax.ppermute(piece, 'zh', shift(4, step))  5.58 us
  transfers between devices with their start and end apart: 18, of which 8 were waited for; matrix products, arithmetic and copies ran while one was open for 1% of the time, Pallas kernels for 6%

profile of v7, /device:TPU:1, one launch (start us, length us, event | category | flops | bytes accessed | tf_op | source)
XLA Modules:
  0.0 125.9 jit_solution(5328097902884013791)
XLA Ops:
  0.6 1.1 copy-done.2
  1.8 3.3 %collective-permute-start.3 = (bf16[4,4,4,128,128]{4,3,2,1,0:T(8,128)(2,1)}, bf16[4,4,4,128,128]{4,3,2,1,0:T(8,128)(2,1)S(1)}, u32[]{:S(2)}, u32[]{:S(2)}) collective-permute-start(bf16[4,4,4,128,128]{4,3,2,1,0:T(8,128)(2,1)} %tiles), channel_id=1, source_target_pairs={{0,8},{8,0},{1,9},{9,1},{2,10},{10,2},{3,11},{11,3},{4,12},{12,4},... | collective-permute-start | bytes 6291464 | tf_op jit(solution)/shard_map/spread_tiles/ppermute | solution.py:256
  5.2 6.9 %collective-permute-start = (bf16[256,384]{1,0:T(8,128)(2,1)S(1)}, bf16[256,384]{1,0:T(8,128)(2,1)S(1)}, u32[]{:S(2)}, u32[]{:S(2)}) collective-permute-start(bf16[256,384]{1,0:T(8,128)(2,1)S(1)} %get-tuple-element.19), channel_id=1, source_target_pairs={{0,224},{1,104},{2,112},{3,216},{4,192},{5,72},{6,80},{7,248},{8,1... | collective-permute-start | bytes 589832 | tf_op jit(solution)/shard_map/spread_features/ppermute | solution.py:254
  12.1 1.6 %collective-permute-start.4 = (bf16[256,384]{1,0:T(8,128)(2,1)S(1)}, bf16[256,384]{1,0:T(8,128)(2,1)S(1)}, u32[]{:S(2)}, u32[]{:S(2)}) collective-permute-start(bf16[256,384]{1,0:T(8,128)(2,1)S(1)} %get-tuple-element.23), channel_id=1, source_target_pairs={{0,224},{1,104},{2,112},{3,216},{4,192},{5,72},{6,80},{7,248},{8,1... | collective-permute-start | bytes 589832 | tf_op jit(solution)/shard_map/spread_features/ppermute | solution.py:254
  13.7 3.6 %collective-permute-start.1 = (s32[4,4,4]{2,1,0:T(4,128)}, s32[4,4,4]{2,1,0:T(4,128)S(1)}, u32[]{:S(2)}, u32[]{:S(2)}) collective-permute-start(s32[4,4,4]{2,1,0:T(4,128)} %cols.1), channel_id=1, source_target_pairs={{0,8},{8,0},{1,9},{9,1},{2,10},{10,2},{3,11},{11,3},{4,12},{12,4},... | collective-permute-start | bytes 776 | tf_op jit(solution)/shard_map/spread_tiles/ppermute | solution.py:256
  18.7 1.6 %copy-done = bf16[4,4,4,128,128]{4,3,2,1,0:T(8,128)(2,1)S(1)} copy-done((bf16[4,4,4,128,128]{4,3,2,1,0:T(8,128)(2,1)S(1)}, bf16[4,4,4,128,128]{4,3,2,1,0:T(8,128)(2,1)}, u32[]{:S(2)}) %copy-start) | copy-done | bytes 2097176
  21.0 0.7 copy-done.5
  21.7 3.6 %spread_tiles.1.refs_0_ = bf16[2,4,512,512]{3,2,1,0:T(8,128)(2,1)S(1)} custom-call(s32[4,4,4]{2,1,0:T(4,128)S(1)} %copy-done.4, s32[4,4,4]{2,1,0:T(4,128)S(1)} %copy-done.5, s32[4,4,4]{2,1,0:T(4,128)S(1)} %collective-permute-done.1.other_cols, s32[4,4,4]{2,1,0:T(4,128)S(1)} %collective-permute-done.2.other_live, bf16[4,4,4,128,128]{4,3,2,1,0:T(8,128)(2,1)S(1)} %copy-done, ...), custom_call_target="tpu_custom_call" | custom-call | bytes 1048576 | tf_op jit(solution)/shard_map/spread_tiles/pallas_call | solution.py:257
  25.3 1.5 %collective-permute-start.5 = (bf16[256,384]{1,0:T(8,128)(2,1)S(1)}, bf16[256,384]{1,0:T(8,128)(2,1)S(1)}, u32[]{:S(2)}, u32[]{:S(2)}) collective-permute-start(bf16[256,384]{1,0:T(8,128)(2,1)S(1)} %collective-permute-done.refs_1_), channel_id=1, source_target_pairs={{0,48},{16,0},{32,16},{48,32},{1,49},{17,1},{33,17},{49,33},{2,50}... | collective-permute-start | bytes 589832 | tf_op jit(solution)/shard_map/spread_features/ppermute | solution.py:228
  26.8 1.1 collective-permute-start.6
  27.9 1.6 %collective-permute-start.7 = (bf16[256,384]{1,0:T(8,128)(2,1)S(1)}, bf16[256,384]{1,0:T(8,128)(2,1)S(1)}, u32[]{:S(2)}, u32[]{:S(2)}) collective-permute-start(bf16[256,384]{1,0:T(8,128)(2,1)S(1)} %collective-permute-done.refs_1_), channel_id=1, source_target_pairs={{0,192},{64,0},{128,64},{192,128},{1,193},{65,1},{129,65},{193,129... | collective-permute-start | bytes 589832 | tf_op jit(solution)/shard_map/spread_features/ppermute | solution.py:228
  29.4 1.0 collective-permute-start.8
  30.4 3.4 %collective-permute-start.9 = (bf16[256,384]{1,0:T(8,128)(2,1)S(1)}, bf16[256,384]{1,0:T(8,128)(2,1)S(1)}, u32[]{:S(2)}, u32[]{:S(2)}) collective-permute-start(bf16[256,384]{1,0:T(8,128)(2,1)S(1)} %collective-permute-done.4.refs_2_), channel_id=1, source_target_pairs={{0,64},{64,128},{128,192},{192,0},{1,65},{65,129},{129,193},{193,1... | collective-permute-start | bytes 589832 | tf_op jit(solution)/shard_map/spread_features/ppermute | solution.py:228
  33.8 5.6 %collective-permute-done.5.refs_2_ = bf16[256,384]{1,0:T(8,128)(2,1)S(1)} collective-permute-done((bf16[256,384]{1,0:T(8,128)(2,1)S(1)}, bf16[256,384]{1,0:T(8,128)(2,1)S(1)}, u32[]{:S(2)}, u32[]{:S(2)}) %collective-permute-start.5) | collective-permute-done | bytes 196640 | tf_op jit(solution)/shard_map/spread_features/ppermute | solution.py:228
  39.4 0.7 aggregate.5.refs_1_
  40.1 1.1 aggregate.6.refs_1_
  42.1 3.3 %collective-permute-done.10.refs_2_ = bf16[256,384]{1,0:T(8,128)(2,1)S(1)} collective-permute-done((bf16[256,384]{1,0:T(8,128)(2,1)S(1)}, bf16[256,384]{1,0:T(8,128)(2,1)S(1)}, u32[]{:S(2)}, u32[]{:S(2)}) %collective-permute-start.10) | collective-permute-done | bytes 196640 | tf_op jit(solution)/shard_map/spread_features/ppermute | solution.py:228
  45.9 23.8 %all_to_all.26.recv = bf16[16,64,384]{2,1,0:T(8,128)(2,1)S(1)} all-to-all(bf16[16,64,384]{2,1,0:T(8,128)(2,1)S(1)} %bitcast.4), channel_id=1, replica_groups=mesh['y'=4,'zh'=4,'core'=2,'x'=4,'zl'=2] {'core','x','zl'}, dimensions={0} | all-to-all | bytes 1572864 | tf_op jit(solution)/shard_map/sum_over_rep/all_to_all | solution.py:275
  69.6 1.0 layer.1
  70.7 17.6 %all_to_all.27 = bf16[16,64,384]{2,1,0:T(8,128)(2,1)S(1)} all-to-all(bf16[16,64,384]{2,1,0:T(8,128)(2,1)S(1)} %get-tuple-element.26), channel_id=1, replica_groups=mesh['y'=4,'zh'=4,'core'=2,'x'=4,'zl'=2] {'x','y'}, dimensions={0} | all-to-all | bytes 1572864 | tf_op jit(solution)/shard_map/exchange_rows/all_to_all | solution.py:284
  88.2 0.7 weight_block.2
  89.0 2.7 %collective-permute-start.11 = (bf16[56,384]{1,0:T(8,128)(2,1)S(1)}, bf16[56,384]{1,0:T(8,128)(2,1)S(1)}, u32[]{:S(2)}, u32[]{:S(2)}) collective-permute-start(bf16[56,384]{1,0:T(8,128)(2,1)S(1)} %get-tuple-element.28), channel_id=1, source_target_pairs={{0,8},{8,0},{1,9},{9,1},{2,10},{10,2},{3,11},{11,3},{4,12},{12,4},... | collective-permute-start | bytes 129032 | tf_op jit(solution)/shard_map/weight_block/ppermute | solution.py:291
  92.1 1.3 collective-permute-start.13
  93.4 1.2 collective-permute-done.12.refs_2_
  94.5 1.5 %collective-permute-done.13.refs_3_ = bf16[56,384]{1,0:T(8,128)(2,1)S(1)} collective-permute-done((bf16[56,384]{1,0:T(8,128)(2,1)S(1)}, bf16[56,384]{1,0:T(8,128)(2,1)S(1)}, u32[]{:S(2)}, u32[]{:S(2)}) %collective-permute-start.13) | collective-permute-done | bytes 43040 | tf_op jit(solution)/shard_map/weight_block/ppermute | solution.py:290
  96.1 3.0 %collective-permute-start.15 = (bf16[56,384]{1,0:T(8,128)(2,1)S(1)}, bf16[56,384]{1,0:T(8,128)(2,1)S(1)}, u32[]{:S(2)}, u32[]{:S(2)}) collective-permute-start(bf16[56,384]{1,0:T(8,128)(2,1)S(1)} %weight_block.3.refs_0_), channel_id=1, source_target_pairs={{0,16},{16,32},{32,48},{48,0},{1,17},{17,33},{33,49},{49,1},{2,18}... | collective-permute-start | bytes 129032 | tf_op jit(solution)/shard_map/sum_over_z/ppermute | solution.py:296
  99.8 3.2 %collective-permute-done.14.refs_1_ = bf16[56,384]{1,0:T(8,128)(2,1)S(1)} collective-permute-done((bf16[56,384]{1,0:T(8,128)(2,1)S(1)}, bf16[56,384]{1,0:T(8,128)(2,1)S(1)}, u32[]{:S(2)}, u32[]{:S(2)}) %collective-permute-start.14) | collective-permute-done | bytes 43040 | tf_op jit(solution)/shard_map/sum_over_z/ppermute | solution.py:296
  103.0 2.5 %collective-permute-done.16.refs_3_ = bf16[56,384]{1,0:T(8,128)(2,1)S(1)} collective-permute-done((bf16[56,384]{1,0:T(8,128)(2,1)S(1)}, bf16[56,384]{1,0:T(8,128)(2,1)S(1)}, u32[]{:S(2)}, u32[]{:S(2)}) %collective-permute-start.16) | collective-permute-done | bytes 43040 | tf_op jit(solution)/shard_map/sum_over_z/ppermute | solution.py:296
  105.6 15.1 %all_to_all.28.own = bf16[16,56,384]{2,1,0:T(8,128)(2,1)S(1)} all-to-all(bf16[16,56,384]{2,1,0:T(8,128)(2,1)S(1)} %sum_over_z.1), channel_id=1, replica_groups=mesh['y'=4,'zh'=4,'core'=2,'x'=4,'zl'=2] {'x','y'}, dimensions={0} | all-to-all | bytes 1376256 | tf_op jit(solution)/shard_map/gather_plane/all_to_all | solution.py:301
  120.7 2.1 %collective-permute-start.17 = (bf16[896,384]{1,0:T(8,128)(2,1)S(1)}, bf16[896,384]{1,0:T(8,128)(2,1)S(1)}, u32[]{:S(2)}, u32[]{:S(2)}) collective-permute-start(bf16[896,384]{1,0:T(8,128)(2,1)S(1)} %bitcast.6), channel_id=1, source_target_pairs={{0,8},{8,0},{1,9},{9,1},{2,10},{10,2},{3,11},{11,3},{4,12},{12,4},... | collective-permute-start | bytes 2064392 | tf_op jit(solution)/shard_map/gather_plane/ppermute | solution.py:302
  122.8 1.1 finish.2
  124.6 1.1 finish.3
  (34 shorter events, 5.5 us)
Async XLA Ops:
  0.6 1.1 copy-start.2
  1.8 16.8 %collective-permute-start.3 = (bf16[4,4,4,128,128]{4,3,2,1,0:T(8,128)(2,1)}, bf16[4,4,4,128,128]{4,3,2,1,0:T(8,128)(2,1)S(1)}, u32[]{:S(2)}, u32[]{:S(2)}) collective-permute-start(bf16[4,4,4,128,128]{4,3,2,1,0:T(8,128)(2,1)} %tiles), channel_id=1, source_target_pairs={{0,8},{8,0},{1,9},{9,1},{2,10},{10,2},{3,11},{11,3},{4,12},{12,4},... | collective-permute-start | bytes 6291464 | tf_op jit(solution)/shard_map/spread_tiles/ppermute | solution.py:256
  5.2 20.1 %collective-permute-start = (bf16[256,384]{1,0:T(8,128)(2,1)S(1)}, bf16[256,384]{1,0:T(8,128)(2,1)S(1)}, u32[]{:S(2)}, u32[]{:S(2)}) collective-permute-start(bf16[256,384]{1,0:T(8,128)(2,1)S(1)} %get-tuple-element.19), channel_id=1, source_target_pairs={{0,224},{1,104},{2,112},{3,216},{4,192},{5,72},{6,80},{7,248},{8,1... | collective-permute-start | bytes 589832 | tf_op jit(solution)/shard_map/spread_features/ppermute | solution.py:254
  12.1 17.4 %collective-permute-start.4 = (bf16[256,384]{1,0:T(8,128)(2,1)S(1)}, bf16[256,384]{1,0:T(8,128)(2,1)S(1)}, u32[]{:S(2)}, u32[]{:S(2)}) collective-permute-start(bf16[256,384]{1,0:T(8,128)(2,1)S(1)} %get-tuple-element.23), channel_id=1, source_target_pairs={{0,224},{1,104},{2,112},{3,216},{4,192},{5,72},{6,80},{7,248},{8,1... | collective-permute-start | bytes 589832 | tf_op jit(solution)/shard_map/spread_features/ppermute | solution.py:254
  13.7 4.6 %collective-permute-start.1 = (s32[4,4,4]{2,1,0:T(4,128)}, s32[4,4,4]{2,1,0:T(4,128)S(1)}, u32[]{:S(2)}, u32[]{:S(2)}) collective-permute-start(s32[4,4,4]{2,1,0:T(4,128)} %cols.1), channel_id=1, source_target_pairs={{0,8},{8,0},{1,9},{9,1},{2,10},{10,2},{3,11},{11,3},{4,12},{12,4},... | collective-permute-start | bytes 776 | tf_op jit(solution)/shard_map/spread_tiles/ppermute | solution.py:256
  17.3 1.4 %collective-permute-start.2 = (s32[4,4,4]{2,1,0:T(4,128)}, s32[4,4,4]{2,1,0:T(4,128)S(1)}, u32[]{:S(2)}, u32[]{:S(2)}) collective-permute-start(s32[4,4,4]{2,1,0:T(4,128)} %live.1), channel_id=1, source_target_pairs={{0,8},{8,0},{1,9},{9,1},{2,10},{10,2},{3,11},{11,3},{4,12},{12,4},... | collective-permute-start | bytes 776 | tf_op jit(solution)/shard_map/spread_tiles/ppermute | solution.py:256
  18.7 1.6 %copy-start = (bf16[4,4,4,128,128]{4,3,2,1,0:T(8,128)(2,1)S(1)}, bf16[4,4,4,128,128]{4,3,2,1,0:T(8,128)(2,1)}, u32[]{:S(2)}) copy-start(bf16[4,4,4,128,128]{4,3,2,1,0:T(8,128)(2,1)} %tiles) | copy-start | bytes 6291460
  20.3 0.7 copy-start.4
  21.0 0.7 copy-start.5
  25.3 14.1 %collective-permute-start.5 = (bf16[256,384]{1,0:T(8,128)(2,1)S(1)}, bf16[256,384]{1,0:T(8,128)(2,1)S(1)}, u32[]{:S(2)}, u32[]{:S(2)}) collective-permute-start(bf16[256,384]{1,0:T(8,128)(2,1)S(1)} %collective-permute-done.refs_1_), channel_id=1, source_target_pairs={{0,48},{16,0},{32,16},{48,32},{1,49},{17,1},{33,17},{49,33},{2,50}... | collective-permute-start | bytes 589832 | tf_op jit(solution)/shard_map/spread_features/ppermute | solution.py:228
  26.8 13.3 %collective-permute-start.6 = (bf16[256,384]{1,0:T(8,128)(2,1)S(1)}, bf16[256,384]{1,0:T(8,128)(2,1)S(1)}, u32[]{:S(2)}, u32[]{:S(2)}) collective-permute-start(bf16[256,384]{1,0:T(8,128)(2,1)S(1)} %collective-permute-done.refs_1_), channel_id=1, source_target_pairs={{0,64},{64,128},{128,192},{192,0},{1,65},{65,129},{129,193},{193,1... | collective-permute-start | bytes 589832 | tf_op jit(solution)/shard_map/spread_features/ppermute | solution.py:228
  27.9 12.3 %collective-permute-start.7 = (bf16[256,384]{1,0:T(8,128)(2,1)S(1)}, bf16[256,384]{1,0:T(8,128)(2,1)S(1)}, u32[]{:S(2)}, u32[]{:S(2)}) collective-permute-start(bf16[256,384]{1,0:T(8,128)(2,1)S(1)} %collective-permute-done.refs_1_), channel_id=1, source_target_pairs={{0,192},{64,0},{128,64},{192,128},{1,193},{65,1},{129,65},{193,129... | collective-permute-start | bytes 589832 | tf_op jit(solution)/shard_map/spread_features/ppermute | solution.py:228
  29.4 11.8 %collective-permute-start.8 = (bf16[256,384]{1,0:T(8,128)(2,1)S(1)}, bf16[256,384]{1,0:T(8,128)(2,1)S(1)}, u32[]{:S(2)}, u32[]{:S(2)}) collective-permute-start(bf16[256,384]{1,0:T(8,128)(2,1)S(1)} %collective-permute-done.4.refs_2_), channel_id=1, source_target_pairs={{0,16},{16,32},{32,48},{48,0},{1,17},{17,33},{33,49},{49,1},{2,18}... | collective-permute-start | bytes 589832 | tf_op jit(solution)/shard_map/spread_features/ppermute | solution.py:228
  30.4 11.2 %collective-permute-start.9 = (bf16[256,384]{1,0:T(8,128)(2,1)S(1)}, bf16[256,384]{1,0:T(8,128)(2,1)S(1)}, u32[]{:S(2)}, u32[]{:S(2)}) collective-permute-start(bf16[256,384]{1,0:T(8,128)(2,1)S(1)} %collective-permute-done.4.refs_2_), channel_id=1, source_target_pairs={{0,64},{64,128},{128,192},{192,0},{1,65},{65,129},{129,193},{193,1... | collective-permute-start | bytes 589832 | tf_op jit(solution)/shard_map/spread_features/ppermute | solution.py:228
  39.4 6.0 %collective-permute-start.10 = (bf16[256,384]{1,0:T(8,128)(2,1)S(1)}, bf16[256,384]{1,0:T(8,128)(2,1)S(1)}, u32[]{:S(2)}, u32[]{:S(2)}) collective-permute-start(bf16[256,384]{1,0:T(8,128)(2,1)S(1)} %collective-permute-done.4.refs_2_), channel_id=1, source_target_pairs={{0,192},{64,0},{128,64},{192,128},{1,193},{65,1},{129,65},{193,129... | collective-permute-start | bytes 589832 | tf_op jit(solution)/shard_map/spread_features/ppermute | solution.py:228
  42.1 27.5 %copy-start.3 = (bf16[64,768]{1,0:T(8,128)(2,1)S(1)}, bf16[64,768]{1,0:T(8,128)(2,1)}, u32[]{:S(2)}) copy-start(bf16[64,768]{1,0:T(8,128)(2,1)} %cot.1) | copy-start | bytes 294916
  45.9 23.8 %copy-start.1 = (bf16[768,768]{1,0:T(8,128)(2,1)S(1)}, bf16[768,768]{1,0:T(8,128)(2,1)}, u32[]{:S(2)}) copy-start(bf16[768,768]{1,0:T(8,128)(2,1)} %weight.1) | copy-start | bytes 3538948
  89.0 4.4 %collective-permute-start.11 = (bf16[56,384]{1,0:T(8,128)(2,1)S(1)}, bf16[56,384]{1,0:T(8,128)(2,1)S(1)}, u32[]{:S(2)}, u32[]{:S(2)}) collective-permute-start(bf16[56,384]{1,0:T(8,128)(2,1)S(1)} %get-tuple-element.28), channel_id=1, source_target_pairs={{0,8},{8,0},{1,9},{9,1},{2,10},{10,2},{3,11},{11,3},{4,12},{12,4},... | collective-permute-start | bytes 129032 | tf_op jit(solution)/shard_map/weight_block/ppermute | solution.py:291
  91.6 2.9 %collective-permute-start.12 = (bf16[56,384]{1,0:T(8,128)(2,1)S(1)}, bf16[56,384]{1,0:T(8,128)(2,1)S(1)}, u32[]{:S(2)}, u32[]{:S(2)}) collective-permute-start(bf16[56,384]{1,0:T(8,128)(2,1)S(1)} %get-tuple-element.27.refs_0_), channel_id=1, source_target_pairs={{0,1},{1,0},{2,3},{3,2},{4,5},{5,4},{6,7},{7,6},{8,9},{9,8},{10,11... | collective-permute-start | bytes 129032 | tf_op jit(solution)/shard_map/weight_block/ppermute | solution.py:289
  92.1 3.9 %collective-permute-start.13 = (bf16[56,384]{1,0:T(8,128)(2,1)S(1)}, bf16[56,384]{1,0:T(8,128)(2,1)S(1)}, u32[]{:S(2)}, u32[]{:S(2)}) collective-permute-start(bf16[56,384]{1,0:T(8,128)(2,1)S(1)} %get-tuple-element.28), channel_id=1, source_target_pairs={{0,9},{1,8},{8,1},{9,0},{2,11},{3,10},{10,3},{11,2},{4,13},{5,12},... | collective-permute-start | bytes 129032 | tf_op jit(solution)/shard_map/weight_block/ppermute | solution.py:290
  96.0 7.0 %collective-permute-start.14 = (bf16[56,384]{1,0:T(8,128)(2,1)S(1)}, bf16[56,384]{1,0:T(8,128)(2,1)S(1)}, u32[]{:S(2)}, u32[]{:S(2)}) collective-permute-start(bf16[56,384]{1,0:T(8,128)(2,1)S(1)} %weight_block.3.refs_0_), channel_id=1, source_target_pairs={{0,32},{16,48},{32,0},{48,16},{1,33},{17,49},{33,1},{49,17},{2,34}... | collective-permute-start | bytes 129032 | tf_op jit(solution)/shard_map/sum_over_z/ppermute | solution.py:296
  96.1 6.9 %collective-permute-start.15 = (bf16[56,384]{1,0:T(8,128)(2,1)S(1)}, bf16[56,384]{1,0:T(8,128)(2,1)S(1)}, u32[]{:S(2)}, u32[]{:S(2)}) collective-permute-start(bf16[56,384]{1,0:T(8,128)(2,1)S(1)} %weight_block.3.refs_0_), channel_id=1, source_target_pairs={{0,16},{16,32},{32,48},{48,0},{1,17},{17,33},{33,49},{49,1},{2,18}... | collective-permute-start | bytes 129032 | tf_op jit(solution)/shard_map/sum_over_z/ppermute | solution.py:296
  99.1 6.4 %collective-permute-start.16 = (bf16[56,384]{1,0:T(8,128)(2,1)S(1)}, bf16[56,384]{1,0:T(8,128)(2,1)S(1)}, u32[]{:S(2)}, u32[]{:S(2)}) collective-permute-start(bf16[56,384]{1,0:T(8,128)(2,1)S(1)} %weight_block.3.refs_0_), channel_id=1, source_target_pairs={{0,48},{16,0},{32,16},{48,32},{1,49},{17,1},{33,17},{49,33},{2,50}... | collective-permute-start | bytes 129032 | tf_op jit(solution)/shard_map/sum_over_z/ppermute | solution.py:296
  120.7 3.8 %collective-permute-start.17 = (bf16[896,384]{1,0:T(8,128)(2,1)S(1)}, bf16[896,384]{1,0:T(8,128)(2,1)S(1)}, u32[]{:S(2)}, u32[]{:S(2)}) collective-permute-start(bf16[896,384]{1,0:T(8,128)(2,1)S(1)} %bitcast.6), channel_id=1, source_target_pairs={{0,8},{8,0},{1,9},{9,1},{2,10},{10,2},{3,11},{11,3},{4,12},{12,4},... | collective-permute-start | bytes 2064392 | tf_op jit(solution)/shard_map/gather_plane/ppermute | solution.py:302

commit v8 on v7

--- a/solution.py
+++ b/solution.py
@@ -16,10 +16,10 @@
 BACK = (2, 1, 3)
 VMEM_LIMIT = 32 * 1024 * 1024
 
-TURN = (((1, 3), (3, 1), (1, 3), (3, 1)), ((2, 0), (0, 2), (2, 0), (0, 2)))
+TURN = (((1, 3), (3, 1), (1, 3), (3, 1)), ((1, 0), (3, 2), (1, 0), (3, 2)))
 OFFSET = (
-    ((2, 3, 0, 1), (2, 1, 0, 3), (2, 1, 3, 0), (1, 3, 0, 2), (1, 0, 2, 3), (0, 2, 3, 1), (0, 2, 1, 3), (3, 1, 2, 0)),
-    ((0, 2, 3, 1), (3, 1, 2, 0), (3, 2, 1, 0), (0, 3, 1, 2), (2, 0, 1, 3), (2, 3, 0, 1), (1, 0, 2, 3), (1, 0, 3, 2)),
+    ((3, 2, 0, 1), (1, 2, 3, 0), (3, 0, 1, 2), (0, 3, 1, 2), (1, 3, 2, 0), (2, 1, 0, 3), (2, 0, 3, 1), (0, 1, 2, 3)),
+    ((0, 3, 1, 2), (2, 0, 3, 1), (2, 0, 1, 3), (0, 1, 2, 3), (1, 2, 3, 0), (3, 1, 0, 2), (3, 2, 0, 1), (1, 3, 2, 0)),
 )
 
 
@@ -260,7 +260,7 @@
             [smem(), smem(), smem(), smem(), vmem(), vmem()],
             vmem(),
         )(tile_cols, tile_mask, *there[1:], tiles, there[0])
-    own[0], mix, bias = lax.optimization_barrier((own[0], mix, bias.reshape(1, 768)))
+    own[0], mix = lax.optimization_barrier((own[0], mix))
     with jax.named_scope("spread_features"):
         early = neighbours(own[0], 3)
     with jax.named_scope("spread_features"):
@@ -279,7 +279,7 @@
             (struct((64, 768), BF), struct((16, 64, 384), BF)),
             [vmem()] * 4,
             (vmem(), vmem()),
-        )(recv.reshape(16, 64, 384), weight, bias, cotangent)
+        )(recv.reshape(16, 64, 384), weight, bias.reshape(1, 768), cotangent)
     with jax.named_scope("exchange_rows"):
         rows = lax.all_to_all(packed.reshape(1024, 384), PLANE, 0, 0, tiled=True)
     with jax.named_scope("weight_block"):

time: 126 us -> 120 us (0.952)
  blocking collectives: 56.4 us -> 31.2 us
  starting transfers between devices: 34.2 us -> 49.9 us
  waiting for transfers between devices: 18 us -> 21.2 us
    all_to_all x1 -> x0, blocking collectives: 23.8 us -> none  [on_device(): lax.all_to_all(partial.reshape(1024, 384), ('core',) + REP, 0, 0, tiled=T...]
    all_to_all x0 -> x1, waiting for transfers between devices: none -> 12.2 us  [on_device(): lax.all_to_all(partial.reshape(1024, 384), ('core',) + REP, 0, 0, tiled=T...]
    all_to_all x0 -> x1, starting transfers between devices: none -> 7.55 us  [on_device(): lax.all_to_all(partial.reshape(1024, 384), ('core',) + REP, 0, 0, tiled=T...]
    ppermute x2, waiting for transfers between devices: 5.58 us -> 1.12 us  [neighbours(): lax.ppermute(piece, 'zh', shift(4, step))]
    ppermute x4, starting transfers between devices: 6.05 us -> 9.23 us  [neighbours(): lax.ppermute(piece, 'y', shift(4, k))]
    ppermute x3, starting transfers between devices: 6.91 us -> 3.84 us  [on_device(): lax.ppermute(value, 'core', shift(2, 1))]
    ppermute x2, starting transfers between devices: 8.55 us -> 11.5 us  [on_device(): own = [lax.ppermute(half, AXES, first_hop()) for half in halves]]
    ppermute x4, waiting for transfers between devices: 3.27 us -> 0.73 us  [neighbours(): lax.ppermute(piece, 'y', shift(4, k))]
  transfers between devices with their start and end apart: 18 -> 19, of which waited for: 8 -> 10; matrix products, arithmetic and copies ran while one was open for 1% -> 1% of each run, Pallas kernels for 6% -> 6%
where the time goes in v8:
time: 120 us
  starting transfers between devices  49.9 us (42%)
  blocking collectives  31.2 us (26%)
  waiting for transfers between devices  21.2 us (18%)
  Pallas kernels  11.8 us (10%)
  local copies, waits for them, and re-layouts  4.13 us (3%)
    all_to_all x1, blocking collectives, on_device(): rows = lax.all_to_all(packed.reshape(1024, 384), PLANE, 0, 0, tiled=True)  17.3 us
    all_to_all x1, blocking collectives, on_device(): mine = lax.all_to_all(whole.reshape(896, 384), PLANE, 0, 0, tiled=True)  13.9 us
    all_to_all x1, waiting for transfers between devices, on_device(): lax.all_to_all(partial.reshape(1024, 384), ('core',) + REP, 0, 0, tiled=T...  12.2 us
    ppermute x2, starting transfers between devices, on_device(): own = [lax.ppermute(half, AXES, first_hop()) for half in halves]  11.5 us
    ppermute x4, starting transfers between devices, neighbours(): lax.ppermute(piece, 'y', shift(4, k))  9.23 us
    all_to_all x1, starting transfers between devices, on_device(): lax.all_to_all(partial.reshape(1024, 384), ('core',) + REP, 0, 0, tiled=T...  7.55 us
    ppermute x3, starting transfers between devices, on_device(): chain = [lax.ppermute(pair, 'zh', shift(4, back)) for back in BACK]  5.72 us
    ppermute x2, starting transfers between devices, neighbours(): lax.ppermute(piece, 'zh', shift(4, step))  4.31 us
  transfers between devices with their start and end apart: 19, of which 10 were waited for; matrix products, arithmetic and copies ran while one was open for 1% of the time, Pallas kernels for 6%

profile of v8, /device:TPU:1, one launch (start us, length us, event | category | flops | bytes accessed | tf_op | source)
XLA Modules:
  0.0 119.8 jit_solution(9424160088190078427)
XLA Ops:
  0.6 1.1 copy-done.2
  1.8 3.3 %collective-permute-start.3 = (bf16[4,4,4,128,128]{4,3,2,1,0:T(8,128)(2,1)}, bf16[4,4,4,128,128]{4,3,2,1,0:T(8,128)(2,1)S(1)}, u32[]{:S(2)}, u32[]{:S(2)}) collective-permute-start(bf16[4,4,4,128,128]{4,3,2,1,0:T(8,128)(2,1)} %tiles), channel_id=1, source_target_pairs={{0,8},{8,0},{1,9},{9,1},{2,10},{10,2},{3,11},{11,3},{4,12},{12,4},... | collective-permute-start | bytes 6291464 | tf_op jit(solution)/shard_map/spread_tiles/ppermute | solution.py:256
  5.2 3.9 %collective-permute-start = (bf16[256,384]{1,0:T(8,128)(2,1)S(1)}, bf16[256,384]{1,0:T(8,128)(2,1)S(1)}, u32[]{:S(2)}, u32[]{:S(2)}) collective-permute-start(bf16[256,384]{1,0:T(8,128)(2,1)S(1)} %get-tuple-element.18), channel_id=1, source_target_pairs={{0,224},{1,248},{2,112},{3,72},{4,80},{5,216},{6,192},{7,104},{8,1... | collective-permute-start | bytes 589832 | tf_op jit(solution)/shard_map/spread_features/ppermute | solution.py:254
  9.0 7.7 %collective-permute-start.4 = (bf16[256,384]{1,0:T(8,128)(2,1)S(1)}, bf16[256,384]{1,0:T(8,128)(2,1)S(1)}, u32[]{:S(2)}, u32[]{:S(2)}) collective-permute-start(bf16[256,384]{1,0:T(8,128)(2,1)S(1)} %get-tuple-element.22), channel_id=1, source_target_pairs={{0,224},{1,248},{2,112},{3,72},{4,80},{5,216},{6,192},{7,104},{8,1... | collective-permute-start | bytes 589832 | tf_op jit(solution)/shard_map/spread_features/ppermute | solution.py:254
  17.2 0.9 collective-permute-done.1.other_cols
  18.2 1.6 %copy-done = bf16[4,4,4,128,128]{4,3,2,1,0:T(8,128)(2,1)S(1)} copy-done((bf16[4,4,4,128,128]{4,3,2,1,0:T(8,128)(2,1)S(1)}, bf16[4,4,4,128,128]{4,3,2,1,0:T(8,128)(2,1)}, u32[]{:S(2)}) %copy-start) | copy-done | bytes 2097176
  21.2 3.6 %spread_tiles.1.refs_0_ = bf16[2,4,512,512]{3,2,1,0:T(8,128)(2,1)S(1)} custom-call(s32[4,4,4]{2,1,0:T(4,128)S(1)} %copy-done.4, s32[4,4,4]{2,1,0:T(4,128)S(1)} %copy-done.5, s32[4,4,4]{2,1,0:T(4,128)S(1)} %collective-permute-done.1.other_cols, s32[4,4,4]{2,1,0:T(4,128)S(1)} %collective-permute-done.2.other_live, bf16[4,4,4,128,128]{4,3,2,1,0:T(8,128)(2,1)S(1)} %copy-done, ...), custom_call_target="tpu_custom_call" | custom-call | bytes 1048576 | tf_op jit(solution)/shard_map/spread_tiles/pallas_call | solution.py:257
  24.9 2.0 %collective-permute-start.5 = (bf16[256,384]{1,0:T(8,128)(2,1)S(1)}, bf16[256,384]{1,0:T(8,128)(2,1)S(1)}, u32[]{:S(2)}, u32[]{:S(2)}) collective-permute-start(bf16[256,384]{1,0:T(8,128)(2,1)S(1)} %collective-permute-done.refs_1_), channel_id=1, source_target_pairs={{0,48},{16,0},{32,16},{48,32},{1,49},{17,1},{33,17},{49,33},{2,50}... | collective-permute-start | bytes 589832 | tf_op jit(solution)/shard_map/spread_features/ppermute | solution.py:228
  26.9 3.5 %collective-permute-start.6 = (bf16[256,384]{1,0:T(8,128)(2,1)S(1)}, bf16[256,384]{1,0:T(8,128)(2,1)S(1)}, u32[]{:S(2)}, u32[]{:S(2)}) collective-permute-start(bf16[256,384]{1,0:T(8,128)(2,1)S(1)} %collective-permute-done.refs_1_), channel_id=1, source_target_pairs={{0,64},{64,128},{128,192},{192,0},{1,65},{65,129},{129,193},{193,1... | collective-permute-start | bytes 589832 | tf_op jit(solution)/shard_map/spread_features/ppermute | solution.py:228
  30.4 2.3 %collective-permute-start.8 = (bf16[256,384]{1,0:T(8,128)(2,1)S(1)}, bf16[256,384]{1,0:T(8,128)(2,1)S(1)}, u32[]{:S(2)}, u32[]{:S(2)}) collective-permute-start(bf16[256,384]{1,0:T(8,128)(2,1)S(1)} %collective-permute-done.4.refs_2_), channel_id=1, source_target_pairs={{0,16},{16,32},{32,48},{48,0},{1,17},{17,33},{33,49},{49,1},{2,18}... | collective-permute-start | bytes 589832 | tf_op jit(solution)/shard_map/spread_features/ppermute | solution.py:228
  32.7 2.3 %collective-permute-start.9 = (bf16[256,384]{1,0:T(8,128)(2,1)S(1)}, bf16[256,384]{1,0:T(8,128)(2,1)S(1)}, u32[]{:S(2)}, u32[]{:S(2)}) collective-permute-start(bf16[256,384]{1,0:T(8,128)(2,1)S(1)} %collective-permute-done.4.refs_2_), channel_id=1, source_target_pairs={{0,64},{64,128},{128,192},{192,0},{1,65},{65,129},{129,193},{193,1... | collective-permute-start | bytes 589832 | tf_op jit(solution)/shard_map/spread_features/ppermute | solution.py:228
  35.0 3.4 %collective-permute-start.10 = (bf16[256,384]{1,0:T(8,128)(2,1)S(1)}, bf16[256,384]{1,0:T(8,128)(2,1)S(1)}, u32[]{:S(2)}, u32[]{:S(2)}) collective-permute-start(bf16[256,384]{1,0:T(8,128)(2,1)S(1)} %collective-permute-done.4.refs_2_), channel_id=1, source_target_pairs={{0,192},{64,0},{128,64},{192,128},{1,193},{65,1},{129,65},{193,129... | collective-permute-start | bytes 589832 | tf_op jit(solution)/shard_map/spread_features/ppermute | solution.py:228
  39.2 1.1 aggregate.6.refs_1_
  40.2 1.1 collective-permute-done.8.refs_2_
  43.0 1.3 %aggregate.9 = bf16[2,8,64,384]{3,2,1,0:T(8,128)(2,1)} custom-call(bf16[2,4,512,512]{3,2,1,0:T(8,128)(2,1)S(1)} %spread_tiles.1.refs_0_, f32[2,512,384]{2,1,0:T(8,128)S(1)} %aggregate.8.refs_1_, bf16[256,384]{1,0:T(8,128)(2,1)S(1)} %collective-permute-done.10.refs_2_), custom_call_target="tpu_custom_call" | custom-call | flops 201326592 | bytes 1048576 | tf_op jit(solution)/shard_map/aggregate/pallas_call | solution.py:234
  44.3 7.5 %all-to-all-start = ((bf16[16,64,384]{2,1,0:T(8,128)(2,1)}), bf16[16,64,384]{2,1,0:T(8,128)(2,1)S(1)}, u32[]{:S(2)}, u32[]{:S(2)}) async-start(bf16[16,64,384]{2,1,0:T(8,128)(2,1)} %bitcast), calls=%async_computation | async-start | bytes 1572864 | tf_op jit(solution)/shard_map/sum_over_rep/all_to_all | solution.py:275
  51.9 12.2 %all-to-all-done.recv = bf16[16,64,384]{2,1,0:T(8,128)(2,1)S(1)} async-done(((bf16[16,64,384]{2,1,0:T(8,128)(2,1)}), bf16[16,64,384]{2,1,0:T(8,128)(2,1)S(1)}, u32[]{:S(2)}, u32[]{:S(2)}) %all-to-all-start) | async-done | bytes 786464 | tf_op jit(solution)/shard_map/sum_over_rep/all_to_all | solution.py:275
  64.1 1.0 layer.1
  65.1 17.3 %all_to_all.26 = bf16[16,64,384]{2,1,0:T(8,128)(2,1)S(1)} all-to-all(bf16[16,64,384]{2,1,0:T(8,128)(2,1)S(1)} %get-tuple-element.24), channel_id=1, replica_groups=mesh['y'=4,'zh'=4,'core'=2,'x'=4,'zl'=2] {'x','y'}, dimensions={0} | all-to-all | bytes 1572864 | tf_op jit(solution)/shard_map/exchange_rows/all_to_all | solution.py:284
  83.2 2.7 %collective-permute-start.11 = (bf16[56,384]{1,0:T(8,128)(2,1)S(1)}, bf16[56,384]{1,0:T(8,128)(2,1)S(1)}, u32[]{:S(2)}, u32[]{:S(2)}) collective-permute-start(bf16[56,384]{1,0:T(8,128)(2,1)S(1)} %get-tuple-element.26), channel_id=1, source_target_pairs={{0,8},{8,0},{1,9},{9,1},{2,10},{10,2},{3,11},{11,3},{4,12},{12,4},... | collective-permute-start | bytes 129032 | tf_op jit(solution)/shard_map/weight_block/ppermute | solution.py:291
  85.9 0.9 collective-permute-start.12
  86.7 0.9 collective-permute-start.13
  87.6 1.2 collective-permute-done.12.refs_2_
  88.7 1.6 %collective-permute-done.13.refs_3_ = bf16[56,384]{1,0:T(8,128)(2,1)S(1)} collective-permute-done((bf16[56,384]{1,0:T(8,128)(2,1)S(1)}, bf16[56,384]{1,0:T(8,128)(2,1)S(1)}, u32[]{:S(2)}, u32[]{:S(2)}) %collective-permute-start.13) | collective-permute-done | bytes 43040 | tf_op jit(solution)/shard_map/weight_block/ppermute | solution.py:290
  90.3 2.1 %collective-permute-start.14 = (bf16[56,384]{1,0:T(8,128)(2,1)S(1)}, bf16[56,384]{1,0:T(8,128)(2,1)S(1)}, u32[]{:S(2)}, u32[]{:S(2)}) collective-permute-start(bf16[56,384]{1,0:T(8,128)(2,1)S(1)} %weight_block.3.refs_0_), channel_id=1, source_target_pairs={{0,32},{16,48},{32,0},{48,16},{1,33},{17,49},{33,1},{49,17},{2,34}... | collective-permute-start | bytes 129032 | tf_op jit(solution)/shard_map/sum_over_z/ppermute | solution.py:296
  92.5 2.8 %collective-permute-start.15 = (bf16[56,384]{1,0:T(8,128)(2,1)S(1)}, bf16[56,384]{1,0:T(8,128)(2,1)S(1)}, u32[]{:S(2)}, u32[]{:S(2)}) collective-permute-start(bf16[56,384]{1,0:T(8,128)(2,1)S(1)} %weight_block.3.refs_0_), channel_id=1, source_target_pairs={{0,16},{16,32},{32,48},{48,0},{1,17},{17,33},{33,49},{49,1},{2,18}... | collective-permute-start | bytes 129032 | tf_op jit(solution)/shard_map/sum_over_z/ppermute | solution.py:296
  96.1 1.3 %collective-permute-done.14.refs_1_ = bf16[56,384]{1,0:T(8,128)(2,1)S(1)} collective-permute-done((bf16[56,384]{1,0:T(8,128)(2,1)S(1)}, bf16[56,384]{1,0:T(8,128)(2,1)S(1)}, u32[]{:S(2)}, u32[]{:S(2)}) %collective-permute-start.14) | collective-permute-done | bytes 43040 | tf_op jit(solution)/shard_map/sum_over_z/ppermute | solution.py:296
  97.4 1.7 %collective-permute-done.15.refs_2_ = bf16[56,384]{1,0:T(8,128)(2,1)S(1)} collective-permute-done((bf16[56,384]{1,0:T(8,128)(2,1)S(1)}, bf16[56,384]{1,0:T(8,128)(2,1)S(1)}, u32[]{:S(2)}, u32[]{:S(2)}) %collective-permute-start.15) | collective-permute-done | bytes 43040 | tf_op jit(solution)/shard_map/sum_over_z/ppermute | solution.py:296
  99.5 13.9 %all_to_all.27.own = bf16[16,56,384]{2,1,0:T(8,128)(2,1)S(1)} all-to-all(bf16[16,56,384]{2,1,0:T(8,128)(2,1)S(1)} %sum_over_z.1), channel_id=1, replica_groups=mesh['y'=4,'zh'=4,'core'=2,'x'=4,'zl'=2] {'x','y'}, dimensions={0} | all-to-all | bytes 1376256 | tf_op jit(solution)/shard_map/gather_plane/all_to_all | solution.py:301
  113.4 3.3 %collective-permute-start.17 = (bf16[896,384]{1,0:T(8,128)(2,1)S(1)}, bf16[896,384]{1,0:T(8,128)(2,1)S(1)}, u32[]{:S(2)}, u32[]{:S(2)}) collective-permute-start(bf16[896,384]{1,0:T(8,128)(2,1)S(1)} %bitcast.5), channel_id=1, source_target_pairs={{0,8},{8,0},{1,9},{9,1},{2,10},{10,2},{3,11},{11,3},{4,12},{12,4},... | collective-permute-start | bytes 2064392 | tf_op jit(solution)/shard_map/gather_plane/ppermute | solution.py:302
  116.7 1.1 finish.2
  118.5 1.1 finish.3
  (37 shorter events, 7.1 us)
Async XLA Ops:
  0.6 1.1 copy-start.2
  1.8 16.4 %collective-permute-start.3 = (bf16[4,4,4,128,128]{4,3,2,1,0:T(8,128)(2,1)}, bf16[4,4,4,128,128]{4,3,2,1,0:T(8,128)(2,1)S(1)}, u32[]{:S(2)}, u32[]{:S(2)}) collective-permute-start(bf16[4,4,4,128,128]{4,3,2,1,0:T(8,128)(2,1)} %tiles), channel_id=1, source_target_pairs={{0,8},{8,0},{1,9},{9,1},{2,10},{10,2},{3,11},{11,3},{4,12},{12,4},... | collective-permute-start | bytes 6291464 | tf_op jit(solution)/shard_map/spread_tiles/ppermute | solution.py:256
  5.2 19.7 %collective-permute-start = (bf16[256,384]{1,0:T(8,128)(2,1)S(1)}, bf16[256,384]{1,0:T(8,128)(2,1)S(1)}, u32[]{:S(2)}, u32[]{:S(2)}) collective-permute-start(bf16[256,384]{1,0:T(8,128)(2,1)S(1)} %get-tuple-element.18), channel_id=1, source_target_pairs={{0,224},{1,248},{2,112},{3,72},{4,80},{5,216},{6,192},{7,104},{8,1... | collective-permute-start | bytes 589832 | tf_op jit(solution)/shard_map/spread_features/ppermute | solution.py:254
  9.0 21.3 %collective-permute-start.4 = (bf16[256,384]{1,0:T(8,128)(2,1)S(1)}, bf16[256,384]{1,0:T(8,128)(2,1)S(1)}, u32[]{:S(2)}, u32[]{:S(2)}) collective-permute-start(bf16[256,384]{1,0:T(8,128)(2,1)S(1)} %get-tuple-element.22), channel_id=1, source_target_pairs={{0,224},{1,248},{2,112},{3,72},{4,80},{5,216},{6,192},{7,104},{8,1... | collective-permute-start | bytes 589832 | tf_op jit(solution)/shard_map/spread_features/ppermute | solution.py:254
  16.7 1.4 %collective-permute-start.1 = (s32[4,4,4]{2,1,0:T(4,128)}, s32[4,4,4]{2,1,0:T(4,128)S(1)}, u32[]{:S(2)}, u32[]{:S(2)}) collective-permute-start(s32[4,4,4]{2,1,0:T(4,128)} %cols.1), channel_id=1, source_target_pairs={{0,8},{8,0},{1,9},{9,1},{2,10},{10,2},{3,11},{11,3},{4,12},{12,4},... | collective-permute-start | bytes 776 | tf_op jit(solution)/shard_map/spread_tiles/ppermute | solution.py:256
  16.7 1.5 %collective-permute-start.2 = (s32[4,4,4]{2,1,0:T(4,128)}, s32[4,4,4]{2,1,0:T(4,128)S(1)}, u32[]{:S(2)}, u32[]{:S(2)}) collective-permute-start(s32[4,4,4]{2,1,0:T(4,128)} %live.1), channel_id=1, source_target_pairs={{0,8},{8,0},{1,9},{9,1},{2,10},{10,2},{3,11},{11,3},{4,12},{12,4},... | collective-permute-start | bytes 776 | tf_op jit(solution)/shard_map/spread_tiles/ppermute | solution.py:256
  18.2 1.6 %copy-start = (bf16[4,4,4,128,128]{4,3,2,1,0:T(8,128)(2,1)S(1)}, bf16[4,4,4,128,128]{4,3,2,1,0:T(8,128)(2,1)}, u32[]{:S(2)}) copy-start(bf16[4,4,4,128,128]{4,3,2,1,0:T(8,128)(2,1)} %tiles) | copy-start | bytes 6291460
  19.8 0.7 copy-start.4
  20.5 0.7 copy-start.5
  24.9 10.1 %collective-permute-start.5 = (bf16[256,384]{1,0:T(8,128)(2,1)S(1)}, bf16[256,384]{1,0:T(8,128)(2,1)S(1)}, u32[]{:S(2)}, u32[]{:S(2)}) collective-permute-start(bf16[256,384]{1,0:T(8,128)(2,1)S(1)} %collective-permute-done.refs_1_), channel_id=1, source_target_pairs={{0,48},{16,0},{32,16},{48,32},{1,49},{17,1},{33,17},{49,33},{2,50}... | collective-permute-start | bytes 589832 | tf_op jit(solution)/shard_map/spread_features/ppermute | solution.py:228
  26.9 12.3 %collective-permute-start.6 = (bf16[256,384]{1,0:T(8,128)(2,1)S(1)}, bf16[256,384]{1,0:T(8,128)(2,1)S(1)}, u32[]{:S(2)}, u32[]{:S(2)}) collective-permute-start(bf16[256,384]{1,0:T(8,128)(2,1)S(1)} %collective-permute-done.refs_1_), channel_id=1, source_target_pairs={{0,64},{64,128},{128,192},{192,0},{1,65},{65,129},{129,193},{193,1... | collective-permute-start | bytes 589832 | tf_op jit(solution)/shard_map/spread_features/ppermute | solution.py:228
  30.4 8.8 %collective-permute-start.7 = (bf16[256,384]{1,0:T(8,128)(2,1)S(1)}, bf16[256,384]{1,0:T(8,128)(2,1)S(1)}, u32[]{:S(2)}, u32[]{:S(2)}) collective-permute-start(bf16[256,384]{1,0:T(8,128)(2,1)S(1)} %collective-permute-done.refs_1_), channel_id=1, source_target_pairs={{0,192},{64,0},{128,64},{192,128},{1,193},{65,1},{129,65},{193,129... | collective-permute-start | bytes 589832 | tf_op jit(solution)/shard_map/spread_features/ppermute | solution.py:228
  30.4 11.0 %collective-permute-start.8 = (bf16[256,384]{1,0:T(8,128)(2,1)S(1)}, bf16[256,384]{1,0:T(8,128)(2,1)S(1)}, u32[]{:S(2)}, u32[]{:S(2)}) collective-permute-start(bf16[256,384]{1,0:T(8,128)(2,1)S(1)} %collective-permute-done.4.refs_2_), channel_id=1, source_target_pairs={{0,16},{16,32},{32,48},{48,0},{1,17},{17,33},{33,49},{49,1},{2,18}... | collective-permute-start | bytes 589832 | tf_op jit(solution)/shard_map/spread_features/ppermute | solution.py:228
  32.7 9.1 %collective-permute-start.9 = (bf16[256,384]{1,0:T(8,128)(2,1)S(1)}, bf16[256,384]{1,0:T(8,128)(2,1)S(1)}, u32[]{:S(2)}, u32[]{:S(2)}) collective-permute-start(bf16[256,384]{1,0:T(8,128)(2,1)S(1)} %collective-permute-done.4.refs_2_), channel_id=1, source_target_pairs={{0,64},{64,128},{128,192},{192,0},{1,65},{65,129},{129,193},{193,1... | collective-permute-start | bytes 589832 | tf_op jit(solution)/shard_map/spread_features/ppermute | solution.py:228
  35.0 8.0 %collective-permute-start.10 = (bf16[256,384]{1,0:T(8,128)(2,1)S(1)}, bf16[256,384]{1,0:T(8,128)(2,1)S(1)}, u32[]{:S(2)}, u32[]{:S(2)}) collective-permute-start(bf16[256,384]{1,0:T(8,128)(2,1)S(1)} %collective-permute-done.4.refs_2_), channel_id=1, source_target_pairs={{0,192},{64,0},{128,64},{192,128},{1,193},{65,1},{129,65},{193,129... | collective-permute-start | bytes 589832 | tf_op jit(solution)/shard_map/spread_features/ppermute | solution.py:228
  42.3 9.6 %copy-start.6 = (f32[768]{0:T(1024)S(1)}, f32[768]{0:T(1024)}, u32[]{:S(2)}) copy-start(f32[768]{0:T(1024)} %param.12) | copy-start | bytes 9220
  42.3 21.8 %copy-start.3 = (bf16[64,768]{1,0:T(8,128)(2,1)S(1)}, bf16[64,768]{1,0:T(8,128)(2,1)}, u32[]{:S(2)}) copy-start(bf16[64,768]{1,0:T(8,128)(2,1)} %cot.1) | copy-start | bytes 294916
  44.3 19.7 %copy-start.1 = (bf16[768,768]{1,0:T(8,128)(2,1)S(1)}, bf16[768,768]{1,0:T(8,128)(2,1)}, u32[]{:S(2)}) copy-start(bf16[768,768]{1,0:T(8,128)(2,1)} %weight.1) | copy-start | bytes 3538948
  44.3 19.7 %all-to-all-start = ((bf16[16,64,384]{2,1,0:T(8,128)(2,1)}), bf16[16,64,384]{2,1,0:T(8,128)(2,1)S(1)}, u32[]{:S(2)}, u32[]{:S(2)}) async-start(bf16[16,64,384]{2,1,0:T(8,128)(2,1)} %bitcast), calls=%async_computation | async-start | bytes 1572864 | tf_op jit(solution)/shard_map/sum_over_rep/all_to_all | solution.py:275
  83.2 4.4 %collective-permute-start.11 = (bf16[56,384]{1,0:T(8,128)(2,1)S(1)}, bf16[56,384]{1,0:T(8,128)(2,1)S(1)}, u32[]{:S(2)}, u32[]{:S(2)}) collective-permute-start(bf16[56,384]{1,0:T(8,128)(2,1)S(1)} %get-tuple-element.26), channel_id=1, source_target_pairs={{0,8},{8,0},{1,9},{9,1},{2,10},{10,2},{3,11},{11,3},{4,12},{12,4},... | collective-permute-start | bytes 129032 | tf_op jit(solution)/shard_map/weight_block/ppermute | solution.py:291
  85.9 2.9 %collective-permute-start.12 = (bf16[56,384]{1,0:T(8,128)(2,1)S(1)}, bf16[56,384]{1,0:T(8,128)(2,1)S(1)}, u32[]{:S(2)}, u32[]{:S(2)}) collective-permute-start(bf16[56,384]{1,0:T(8,128)(2,1)S(1)} %get-tuple-element.25.refs_0_), channel_id=1, source_target_pairs={{0,1},{1,0},{2,3},{3,2},{4,5},{5,4},{6,7},{7,6},{8,9},{9,8},{10,11... | collective-permute-start | bytes 129032 | tf_op jit(solution)/shard_map/weight_block/ppermute | solution.py:289
  86.7 3.6 %collective-permute-start.13 = (bf16[56,384]{1,0:T(8,128)(2,1)S(1)}, bf16[56,384]{1,0:T(8,128)(2,1)S(1)}, u32[]{:S(2)}, u32[]{:S(2)}) collective-permute-start(bf16[56,384]{1,0:T(8,128)(2,1)S(1)} %get-tuple-element.26), channel_id=1, source_target_pairs={{0,9},{1,8},{8,1},{9,0},{2,11},{3,10},{10,3},{11,2},{4,13},{5,12},... | collective-permute-start | bytes 129032 | tf_op jit(solution)/shard_map/weight_block/ppermute | solution.py:290
  90.3 7.0 %collective-permute-start.14 = (bf16[56,384]{1,0:T(8,128)(2,1)S(1)}, bf16[56,384]{1,0:T(8,128)(2,1)S(1)}, u32[]{:S(2)}, u32[]{:S(2)}) collective-permute-start(bf16[56,384]{1,0:T(8,128)(2,1)S(1)} %weight_block.3.refs_0_), channel_id=1, source_target_pairs={{0,32},{16,48},{32,0},{48,16},{1,33},{17,49},{33,1},{49,17},{2,34}... | collective-permute-start | bytes 129032 | tf_op jit(solution)/shard_map/sum_over_z/ppermute | solution.py:296
  92.5 6.6 %collective-permute-start.15 = (bf16[56,384]{1,0:T(8,128)(2,1)S(1)}, bf16[56,384]{1,0:T(8,128)(2,1)S(1)}, u32[]{:S(2)}, u32[]{:S(2)}) collective-permute-start(bf16[56,384]{1,0:T(8,128)(2,1)S(1)} %weight_block.3.refs_0_), channel_id=1, source_target_pairs={{0,16},{16,32},{32,48},{48,0},{1,17},{17,33},{33,49},{49,1},{2,18}... | collective-permute-start | bytes 129032 | tf_op jit(solution)/shard_map/sum_over_z/ppermute | solution.py:296
  95.3 4.2 %collective-permute-start.16 = (bf16[56,384]{1,0:T(8,128)(2,1)S(1)}, bf16[56,384]{1,0:T(8,128)(2,1)S(1)}, u32[]{:S(2)}, u32[]{:S(2)}) collective-permute-start(bf16[56,384]{1,0:T(8,128)(2,1)S(1)} %weight_block.3.refs_0_), channel_id=1, source_target_pairs={{0,48},{16,0},{32,16},{48,32},{1,49},{17,1},{33,17},{49,33},{2,50}... | collective-permute-start | bytes 129032 | tf_op jit(solution)/shard_map/sum_over_z/ppermute | solution.py:296
  113.4 5.1 %collective-permute-start.17 = (bf16[896,384]{1,0:T(8,128)(2,1)S(1)}, bf16[896,384]{1,0:T(8,128)(2,1)S(1)}, u32[]{:S(2)}, u32[]{:S(2)}) collective-permute-start(bf16[896,384]{1,0:T(8,128)(2,1)S(1)} %bitcast.5), channel_id=1, source_target_pairs={{0,8},{8,0},{1,9},{9,1},{2,10},{10,2},{3,11},{11,3},{4,12},{12,4},... | collective-permute-start | bytes 2064392 | tf_op jit(solution)/shard_map/gather_plane/ppermute | solution.py:302

commit v9 on v8

--- a/solution.py
+++ b/solution.py
@@ -16,10 +16,10 @@
 BACK = (2, 1, 3)
 VMEM_LIMIT = 32 * 1024 * 1024
 
-TURN = (((1, 3), (3, 1), (1, 3), (3, 1)), ((1, 0), (3, 2), (1, 0), (3, 2)))
+TURN = (((1, 0), (3, 2), (1, 0), (3, 2)), ((2, 0), (0, 2), (2, 0), (0, 2)))
 OFFSET = (
-    ((3, 2, 0, 1), (1, 2, 3, 0), (3, 0, 1, 2), (0, 3, 1, 2), (1, 3, 2, 0), (2, 1, 0, 3), (2, 0, 3, 1), (0, 1, 2, 3)),
-    ((0, 3, 1, 2), (2, 0, 3, 1), (2, 0, 1, 3), (0, 1, 2, 3), (1, 2, 3, 0), (3, 1, 0, 2), (3, 2, 0, 1), (1, 3, 2, 0)),
+    ((3, 2, 0, 1), (2, 0, 1, 3), (0, 2, 3, 1), (1, 3, 2, 0), (2, 0, 1, 3), (0, 1, 3, 2), (1, 3, 0, 2), (3, 1, 2, 0)),
+    ((3, 2, 0, 1), (2, 1, 3, 0), (1, 2, 0, 3), (3, 0, 2, 1), (1, 0, 2, 3), (3, 1, 0, 2), (1, 3, 2, 0), (0, 3, 1, 2)),
 )
 
 

time: 120 us -> 120 us (level)
  starting transfers between devices: 49.9 us -> 44.6 us
  waiting for transfers between devices: 21.2 us -> 25.1 us
    ppermute x4, starting transfers between devices: 9.23 us -> 3.35 us  [neighbours(): lax.ppermute(piece, 'y', shift(4, k))]
    ppermute x2, waiting for transfers between devices: 1.12 us -> 5.19 us  [neighbours(): lax.ppermute(piece, 'zh', shift(4, step))]
    ppermute x3, starting transfers between devices: 3.84 us -> 7.45 us  [on_device(): lax.ppermute(value, 'core', shift(2, 1))]
    ppermute x2, starting transfers between devices: 11.5 us -> 8.01 us  [on_device(): own = [lax.ppermute(half, AXES, first_hop()) for half in halves]]
    all_to_all x1, starting transfers between devices: 7.55 us -> 4.64 us  [on_device(): lax.all_to_all(partial.reshape(1024, 384), ('core',) + REP, 0, 0, tiled=T...]
    ppermute x2, starting transfers between devices: 4.31 us -> 7.04 us  [neighbours(): lax.ppermute(piece, 'zh', shift(4, step))]
    ppermute x3, waiting for transfers between devices: 3.39 us -> 2.16 us  [on_device(): chain = [lax.ppermute(pair, 'zh', shift(4, back)) for back in BACK]]
  transfers between devices with their start and end apart: 19 -> 19, of which waited for: 10 -> 11; matrix products, arithmetic and copies ran while one was open for 1% -> 1% of each run, Pallas kernels for 6% -> 6%
where the time goes in v9:
time: 120 us; the launch traced here: 119 us
  starting transfers between devices  44.6 us (37%)
  blocking collectives  32 us (27%)
  waiting for transfers between devices  25.1 us (21%)
  Pallas kernels  11.8 us (10%)
  local copies, waits for them, and re-layouts  4.13 us (3%)
    all_to_all x1, blocking collectives, on_device(): rows = lax.all_to_all(packed.reshape(1024, 384), PLANE, 0, 0, tiled=True)  18.1 us
    all_to_all x1, blocking collectives, on_device(): mine = lax.all_to_all(whole.reshape(896, 384), PLANE, 0, 0, tiled=True)  13.9 us
    all_to_all x1, waiting for transfers between devices, on_device(): lax.all_to_all(partial.reshape(1024, 384), ('core',) + REP, 0, 0, tiled=T...  12.2 us
    ppermute x2, starting transfers between devices, on_device(): own = [lax.ppermute(half, AXES, first_hop()) for half in halves]  8.01 us
    ppermute x3, starting transfers between devices, on_device(): lax.ppermute(value, 'core', shift(2, 1))  7.45 us
    ppermute x2, starting transfers between devices, neighbours(): lax.ppermute(piece, 'zh', shift(4, step))  7.04 us
    ppermute x3, starting transfers between devices, on_device(): chain = [lax.ppermute(pair, 'zh', shift(4, back)) for back in BACK]  6.35 us
    ppermute x2, waiting for transfers between devices, neighbours(): lax.ppermute(piece, 'zh', shift(4, step))  5.19 us
  transfers between devices with their start and end apart: 19, of which 11 were waited for; matrix products, arithmetic and copies ran while one was open for 1% of the time, Pallas kernels for 6%

profile of v9, /device:TPU:1, one launch (start us, length us, event | category | flops | bytes accessed | tf_op | source)
XLA Modules:
  0.0 119.2 jit_solution(5210512011344297272)
XLA Ops:
  0.6 1.1 copy-done.2
  1.8 3.3 %collective-permute-start.3 = (bf16[4,4,4,128,128]{4,3,2,1,0:T(8,128)(2,1)}, bf16[4,4,4,128,128]{4,3,2,1,0:T(8,128)(2,1)S(1)}, u32[]{:S(2)}, u32[]{:S(2)}) collective-permute-start(bf16[4,4,4,128,128]{4,3,2,1,0:T(8,128)(2,1)} %tiles), channel_id=1, source_target_pairs={{0,8},{8,0},{1,9},{9,1},{2,10},{10,2},{3,11},{11,3},{4,12},{12,4},... | collective-permute-start | bytes 6291464 | tf_op jit(solution)/shard_map/spread_tiles/ppermute | solution.py:256
  5.3 7.9 %collective-permute-start.4 = (bf16[256,384]{1,0:T(8,128)(2,1)S(1)}, bf16[256,384]{1,0:T(8,128)(2,1)S(1)}, u32[]{:S(2)}, u32[]{:S(2)}) collective-permute-start(bf16[256,384]{1,0:T(8,128)(2,1)S(1)} %get-tuple-element.22), channel_id=1, source_target_pairs={{0,224},{1,152},{2,112},{3,40},{4,80},{5,8},{6,192},{7,184},{8,0},... | collective-permute-start | bytes 589832 | tf_op jit(solution)/shard_map/spread_features/ppermute | solution.py:254
  13.2 4.1 %collective-permute-start.1 = (s32[4,4,4]{2,1,0:T(4,128)}, s32[4,4,4]{2,1,0:T(4,128)S(1)}, u32[]{:S(2)}, u32[]{:S(2)}) collective-permute-start(s32[4,4,4]{2,1,0:T(4,128)} %cols.1), channel_id=1, source_target_pairs={{0,8},{8,0},{1,9},{9,1},{2,10},{10,2},{3,11},{11,3},{4,12},{12,4},... | collective-permute-start | bytes 776 | tf_op jit(solution)/shard_map/spread_tiles/ppermute | solution.py:256
  17.3 1.0 collective-permute-done.1.other_cols
  18.7 1.6 %copy-done = bf16[4,4,4,128,128]{4,3,2,1,0:T(8,128)(2,1)S(1)} copy-done((bf16[4,4,4,128,128]{4,3,2,1,0:T(8,128)(2,1)S(1)}, bf16[4,4,4,128,128]{4,3,2,1,0:T(8,128)(2,1)}, u32[]{:S(2)}) %copy-start) | copy-done | bytes 2097176
  21.7 3.6 %spread_tiles.1.refs_0_ = bf16[2,4,512,512]{3,2,1,0:T(8,128)(2,1)S(1)} custom-call(s32[4,4,4]{2,1,0:T(4,128)S(1)} %copy-done.4, s32[4,4,4]{2,1,0:T(4,128)S(1)} %copy-done.5, s32[4,4,4]{2,1,0:T(4,128)S(1)} %collective-permute-done.1.other_cols, s32[4,4,4]{2,1,0:T(4,128)S(1)} %collective-permute-done.2.other_live, bf16[4,4,4,128,128]{4,3,2,1,0:T(8,128)(2,1)S(1)} %copy-done, ...), custom_call_target="tpu_custom_call" | custom-call | bytes 1048576 | tf_op jit(solution)/shard_map/spread_tiles/pallas_call | solution.py:257
  25.3 7.0 %collective-permute-start.5 = (bf16[256,384]{1,0:T(8,128)(2,1)S(1)}, bf16[256,384]{1,0:T(8,128)(2,1)S(1)}, u32[]{:S(2)}, u32[]{:S(2)}) collective-permute-start(bf16[256,384]{1,0:T(8,128)(2,1)S(1)} %collective-permute-done.refs_1_), channel_id=1, source_target_pairs={{0,48},{16,0},{32,16},{48,32},{1,49},{17,1},{33,17},{49,33},{2,50}... | collective-permute-start | bytes 589832 | tf_op jit(solution)/shard_map/spread_features/ppermute | solution.py:228
  32.3 2.7 %collective-permute-start.7 = (bf16[256,384]{1,0:T(8,128)(2,1)S(1)}, bf16[256,384]{1,0:T(8,128)(2,1)S(1)}, u32[]{:S(2)}, u32[]{:S(2)}) collective-permute-start(bf16[256,384]{1,0:T(8,128)(2,1)S(1)} %collective-permute-done.refs_1_), channel_id=1, source_target_pairs={{0,192},{64,0},{128,64},{192,128},{1,193},{65,1},{129,65},{193,129... | collective-permute-start | bytes 589832 | tf_op jit(solution)/shard_map/spread_features/ppermute | solution.py:228
  35.0 2.0 %collective-permute-done.5.refs_2_ = bf16[256,384]{1,0:T(8,128)(2,1)S(1)} collective-permute-done((bf16[256,384]{1,0:T(8,128)(2,1)S(1)}, bf16[256,384]{1,0:T(8,128)(2,1)S(1)}, u32[]{:S(2)}, u32[]{:S(2)}) %collective-permute-start.5) | collective-permute-done | bytes 196640 | tf_op jit(solution)/shard_map/spread_features/ppermute | solution.py:228
  38.4 1.4 %collective-permute-done.6.refs_3_ = bf16[256,384]{1,0:T(8,128)(2,1)S(1)} collective-permute-done((bf16[256,384]{1,0:T(8,128)(2,1)S(1)}, bf16[256,384]{1,0:T(8,128)(2,1)S(1)}, u32[]{:S(2)}, u32[]{:S(2)}) %collective-permute-start.6) | collective-permute-done | bytes 196640 | tf_op jit(solution)/shard_map/spread_features/ppermute | solution.py:228
  39.9 1.1 aggregate.6.refs_1_
  40.9 3.2 %collective-permute-done.8.refs_2_ = bf16[256,384]{1,0:T(8,128)(2,1)S(1)} collective-permute-done((bf16[256,384]{1,0:T(8,128)(2,1)S(1)}, bf16[256,384]{1,0:T(8,128)(2,1)S(1)}, u32[]{:S(2)}, u32[]{:S(2)}) %collective-permute-start.8) | collective-permute-done | bytes 196640 | tf_op jit(solution)/shard_map/spread_features/ppermute | solution.py:228
  45.1 1.3 %aggregate.9 = bf16[2,8,64,384]{3,2,1,0:T(8,128)(2,1)} custom-call(bf16[2,4,512,512]{3,2,1,0:T(8,128)(2,1)S(1)} %spread_tiles.1.refs_0_, f32[2,512,384]{2,1,0:T(8,128)S(1)} %aggregate.8.refs_1_, bf16[256,384]{1,0:T(8,128)(2,1)S(1)} %collective-permute-done.10.refs_2_), custom_call_target="tpu_custom_call" | custom-call | flops 201326592 | bytes 1048576 | tf_op jit(solution)/shard_map/aggregate/pallas_call | solution.py:234
  46.4 4.6 %all-to-all-start = ((bf16[16,64,384]{2,1,0:T(8,128)(2,1)}), bf16[16,64,384]{2,1,0:T(8,128)(2,1)S(1)}, u32[]{:S(2)}, u32[]{:S(2)}) async-start(bf16[16,64,384]{2,1,0:T(8,128)(2,1)} %bitcast), calls=%async_computation | async-start | bytes 1572864 | tf_op jit(solution)/shard_map/sum_over_rep/all_to_all | solution.py:275
  51.1 12.2 %all-to-all-done.recv = bf16[16,64,384]{2,1,0:T(8,128)(2,1)S(1)} async-done(((bf16[16,64,384]{2,1,0:T(8,128)(2,1)}), bf16[16,64,384]{2,1,0:T(8,128)(2,1)S(1)}, u32[]{:S(2)}, u32[]{:S(2)}) %all-to-all-start) | async-done | bytes 786464 | tf_op jit(solution)/shard_map/sum_over_rep/all_to_all | solution.py:275
  63.2 1.0 layer.1
  64.3 18.1 %all_to_all.26 = bf16[16,64,384]{2,1,0:T(8,128)(2,1)S(1)} all-to-all(bf16[16,64,384]{2,1,0:T(8,128)(2,1)S(1)} %get-tuple-element.24), channel_id=1, replica_groups=mesh['y'=4,'zh'=4,'core'=2,'x'=4,'zl'=2] {'x','y'}, dimensions={0} | all-to-all | bytes 1572864 | tf_op jit(solution)/shard_map/exchange_rows/all_to_all | solution.py:284
  82.4 0.7 weight_block.2
  83.1 2.7 %collective-permute-start.11 = (bf16[56,384]{1,0:T(8,128)(2,1)S(1)}, bf16[56,384]{1,0:T(8,128)(2,1)S(1)}, u32[]{:S(2)}, u32[]{:S(2)}) collective-permute-start(bf16[56,384]{1,0:T(8,128)(2,1)S(1)} %get-tuple-element.26), channel_id=1, source_target_pairs={{0,8},{8,0},{1,9},{9,1},{2,10},{10,2},{3,11},{11,3},{4,12},{12,4},... | collective-permute-start | bytes 129032 | tf_op jit(solution)/shard_map/weight_block/ppermute | solution.py:291
  85.8 0.9 collective-permute-start.12
  86.7 0.9 collective-permute-start.13
  87.6 1.2 collective-permute-done.12.refs_2_
  88.7 1.6 %collective-permute-done.13.refs_3_ = bf16[56,384]{1,0:T(8,128)(2,1)S(1)} collective-permute-done((bf16[56,384]{1,0:T(8,128)(2,1)S(1)}, bf16[56,384]{1,0:T(8,128)(2,1)S(1)}, u32[]{:S(2)}, u32[]{:S(2)}) %collective-permute-start.13) | collective-permute-done | bytes 43040 | tf_op jit(solution)/shard_map/weight_block/ppermute | solution.py:290
  90.3 2.8 %collective-permute-start.14 = (bf16[56,384]{1,0:T(8,128)(2,1)S(1)}, bf16[56,384]{1,0:T(8,128)(2,1)S(1)}, u32[]{:S(2)}, u32[]{:S(2)}) collective-permute-start(bf16[56,384]{1,0:T(8,128)(2,1)S(1)} %weight_block.3.refs_0_), channel_id=1, source_target_pairs={{0,32},{16,48},{32,0},{48,16},{1,33},{17,49},{33,1},{49,17},{2,34}... | collective-permute-start | bytes 129032 | tf_op jit(solution)/shard_map/sum_over_z/ppermute | solution.py:296
  93.1 0.7 collective-permute-start.15
  93.8 2.9 %collective-permute-start.16 = (bf16[56,384]{1,0:T(8,128)(2,1)S(1)}, bf16[56,384]{1,0:T(8,128)(2,1)S(1)}, u32[]{:S(2)}, u32[]{:S(2)}) collective-permute-start(bf16[56,384]{1,0:T(8,128)(2,1)S(1)} %weight_block.3.refs_0_), channel_id=1, source_target_pairs={{0,48},{16,0},{32,16},{48,32},{1,49},{17,1},{33,17},{49,33},{2,50}... | collective-permute-start | bytes 129032 | tf_op jit(solution)/shard_map/sum_over_z/ppermute | solution.py:296
  97.3 1.4 %collective-permute-done.15.refs_2_ = bf16[56,384]{1,0:T(8,128)(2,1)S(1)} collective-permute-done((bf16[56,384]{1,0:T(8,128)(2,1)S(1)}, bf16[56,384]{1,0:T(8,128)(2,1)S(1)}, u32[]{:S(2)}, u32[]{:S(2)}) %collective-permute-start.15) | collective-permute-done | bytes 43040 | tf_op jit(solution)/shard_map/sum_over_z/ppermute | solution.py:296
  98.9 13.9 %all_to_all.27.own = bf16[16,56,384]{2,1,0:T(8,128)(2,1)S(1)} all-to-all(bf16[16,56,384]{2,1,0:T(8,128)(2,1)S(1)} %sum_over_z.1), channel_id=1, replica_groups=mesh['y'=4,'zh'=4,'core'=2,'x'=4,'zl'=2] {'x','y'}, dimensions={0} | all-to-all | bytes 1376256 | tf_op jit(solution)/shard_map/gather_plane/all_to_all | solution.py:301
  112.8 3.3 %collective-permute-start.17 = (bf16[896,384]{1,0:T(8,128)(2,1)S(1)}, bf16[896,384]{1,0:T(8,128)(2,1)S(1)}, u32[]{:S(2)}, u32[]{:S(2)}) collective-permute-start(bf16[896,384]{1,0:T(8,128)(2,1)S(1)} %bitcast.5), channel_id=1, source_target_pairs={{0,8},{8,0},{1,9},{9,1},{2,10},{10,2},{3,11},{11,3},{4,12},{12,4},... | collective-permute-start | bytes 2064392 | tf_op jit(solution)/shard_map/gather_plane/ppermute | solution.py:302
  116.1 1.1 finish.2
  117.9 1.1 finish.3
  (37 shorter events, 5.7 us)
Async XLA Ops:
  0.6 1.1 copy-start.2
  1.8 16.8 %collective-permute-start.3 = (bf16[4,4,4,128,128]{4,3,2,1,0:T(8,128)(2,1)}, bf16[4,4,4,128,128]{4,3,2,1,0:T(8,128)(2,1)S(1)}, u32[]{:S(2)}, u32[]{:S(2)}) collective-permute-start(bf16[4,4,4,128,128]{4,3,2,1,0:T(8,128)(2,1)} %tiles), channel_id=1, source_target_pairs={{0,8},{8,0},{1,9},{9,1},{2,10},{10,2},{3,11},{11,3},{4,12},{12,4},... | collective-permute-start | bytes 6291464 | tf_op jit(solution)/shard_map/spread_tiles/ppermute | solution.py:256
  5.2 20.1 %collective-permute-start = (bf16[256,384]{1,0:T(8,128)(2,1)S(1)}, bf16[256,384]{1,0:T(8,128)(2,1)S(1)}, u32[]{:S(2)}, u32[]{:S(2)}) collective-permute-start(bf16[256,384]{1,0:T(8,128)(2,1)S(1)} %get-tuple-element.18), channel_id=1, source_target_pairs={{0,224},{1,152},{2,112},{3,40},{4,80},{5,8},{6,192},{7,184},{8,0},... | collective-permute-start | bytes 589832 | tf_op jit(solution)/shard_map/spread_features/ppermute | solution.py:254
  5.3 29.8 %collective-permute-start.4 = (bf16[256,384]{1,0:T(8,128)(2,1)S(1)}, bf16[256,384]{1,0:T(8,128)(2,1)S(1)}, u32[]{:S(2)}, u32[]{:S(2)}) collective-permute-start(bf16[256,384]{1,0:T(8,128)(2,1)S(1)} %get-tuple-element.22), channel_id=1, source_target_pairs={{0,224},{1,152},{2,112},{3,40},{4,80},{5,8},{6,192},{7,184},{8,0},... | collective-permute-start | bytes 589832 | tf_op jit(solution)/shard_map/spread_features/ppermute | solution.py:254
  13.2 5.2 %collective-permute-start.1 = (s32[4,4,4]{2,1,0:T(4,128)}, s32[4,4,4]{2,1,0:T(4,128)S(1)}, u32[]{:S(2)}, u32[]{:S(2)}) collective-permute-start(s32[4,4,4]{2,1,0:T(4,128)} %cols.1), channel_id=1, source_target_pairs={{0,8},{8,0},{1,9},{9,1},{2,10},{10,2},{3,11},{11,3},{4,12},{12,4},... | collective-permute-start | bytes 776 | tf_op jit(solution)/shard_map/spread_tiles/ppermute | solution.py:256
  17.3 1.4 %collective-permute-start.2 = (s32[4,4,4]{2,1,0:T(4,128)}, s32[4,4,4]{2,1,0:T(4,128)S(1)}, u32[]{:S(2)}, u32[]{:S(2)}) collective-permute-start(s32[4,4,4]{2,1,0:T(4,128)} %live.1), channel_id=1, source_target_pairs={{0,8},{8,0},{1,9},{9,1},{2,10},{10,2},{3,11},{11,3},{4,12},{12,4},... | collective-permute-start | bytes 776 | tf_op jit(solution)/shard_map/spread_tiles/ppermute | solution.py:256
  18.7 1.6 %copy-start = (bf16[4,4,4,128,128]{4,3,2,1,0:T(8,128)(2,1)S(1)}, bf16[4,4,4,128,128]{4,3,2,1,0:T(8,128)(2,1)}, u32[]{:S(2)}) copy-start(bf16[4,4,4,128,128]{4,3,2,1,0:T(8,128)(2,1)} %tiles) | copy-start | bytes 6291460
  20.3 0.7 copy-start.4
  21.0 0.7 copy-start.5
  25.3 11.7 %collective-permute-start.5 = (bf16[256,384]{1,0:T(8,128)(2,1)S(1)}, bf16[256,384]{1,0:T(8,128)(2,1)S(1)}, u32[]{:S(2)}, u32[]{:S(2)}) collective-permute-start(bf16[256,384]{1,0:T(8,128)(2,1)S(1)} %collective-permute-done.refs_1_), channel_id=1, source_target_pairs={{0,48},{16,0},{32,16},{48,32},{1,49},{17,1},{33,17},{49,33},{2,50}... | collective-permute-start | bytes 589832 | tf_op jit(solution)/shard_map/spread_features/ppermute | solution.py:228
  32.3 7.5 %collective-permute-start.6 = (bf16[256,384]{1,0:T(8,128)(2,1)S(1)}, bf16[256,384]{1,0:T(8,128)(2,1)S(1)}, u32[]{:S(2)}, u32[]{:S(2)}) collective-permute-start(bf16[256,384]{1,0:T(8,128)(2,1)S(1)} %collective-permute-done.refs_1_), channel_id=1, source_target_pairs={{0,64},{64,128},{128,192},{192,0},{1,65},{65,129},{129,193},{193,1... | collective-permute-start | bytes 589832 | tf_op jit(solution)/shard_map/spread_features/ppermute | solution.py:228
  32.3 7.5 %collective-permute-start.7 = (bf16[256,384]{1,0:T(8,128)(2,1)S(1)}, bf16[256,384]{1,0:T(8,128)(2,1)S(1)}, u32[]{:S(2)}, u32[]{:S(2)}) collective-permute-start(bf16[256,384]{1,0:T(8,128)(2,1)S(1)} %collective-permute-done.refs_1_), channel_id=1, source_target_pairs={{0,192},{64,0},{128,64},{192,128},{1,193},{65,1},{129,65},{193,129... | collective-permute-start | bytes 589832 | tf_op jit(solution)/shard_map/spread_features/ppermute | solution.py:228
  35.0 9.1 %collective-permute-start.8 = (bf16[256,384]{1,0:T(8,128)(2,1)S(1)}, bf16[256,384]{1,0:T(8,128)(2,1)S(1)}, u32[]{:S(2)}, u32[]{:S(2)}) collective-permute-start(bf16[256,384]{1,0:T(8,128)(2,1)S(1)} %collective-permute-done.4.refs_2_), channel_id=1, source_target_pairs={{0,16},{16,32},{32,48},{48,0},{1,17},{17,33},{33,49},{49,1},{2,18}... | collective-permute-start | bytes 589832 | tf_op jit(solution)/shard_map/spread_features/ppermute | solution.py:228
  35.0 9.5 %collective-permute-start.9 = (bf16[256,384]{1,0:T(8,128)(2,1)S(1)}, bf16[256,384]{1,0:T(8,128)(2,1)S(1)}, u32[]{:S(2)}, u32[]{:S(2)}) collective-permute-start(bf16[256,384]{1,0:T(8,128)(2,1)S(1)} %collective-permute-done.4.refs_2_), channel_id=1, source_target_pairs={{0,64},{64,128},{128,192},{192,0},{1,65},{65,129},{129,193},{193,1... | collective-permute-start | bytes 589832 | tf_op jit(solution)/shard_map/spread_features/ppermute | solution.py:228
  37.0 8.0 %collective-permute-start.10 = (bf16[256,384]{1,0:T(8,128)(2,1)S(1)}, bf16[256,384]{1,0:T(8,128)(2,1)S(1)}, u32[]{:S(2)}, u32[]{:S(2)}) collective-permute-start(bf16[256,384]{1,0:T(8,128)(2,1)S(1)} %collective-permute-done.4.refs_2_), channel_id=1, source_target_pairs={{0,192},{64,0},{128,64},{192,128},{1,193},{65,1},{129,65},{193,129... | collective-permute-start | bytes 589832 | tf_op jit(solution)/shard_map/spread_features/ppermute | solution.py:228
  45.0 6.0 %copy-start.6 = (f32[768]{0:T(1024)S(1)}, f32[768]{0:T(1024)}, u32[]{:S(2)}) copy-start(f32[768]{0:T(1024)} %param.12) | copy-start | bytes 9220
  45.0 18.2 %copy-start.3 = (bf16[64,768]{1,0:T(8,128)(2,1)S(1)}, bf16[64,768]{1,0:T(8,128)(2,1)}, u32[]{:S(2)}) copy-start(bf16[64,768]{1,0:T(8,128)(2,1)} %cot.1) | copy-start | bytes 294916
  46.4 16.8 %copy-start.1 = (bf16[768,768]{1,0:T(8,128)(2,1)S(1)}, bf16[768,768]{1,0:T(8,128)(2,1)}, u32[]{:S(2)}) copy-start(bf16[768,768]{1,0:T(8,128)(2,1)} %weight.1) | copy-start | bytes 3538948
  46.4 16.8 %all-to-all-start = ((bf16[16,64,384]{2,1,0:T(8,128)(2,1)}), bf16[16,64,384]{2,1,0:T(8,128)(2,1)S(1)}, u32[]{:S(2)}, u32[]{:S(2)}) async-start(bf16[16,64,384]{2,1,0:T(8,128)(2,1)} %bitcast), calls=%async_computation | async-start | bytes 1572864 | tf_op jit(solution)/shard_map/sum_over_rep/all_to_all | solution.py:275
  83.1 4.4 %collective-permute-start.11 = (bf16[56,384]{1,0:T(8,128)(2,1)S(1)}, bf16[56,384]{1,0:T(8,128)(2,1)S(1)}, u32[]{:S(2)}, u32[]{:S(2)}) collective-permute-start(bf16[56,384]{1,0:T(8,128)(2,1)S(1)} %get-tuple-element.26), channel_id=1, source_target_pairs={{0,8},{8,0},{1,9},{9,1},{2,10},{10,2},{3,11},{11,3},{4,12},{12,4},... | collective-permute-start | bytes 129032 | tf_op jit(solution)/shard_map/weight_block/ppermute | solution.py:291
  85.8 2.9 %collective-permute-start.12 = (bf16[56,384]{1,0:T(8,128)(2,1)S(1)}, bf16[56,384]{1,0:T(8,128)(2,1)S(1)}, u32[]{:S(2)}, u32[]{:S(2)}) collective-permute-start(bf16[56,384]{1,0:T(8,128)(2,1)S(1)} %get-tuple-element.25.refs_0_), channel_id=1, source_target_pairs={{0,1},{1,0},{2,3},{3,2},{4,5},{5,4},{6,7},{7,6},{8,9},{9,8},{10,11... | collective-permute-start | bytes 129032 | tf_op jit(solution)/shard_map/weight_block/ppermute | solution.py:289
  86.7 3.6 %collective-permute-start.13 = (bf16[56,384]{1,0:T(8,128)(2,1)S(1)}, bf16[56,384]{1,0:T(8,128)(2,1)S(1)}, u32[]{:S(2)}, u32[]{:S(2)}) collective-permute-start(bf16[56,384]{1,0:T(8,128)(2,1)S(1)} %get-tuple-element.26), channel_id=1, source_target_pairs={{0,9},{1,8},{8,1},{9,0},{2,11},{3,10},{10,3},{11,2},{4,13},{5,12},... | collective-permute-start | bytes 129032 | tf_op jit(solution)/shard_map/weight_block/ppermute | solution.py:290
  90.3 7.0 %collective-permute-start.14 = (bf16[56,384]{1,0:T(8,128)(2,1)S(1)}, bf16[56,384]{1,0:T(8,128)(2,1)S(1)}, u32[]{:S(2)}, u32[]{:S(2)}) collective-permute-start(bf16[56,384]{1,0:T(8,128)(2,1)S(1)} %weight_block.3.refs_0_), channel_id=1, source_target_pairs={{0,32},{16,48},{32,0},{48,16},{1,33},{17,49},{33,1},{49,17},{2,34}... | collective-permute-start | bytes 129032 | tf_op jit(solution)/shard_map/sum_over_z/ppermute | solution.py:296
  93.1 5.6 %collective-permute-start.15 = (bf16[56,384]{1,0:T(8,128)(2,1)S(1)}, bf16[56,384]{1,0:T(8,128)(2,1)S(1)}, u32[]{:S(2)}, u32[]{:S(2)}) collective-permute-start(bf16[56,384]{1,0:T(8,128)(2,1)S(1)} %weight_block.3.refs_0_), channel_id=1, source_target_pairs={{0,16},{16,32},{32,48},{48,0},{1,17},{17,33},{33,49},{49,1},{2,18}... | collective-permute-start | bytes 129032 | tf_op jit(solution)/shard_map/sum_over_z/ppermute | solution.py:296
  93.8 5.0 %collective-permute-start.16 = (bf16[56,384]{1,0:T(8,128)(2,1)S(1)}, bf16[56,384]{1,0:T(8,128)(2,1)S(1)}, u32[]{:S(2)}, u32[]{:S(2)}) collective-permute-start(bf16[56,384]{1,0:T(8,128)(2,1)S(1)} %weight_block.3.refs_0_), channel_id=1, source_target_pairs={{0,48},{16,0},{32,16},{48,32},{1,49},{17,1},{33,17},{49,33},{2,50}... | collective-permute-start | bytes 129032 | tf_op jit(solution)/shard_map/sum_over_z/ppermute | solution.py:296
  112.8 5.1 %collective-permute-start.17 = (bf16[896,384]{1,0:T(8,128)(2,1)S(1)}, bf16[896,384]{1,0:T(8,128)(2,1)S(1)}, u32[]{:S(2)}, u32[]{:S(2)}) collective-permute-start(bf16[896,384]{1,0:T(8,128)(2,1)S(1)} %bitcast.5), channel_id=1, source_target_pairs={{0,8},{8,0},{1,9},{9,1},{2,10},{10,2},{3,11},{11,3},{4,12},{12,4},... | collective-permute-start | bytes 2064392 | tf_op jit(solution)/shard_map/gather_plane/ppermute | solution.py:302

commit v10 on v9

--- a/solution.py
+++ b/solution.py
@@ -130,28 +130,14 @@
     for d, at in enumerate((core, 1 - core)):
         total = (begun[d] + terms(d, mix, keys, refs[:-1])).astype(BF)
         for r in range(8):
-            refs[-1][at, r] = total[r * 64 : (r + 1) * 64]
-
-
-def layer_kernel(recv, weight, bias, cot, out, packed):
-    halves = []
-    for c in range(2):
-        total = recv[8 * c].astype(F32)
-        for r in range(1, 8):
-            total = total + recv[8 * c + r].astype(F32)
-        halves.append(total.astype(BF))
-    mixed = jnp.concatenate(halves, axis=1)
-    pre = jnp.dot(mixed, weight[...], preferred_element_type=F32) + bias[...]
-    sig = jax.nn.sigmoid(pre)
-    out[...] = (pre * sig).astype(BF)
-    grad = cot[...].astype(F32) * sig * (1.0 + pre * (1.0 - sig))
-    low = grad.astype(BF).astype(F32)
-    wide = mixed.astype(F32)
-    for i in range(4):
-        part = wide[:, i * 192 : (i + 1) * 192]
-        for j in range(4):
-            both = jnp.concatenate([part, low[:, j * 192 : (j + 1) * 192]], axis=1)
-            packed[i * 4 + j] = both.astype(BF)
+            refs[-1][r, at] = total[r * 64 : (r + 1) * 64]
+
+
+def rows_kernel(recv, out):
+    total = recv[0].astype(F32)
+    for r in range(1, 8):
+        total = total + recv[r].astype(F32)
+    out[...] = total.astype(BF)
 
 
 def with_bias(block, row):
@@ -159,68 +145,79 @@
     low = row - high
     at = lax.broadcasted_iota(jnp.int32, (8, 384), 0)
     extra = jnp.where(at == 0, high, jnp.where(at == 1, low, 0.0))
-    return jnp.concatenate([block, extra], axis=0)
-
-
-def block_kernel(recv, keep, send):
-    data = recv[...]
-    left = data[:, :192]
-    right = data[:, 192:]
-    block = lax.dot_general(left, right, (((0,), (0,)), ((), ())), preferred_element_type=F32)
-    row = jnp.sum(right.astype(F32), axis=0, keepdims=True)
-    row = jnp.concatenate([row, row], axis=1)
-    halves = [
-        with_bias(
-            jnp.concatenate([block[h * 96 : h * 96 + 48], block[h * 96 + 48 : h * 96 + 96]], axis=1),
-            row,
-        ).astype(BF)
-        for h in range(2)
-    ]
+    return jnp.concatenate([block, extra], axis=0).astype(BF)
+
+
+def layer_kernel(mine, other, weight, bias, cot, other_cot, out, packed):
     first = lax.axis_index("core") == 0
-    keep[...] = jnp.where(first, halves[0], halves[1])
-    send[...] = jnp.where(first, halves[1], halves[0])
+    left = jnp.where(first, mine[...], other[...]).reshape(128, 384)
+    right = jnp.where(first, other[...], mine[...]).reshape(128, 384)
+    mixed = jnp.concatenate([left, right], axis=1)
+    pre = jnp.dot(mixed, weight[...], preferred_element_type=F32) + bias[...]
+    sig = jax.nn.sigmoid(pre)
+    act = pre * sig
+    out[...] = jnp.where(first, act[:64], act[64:]).astype(BF)
+    both = jnp.concatenate(
+        [jnp.where(first, cot[...], other_cot[...]), jnp.where(first, other_cot[...], cot[...])], axis=0
+    )
+    grad = both.astype(F32) * sig * (1.0 + pre * (1.0 - sig))
+    low = jnp.where(first, grad[:, :384], grad[:, 384:]).astype(BF)
+    block = lax.dot_general(mixed, low, (((0,), (0,)), ((), ())), preferred_element_type=F32)
+    row = jnp.sum(low.astype(F32), axis=0, keepdims=True)
+    for i in range(16):
+        packed[i] = with_bias(block[i * 48 : (i + 1) * 48], row)
 
 
 def resplit(total):
-    row = total[48:49] + total[49:50]
-    return with_bias(total[:48], row).astype(BF)
+    return with_bias(total[:48], total[48:49] + total[49:50])
+
+
+def plane_kernel(recv, out):
+    total = recv[0].astype(F32)
+    for r in range(1, 16):
+        total = total + recv[r].astype(F32)
+    out[...] = resplit(total)
+
+
+def pair_kernel(one, two, out):
+    out[...] = resplit(one[...].astype(F32) + two[...].astype(F32))
 
 
 def four_kernel(copies, one, two, three, four, out):
     total = (one[...].astype(F32) + two[...].astype(F32)) + (three[...].astype(F32) + four[...].astype(F32))
     value = resplit(total)
-    if copies is None:
-        out[...] = value
-    else:
-        for i in range(copies):
-            out[i] = value
-
-
-def write_rows(source, at, grad, rows, sems):
+    for i in range(copies):
+        out[i] = value
+
+
+def write_columns(source, at, grad, rows, sems):
+    start = pl.multiple_of(at * 384, 384)
     copies = []
     for i in range(4):
-        pieces = [source[i * 4 + j].astype(F32) for j in range(4)]
-        for h in range(2):
-            rows[i, h * 48 : (h + 1) * 48] = jnp.concatenate(
-                [piece[:48, h * 192 : (h + 1) * 192] for piece in pieces], axis=1
-            )
-        start = pl.multiple_of(i * 192 + at * 96, 32)
-        copies.append(pltpu.make_async_copy(rows.at[i], grad.at[pl.ds(start, 96)], sems.at[i]))
+        for j in range(4):
+            rows[i, j * 48 : (j + 1) * 48] = source[i * 4 + j].astype(F32)[:48]
+        copies.append(
+            pltpu.make_async_copy(rows.at[i], grad.at[pl.ds(i * 192, 192), pl.ds(start, 384)], sems.at[i])
+        )
         copies[-1].start()
     return copies
 
 
-def own_half_kernel(own, grad, bias, rows, sems):
-    copies = write_rows(own, lax.axis_index("core"), grad, rows, sems)
-    parts = [own[j].astype(F32) for j in range(4)]
-    bias[...] = jnp.concatenate([part[48:49, :192] + part[49:50, :192] for part in parts], axis=1)
+def own_half_kernel(own, grad, rows, sems):
+    for copy in write_columns(own, lax.axis_index("core"), grad, rows, sems):
+        copy.wait()
+
+
+def other_half_kernel(own, other, begun, grad, bias, rows, sems):
+    del begun
+    copies = write_columns(other, 1 - lax.axis_index("core"), grad, rows, sems)
+    first = lax.axis_index("core") == 0
+    mine, theirs = own[0].astype(F32), other[0].astype(F32)
+    mine = mine[48:49] + mine[49:50]
+    theirs = theirs[48:49] + theirs[49:50]
+    row = jnp.concatenate([jnp.where(first, mine, theirs), jnp.where(first, theirs, mine)], axis=1)
+    bias[...] = row.reshape(768)
     for copy in copies:
-        copy.wait()
-
-
-def other_half_kernel(other, begun, grad, rows, sems):
-    del begun
-    for copy in write_rows(other, 1 - lax.axis_index("core"), grad, rows, sems):
         copy.wait()
 
 
@@ -233,7 +230,7 @@
     extra = [] if begun is None else [begun]
     return call(
         lambda *refs: kernel(keys, *refs),
-        struct((2, 8, 64, 384), BF) if last else struct((2, 512, 384), F32),
+        struct((8, 2, 64, 384), BF) if last else struct((2, 512, 384), F32),
         [vmem()] * (1 + len(extra) + len(parts)),
         vmem(),
         aliases={1: 0} if extra and not last else None,
@@ -254,13 +251,14 @@
         own = [lax.ppermute(half, AXES, first_hop()) for half in halves]
     with jax.named_scope("spread_tiles"):
         there = [lax.ppermute(value, "core", shift(2, 1)) for value in (tiles, tile_cols, tile_mask)]
+        other_cot = lax.ppermute(cotangent, "core", shift(2, 1))
         mix = call(
             spread_kernel,
             struct((2, 4, 512, 512), BF),
             [smem(), smem(), smem(), smem(), vmem(), vmem()],
             vmem(),
         )(tile_cols, tile_mask, *there[1:], tiles, there[0])
-    own[0], mix = lax.optimization_barrier((own[0], mix))
+    own[0], mix, other_cot = lax.optimization_barrier((own[0], mix, other_cot))
     with jax.named_scope("spread_features"):
         early = neighbours(own[0], 3)
     with jax.named_scope("spread_features"):
@@ -272,52 +270,42 @@
         begun = product(next_kernel, [(BACK[1], 1)], mix, late[1:2], begun)
         partial = product(last_kernel, [(BACK[2], 1)], mix, late[2:], begun)
     with jax.named_scope("sum_over_rep"):
-        recv = lax.all_to_all(partial.reshape(1024, 384), ("core",) + REP, 0, 0, tiled=True)
+        recv = lax.all_to_all(partial, REP, 0, 0, tiled=True)
+        mixed = call(rows_kernel, struct((2, 64, 384), BF), [vmem()], vmem())(recv)
+        other_mixed = lax.ppermute(mixed, "core", shift(2, 1))
     with jax.named_scope("layer"):
         output, packed = call(
             layer_kernel,
-            (struct((64, 768), BF), struct((16, 64, 384), BF)),
-            [vmem()] * 4,
+            (struct((64, 768), BF), struct((16, 56, 384), BF)),
+            [vmem()] * 6,
             (vmem(), vmem()),
-        )(recv.reshape(16, 64, 384), weight, bias.reshape(1, 768), cotangent)
-    with jax.named_scope("exchange_rows"):
-        rows = lax.all_to_all(packed.reshape(1024, 384), PLANE, 0, 0, tiled=True)
-    with jax.named_scope("weight_block"):
-        keep, send = call(
-            block_kernel, (struct((56, 384), BF), struct((56, 384), BF)), [vmem()], (vmem(), vmem())
-        )(rows)
-        beside = lax.ppermute(keep, "zl", shift(2, 1))
-        across = lax.ppermute(send, ("core", "zl"), [(0, 3), (1, 2), (2, 1), (3, 0)])
-        other = lax.ppermute(send, "core", shift(2, 1))
-        pair = call(
-            lambda *refs: four_kernel(None, *refs), struct((56, 384), BF), [vmem()] * 4, vmem()
-        )(keep, other, beside, across)
+        )(mixed, other_mixed, weight, bias.reshape(1, 768), cotangent, other_cot)
+    with jax.named_scope("sum_over_plane"):
+        recv = lax.all_to_all(packed.reshape(896, 384), PLANE, 0, 0, tiled=True)
+        part = call(plane_kernel, struct((56, 384), BF), [vmem()], vmem())(recv.reshape(16, 56, 384))
     with jax.named_scope("sum_over_z"):
-        chain = [lax.ppermute(pair, "zh", shift(4, back)) for back in BACK]
+        beside = lax.ppermute(part, "zl", shift(2, 1))
+        part = call(pair_kernel, struct((56, 384), BF), [vmem()] * 2, vmem())(part, beside)
+        chain = [lax.ppermute(part, "zh", shift(4, back)) for back in BACK]
         whole = call(
             lambda *refs: four_kernel(16, *refs), struct((16, 56, 384), BF), [vmem()] * 4, vmem()
-        )(pair, *chain)
+        )(part, *chain)
     with jax.named_scope("gather_plane"):
         mine = lax.all_to_all(whole.reshape(896, 384), PLANE, 0, 0, tiled=True)
-        theirs = lax.ppermute(mine, "core", shift(2, 1))
+        theirs = lax.ppermute(mine, "core", shift(2, 1)).reshape(16, 56, 384)
+        mine = mine.reshape(16, 56, 384)
     with jax.named_scope("finish"):
-        scratch = [pltpu.VMEM((4, 96, 768), F32), pltpu.SemaphoreType.DMA((4,))]
-        grad, grad_bias = call(
-            own_half_kernel,
-            (struct((768, 768), F32), struct((1, 768), F32)),
-            [vmem()],
+        scratch = [pltpu.VMEM((4, 192, 384), F32), pltpu.SemaphoreType.DMA((4,))]
+        grad = call(own_half_kernel, struct((768, 768), F32), [vmem()], anyspace(), scratch)(mine)
+        grad_weight, grad_bias = call(
+            other_half_kernel,
+            (struct((768, 768), F32), struct((768,), F32)),
+            [vmem(), vmem(), anyspace()],
             (anyspace(), vmem()),
             scratch,
-        )(mine.reshape(16, 56, 384))
-        grad_weight = call(
-            other_half_kernel,
-            struct((768, 768), F32),
-            [vmem(), anyspace()],
-            anyspace(),
-            scratch,
-            aliases={1: 0},
-        )(theirs.reshape(16, 56, 384), grad)
-    return output, grad_weight, grad_bias.reshape(768)
+            aliases={2: 0},
+        )(mine, theirs, grad)
+    return output, grad_weight, grad_bias
 
 
 def solution(mesh):

time: 120 us -> 116 us (0.967)
  waiting for transfers between devices: 25.1 us -> 13.3 us
  blocking collectives: 32 us -> 43.6 us
  starting transfers between devices: 44.6 us -> 43 us
    all_to_all x1 -> x0, waiting for transfers between devices: 12.2 us -> none  [on_device(): lax.all_to_all(partial.reshape(1024, 384), ('core',) + REP, 0, 0, tiled=T...]
    all_to_all x1 -> x2, blocking collectives: 18.1 us -> 30.1 us  [the longest x1 15.6 us: on_device(): recv = lax.all_to_all(packed.reshape(896, 384), PLANE, 0, 0, tiled=True)]
    ppermute x7, starting transfers between devices: 14.1 us -> 25.4 us  [the longest x3 8.75 us: on_device(): chain = [lax.ppermute(part, 'zh', shift(4, back)) for back in BACK]]
    ppermute x2, starting transfers between devices: 8.01 us -> 0.1 us  [on_device(): own = [lax.ppermute(half, AXES, first_hop()) for half in halves]]
    all_to_all x1 -> x0, starting transfers between devices: 4.64 us -> none  [on_device(): lax.all_to_all(partial.reshape(1024, 384), ('core',) + REP, 0, 0, tiled=T...]
    pallas_call x10 -> x11, Pallas kernels: 8.06 us -> 7.09 us  [the longest x5 3.1 us: product(): call(lambda *refs: kernel(keys, *refs), struct((8, 2, 64, 384), BF) if la...]
  transfers between devices with their start and end apart: 19 -> 18, of which waited for: 11 -> 9; matrix products, arithmetic and copies ran while one was open for 1% -> 0% of each run, Pallas kernels for 6% -> 6%
where the time goes in v10:
time: 116 us
  blocking collectives  43.6 us (38%)
  starting transfers between devices  43 us (37%)
  waiting for transfers between devices  13.3 us (11%)
  Pallas kernels  10.8 us (9%)
  local copies, waits for them, and re-layouts  4.13 us (4%)
    all_to_all x1, blocking collectives, on_device(): recv = lax.all_to_all(packed.reshape(896, 384), PLANE, 0, 0, tiled=True)  15.6 us
    all_to_all x1, blocking collectives, on_device(): recv = lax.all_to_all(partial, REP, 0, 0, tiled=True)  14.5 us
    all_to_all x1, blocking collectives, on_device(): mine = lax.all_to_all(whole.reshape(896, 384), PLANE, 0, 0, tiled=True)  13.5 us
    ppermute x3, starting transfers between devices, on_device(): chain = [lax.ppermute(part, 'zh', shift(4, back)) for back in BACK]  8.75 us
    ppermute x1, starting transfers between devices, on_device(): other_cot = lax.ppermute(cotangent, 'core', shift(2, 1))  7.9 us
    ppermute x3, starting transfers between devices, on_device(): lax.ppermute(value, 'core', shift(2, 1))  7.79 us
    ppermute x2, starting transfers between devices, neighbours(): lax.ppermute(piece, 'zh', shift(4, step))  6.01 us
    ppermute x2, waiting for transfers between devices, neighbours(): lax.ppermute(piece, 'zh', shift(4, step))  4.97 us
  transfers between devices with their start and end apart: 18, of which 9 were waited for; matrix products, arithmetic and copies ran while one was open for 0% of the time, Pallas kernels for 6%

profile of v10, /device:TPU:1, one launch (start us, length us, event | category | flops | bytes accessed | tf_op | source)
XLA Modules:
  0.0 115.9 jit_solution(7029744057756793781)
XLA Ops:
  0.6 1.1 copy-done.2
  1.8 3.3 %collective-permute-start.3 = (bf16[4,4,4,128,128]{4,3,2,1,0:T(8,128)(2,1)}, bf16[4,4,4,128,128]{4,3,2,1,0:T(8,128)(2,1)S(1)}, u32[]{:S(2)}, u32[]{:S(2)}) collective-permute-start(bf16[4,4,4,128,128]{4,3,2,1,0:T(8,128)(2,1)} %tiles), channel_id=1, source_target_pairs={{0,8},{8,0},{1,9},{9,1},{2,10},{10,2},{3,11},{11,3},{4,12},{12,4},... | collective-permute-start | bytes 6291464 | tf_op jit(solution)/shard_map/spread_tiles/ppermute | solution.py:253
  5.3 7.9 %collective-permute-start.4 = (bf16[64,768]{1,0:T(8,128)(2,1)}, bf16[64,768]{1,0:T(8,128)(2,1)S(1)}, u32[]{:S(2)}, u32[]{:S(2)}) collective-permute-start(bf16[64,768]{1,0:T(8,128)(2,1)} %cot.1), channel_id=1, source_target_pairs={{0,8},{8,0},{1,9},{9,1},{2,10},{10,2},{3,11},{11,3},{4,12},{12,4},... | collective-permute-start | bytes 294920 | tf_op jit(solution)/shard_map/spread_tiles/ppermute | solution.py:254
  13.2 4.1 %collective-permute-start.1 = (s32[4,4,4]{2,1,0:T(4,128)}, s32[4,4,4]{2,1,0:T(4,128)S(1)}, u32[]{:S(2)}, u32[]{:S(2)}) collective-permute-start(s32[4,4,4]{2,1,0:T(4,128)} %cols.1), channel_id=1, source_target_pairs={{0,8},{8,0},{1,9},{9,1},{2,10},{10,2},{3,11},{11,3},{4,12},{12,4},... | collective-permute-start | bytes 776 | tf_op jit(solution)/shard_map/spread_tiles/ppermute | solution.py:253
  17.3 1.0 collective-permute-done.1.other_cols
  18.7 1.0 collective-permute-done.2.other_live
  19.7 1.6 %copy-done = bf16[4,4,4,128,128]{4,3,2,1,0:T(8,128)(2,1)S(1)} copy-done((bf16[4,4,4,128,128]{4,3,2,1,0:T(8,128)(2,1)S(1)}, bf16[4,4,4,128,128]{4,3,2,1,0:T(8,128)(2,1)}, u32[]{:S(2)}) %copy-start) | copy-done | bytes 2097176
  21.3 0.7 copy-done.4
  22.0 0.7 copy-done.5
  22.7 3.6 %spread_tiles.1.refs_0_ = bf16[2,4,512,512]{3,2,1,0:T(8,128)(2,1)S(1)} custom-call(s32[4,4,4]{2,1,0:T(4,128)S(1)} %copy-done.4, s32[4,4,4]{2,1,0:T(4,128)S(1)} %copy-done.5, s32[4,4,4]{2,1,0:T(4,128)S(1)} %collective-permute-done.1.other_cols, s32[4,4,4]{2,1,0:T(4,128)S(1)} %collective-permute-done.2.other_live, bf16[4,4,4,128,128]{4,3,2,1,0:T(8,128)(2,1)S(1)} %copy-done, ...), custom_call_target="tpu_custom_call" | custom-call | bytes 1048576 | tf_op jit(solution)/shard_map/spread_tiles/pallas_call | solution.py:255
  26.4 6.0 %collective-permute-start.6 = (bf16[256,384]{1,0:T(8,128)(2,1)S(1)}, bf16[256,384]{1,0:T(8,128)(2,1)S(1)}, u32[]{:S(2)}, u32[]{:S(2)}) collective-permute-start(bf16[256,384]{1,0:T(8,128)(2,1)S(1)} %collective-permute-done.refs_1_), channel_id=1, source_target_pairs={{0,48},{16,0},{32,16},{48,32},{1,49},{17,1},{33,17},{49,33},{2,50}... | collective-permute-start | bytes 589832 | tf_op jit(solution)/shard_map/spread_features/ppermute | solution.py:225
  32.4 2.7 %collective-permute-start.8 = (bf16[256,384]{1,0:T(8,128)(2,1)S(1)}, bf16[256,384]{1,0:T(8,128)(2,1)S(1)}, u32[]{:S(2)}, u32[]{:S(2)}) collective-permute-start(bf16[256,384]{1,0:T(8,128)(2,1)S(1)} %collective-permute-done.refs_1_), channel_id=1, source_target_pairs={{0,192},{64,0},{128,64},{192,128},{1,193},{65,1},{129,65},{193,129... | collective-permute-start | bytes 589832 | tf_op jit(solution)/shard_map/spread_features/ppermute | solution.py:225
  35.1 3.1 %collective-permute-done.6.refs_2_ = bf16[256,384]{1,0:T(8,128)(2,1)S(1)} collective-permute-done((bf16[256,384]{1,0:T(8,128)(2,1)S(1)}, bf16[256,384]{1,0:T(8,128)(2,1)S(1)}, u32[]{:S(2)}, u32[]{:S(2)}) %collective-permute-start.6) | collective-permute-done | bytes 196640 | tf_op jit(solution)/shard_map/spread_features/ppermute | solution.py:225
  38.2 1.0 collective-permute-start.11
  39.2 0.7 aggregate.5.refs_1_
  40.4 1.1 aggregate.6.refs_1_
  41.5 1.9 %collective-permute-done.9.refs_2_ = bf16[256,384]{1,0:T(8,128)(2,1)S(1)} collective-permute-done((bf16[256,384]{1,0:T(8,128)(2,1)S(1)}, bf16[256,384]{1,0:T(8,128)(2,1)S(1)}, u32[]{:S(2)}, u32[]{:S(2)}) %collective-permute-start.9) | collective-permute-done | bytes 196640 | tf_op jit(solution)/shard_map/spread_features/ppermute | solution.py:225
  44.8 14.5 %all_to_all.20.recv = bf16[8,2,64,384]{3,2,1,0:T(8,128)(2,1)S(1)} all-to-all(bf16[8,2,64,384]{3,2,1,0:T(8,128)(2,1)S(1)} %aggregate.9), channel_id=1, replica_groups=mesh['y'=4,'zh'=4,'core'=2,'x'=4,'zl'=2] {'x','zl'}, dimensions={0} | all-to-all | bytes 1572864 | tf_op jit(solution)/shard_map/sum_over_rep/all_to_all | solution.py:273
  59.4 3.3 %collective-permute-start.12 = (bf16[2,64,384]{2,1,0:T(8,128)(2,1)S(1)}, bf16[2,64,384]{2,1,0:T(8,128)(2,1)S(1)}, u32[]{:S(2)}, u32[]{:S(2)}) collective-permute-start(bf16[2,64,384]{2,1,0:T(8,128)(2,1)S(1)} %sum_over_rep.1.mine), channel_id=1, source_target_pairs={{0,8},{8,0},{1,9},{9,1},{2,10},{10,2},{3,11},{11,3},{4,12},{12,4},... | collective-permute-start | bytes 294920 | tf_op jit(solution)/shard_map/sum_over_rep/ppermute | solution.py:275
  62.7 0.9 collective-permute-done.12.other
  63.7 1.1 layer.1
  64.7 15.6 %all_to_all.21.recv = bf16[16,56,384]{2,1,0:T(8,128)(2,1)S(1)} all-to-all(bf16[16,56,384]{2,1,0:T(8,128)(2,1)S(1)} %get-tuple-element.24), channel_id=1, replica_groups=mesh['y'=4,'zh'=4,'core'=2,'x'=4,'zl'=2] {'x','y'}, dimensions={0} | all-to-all | bytes 1376256 | tf_op jit(solution)/shard_map/sum_over_plane/all_to_all | solution.py:284
  80.4 0.7 collective-permute-start.13
  81.1 2.2 %collective-permute-done.13.two = bf16[56,384]{1,0:T(8,128)(2,1)S(1)} collective-permute-done((bf16[56,384]{1,0:T(8,128)(2,1)S(1)}, bf16[56,384]{1,0:T(8,128)(2,1)S(1)}, u32[]{:S(2)}, u32[]{:S(2)}) %collective-permute-start.13) | collective-permute-done | bytes 43040 | tf_op jit(solution)/shard_map/sum_over_z/ppermute | solution.py:287
  83.4 5.2 %collective-permute-start.14 = (bf16[56,384]{1,0:T(8,128)(2,1)S(1)}, bf16[56,384]{1,0:T(8,128)(2,1)S(1)}, u32[]{:S(2)}, u32[]{:S(2)}) collective-permute-start(bf16[56,384]{1,0:T(8,128)(2,1)S(1)} %sum_over_z.2.refs_0_), channel_id=1, source_target_pairs={{0,32},{16,48},{32,0},{48,16},{1,33},{17,49},{33,1},{49,17},{2,34}... | collective-permute-start | bytes 129032 | tf_op jit(solution)/shard_map/sum_over_z/ppermute | solution.py:289
  89.2 2.9 %collective-permute-start.16 = (bf16[56,384]{1,0:T(8,128)(2,1)S(1)}, bf16[56,384]{1,0:T(8,128)(2,1)S(1)}, u32[]{:S(2)}, u32[]{:S(2)}) collective-permute-start(bf16[56,384]{1,0:T(8,128)(2,1)S(1)} %sum_over_z.2.refs_0_), channel_id=1, source_target_pairs={{0,48},{16,0},{32,16},{48,32},{1,49},{17,1},{33,17},{49,33},{2,50}... | collective-permute-start | bytes 129032 | tf_op jit(solution)/shard_map/sum_over_z/ppermute | solution.py:289
  92.1 1.9 %collective-permute-done.15.refs_2_ = bf16[56,384]{1,0:T(8,128)(2,1)S(1)} collective-permute-done((bf16[56,384]{1,0:T(8,128)(2,1)S(1)}, bf16[56,384]{1,0:T(8,128)(2,1)S(1)}, u32[]{:S(2)}, u32[]{:S(2)}) %collective-permute-start.15) | collective-permute-done | bytes 43040 | tf_op jit(solution)/shard_map/sum_over_z/ppermute | solution.py:289
  94.1 13.5 %all_to_all.22.own = bf16[16,56,384]{2,1,0:T(8,128)(2,1)S(1)} all-to-all(bf16[16,56,384]{2,1,0:T(8,128)(2,1)S(1)} %sum_over_z.3), channel_id=1, replica_groups=mesh['y'=4,'zh'=4,'core'=2,'x'=4,'zl'=2] {'x','y'}, dimensions={0} | all-to-all | bytes 1376256 | tf_op jit(solution)/shard_map/gather_plane/all_to_all | solution.py:294
  107.6 4.7 %collective-permute-start.17 = (bf16[896,384]{1,0:T(8,128)(2,1)S(1)}, bf16[896,384]{1,0:T(8,128)(2,1)S(1)}, u32[]{:S(2)}, u32[]{:S(2)}) collective-permute-start(bf16[896,384]{1,0:T(8,128)(2,1)S(1)} %bitcast.2), channel_id=1, source_target_pairs={{0,8},{8,0},{1,9},{9,1},{2,10},{10,2},{3,11},{11,3},{4,12},{12,4},... | collective-permute-start | bytes 2064392 | tf_op jit(solution)/shard_map/gather_plane/ppermute | solution.py:295
  112.3 1.1 finish.2.begun
  113.4 0.7 collective-permute-done.17
  114.1 1.6 %finish.3 = (f32[768,768]{1,0:T(8,128)}, f32[768]{0:T(1024)}) custom-call(bf16[16,56,384]{2,1,0:T(8,128)(2,1)S(1)} %all_to_all.22.own, bf16[16,56,384]{2,1,0:T(8,128)(2,1)S(1)} %bitcast.3, f32[768,768]{1,0:T(8,128)} %finish.2.begun), custom_call_target="tpu_custom_call", output_to_operand_aliasing={{0}: (2, {})} | custom-call | bytes 1048576 | tf_op jit(solution)/shard_map/finish/pallas_call | solution.py:300
  (36 shorter events, 3.4 us)
Async XLA Ops:
  0.6 1.1 copy-start.2
  1.8 17.9 %collective-permute-start.3 = (bf16[4,4,4,128,128]{4,3,2,1,0:T(8,128)(2,1)}, bf16[4,4,4,128,128]{4,3,2,1,0:T(8,128)(2,1)S(1)}, u32[]{:S(2)}, u32[]{:S(2)}) collective-permute-start(bf16[4,4,4,128,128]{4,3,2,1,0:T(8,128)(2,1)} %tiles), channel_id=1, source_target_pairs={{0,8},{8,0},{1,9},{9,1},{2,10},{10,2},{3,11},{11,3},{4,12},{12,4},... | collective-permute-start | bytes 6291464 | tf_op jit(solution)/shard_map/spread_tiles/ppermute | solution.py:253
  5.2 21.2 %collective-permute-start = (bf16[256,384]{1,0:T(8,128)(2,1)S(1)}, bf16[256,384]{1,0:T(8,128)(2,1)S(1)}, u32[]{:S(2)}, u32[]{:S(2)}) collective-permute-start(bf16[256,384]{1,0:T(8,128)(2,1)S(1)} %get-tuple-element.17), channel_id=1, source_target_pairs={{0,224},{1,152},{2,112},{3,40},{4,80},{5,8},{6,192},{7,184},{8,0},... | collective-permute-start | bytes 589832 | tf_op jit(solution)/shard_map/spread_features/ppermute | solution.py:251
  5.3 21.1 %collective-permute-start.4 = (bf16[64,768]{1,0:T(8,128)(2,1)}, bf16[64,768]{1,0:T(8,128)(2,1)S(1)}, u32[]{:S(2)}, u32[]{:S(2)}) collective-permute-start(bf16[64,768]{1,0:T(8,128)(2,1)} %cot.1), channel_id=1, source_target_pairs={{0,8},{8,0},{1,9},{9,1},{2,10},{10,2},{3,11},{11,3},{4,12},{12,4},... | collective-permute-start | bytes 294920 | tf_op jit(solution)/shard_map/spread_tiles/ppermute | solution.py:254
  13.2 21.9 %collective-permute-start.5 = (bf16[256,384]{1,0:T(8,128)(2,1)S(1)}, bf16[256,384]{1,0:T(8,128)(2,1)S(1)}, u32[]{:S(2)}, u32[]{:S(2)}) collective-permute-start(bf16[256,384]{1,0:T(8,128)(2,1)S(1)} %get-tuple-element.21), channel_id=1, source_target_pairs={{0,224},{1,152},{2,112},{3,40},{4,80},{5,8},{6,192},{7,184},{8,0},... | collective-permute-start | bytes 589832 | tf_op jit(solution)/shard_map/spread_features/ppermute | solution.py:251
  13.2 5.2 %collective-permute-start.1 = (s32[4,4,4]{2,1,0:T(4,128)}, s32[4,4,4]{2,1,0:T(4,128)S(1)}, u32[]{:S(2)}, u32[]{:S(2)}) collective-permute-start(s32[4,4,4]{2,1,0:T(4,128)} %cols.1), channel_id=1, source_target_pairs={{0,8},{8,0},{1,9},{9,1},{2,10},{10,2},{3,11},{11,3},{4,12},{12,4},... | collective-permute-start | bytes 776 | tf_op jit(solution)/shard_map/spread_tiles/ppermute | solution.py:253
  18.3 1.4 %collective-permute-start.2 = (s32[4,4,4]{2,1,0:T(4,128)}, s32[4,4,4]{2,1,0:T(4,128)S(1)}, u32[]{:S(2)}, u32[]{:S(2)}) collective-permute-start(s32[4,4,4]{2,1,0:T(4,128)} %live.1), channel_id=1, source_target_pairs={{0,8},{8,0},{1,9},{9,1},{2,10},{10,2},{3,11},{11,3},{4,12},{12,4},... | collective-permute-start | bytes 776 | tf_op jit(solution)/shard_map/spread_tiles/ppermute | solution.py:253
  19.7 1.6 %copy-start = (bf16[4,4,4,128,128]{4,3,2,1,0:T(8,128)(2,1)S(1)}, bf16[4,4,4,128,128]{4,3,2,1,0:T(8,128)(2,1)}, u32[]{:S(2)}) copy-start(bf16[4,4,4,128,128]{4,3,2,1,0:T(8,128)(2,1)} %tiles) | copy-start | bytes 6291460
  21.3 0.7 copy-start.4
  22.0 0.7 copy-start.5
  26.4 11.8 %collective-permute-start.6 = (bf16[256,384]{1,0:T(8,128)(2,1)S(1)}, bf16[256,384]{1,0:T(8,128)(2,1)S(1)}, u32[]{:S(2)}, u32[]{:S(2)}) collective-permute-start(bf16[256,384]{1,0:T(8,128)(2,1)S(1)} %collective-permute-done.refs_1_), channel_id=1, source_target_pairs={{0,48},{16,0},{32,16},{48,32},{1,49},{17,1},{33,17},{49,33},{2,50}... | collective-permute-start | bytes 589832 | tf_op jit(solution)/shard_map/spread_features/ppermute | solution.py:225
  32.4 8.0 %collective-permute-start.7 = (bf16[256,384]{1,0:T(8,128)(2,1)S(1)}, bf16[256,384]{1,0:T(8,128)(2,1)S(1)}, u32[]{:S(2)}, u32[]{:S(2)}) collective-permute-start(bf16[256,384]{1,0:T(8,128)(2,1)S(1)} %collective-permute-done.refs_1_), channel_id=1, source_target_pairs={{0,64},{64,128},{128,192},{192,0},{1,65},{65,129},{129,193},{193,1... | collective-permute-start | bytes 589832 | tf_op jit(solution)/shard_map/spread_features/ppermute | solution.py:225
  32.4 8.0 %collective-permute-start.8 = (bf16[256,384]{1,0:T(8,128)(2,1)S(1)}, bf16[256,384]{1,0:T(8,128)(2,1)S(1)}, u32[]{:S(2)}, u32[]{:S(2)}) collective-permute-start(bf16[256,384]{1,0:T(8,128)(2,1)S(1)} %collective-permute-done.refs_1_), channel_id=1, source_target_pairs={{0,192},{64,0},{128,64},{192,128},{1,193},{65,1},{129,65},{193,129... | collective-permute-start | bytes 589832 | tf_op jit(solution)/shard_map/spread_features/ppermute | solution.py:225
  35.0 8.3 %collective-permute-start.9 = (bf16[256,384]{1,0:T(8,128)(2,1)S(1)}, bf16[256,384]{1,0:T(8,128)(2,1)S(1)}, u32[]{:S(2)}, u32[]{:S(2)}) collective-permute-start(bf16[256,384]{1,0:T(8,128)(2,1)S(1)} %collective-permute-done.5.refs_2_), channel_id=1, source_target_pairs={{0,16},{16,32},{32,48},{48,0},{1,17},{17,33},{33,49},{49,1},{2,18}... | collective-permute-start | bytes 589832 | tf_op jit(solution)/shard_map/spread_features/ppermute | solution.py:225
  35.0 8.8 %collective-permute-start.10 = (bf16[256,384]{1,0:T(8,128)(2,1)S(1)}, bf16[256,384]{1,0:T(8,128)(2,1)S(1)}, u32[]{:S(2)}, u32[]{:S(2)}) collective-permute-start(bf16[256,384]{1,0:T(8,128)(2,1)S(1)} %collective-permute-done.5.refs_2_), channel_id=1, source_target_pairs={{0,64},{64,128},{128,192},{192,0},{1,65},{65,129},{129,193},{193,1... | collective-permute-start | bytes 589832 | tf_op jit(solution)/shard_map/spread_features/ppermute | solution.py:225
  38.2 6.1 %collective-permute-start.11 = (bf16[256,384]{1,0:T(8,128)(2,1)S(1)}, bf16[256,384]{1,0:T(8,128)(2,1)S(1)}, u32[]{:S(2)}, u32[]{:S(2)}) collective-permute-start(bf16[256,384]{1,0:T(8,128)(2,1)S(1)} %collective-permute-done.5.refs_2_), channel_id=1, source_target_pairs={{0,192},{64,0},{128,64},{192,128},{1,193},{65,1},{129,65},{193,129... | collective-permute-start | bytes 589832 | tf_op jit(solution)/shard_map/spread_features/ppermute | solution.py:225
  44.7 18.0 %copy-start.6 = (f32[768]{0:T(1024)S(1)}, f32[768]{0:T(1024)}, u32[]{:S(2)}) copy-start(f32[768]{0:T(1024)} %param.12) | copy-start | bytes 9220
  44.7 18.9 %copy-start.1 = (bf16[768,768]{1,0:T(8,128)(2,1)S(1)}, bf16[768,768]{1,0:T(8,128)(2,1)}, u32[]{:S(2)}) copy-start(bf16[768,768]{1,0:T(8,128)(2,1)} %weight.1) | copy-start | bytes 3538948
  44.8 18.9 %copy-start.3 = (bf16[64,768]{1,0:T(8,128)(2,1)S(1)}, bf16[64,768]{1,0:T(8,128)(2,1)}, u32[]{:S(2)}) copy-start(bf16[64,768]{1,0:T(8,128)(2,1)} %cot.1) | copy-start | bytes 294916
  59.4 4.3 %collective-permute-start.12 = (bf16[2,64,384]{2,1,0:T(8,128)(2,1)S(1)}, bf16[2,64,384]{2,1,0:T(8,128)(2,1)S(1)}, u32[]{:S(2)}, u32[]{:S(2)}) collective-permute-start(bf16[2,64,384]{2,1,0:T(8,128)(2,1)S(1)} %sum_over_rep.1.mine), channel_id=1, source_target_pairs={{0,8},{8,0},{1,9},{9,1},{2,10},{10,2},{3,11},{11,3},{4,12},{12,4},... | collective-permute-start | bytes 294920 | tf_op jit(solution)/shard_map/sum_over_rep/ppermute | solution.py:275
  80.4 3.0 %collective-permute-start.13 = (bf16[56,384]{1,0:T(8,128)(2,1)S(1)}, bf16[56,384]{1,0:T(8,128)(2,1)S(1)}, u32[]{:S(2)}, u32[]{:S(2)}) collective-permute-start(bf16[56,384]{1,0:T(8,128)(2,1)S(1)} %sum_over_plane.1.one), channel_id=1, source_target_pairs={{0,1},{1,0},{2,3},{3,2},{4,5},{5,4},{6,7},{7,6},{8,9},{9,8},{10,11... | collective-permute-start | bytes 129032 | tf_op jit(solution)/shard_map/sum_over_z/ppermute | solution.py:287
  83.4 8.8 %collective-permute-start.14 = (bf16[56,384]{1,0:T(8,128)(2,1)S(1)}, bf16[56,384]{1,0:T(8,128)(2,1)S(1)}, u32[]{:S(2)}, u32[]{:S(2)}) collective-permute-start(bf16[56,384]{1,0:T(8,128)(2,1)S(1)} %sum_over_z.2.refs_0_), channel_id=1, source_target_pairs={{0,32},{16,48},{32,0},{48,16},{1,33},{17,49},{33,1},{49,17},{2,34}... | collective-permute-start | bytes 129032 | tf_op jit(solution)/shard_map/sum_over_z/ppermute | solution.py:289
  88.6 5.4 %collective-permute-start.15 = (bf16[56,384]{1,0:T(8,128)(2,1)S(1)}, bf16[56,384]{1,0:T(8,128)(2,1)S(1)}, u32[]{:S(2)}, u32[]{:S(2)}) collective-permute-start(bf16[56,384]{1,0:T(8,128)(2,1)S(1)} %sum_over_z.2.refs_0_), channel_id=1, source_target_pairs={{0,16},{16,32},{32,48},{48,0},{1,17},{17,33},{33,49},{49,1},{2,18}... | collective-permute-start | bytes 129032 | tf_op jit(solution)/shard_map/sum_over_z/ppermute | solution.py:289
  89.2 4.8 %collective-permute-start.16 = (bf16[56,384]{1,0:T(8,128)(2,1)S(1)}, bf16[56,384]{1,0:T(8,128)(2,1)S(1)}, u32[]{:S(2)}, u32[]{:S(2)}) collective-permute-start(bf16[56,384]{1,0:T(8,128)(2,1)S(1)} %sum_over_z.2.refs_0_), channel_id=1, source_target_pairs={{0,48},{16,0},{32,16},{48,32},{1,49},{17,1},{33,17},{49,33},{2,50}... | collective-permute-start | bytes 129032 | tf_op jit(solution)/shard_map/sum_over_z/ppermute | solution.py:289
  107.6 6.5 %collective-permute-start.17 = (bf16[896,384]{1,0:T(8,128)(2,1)S(1)}, bf16[896,384]{1,0:T(8,128)(2,1)S(1)}, u32[]{:S(2)}, u32[]{:S(2)}) collective-permute-start(bf16[896,384]{1,0:T(8,128)(2,1)S(1)} %bitcast.2), channel_id=1, source_target_pairs={{0,8},{8,0},{1,9},{9,1},{2,10},{10,2},{3,11},{11,3},{4,12},{12,4},... | collective-permute-start | bytes 2064392 | tf_op jit(solution)/shard_map/gather_plane/ppermute | solution.py:295

commit v11 on v10

--- a/solution.py
+++ b/solution.py
@@ -82,16 +82,15 @@
         copy.wait()
 
 
-def spread_kernel(cols, live, other_cols, other_live, tiles, other_tiles, out):
-    for d, (col, on, tile) in enumerate(((cols, live, tiles), (other_cols, other_live, other_tiles))):
+def spread_kernel(picks, other_picks, tiles, other_tiles, out):
+    for d, (pick, tile) in enumerate(((picks, tiles), (other_picks, other_tiles))):
         for b in range(4):
             for s in range(4):
-                picks = [jnp.where(on[b, s, k] != 0, col[b, s, k], -1) for k in range(4)]
                 parts = [tile[b, s, k].astype(F32) for k in range(4)]
                 for c in range(4):
                     total = jnp.zeros((128, 128), F32)
-                    for pick, part in zip(picks, parts):
-                        total = total + jnp.where(pick == c, part, 0.0)
+                    for k in range(4):
+                        total = total + jnp.where(pick[b, s, k] == c, parts[k], 0.0)
                     out[d, s, b * 128 : (b + 1) * 128, c * 128 : (c + 1) * 128] = total.astype(BF)
 
 
@@ -208,15 +207,17 @@
         copy.wait()
 
 
-def other_half_kernel(own, other, begun, grad, bias, rows, sems):
+def other_half_kernel(own, other, begun, grad, bias, rows, sems, row, row_sem):
     del begun
-    copies = write_columns(other, 1 - lax.axis_index("core"), grad, rows, sems)
     first = lax.axis_index("core") == 0
     mine, theirs = own[0].astype(F32), other[0].astype(F32)
     mine = mine[48:49] + mine[49:50]
     theirs = theirs[48:49] + theirs[49:50]
-    row = jnp.concatenate([jnp.where(first, mine, theirs), jnp.where(first, theirs, mine)], axis=1)
-    bias[...] = row.reshape(768)
+    both = jnp.concatenate([jnp.where(first, mine, theirs), jnp.where(first, theirs, mine)], axis=1)
+    row[...] = both.reshape(768)
+    copies = [pltpu.make_async_copy(row, bias, row_sem)]
+    copies[0].start()
+    copies += write_columns(other, 1 - lax.axis_index("core"), grad, rows, sems)
     for copy in copies:
         copy.wait()
 
@@ -247,18 +248,18 @@
             (vmem(), vmem()),
             [pltpu.SemaphoreType.DMA((2,))],
         )(features)
-        *halves, tiles = lax.optimization_barrier((*halves, tiles))
+        *halves, tiles, tile_cols, tile_mask = lax.optimization_barrier((*halves, tiles, tile_cols, tile_mask))
         own = [lax.ppermute(half, AXES, first_hop()) for half in halves]
     with jax.named_scope("spread_tiles"):
-        there = [lax.ppermute(value, "core", shift(2, 1)) for value in (tiles, tile_cols, tile_mask)]
-        other_cot = lax.ppermute(cotangent, "core", shift(2, 1))
+        picks = jnp.where(tile_mask != 0, tile_cols, -1)
+        there = [lax.ppermute(value, "core", shift(2, 1)) for value in (picks, tiles)]
         mix = call(
             spread_kernel,
             struct((2, 4, 512, 512), BF),
-            [smem(), smem(), smem(), smem(), vmem(), vmem()],
+            [smem(), smem(), vmem(), vmem()],
             vmem(),
-        )(tile_cols, tile_mask, *there[1:], tiles, there[0])
-    own[0], mix, other_cot = lax.optimization_barrier((own[0], mix, other_cot))
+        )(picks, there[0], tiles, there[1])
+    own[0], mix = lax.optimization_barrier((own[0], mix))
     with jax.named_scope("spread_features"):
         early = neighbours(own[0], 3)
     with jax.named_scope("spread_features"):
@@ -266,6 +267,8 @@
     with jax.named_scope("aggregate"):
         begun = product(first_kernel, [(0, 0), (0, 1)], mix, own)
         begun = product(next_kernel, [(back, 0) for back in BACK], mix, early, begun)
+        other_cot = lax.ppermute(cotangent, "core", shift(2, 1))
+        begun, other_cot = lax.optimization_barrier((begun, other_cot))
         begun = product(next_kernel, [(BACK[0], 1)], mix, late[:1], begun)
         begun = product(next_kernel, [(BACK[1], 1)], mix, late[1:2], begun)
         partial = product(last_kernel, [(BACK[2], 1)], mix, late[2:], begun)
@@ -301,8 +304,8 @@
             other_half_kernel,
             (struct((768, 768), F32), struct((768,), F32)),
             [vmem(), vmem(), anyspace()],
-            (anyspace(), vmem()),
-            scratch,
+            (anyspace(), hbm()),
+            scratch + [pltpu.VMEM((768,), F32), pltpu.SemaphoreType.DMA],
             aliases={2: 0},
         )(mine, theirs, grad)
     return output, grad_weight, grad_bias

time: 116 us -> 116 us (level)
  waiting for transfers between devices: 13.3 us -> 11.2 us
  blocking collectives: 43.6 us -> 45.3 us
  local copies, waits for them, and re-layouts: 4.13 us -> 2.74 us
  starting transfers between devices: 43 us -> 44.3 us
    ppermute x2, starting transfers between devices: 0.1 us -> 8.01 us  [on_device(): own = [lax.ppermute(half, AXES, first_hop()) for half in halves]]
    ppermute x1, starting transfers between devices: 7.9 us -> 0.01 us  [on_device(): other_cot = lax.ppermute(cotangent, 'core', shift(2, 1))]
    ppermute x2, waiting for transfers between devices: 4.97 us -> 2.07 us  [neighbours(): lax.ppermute(piece, 'zh', shift(4, step))]
    ppermute x2, starting transfers between devices: 6.01 us -> 8.54 us  [neighbours(): lax.ppermute(piece, 'zh', shift(4, step))]
    ppermute x3, starting transfers between devices: 8.75 us -> 6.99 us  [on_device(): chain = [lax.ppermute(part, 'zh', shift(4, back)) for back in BACK]]
    ppermute x4, starting transfers between devices: 3.68 us -> 5.34 us  [neighbours(): lax.ppermute(piece, 'y', shift(4, k))]
    ppermute x4, waiting for transfers between devices: 0.55 us -> 2.15 us  [neighbours(): lax.ppermute(piece, 'y', shift(4, k))]
    all_to_all x1, blocking collectives: 14.5 us -> 16 us  [on_device(): recv = lax.all_to_all(partial, REP, 0, 0, tiled=True)]
  transfers between devices with their start and end apart: 18 -> 17, of which waited for: 9 -> 8; matrix products, arithmetic and copies ran while one was open for 0% -> 1% of each run, Pallas kernels for 6% -> 6%
where the time goes in v11:
time: 116 us; the launch traced here: 115 us
  blocking collectives  45.3 us (39%)
  starting transfers between devices  44.3 us (38%)
  waiting for transfers between devices  11.2 us (10%)
  Pallas kernels  10 us (9%)
  local copies, waits for them, and re-layouts  2.74 us (2%)
    all_to_all x1, blocking collectives, on_device(): recv = lax.all_to_all(packed.reshape(896, 384), PLANE, 0, 0, tiled=True)  16.4 us
    all_to_all x1, blocking collectives, on_device(): recv = lax.all_to_all(partial, REP, 0, 0, tiled=True)  16 us
    all_to_all x1, blocking collectives, on_device(): mine = lax.all_to_all(whole.reshape(896, 384), PLANE, 0, 0, tiled=True)  12.8 us
    ppermute x2, starting transfers between devices, neighbours(): lax.ppermute(piece, 'zh', shift(4, step))  8.54 us
    ppermute x2, starting transfers between devices, on_device(): own = [lax.ppermute(half, AXES, first_hop()) for half in halves]  8.01 us
    ppermute x2, starting transfers between devices, on_device(): lax.ppermute(value, 'core', shift(2, 1))  7.45 us
    ppermute x3, starting transfers between devices, on_device(): chain = [lax.ppermute(part, 'zh', shift(4, back)) for back in BACK]  6.99 us
    ppermute x4, starting transfers between devices, neighbours(): lax.ppermute(piece, 'y', shift(4, k))  5.34 us
  transfers between devices with their start and end apart: 17, of which 8 were waited for; matrix products, arithmetic and copies ran while one was open for 1% of the time, Pallas kernels for 6%

profile of v11, /device:TPU:1, one launch (start us, length us, event | category | flops | bytes accessed | tf_op | source)
XLA Modules:
  0.0 115.2 jit_solution(6168215376111447892)
XLA Ops:
  0.6 1.1 copy-done.2
  1.8 3.3 %collective-permute-start.2 = (bf16[4,4,4,128,128]{4,3,2,1,0:T(8,128)(2,1)}, bf16[4,4,4,128,128]{4,3,2,1,0:T(8,128)(2,1)S(1)}, u32[]{:S(2)}, u32[]{:S(2)}) collective-permute-start(bf16[4,4,4,128,128]{4,3,2,1,0:T(8,128)(2,1)} %tiles), channel_id=1, source_target_pairs={{0,8},{8,0},{1,9},{9,1},{2,10},{10,2},{3,11},{11,3},{4,12},{12,4},... | collective-permute-start | bytes 6291464 | tf_op jit(solution)/shard_map/spread_tiles/ppermute | solution.py:255
  5.3 7.9 %collective-permute-start.3 = (bf16[256,384]{1,0:T(8,128)(2,1)S(1)}, bf16[256,384]{1,0:T(8,128)(2,1)S(1)}, u32[]{:S(2)}, u32[]{:S(2)}) collective-permute-start(bf16[256,384]{1,0:T(8,128)(2,1)S(1)} %get-tuple-element.26), channel_id=1, source_target_pairs={{0,224},{1,152},{2,112},{3,40},{4,80},{5,8},{6,192},{7,184},{8,0},... | collective-permute-start | bytes 589832 | tf_op jit(solution)/shard_map/spread_features/ppermute | solution.py:252
  13.2 0.7 compare_select_fusion.picks
  13.9 4.1 %collective-permute-start.1 = (s32[4,4,4]{2,1,0:T(4,128)S(1)}, s32[4,4,4]{2,1,0:T(4,128)S(1)}, u32[]{:S(2)}, u32[]{:S(2)}) collective-permute-start(s32[4,4,4]{2,1,0:T(4,128)S(1)} %compare_select_fusion.picks), channel_id=1, source_target_pairs={{0,8},{8,0},{1,9},{9,1},{2,10},{10,2},{3,11},{11,3},{4,12},{12,4},... | collective-permute-start | bytes 776 | tf_op jit(solution)/shard_map/spread_tiles/ppermute | solution.py:255
  18.0 0.8 collective-permute-done.1.other_picks
  18.8 1.6 %copy-done = bf16[4,4,4,128,128]{4,3,2,1,0:T(8,128)(2,1)S(1)} copy-done((bf16[4,4,4,128,128]{4,3,2,1,0:T(8,128)(2,1)S(1)}, bf16[4,4,4,128,128]{4,3,2,1,0:T(8,128)(2,1)}, u32[]{:S(2)}) %copy-start) | copy-done | bytes 2097176
  20.4 3.4 %spread_tiles.1.refs_0_ = bf16[2,4,512,512]{3,2,1,0:T(8,128)(2,1)S(1)} custom-call(s32[4,4,4]{2,1,0:T(4,128)S(1)} %compare_select_fusion.picks, s32[4,4,4]{2,1,0:T(4,128)S(1)} %collective-permute-done.1.other_picks, bf16[4,4,4,128,128]{4,3,2,1,0:T(8,128)(2,1)S(1)} %copy-done, bf16[4,4,4,128,128]{4,3,2,1,0:T(8,128)(2,1)S(1)} %collective-permute-done.2.other_tiles), custom_call_target="tpu_custom_call" | custom-call | bytes 1048576 | tf_op jit(solution)/shard_map/spread_tiles/pallas_call | solution.py:256
  23.8 8.5 %collective-permute-start.4 = (bf16[256,384]{1,0:T(8,128)(2,1)S(1)}, bf16[256,384]{1,0:T(8,128)(2,1)S(1)}, u32[]{:S(2)}, u32[]{:S(2)}) collective-permute-start(bf16[256,384]{1,0:T(8,128)(2,1)S(1)} %collective-permute-done.refs_1_), channel_id=1, source_target_pairs={{0,48},{16,0},{32,16},{48,32},{1,49},{17,1},{33,17},{49,33},{2,50}... | collective-permute-start | bytes 589832 | tf_op jit(solution)/shard_map/spread_features/ppermute | solution.py:226
  32.3 2.7 %collective-permute-start.6 = (bf16[256,384]{1,0:T(8,128)(2,1)S(1)}, bf16[256,384]{1,0:T(8,128)(2,1)S(1)}, u32[]{:S(2)}, u32[]{:S(2)}) collective-permute-start(bf16[256,384]{1,0:T(8,128)(2,1)S(1)} %collective-permute-done.refs_1_), channel_id=1, source_target_pairs={{0,192},{64,0},{128,64},{192,128},{1,193},{65,1},{129,65},{193,129... | collective-permute-start | bytes 589832 | tf_op jit(solution)/shard_map/spread_features/ppermute | solution.py:226
  35.0 2.7 %collective-permute-start.10 = (bf16[256,384]{1,0:T(8,128)(2,1)S(1)}, bf16[256,384]{1,0:T(8,128)(2,1)S(1)}, u32[]{:S(2)}, u32[]{:S(2)}) collective-permute-start(bf16[256,384]{1,0:T(8,128)(2,1)S(1)} %collective-permute-done.3.refs_2_), channel_id=1, source_target_pairs={{0,192},{64,0},{128,64},{192,128},{1,193},{65,1},{129,65},{193,129... | collective-permute-start | bytes 589832 | tf_op jit(solution)/shard_map/spread_features/ppermute | solution.py:226
  37.7 2.1 %collective-permute-done.5.refs_3_ = bf16[256,384]{1,0:T(8,128)(2,1)S(1)} collective-permute-done((bf16[256,384]{1,0:T(8,128)(2,1)S(1)}, bf16[256,384]{1,0:T(8,128)(2,1)S(1)}, u32[]{:S(2)}, u32[]{:S(2)}) %collective-permute-start.5) | collective-permute-done | bytes 196640 | tf_op jit(solution)/shard_map/spread_features/ppermute | solution.py:226
  39.9 0.7 aggregate.5.refs_1_
  40.6 1.1 aggregate.6.refs_1_
  41.7 2.1 %collective-permute-done.8.refs_2_ = bf16[256,384]{1,0:T(8,128)(2,1)S(1)} collective-permute-done((bf16[256,384]{1,0:T(8,128)(2,1)S(1)}, bf16[256,384]{1,0:T(8,128)(2,1)S(1)}, u32[]{:S(2)}, u32[]{:S(2)}) %collective-permute-start.8) | collective-permute-done | bytes 196640 | tf_op jit(solution)/shard_map/spread_features/ppermute | solution.py:226
  44.2 0.4 aggregate.8.refs_1_
  45.1 16.0 %all_to_all.20.recv = bf16[8,2,64,384]{3,2,1,0:T(8,128)(2,1)S(1)} all-to-all(bf16[8,2,64,384]{3,2,1,0:T(8,128)(2,1)S(1)} %aggregate.9), channel_id=1, replica_groups=mesh['y'=4,'zh'=4,'core'=2,'x'=4,'zl'=2] {'x','zl'}, dimensions={0} | all-to-all | bytes 1572864 | tf_op jit(solution)/shard_map/sum_over_rep/all_to_all | solution.py:276
  61.3 2.0 %collective-permute-start.11 = (bf16[2,64,384]{2,1,0:T(8,128)(2,1)S(1)}, bf16[2,64,384]{2,1,0:T(8,128)(2,1)S(1)}, u32[]{:S(2)}, u32[]{:S(2)}) collective-permute-start(bf16[2,64,384]{2,1,0:T(8,128)(2,1)S(1)} %sum_over_rep.1.mine), channel_id=1, source_target_pairs={{0,8},{8,0},{1,9},{9,1},{2,10},{10,2},{3,11},{11,3},{4,12},{12,4},... | collective-permute-start | bytes 294920 | tf_op jit(solution)/shard_map/sum_over_rep/ppermute | solution.py:278
  63.3 0.9 collective-permute-done.11.other
  64.3 1.1 layer.1
  65.3 16.4 %all_to_all.21.recv = bf16[16,56,384]{2,1,0:T(8,128)(2,1)S(1)} all-to-all(bf16[16,56,384]{2,1,0:T(8,128)(2,1)S(1)} %get-tuple-element.30), channel_id=1, replica_groups=mesh['y'=4,'zh'=4,'core'=2,'x'=4,'zl'=2] {'x','y'}, dimensions={0} | all-to-all | bytes 1376256 | tf_op jit(solution)/shard_map/sum_over_plane/all_to_all | solution.py:287
  81.9 0.7 collective-permute-start.12
  82.6 2.2 %collective-permute-done.12.two = bf16[56,384]{1,0:T(8,128)(2,1)S(1)} collective-permute-done((bf16[56,384]{1,0:T(8,128)(2,1)S(1)}, bf16[56,384]{1,0:T(8,128)(2,1)S(1)}, u32[]{:S(2)}, u32[]{:S(2)}) %collective-permute-start.12) | collective-permute-done | bytes 43040 | tf_op jit(solution)/shard_map/sum_over_z/ppermute | solution.py:290
  84.9 3.4 %collective-permute-start.13 = (bf16[56,384]{1,0:T(8,128)(2,1)S(1)}, bf16[56,384]{1,0:T(8,128)(2,1)S(1)}, u32[]{:S(2)}, u32[]{:S(2)}) collective-permute-start(bf16[56,384]{1,0:T(8,128)(2,1)S(1)} %sum_over_z.2.refs_0_), channel_id=1, source_target_pairs={{0,32},{16,48},{32,0},{48,16},{1,33},{17,49},{33,1},{49,17},{2,34}... | collective-permute-start | bytes 129032 | tf_op jit(solution)/shard_map/sum_over_z/ppermute | solution.py:292
  88.3 3.5 %collective-permute-start.15 = (bf16[56,384]{1,0:T(8,128)(2,1)S(1)}, bf16[56,384]{1,0:T(8,128)(2,1)S(1)}, u32[]{:S(2)}, u32[]{:S(2)}) collective-permute-start(bf16[56,384]{1,0:T(8,128)(2,1)S(1)} %sum_over_z.2.refs_0_), channel_id=1, source_target_pairs={{0,48},{16,0},{32,16},{48,32},{1,49},{17,1},{33,17},{49,33},{2,50}... | collective-permute-start | bytes 129032 | tf_op jit(solution)/shard_map/sum_over_z/ppermute | solution.py:292
  91.9 1.4 %collective-permute-done.14.refs_2_ = bf16[56,384]{1,0:T(8,128)(2,1)S(1)} collective-permute-done((bf16[56,384]{1,0:T(8,128)(2,1)S(1)}, bf16[56,384]{1,0:T(8,128)(2,1)S(1)}, u32[]{:S(2)}, u32[]{:S(2)}) %collective-permute-start.14) | collective-permute-done | bytes 43040 | tf_op jit(solution)/shard_map/sum_over_z/ppermute | solution.py:292
  93.3 0.8 collective-permute-done.15.refs_3_
  94.2 12.8 %all_to_all.22.own = bf16[16,56,384]{2,1,0:T(8,128)(2,1)S(1)} all-to-all(bf16[16,56,384]{2,1,0:T(8,128)(2,1)S(1)} %sum_over_z.3), channel_id=1, replica_groups=mesh['y'=4,'zh'=4,'core'=2,'x'=4,'zl'=2] {'x','y'}, dimensions={0} | all-to-all | bytes 1376256 | tf_op jit(solution)/shard_map/gather_plane/all_to_all | solution.py:297
  107.0 5.2 %collective-permute-start.16 = (bf16[896,384]{1,0:T(8,128)(2,1)S(1)}, bf16[896,384]{1,0:T(8,128)(2,1)S(1)}, u32[]{:S(2)}, u32[]{:S(2)}) collective-permute-start(bf16[896,384]{1,0:T(8,128)(2,1)S(1)} %bitcast.2), channel_id=1, source_target_pairs={{0,8},{8,0},{1,9},{9,1},{2,10},{10,2},{3,11},{11,3},{4,12},{12,4},... | collective-permute-start | bytes 2064392 | tf_op jit(solution)/shard_map/gather_plane/ppermute | solution.py:298
  112.2 1.1 finish.2.begun
  113.3 0.7 collective-permute-done.16
  114.0 1.1 finish.3
  (31 shorter events, 1.4 us)
Async XLA Ops:
  0.6 1.1 copy-start.2
  1.8 17.0 %collective-permute-start.2 = (bf16[4,4,4,128,128]{4,3,2,1,0:T(8,128)(2,1)}, bf16[4,4,4,128,128]{4,3,2,1,0:T(8,128)(2,1)S(1)}, u32[]{:S(2)}, u32[]{:S(2)}) collective-permute-start(bf16[4,4,4,128,128]{4,3,2,1,0:T(8,128)(2,1)} %tiles), channel_id=1, source_target_pairs={{0,8},{8,0},{1,9},{9,1},{2,10},{10,2},{3,11},{11,3},{4,12},{12,4},... | collective-permute-start | bytes 6291464 | tf_op jit(solution)/shard_map/spread_tiles/ppermute | solution.py:255
  5.2 18.6 %collective-permute-start = (bf16[256,384]{1,0:T(8,128)(2,1)S(1)}, bf16[256,384]{1,0:T(8,128)(2,1)S(1)}, u32[]{:S(2)}, u32[]{:S(2)}) collective-permute-start(bf16[256,384]{1,0:T(8,128)(2,1)S(1)} %get-tuple-element.20), channel_id=1, source_target_pairs={{0,224},{1,152},{2,112},{3,40},{4,80},{5,8},{6,192},{7,184},{8,0},... | collective-permute-start | bytes 589832 | tf_op jit(solution)/shard_map/spread_features/ppermute | solution.py:252
  5.3 29.8 %collective-permute-start.3 = (bf16[256,384]{1,0:T(8,128)(2,1)S(1)}, bf16[256,384]{1,0:T(8,128)(2,1)S(1)}, u32[]{:S(2)}, u32[]{:S(2)}) collective-permute-start(bf16[256,384]{1,0:T(8,128)(2,1)S(1)} %get-tuple-element.26), channel_id=1, source_target_pairs={{0,224},{1,152},{2,112},{3,40},{4,80},{5,8},{6,192},{7,184},{8,0},... | collective-permute-start | bytes 589832 | tf_op jit(solution)/shard_map/spread_features/ppermute | solution.py:252
  13.9 4.9 %collective-permute-start.1 = (s32[4,4,4]{2,1,0:T(4,128)S(1)}, s32[4,4,4]{2,1,0:T(4,128)S(1)}, u32[]{:S(2)}, u32[]{:S(2)}) collective-permute-start(s32[4,4,4]{2,1,0:T(4,128)S(1)} %compare_select_fusion.picks), channel_id=1, source_target_pairs={{0,8},{8,0},{1,9},{9,1},{2,10},{10,2},{3,11},{11,3},{4,12},{12,4},... | collective-permute-start | bytes 776 | tf_op jit(solution)/shard_map/spread_tiles/ppermute | solution.py:255
  18.8 1.6 %copy-start = (bf16[4,4,4,128,128]{4,3,2,1,0:T(8,128)(2,1)S(1)}, bf16[4,4,4,128,128]{4,3,2,1,0:T(8,128)(2,1)}, u32[]{:S(2)}) copy-start(bf16[4,4,4,128,128]{4,3,2,1,0:T(8,128)(2,1)} %tiles) | copy-start | bytes 6291460
  20.4 19.4 %copy-start.3 = (bf16[64,768]{1,0:T(8,128)(2,1)S(1)}, bf16[64,768]{1,0:T(8,128)(2,1)}, u32[]{:S(2)}) copy-start(bf16[64,768]{1,0:T(8,128)(2,1)} %cot.1) | copy-start | bytes 294916
  23.8 11.2 %collective-permute-start.4 = (bf16[256,384]{1,0:T(8,128)(2,1)S(1)}, bf16[256,384]{1,0:T(8,128)(2,1)S(1)}, u32[]{:S(2)}, u32[]{:S(2)}) collective-permute-start(bf16[256,384]{1,0:T(8,128)(2,1)S(1)} %collective-permute-done.refs_1_), channel_id=1, source_target_pairs={{0,48},{16,0},{32,16},{48,32},{1,49},{17,1},{33,17},{49,33},{2,50}... | collective-permute-start | bytes 589832 | tf_op jit(solution)/shard_map/spread_features/ppermute | solution.py:226
  32.3 7.5 %collective-permute-start.5 = (bf16[256,384]{1,0:T(8,128)(2,1)S(1)}, bf16[256,384]{1,0:T(8,128)(2,1)S(1)}, u32[]{:S(2)}, u32[]{:S(2)}) collective-permute-start(bf16[256,384]{1,0:T(8,128)(2,1)S(1)} %collective-permute-done.refs_1_), channel_id=1, source_target_pairs={{0,64},{64,128},{128,192},{192,0},{1,65},{65,129},{129,193},{193,1... | collective-permute-start | bytes 589832 | tf_op jit(solution)/shard_map/spread_features/ppermute | solution.py:226
  32.3 8.2 %collective-permute-start.6 = (bf16[256,384]{1,0:T(8,128)(2,1)S(1)}, bf16[256,384]{1,0:T(8,128)(2,1)S(1)}, u32[]{:S(2)}, u32[]{:S(2)}) collective-permute-start(bf16[256,384]{1,0:T(8,128)(2,1)S(1)} %collective-permute-done.refs_1_), channel_id=1, source_target_pairs={{0,192},{64,0},{128,64},{192,128},{1,193},{65,1},{129,65},{193,129... | collective-permute-start | bytes 589832 | tf_op jit(solution)/shard_map/spread_features/ppermute | solution.py:226
  35.0 8.7 %collective-permute-start.8 = (bf16[256,384]{1,0:T(8,128)(2,1)S(1)}, bf16[256,384]{1,0:T(8,128)(2,1)S(1)}, u32[]{:S(2)}, u32[]{:S(2)}) collective-permute-start(bf16[256,384]{1,0:T(8,128)(2,1)S(1)} %collective-permute-done.3.refs_2_), channel_id=1, source_target_pairs={{0,16},{16,32},{32,48},{48,0},{1,17},{17,33},{33,49},{49,1},{2,18}... | collective-permute-start | bytes 589832 | tf_op jit(solution)/shard_map/spread_features/ppermute | solution.py:226
  35.0 9.2 %collective-permute-start.9 = (bf16[256,384]{1,0:T(8,128)(2,1)S(1)}, bf16[256,384]{1,0:T(8,128)(2,1)S(1)}, u32[]{:S(2)}, u32[]{:S(2)}) collective-permute-start(bf16[256,384]{1,0:T(8,128)(2,1)S(1)} %collective-permute-done.3.refs_2_), channel_id=1, source_target_pairs={{0,64},{64,128},{128,192},{192,0},{1,65},{65,129},{129,193},{193,1... | collective-permute-start | bytes 589832 | tf_op jit(solution)/shard_map/spread_features/ppermute | solution.py:226
  35.0 9.6 %collective-permute-start.10 = (bf16[256,384]{1,0:T(8,128)(2,1)S(1)}, bf16[256,384]{1,0:T(8,128)(2,1)S(1)}, u32[]{:S(2)}, u32[]{:S(2)}) collective-permute-start(bf16[256,384]{1,0:T(8,128)(2,1)S(1)} %collective-permute-done.3.refs_2_), channel_id=1, source_target_pairs={{0,192},{64,0},{128,64},{192,128},{1,193},{65,1},{129,65},{193,129... | collective-permute-start | bytes 589832 | tf_op jit(solution)/shard_map/spread_features/ppermute | solution.py:226
  39.9 1.8 %collective-permute-start.7 = (bf16[64,768]{1,0:T(8,128)(2,1)S(1)}, bf16[64,768]{1,0:T(8,128)(2,1)S(1)}, u32[]{:S(2)}, u32[]{:S(2)}) collective-permute-start(bf16[64,768]{1,0:T(8,128)(2,1)S(1)} %copy-done.3), channel_id=1, source_target_pairs={{0,8},{8,0},{1,9},{9,1},{2,10},{10,2},{3,11},{11,3},{4,12},{12,4},... | collective-permute-start | bytes 294920 | tf_op jit(solution)/shard_map/aggregate/ppermute | solution.py:270
  45.1 18.2 %copy-start.4 = (f32[768]{0:T(1024)S(1)}, f32[768]{0:T(1024)}, u32[]{:S(2)}) copy-start(f32[768]{0:T(1024)} %param.12) | copy-start | bytes 9220
  45.1 19.1 %copy-start.1 = (bf16[768,768]{1,0:T(8,128)(2,1)S(1)}, bf16[768,768]{1,0:T(8,128)(2,1)}, u32[]{:S(2)}) copy-start(bf16[768,768]{1,0:T(8,128)(2,1)} %weight.1) | copy-start | bytes 3538948
  61.3 3.0 %collective-permute-start.11 = (bf16[2,64,384]{2,1,0:T(8,128)(2,1)S(1)}, bf16[2,64,384]{2,1,0:T(8,128)(2,1)S(1)}, u32[]{:S(2)}, u32[]{:S(2)}) collective-permute-start(bf16[2,64,384]{2,1,0:T(8,128)(2,1)S(1)} %sum_over_rep.1.mine), channel_id=1, source_target_pairs={{0,8},{8,0},{1,9},{9,1},{2,10},{10,2},{3,11},{11,3},{4,12},{12,4},... | collective-permute-start | bytes 294920 | tf_op jit(solution)/shard_map/sum_over_rep/ppermute | solution.py:278
  81.9 3.0 %collective-permute-start.12 = (bf16[56,384]{1,0:T(8,128)(2,1)S(1)}, bf16[56,384]{1,0:T(8,128)(2,1)S(1)}, u32[]{:S(2)}, u32[]{:S(2)}) collective-permute-start(bf16[56,384]{1,0:T(8,128)(2,1)S(1)} %sum_over_plane.1.one), channel_id=1, source_target_pairs={{0,1},{1,0},{2,3},{3,2},{4,5},{5,4},{6,7},{7,6},{8,9},{9,8},{10,11... | collective-permute-start | bytes 129032 | tf_op jit(solution)/shard_map/sum_over_z/ppermute | solution.py:290
  84.9 7.0 %collective-permute-start.13 = (bf16[56,384]{1,0:T(8,128)(2,1)S(1)}, bf16[56,384]{1,0:T(8,128)(2,1)S(1)}, u32[]{:S(2)}, u32[]{:S(2)}) collective-permute-start(bf16[56,384]{1,0:T(8,128)(2,1)S(1)} %sum_over_z.2.refs_0_), channel_id=1, source_target_pairs={{0,32},{16,48},{32,0},{48,16},{1,33},{17,49},{33,1},{49,17},{2,34}... | collective-permute-start | bytes 129032 | tf_op jit(solution)/shard_map/sum_over_z/ppermute | solution.py:292
  88.3 5.0 %collective-permute-start.14 = (bf16[56,384]{1,0:T(8,128)(2,1)S(1)}, bf16[56,384]{1,0:T(8,128)(2,1)S(1)}, u32[]{:S(2)}, u32[]{:S(2)}) collective-permute-start(bf16[56,384]{1,0:T(8,128)(2,1)S(1)} %sum_over_z.2.refs_0_), channel_id=1, source_target_pairs={{0,16},{16,32},{32,48},{48,0},{1,17},{17,33},{33,49},{49,1},{2,18}... | collective-permute-start | bytes 129032 | tf_op jit(solution)/shard_map/sum_over_z/ppermute | solution.py:292
  88.3 5.8 %collective-permute-start.15 = (bf16[56,384]{1,0:T(8,128)(2,1)S(1)}, bf16[56,384]{1,0:T(8,128)(2,1)S(1)}, u32[]{:S(2)}, u32[]{:S(2)}) collective-permute-start(bf16[56,384]{1,0:T(8,128)(2,1)S(1)} %sum_over_z.2.refs_0_), channel_id=1, source_target_pairs={{0,48},{16,0},{32,16},{48,32},{1,49},{17,1},{33,17},{49,33},{2,50}... | collective-permute-start | bytes 129032 | tf_op jit(solution)/shard_map/sum_over_z/ppermute | solution.py:292
  107.0 7.0 %collective-permute-start.16 = (bf16[896,384]{1,0:T(8,128)(2,1)S(1)}, bf16[896,384]{1,0:T(8,128)(2,1)S(1)}, u32[]{:S(2)}, u32[]{:S(2)}) collective-permute-start(bf16[896,384]{1,0:T(8,128)(2,1)S(1)} %bitcast.2), channel_id=1, source_target_pairs={{0,8},{8,0},{1,9},{9,1},{2,10},{10,2},{3,11},{11,3},{4,12},{12,4},... | collective-permute-start | bytes 2064392 | tf_op jit(solution)/shard_map/gather_plane/ppermute | solution.py:298

commit v12 on v11

--- a/solution.py
+++ b/solution.py
@@ -14,6 +14,7 @@
 BF = jnp.bfloat16
 F32 = jnp.float32
 BACK = (2, 1, 3)
+NEAR = (1, 3, 2)
 VMEM_LIMIT = 32 * 1024 * 1024
 
 TURN = (((1, 0), (3, 2), (1, 0), (3, 2)), ((2, 0), (0, 2), (2, 0), (0, 2)))
@@ -222,8 +223,11 @@
         copy.wait()
 
 
-def neighbours(piece, step):
-    return [lax.ppermute(piece, "zh", shift(4, step))] + [lax.ppermute(piece, "y", shift(4, k)) for k in BACK[1:]]
+def neighbours(piece, order, step):
+    return [
+        lax.ppermute(piece, "zh", shift(4, step)) if back == 2 else lax.ppermute(piece, "y", shift(4, back))
+        for back in order
+    ]
 
 
 def product(kernel, keys, mix, parts, begun=None):
@@ -261,12 +265,12 @@
         )(picks, there[0], tiles, there[1])
     own[0], mix = lax.optimization_barrier((own[0], mix))
     with jax.named_scope("spread_features"):
-        early = neighbours(own[0], 3)
+        early = neighbours(own[0], NEAR, 3)
     with jax.named_scope("spread_features"):
-        late = neighbours(own[1], 1)
+        late = neighbours(own[1], BACK, 1)
     with jax.named_scope("aggregate"):
         begun = product(first_kernel, [(0, 0), (0, 1)], mix, own)
-        begun = product(next_kernel, [(back, 0) for back in BACK], mix, early, begun)
+        begun = product(next_kernel, [(back, 0) for back in NEAR], mix, early, begun)
         other_cot = lax.ppermute(cotangent, "core", shift(2, 1))
         begun, other_cot = lax.optimization_barrier((begun, other_cot))
         begun = product(next_kernel, [(BACK[0], 1)], mix, late[:1], begun)

time: 116 us -> 114 us (0.983)
    ppermute x2, waiting for transfers between devices: 2.07 us -> 4.21 us  [neighbours(): lax.ppermute(piece, 'zh', shift(4, step))]
    ppermute x4, waiting for transfers between devices: 2.15 us -> 0.01 us  [neighbours(): lax.ppermute(piece, 'y', shift(4, back))]
  transfers between devices with their start and end apart: 17 -> 17, of which waited for: 8 -> 9; matrix products, arithmetic and copies ran while one was open for 1% -> 1% of each run, Pallas kernels for 6% -> 6%
where the time goes in v12:
time: 114 us
  blocking collectives  45.2 us (40%)
  starting transfers between devices  43.5 us (38%)
  waiting for transfers between devices  10.9 us (10%)
  Pallas kernels  10 us (9%)
  local copies, waits for them, and re-layouts  2.74 us (2%)
    all_to_all x1, blocking collectives, on_device(): recv = lax.all_to_all(partial, REP, 0, 0, tiled=True)  16.1 us
    all_to_all x1, blocking collectives, on_device(): recv = lax.all_to_all(packed.reshape(896, 384), PLANE, 0, 0, tiled=True)  15.6 us
    all_to_all x1, blocking collectives, on_device(): mine = lax.all_to_all(whole.reshape(896, 384), PLANE, 0, 0, tiled=True)  13.4 us
    ppermute x2, starting transfers between devices, neighbours(): lax.ppermute(piece, 'zh', shift(4, step))  8.46 us
    ppermute x2, starting transfers between devices, on_device(): own = [lax.ppermute(half, AXES, first_hop()) for half in halves]  8.01 us
    ppermute x2, starting transfers between devices, on_device(): lax.ppermute(value, 'core', shift(2, 1))  7.45 us
    ppermute x3, starting transfers between devices, on_device(): chain = [lax.ppermute(part, 'zh', shift(4, back)) for back in BACK]  6.74 us
    ppermute x4, starting transfers between devices, neighbours(): lax.ppermute(piece, 'y', shift(4, back))  5.41 us
  transfers between devices with their start and end apart: 17, of which 9 were waited for; matrix products, arithmetic and copies ran while one was open for 1% of the time, Pallas kernels for 6%

profile of v12, /device:TPU:1, one launch (start us, length us, event | category | flops | bytes accessed | tf_op | source)
XLA Modules:
  0.0 113.9 jit_solution(15668497488922508126)
XLA Ops:
  0.6 1.1 copy-done.2
  1.8 3.3 %collective-permute-start.2 = (bf16[4,4,4,128,128]{4,3,2,1,0:T(8,128)(2,1)}, bf16[4,4,4,128,128]{4,3,2,1,0:T(8,128)(2,1)S(1)}, u32[]{:S(2)}, u32[]{:S(2)}) collective-permute-start(bf16[4,4,4,128,128]{4,3,2,1,0:T(8,128)(2,1)} %tiles), channel_id=1, source_target_pairs={{0,8},{8,0},{1,9},{9,1},{2,10},{10,2},{3,11},{11,3},{4,12},{12,4},... | collective-permute-start | bytes 6291464 | tf_op jit(solution)/shard_map/spread_tiles/ppermute | solution.py:259
  5.3 7.9 %collective-permute-start.3 = (bf16[256,384]{1,0:T(8,128)(2,1)S(1)}, bf16[256,384]{1,0:T(8,128)(2,1)S(1)}, u32[]{:S(2)}, u32[]{:S(2)}) collective-permute-start(bf16[256,384]{1,0:T(8,128)(2,1)S(1)} %get-tuple-element.26), channel_id=1, source_target_pairs={{0,224},{1,152},{2,112},{3,40},{4,80},{5,8},{6,192},{7,184},{8,0},... | collective-permute-start | bytes 589832 | tf_op jit(solution)/shard_map/spread_features/ppermute | solution.py:256
  13.2 0.7 compare_select_fusion.picks
  13.9 4.1 %collective-permute-start.1 = (s32[4,4,4]{2,1,0:T(4,128)S(1)}, s32[4,4,4]{2,1,0:T(4,128)S(1)}, u32[]{:S(2)}, u32[]{:S(2)}) collective-permute-start(s32[4,4,4]{2,1,0:T(4,128)S(1)} %compare_select_fusion.picks), channel_id=1, source_target_pairs={{0,8},{8,0},{1,9},{9,1},{2,10},{10,2},{3,11},{11,3},{4,12},{12,4},... | collective-permute-start | bytes 776 | tf_op jit(solution)/shard_map/spread_tiles/ppermute | solution.py:259
  18.0 0.8 collective-permute-done.1.other_picks
  18.8 1.6 %copy-done = bf16[4,4,4,128,128]{4,3,2,1,0:T(8,128)(2,1)S(1)} copy-done((bf16[4,4,4,128,128]{4,3,2,1,0:T(8,128)(2,1)S(1)}, bf16[4,4,4,128,128]{4,3,2,1,0:T(8,128)(2,1)}, u32[]{:S(2)}) %copy-start) | copy-done | bytes 2097176
  20.4 3.4 %spread_tiles.1.refs_0_ = bf16[2,4,512,512]{3,2,1,0:T(8,128)(2,1)S(1)} custom-call(s32[4,4,4]{2,1,0:T(4,128)S(1)} %compare_select_fusion.picks, s32[4,4,4]{2,1,0:T(4,128)S(1)} %collective-permute-done.1.other_picks, bf16[4,4,4,128,128]{4,3,2,1,0:T(8,128)(2,1)S(1)} %copy-done, bf16[4,4,4,128,128]{4,3,2,1,0:T(8,128)(2,1)S(1)} %collective-permute-done.2.other_tiles), custom_call_target="tpu_custom_call" | custom-call | bytes 1048576 | tf_op jit(solution)/shard_map/spread_tiles/pallas_call | solution.py:260
  23.9 2.7 %collective-permute-start.5 = (bf16[256,384]{1,0:T(8,128)(2,1)S(1)}, bf16[256,384]{1,0:T(8,128)(2,1)S(1)}, u32[]{:S(2)}, u32[]{:S(2)}) collective-permute-start(bf16[256,384]{1,0:T(8,128)(2,1)S(1)} %collective-permute-done.refs_1_), channel_id=1, source_target_pairs={{0,192},{64,0},{128,64},{192,128},{1,193},{65,1},{129,65},{193,129... | collective-permute-start | bytes 589832 | tf_op jit(solution)/shard_map/spread_features/ppermute | solution.py:228
  26.6 8.5 %collective-permute-start.6 = (bf16[256,384]{1,0:T(8,128)(2,1)S(1)}, bf16[256,384]{1,0:T(8,128)(2,1)S(1)}, u32[]{:S(2)}, u32[]{:S(2)}) collective-permute-start(bf16[256,384]{1,0:T(8,128)(2,1)S(1)} %collective-permute-done.refs_1_), channel_id=1, source_target_pairs={{0,48},{16,0},{32,16},{48,32},{1,49},{17,1},{33,17},{49,33},{2,50}... | collective-permute-start | bytes 589832 | tf_op jit(solution)/shard_map/spread_features/ppermute | solution.py:228
  35.0 2.7 %collective-permute-start.10 = (bf16[256,384]{1,0:T(8,128)(2,1)S(1)}, bf16[256,384]{1,0:T(8,128)(2,1)S(1)}, u32[]{:S(2)}, u32[]{:S(2)}) collective-permute-start(bf16[256,384]{1,0:T(8,128)(2,1)S(1)} %collective-permute-done.3.refs_2_), channel_id=1, source_target_pairs={{0,192},{64,0},{128,64},{192,128},{1,193},{65,1},{129,65},{193,129... | collective-permute-start | bytes 589832 | tf_op jit(solution)/shard_map/spread_features/ppermute | solution.py:228
  37.7 0.7 aggregate.5.refs_1_
  38.4 1.2 %collective-permute-done.6.refs_4_ = bf16[256,384]{1,0:T(8,128)(2,1)S(1)} collective-permute-done((bf16[256,384]{1,0:T(8,128)(2,1)S(1)}, bf16[256,384]{1,0:T(8,128)(2,1)S(1)}, u32[]{:S(2)}, u32[]{:S(2)}) %collective-permute-start.6) | collective-permute-done | bytes 196640 | tf_op jit(solution)/shard_map/spread_features/ppermute | solution.py:228
  39.6 1.1 aggregate.6.refs_1_
  40.7 3.0 %collective-permute-done.8.refs_2_ = bf16[256,384]{1,0:T(8,128)(2,1)S(1)} collective-permute-done((bf16[256,384]{1,0:T(8,128)(2,1)S(1)}, bf16[256,384]{1,0:T(8,128)(2,1)S(1)}, u32[]{:S(2)}, u32[]{:S(2)}) %collective-permute-start.8) | collective-permute-done | bytes 196640 | tf_op jit(solution)/shard_map/spread_features/ppermute | solution.py:228
  43.7 0.4 aggregate.7.refs_1_
  44.2 0.4 aggregate.8.refs_1_
  45.1 16.1 %all_to_all.20.recv = bf16[8,2,64,384]{3,2,1,0:T(8,128)(2,1)S(1)} all-to-all(bf16[8,2,64,384]{3,2,1,0:T(8,128)(2,1)S(1)} %aggregate.9), channel_id=1, replica_groups=mesh['y'=4,'zh'=4,'core'=2,'x'=4,'zl'=2] {'x','zl'}, dimensions={0} | all-to-all | bytes 1572864 | tf_op jit(solution)/shard_map/sum_over_rep/all_to_all | solution.py:280
  61.4 1.9 %collective-permute-start.11 = (bf16[2,64,384]{2,1,0:T(8,128)(2,1)S(1)}, bf16[2,64,384]{2,1,0:T(8,128)(2,1)S(1)}, u32[]{:S(2)}, u32[]{:S(2)}) collective-permute-start(bf16[2,64,384]{2,1,0:T(8,128)(2,1)S(1)} %sum_over_rep.1.mine), channel_id=1, source_target_pairs={{0,8},{8,0},{1,9},{9,1},{2,10},{10,2},{3,11},{11,3},{4,12},{12,4},... | collective-permute-start | bytes 294920 | tf_op jit(solution)/shard_map/sum_over_rep/ppermute | solution.py:282
  63.3 0.9 collective-permute-done.11.other
  64.3 1.1 layer.1
  65.3 15.6 %all_to_all.21.recv = bf16[16,56,384]{2,1,0:T(8,128)(2,1)S(1)} all-to-all(bf16[16,56,384]{2,1,0:T(8,128)(2,1)S(1)} %get-tuple-element.30), channel_id=1, replica_groups=mesh['y'=4,'zh'=4,'core'=2,'x'=4,'zl'=2] {'x','y'}, dimensions={0} | all-to-all | bytes 1376256 | tf_op jit(solution)/shard_map/sum_over_plane/all_to_all | solution.py:291
  81.0 0.7 collective-permute-start.12
  81.7 2.3 %collective-permute-done.12.two = bf16[56,384]{1,0:T(8,128)(2,1)S(1)} collective-permute-done((bf16[56,384]{1,0:T(8,128)(2,1)S(1)}, bf16[56,384]{1,0:T(8,128)(2,1)S(1)}, u32[]{:S(2)}, u32[]{:S(2)}) %collective-permute-start.12) | collective-permute-done | bytes 43040 | tf_op jit(solution)/shard_map/sum_over_z/ppermute | solution.py:294
  84.0 3.2 %collective-permute-start.13 = (bf16[56,384]{1,0:T(8,128)(2,1)S(1)}, bf16[56,384]{1,0:T(8,128)(2,1)S(1)}, u32[]{:S(2)}, u32[]{:S(2)}) collective-permute-start(bf16[56,384]{1,0:T(8,128)(2,1)S(1)} %sum_over_z.2.refs_0_), channel_id=1, source_target_pairs={{0,32},{16,48},{32,0},{48,16},{1,33},{17,49},{33,1},{49,17},{2,34}... | collective-permute-start | bytes 129032 | tf_op jit(solution)/shard_map/sum_over_z/ppermute | solution.py:296
  87.2 3.6 %collective-permute-start.15 = (bf16[56,384]{1,0:T(8,128)(2,1)S(1)}, bf16[56,384]{1,0:T(8,128)(2,1)S(1)}, u32[]{:S(2)}, u32[]{:S(2)}) collective-permute-start(bf16[56,384]{1,0:T(8,128)(2,1)S(1)} %sum_over_z.2.refs_0_), channel_id=1, source_target_pairs={{0,48},{16,0},{32,16},{48,32},{1,49},{17,1},{33,17},{49,33},{2,50}... | collective-permute-start | bytes 129032 | tf_op jit(solution)/shard_map/sum_over_z/ppermute | solution.py:296
  90.9 1.6 %collective-permute-done.14.refs_2_ = bf16[56,384]{1,0:T(8,128)(2,1)S(1)} collective-permute-done((bf16[56,384]{1,0:T(8,128)(2,1)S(1)}, bf16[56,384]{1,0:T(8,128)(2,1)S(1)}, u32[]{:S(2)}, u32[]{:S(2)}) %collective-permute-start.14) | collective-permute-done | bytes 43040 | tf_op jit(solution)/shard_map/sum_over_z/ppermute | solution.py:296
  92.7 13.4 %all_to_all.22.own = bf16[16,56,384]{2,1,0:T(8,128)(2,1)S(1)} all-to-all(bf16[16,56,384]{2,1,0:T(8,128)(2,1)S(1)} %sum_over_z.3), channel_id=1, replica_groups=mesh['y'=4,'zh'=4,'core'=2,'x'=4,'zl'=2] {'x','y'}, dimensions={0} | all-to-all | bytes 1376256 | tf_op jit(solution)/shard_map/gather_plane/all_to_all | solution.py:301
  106.1 4.8 %collective-permute-start.16 = (bf16[896,384]{1,0:T(8,128)(2,1)S(1)}, bf16[896,384]{1,0:T(8,128)(2,1)S(1)}, u32[]{:S(2)}, u32[]{:S(2)}) collective-permute-start(bf16[896,384]{1,0:T(8,128)(2,1)S(1)} %bitcast.2), channel_id=1, source_target_pairs={{0,8},{8,0},{1,9},{9,1},{2,10},{10,2},{3,11},{11,3},{4,12},{12,4},... | collective-permute-start | bytes 2064392 | tf_op jit(solution)/shard_map/gather_plane/ppermute | solution.py:302
  110.9 1.1 finish.2.begun
  112.0 0.7 collective-permute-done.16
  112.7 1.1 finish.3
  (31 shorter events, 1.3 us)
Async XLA Ops:
  0.6 1.1 copy-start.2
  1.8 17.0 %collective-permute-start.2 = (bf16[4,4,4,128,128]{4,3,2,1,0:T(8,128)(2,1)}, bf16[4,4,4,128,128]{4,3,2,1,0:T(8,128)(2,1)S(1)}, u32[]{:S(2)}, u32[]{:S(2)}) collective-permute-start(bf16[4,4,4,128,128]{4,3,2,1,0:T(8,128)(2,1)} %tiles), channel_id=1, source_target_pairs={{0,8},{8,0},{1,9},{9,1},{2,10},{10,2},{3,11},{11,3},{4,12},{12,4},... | collective-permute-start | bytes 6291464 | tf_op jit(solution)/shard_map/spread_tiles/ppermute | solution.py:259
  5.2 18.6 %collective-permute-start = (bf16[256,384]{1,0:T(8,128)(2,1)S(1)}, bf16[256,384]{1,0:T(8,128)(2,1)S(1)}, u32[]{:S(2)}, u32[]{:S(2)}) collective-permute-start(bf16[256,384]{1,0:T(8,128)(2,1)S(1)} %get-tuple-element.20), channel_id=1, source_target_pairs={{0,224},{1,152},{2,112},{3,40},{4,80},{5,8},{6,192},{7,184},{8,0},... | collective-permute-start | bytes 589832 | tf_op jit(solution)/shard_map/spread_features/ppermute | solution.py:256
  5.3 29.8 %collective-permute-start.3 = (bf16[256,384]{1,0:T(8,128)(2,1)S(1)}, bf16[256,384]{1,0:T(8,128)(2,1)S(1)}, u32[]{:S(2)}, u32[]{:S(2)}) collective-permute-start(bf16[256,384]{1,0:T(8,128)(2,1)S(1)} %get-tuple-element.26), channel_id=1, source_target_pairs={{0,224},{1,152},{2,112},{3,40},{4,80},{5,8},{6,192},{7,184},{8,0},... | collective-permute-start | bytes 589832 | tf_op jit(solution)/shard_map/spread_features/ppermute | solution.py:256
  13.9 4.9 %collective-permute-start.1 = (s32[4,4,4]{2,1,0:T(4,128)S(1)}, s32[4,4,4]{2,1,0:T(4,128)S(1)}, u32[]{:S(2)}, u32[]{:S(2)}) collective-permute-start(s32[4,4,4]{2,1,0:T(4,128)S(1)} %compare_select_fusion.picks), channel_id=1, source_target_pairs={{0,8},{8,0},{1,9},{9,1},{2,10},{10,2},{3,11},{11,3},{4,12},{12,4},... | collective-permute-start | bytes 776 | tf_op jit(solution)/shard_map/spread_tiles/ppermute | solution.py:259
  18.8 1.6 %copy-start = (bf16[4,4,4,128,128]{4,3,2,1,0:T(8,128)(2,1)S(1)}, bf16[4,4,4,128,128]{4,3,2,1,0:T(8,128)(2,1)}, u32[]{:S(2)}) copy-start(bf16[4,4,4,128,128]{4,3,2,1,0:T(8,128)(2,1)} %tiles) | copy-start | bytes 6291460
  20.4 17.3 %copy-start.3 = (bf16[64,768]{1,0:T(8,128)(2,1)S(1)}, bf16[64,768]{1,0:T(8,128)(2,1)}, u32[]{:S(2)}) copy-start(bf16[64,768]{1,0:T(8,128)(2,1)} %cot.1) | copy-start | bytes 294916
  23.8 11.2 %collective-permute-start.4 = (bf16[256,384]{1,0:T(8,128)(2,1)S(1)}, bf16[256,384]{1,0:T(8,128)(2,1)S(1)}, u32[]{:S(2)}, u32[]{:S(2)}) collective-permute-start(bf16[256,384]{1,0:T(8,128)(2,1)S(1)} %collective-permute-done.refs_1_), channel_id=1, source_target_pairs={{0,64},{64,128},{128,192},{192,0},{1,65},{65,129},{129,193},{193,1... | collective-permute-start | bytes 589832 | tf_op jit(solution)/shard_map/spread_features/ppermute | solution.py:228
  23.9 13.8 %collective-permute-start.5 = (bf16[256,384]{1,0:T(8,128)(2,1)S(1)}, bf16[256,384]{1,0:T(8,128)(2,1)S(1)}, u32[]{:S(2)}, u32[]{:S(2)}) collective-permute-start(bf16[256,384]{1,0:T(8,128)(2,1)S(1)} %collective-permute-done.refs_1_), channel_id=1, source_target_pairs={{0,192},{64,0},{128,64},{192,128},{1,193},{65,1},{129,65},{193,129... | collective-permute-start | bytes 589832 | tf_op jit(solution)/shard_map/spread_features/ppermute | solution.py:228
  26.6 13.1 %collective-permute-start.6 = (bf16[256,384]{1,0:T(8,128)(2,1)S(1)}, bf16[256,384]{1,0:T(8,128)(2,1)S(1)}, u32[]{:S(2)}, u32[]{:S(2)}) collective-permute-start(bf16[256,384]{1,0:T(8,128)(2,1)S(1)} %collective-permute-done.refs_1_), channel_id=1, source_target_pairs={{0,48},{16,0},{32,16},{48,32},{1,49},{17,1},{33,17},{49,33},{2,50}... | collective-permute-start | bytes 589832 | tf_op jit(solution)/shard_map/spread_features/ppermute | solution.py:228
  35.0 8.7 %collective-permute-start.8 = (bf16[256,384]{1,0:T(8,128)(2,1)S(1)}, bf16[256,384]{1,0:T(8,128)(2,1)S(1)}, u32[]{:S(2)}, u32[]{:S(2)}) collective-permute-start(bf16[256,384]{1,0:T(8,128)(2,1)S(1)} %collective-permute-done.3.refs_2_), channel_id=1, source_target_pairs={{0,16},{16,32},{32,48},{48,0},{1,17},{17,33},{33,49},{49,1},{2,18}... | collective-permute-start | bytes 589832 | tf_op jit(solution)/shard_map/spread_features/ppermute | solution.py:228
  35.0 9.2 %collective-permute-start.9 = (bf16[256,384]{1,0:T(8,128)(2,1)S(1)}, bf16[256,384]{1,0:T(8,128)(2,1)S(1)}, u32[]{:S(2)}, u32[]{:S(2)}) collective-permute-start(bf16[256,384]{1,0:T(8,128)(2,1)S(1)} %collective-permute-done.3.refs_2_), channel_id=1, source_target_pairs={{0,64},{64,128},{128,192},{192,0},{1,65},{65,129},{129,193},{193,1... | collective-permute-start | bytes 589832 | tf_op jit(solution)/shard_map/spread_features/ppermute | solution.py:228
  35.0 9.6 %collective-permute-start.10 = (bf16[256,384]{1,0:T(8,128)(2,1)S(1)}, bf16[256,384]{1,0:T(8,128)(2,1)S(1)}, u32[]{:S(2)}, u32[]{:S(2)}) collective-permute-start(bf16[256,384]{1,0:T(8,128)(2,1)S(1)} %collective-permute-done.3.refs_2_), channel_id=1, source_target_pairs={{0,192},{64,0},{128,64},{192,128},{1,193},{65,1},{129,65},{193,129... | collective-permute-start | bytes 589832 | tf_op jit(solution)/shard_map/spread_features/ppermute | solution.py:228
  37.7 3.0 %collective-permute-start.7 = (bf16[64,768]{1,0:T(8,128)(2,1)S(1)}, bf16[64,768]{1,0:T(8,128)(2,1)S(1)}, u32[]{:S(2)}, u32[]{:S(2)}) collective-permute-start(bf16[64,768]{1,0:T(8,128)(2,1)S(1)} %copy-done.3), channel_id=1, source_target_pairs={{0,8},{8,0},{1,9},{9,1},{2,10},{10,2},{3,11},{11,3},{4,12},{12,4},... | collective-permute-start | bytes 294920 | tf_op jit(solution)/shard_map/aggregate/ppermute | solution.py:274
  45.1 18.2 %copy-start.4 = (f32[768]{0:T(1024)S(1)}, f32[768]{0:T(1024)}, u32[]{:S(2)}) copy-start(f32[768]{0:T(1024)} %param.12) | copy-start | bytes 9220
  45.1 19.1 %copy-start.1 = (bf16[768,768]{1,0:T(8,128)(2,1)S(1)}, bf16[768,768]{1,0:T(8,128)(2,1)}, u32[]{:S(2)}) copy-start(bf16[768,768]{1,0:T(8,128)(2,1)} %weight.1) | copy-start | bytes 3538948
  61.4 2.9 %collective-permute-start.11 = (bf16[2,64,384]{2,1,0:T(8,128)(2,1)S(1)}, bf16[2,64,384]{2,1,0:T(8,128)(2,1)S(1)}, u32[]{:S(2)}, u32[]{:S(2)}) collective-permute-start(bf16[2,64,384]{2,1,0:T(8,128)(2,1)S(1)} %sum_over_rep.1.mine), channel_id=1, source_target_pairs={{0,8},{8,0},{1,9},{9,1},{2,10},{10,2},{3,11},{11,3},{4,12},{12,4},... | collective-permute-start | bytes 294920 | tf_op jit(solution)/shard_map/sum_over_rep/ppermute | solution.py:282
  81.0 3.0 %collective-permute-start.12 = (bf16[56,384]{1,0:T(8,128)(2,1)S(1)}, bf16[56,384]{1,0:T(8,128)(2,1)S(1)}, u32[]{:S(2)}, u32[]{:S(2)}) collective-permute-start(bf16[56,384]{1,0:T(8,128)(2,1)S(1)} %sum_over_plane.1.one), channel_id=1, source_target_pairs={{0,1},{1,0},{2,3},{3,2},{4,5},{5,4},{6,7},{7,6},{8,9},{9,8},{10,11... | collective-permute-start | bytes 129032 | tf_op jit(solution)/shard_map/sum_over_z/ppermute | solution.py:294
  84.0 6.9 %collective-permute-start.13 = (bf16[56,384]{1,0:T(8,128)(2,1)S(1)}, bf16[56,384]{1,0:T(8,128)(2,1)S(1)}, u32[]{:S(2)}, u32[]{:S(2)}) collective-permute-start(bf16[56,384]{1,0:T(8,128)(2,1)S(1)} %sum_over_z.2.refs_0_), channel_id=1, source_target_pairs={{0,32},{16,48},{32,0},{48,16},{1,33},{17,49},{33,1},{49,17},{2,34}... | collective-permute-start | bytes 129032 | tf_op jit(solution)/shard_map/sum_over_z/ppermute | solution.py:296
  87.2 5.3 %collective-permute-start.14 = (bf16[56,384]{1,0:T(8,128)(2,1)S(1)}, bf16[56,384]{1,0:T(8,128)(2,1)S(1)}, u32[]{:S(2)}, u32[]{:S(2)}) collective-permute-start(bf16[56,384]{1,0:T(8,128)(2,1)S(1)} %sum_over_z.2.refs_0_), channel_id=1, source_target_pairs={{0,16},{16,32},{32,48},{48,0},{1,17},{17,33},{33,49},{49,1},{2,18}... | collective-permute-start | bytes 129032 | tf_op jit(solution)/shard_map/sum_over_z/ppermute | solution.py:296
  87.2 5.4 %collective-permute-start.15 = (bf16[56,384]{1,0:T(8,128)(2,1)S(1)}, bf16[56,384]{1,0:T(8,128)(2,1)S(1)}, u32[]{:S(2)}, u32[]{:S(2)}) collective-permute-start(bf16[56,384]{1,0:T(8,128)(2,1)S(1)} %sum_over_z.2.refs_0_), channel_id=1, source_target_pairs={{0,48},{16,0},{32,16},{48,32},{1,49},{17,1},{33,17},{49,33},{2,50}... | collective-permute-start | bytes 129032 | tf_op jit(solution)/shard_map/sum_over_z/ppermute | solution.py:296
  106.1 6.6 %collective-permute-start.16 = (bf16[896,384]{1,0:T(8,128)(2,1)S(1)}, bf16[896,384]{1,0:T(8,128)(2,1)S(1)}, u32[]{:S(2)}, u32[]{:S(2)}) collective-permute-start(bf16[896,384]{1,0:T(8,128)(2,1)S(1)} %bitcast.2), channel_id=1, source_target_pairs={{0,8},{8,0},{1,9},{9,1},{2,10},{10,2},{3,11},{11,3},{4,12},{12,4},... | collective-permute-start | bytes 2064392 | tf_op jit(solution)/shard_map/gather_plane/ppermute | solution.py:302

commit v13 on v12

--- a/solution.py
+++ b/solution.py
@@ -183,8 +183,8 @@
     out[...] = resplit(one[...].astype(F32) + two[...].astype(F32))
 
 
-def four_kernel(copies, one, two, three, four, out):
-    total = (one[...].astype(F32) + two[...].astype(F32)) + (three[...].astype(F32) + four[...].astype(F32))
+def four_kernel(copies, own, back, ahead, across, out):
+    total = (own[...].astype(F32) + across[...].astype(F32)) + (back[...].astype(F32) + ahead[...].astype(F32))
     value = resplit(total)
     for i in range(copies):
         out[i] = value
@@ -274,8 +274,7 @@
         other_cot = lax.ppermute(cotangent, "core", shift(2, 1))
         begun, other_cot = lax.optimization_barrier((begun, other_cot))
         begun = product(next_kernel, [(BACK[0], 1)], mix, late[:1], begun)
-        begun = product(next_kernel, [(BACK[1], 1)], mix, late[1:2], begun)
-        partial = product(last_kernel, [(BACK[2], 1)], mix, late[2:], begun)
+        partial = product(last_kernel, [(back, 1) for back in BACK[1:]], mix, late[1:], begun)
     with jax.named_scope("sum_over_rep"):
         recv = lax.all_to_all(partial, REP, 0, 0, tiled=True)
         mixed = call(rows_kernel, struct((2, 64, 384), BF), [vmem()], vmem())(recv)
@@ -293,7 +292,7 @@
     with jax.named_scope("sum_over_z"):
         beside = lax.ppermute(part, "zl", shift(2, 1))
         part = call(pair_kernel, struct((56, 384), BF), [vmem()] * 2, vmem())(part, beside)
-        chain = [lax.ppermute(part, "zh", shift(4, back)) for back in BACK]
+        chain = [lax.ppermute(part, "zh", shift(4, back)) for back in NEAR]
         whole = call(
             lambda *refs: four_kernel(16, *refs), struct((16, 56, 384), BF), [vmem()] * 4, vmem()
         )(part, *chain)

time: 114 us -> 117 us (1.026)
  waiting for transfers between devices: 10.9 us -> 14.6 us
    ppermute x3, waiting for transfers between devices: 1.84 us -> 4.35 us  [on_device(): chain = [lax.ppermute(part, 'zh', shift(4, back)) for back in NEAR]]
    ppermute x2, waiting for transfers between devices: 4.21 us -> 5.42 us  [neighbours(): lax.ppermute(piece, 'zh', shift(4, step))]
    ppermute x4, starting transfers between devices: 5.41 us -> 4.2 us  [neighbours(): lax.ppermute(piece, 'y', shift(4, back))]
    pallas_call x5 -> x4, Pallas kernels: 3.11 us -> 2.94 us  [product(): call(lambda *refs: kernel(keys, *refs), struct((8, 2, 64, 384), BF) if la...]
  transfers between devices with their start and end apart: 17 -> 17, of which waited for: 9 -> 7; matrix products, arithmetic and copies ran while one was open for 1% -> 1% of each run, Pallas kernels for 6% -> 6%
where the time goes in v13:
time: 117 us
  blocking collectives  44.9 us (38%)
  starting transfers between devices  42.8 us (37%)
  waiting for transfers between devices  14.6 us (12%)
  Pallas kernels  9.84 us (8%)
  local copies, waits for them, and re-layouts  2.74 us (2%)
    all_to_all x1, blocking collectives, on_device(): recv = lax.all_to_all(partial, REP, 0, 0, tiled=True)  16.1 us
    all_to_all x1, blocking collectives, on_device(): recv = lax.all_to_all(packed.reshape(896, 384), PLANE, 0, 0, tiled=True)  15.6 us
    all_to_all x1, blocking collectives, on_device(): mine = lax.all_to_all(whole.reshape(896, 384), PLANE, 0, 0, tiled=True)  13.2 us
    ppermute x2, starting transfers between devices, neighbours(): lax.ppermute(piece, 'zh', shift(4, step))  8.46 us
    ppermute x2, starting transfers between devices, on_device(): own = [lax.ppermute(half, AXES, first_hop()) for half in halves]  8.01 us
    ppermute x2, starting transfers between devices, on_device(): lax.ppermute(value, 'core', shift(2, 1))  7.45 us
    ppermute x3, starting transfers between devices, on_device(): chain = [lax.ppermute(part, 'zh', shift(4, back)) for back in NEAR]  6.72 us
    ppermute x2, waiting for transfers between devices, neighbours(): lax.ppermute(piece, 'zh', shift(4, step))  5.42 us
  transfers between devices with their start and end apart: 17, of which 7 were waited for; matrix products, arithmetic and copies ran while one was open for 1% of the time, Pallas kernels for 6%

profile of v13, /device:TPU:1, one launch (start us, length us, event | category | flops | bytes accessed | tf_op | source)
XLA Modules:
  0.0 116.5 jit_solution(5437661152721944339)
XLA Ops:
  0.6 1.1 copy-done.2
  1.8 3.3 %collective-permute-start.2 = (bf16[4,4,4,128,128]{4,3,2,1,0:T(8,128)(2,1)}, bf16[4,4,4,128,128]{4,3,2,1,0:T(8,128)(2,1)S(1)}, u32[]{:S(2)}, u32[]{:S(2)}) collective-permute-start(bf16[4,4,4,128,128]{4,3,2,1,0:T(8,128)(2,1)} %tiles), channel_id=1, source_target_pairs={{0,8},{8,0},{1,9},{9,1},{2,10},{10,2},{3,11},{11,3},{4,12},{12,4},... | collective-permute-start | bytes 6291464 | tf_op jit(solution)/shard_map/spread_tiles/ppermute | solution.py:259
  5.3 7.9 %collective-permute-start.3 = (bf16[256,384]{1,0:T(8,128)(2,1)S(1)}, bf16[256,384]{1,0:T(8,128)(2,1)S(1)}, u32[]{:S(2)}, u32[]{:S(2)}) collective-permute-start(bf16[256,384]{1,0:T(8,128)(2,1)S(1)} %get-tuple-element.26), channel_id=1, source_target_pairs={{0,224},{1,152},{2,112},{3,40},{4,80},{5,8},{6,192},{7,184},{8,0},... | collective-permute-start | bytes 589832 | tf_op jit(solution)/shard_map/spread_features/ppermute | solution.py:256
  13.2 0.7 compare_select_fusion.picks
  13.9 4.1 %collective-permute-start.1 = (s32[4,4,4]{2,1,0:T(4,128)S(1)}, s32[4,4,4]{2,1,0:T(4,128)S(1)}, u32[]{:S(2)}, u32[]{:S(2)}) collective-permute-start(s32[4,4,4]{2,1,0:T(4,128)S(1)} %compare_select_fusion.picks), channel_id=1, source_target_pairs={{0,8},{8,0},{1,9},{9,1},{2,10},{10,2},{3,11},{11,3},{4,12},{12,4},... | collective-permute-start | bytes 776 | tf_op jit(solution)/shard_map/spread_tiles/ppermute | solution.py:259
  18.0 0.8 collective-permute-done.1.other_picks
  18.8 1.6 %copy-done = bf16[4,4,4,128,128]{4,3,2,1,0:T(8,128)(2,1)S(1)} copy-done((bf16[4,4,4,128,128]{4,3,2,1,0:T(8,128)(2,1)S(1)}, bf16[4,4,4,128,128]{4,3,2,1,0:T(8,128)(2,1)}, u32[]{:S(2)}) %copy-start) | copy-done | bytes 2097176
  20.4 3.4 %spread_tiles.1.refs_0_ = bf16[2,4,512,512]{3,2,1,0:T(8,128)(2,1)S(1)} custom-call(s32[4,4,4]{2,1,0:T(4,128)S(1)} %compare_select_fusion.picks, s32[4,4,4]{2,1,0:T(4,128)S(1)} %collective-permute-done.1.other_picks, bf16[4,4,4,128,128]{4,3,2,1,0:T(8,128)(2,1)S(1)} %copy-done, bf16[4,4,4,128,128]{4,3,2,1,0:T(8,128)(2,1)S(1)} %collective-permute-done.2.other_tiles), custom_call_target="tpu_custom_call" | custom-call | bytes 1048576 | tf_op jit(solution)/shard_map/spread_tiles/pallas_call | solution.py:260
  23.9 2.7 %collective-permute-start.5 = (bf16[256,384]{1,0:T(8,128)(2,1)S(1)}, bf16[256,384]{1,0:T(8,128)(2,1)S(1)}, u32[]{:S(2)}, u32[]{:S(2)}) collective-permute-start(bf16[256,384]{1,0:T(8,128)(2,1)S(1)} %collective-permute-done.refs_1_), channel_id=1, source_target_pairs={{0,192},{64,0},{128,64},{192,128},{1,193},{65,1},{129,65},{193,129... | collective-permute-start | bytes 589832 | tf_op jit(solution)/shard_map/spread_features/ppermute | solution.py:228
  26.6 8.5 %collective-permute-start.6 = (bf16[256,384]{1,0:T(8,128)(2,1)S(1)}, bf16[256,384]{1,0:T(8,128)(2,1)S(1)}, u32[]{:S(2)}, u32[]{:S(2)}) collective-permute-start(bf16[256,384]{1,0:T(8,128)(2,1)S(1)} %collective-permute-done.refs_1_), channel_id=1, source_target_pairs={{0,48},{16,0},{32,16},{48,32},{1,49},{17,1},{33,17},{49,33},{2,50}... | collective-permute-start | bytes 589832 | tf_op jit(solution)/shard_map/spread_features/ppermute | solution.py:228
  35.0 1.5 %collective-permute-start.9 = (bf16[256,384]{1,0:T(8,128)(2,1)S(1)}, bf16[256,384]{1,0:T(8,128)(2,1)S(1)}, u32[]{:S(2)}, u32[]{:S(2)}) collective-permute-start(bf16[256,384]{1,0:T(8,128)(2,1)S(1)} %collective-permute-done.3.refs_2_), channel_id=1, source_target_pairs={{0,64},{64,128},{128,192},{192,0},{1,65},{65,129},{129,193},{193,1... | collective-permute-start | bytes 589832 | tf_op jit(solution)/shard_map/spread_features/ppermute | solution.py:228
  36.5 0.7 aggregate.4.refs_1_
  37.2 2.4 %collective-permute-done.6.refs_4_ = bf16[256,384]{1,0:T(8,128)(2,1)S(1)} collective-permute-done((bf16[256,384]{1,0:T(8,128)(2,1)S(1)}, bf16[256,384]{1,0:T(8,128)(2,1)S(1)}, u32[]{:S(2)}, u32[]{:S(2)}) %collective-permute-start.6) | collective-permute-done | bytes 196640 | tf_op jit(solution)/shard_map/spread_features/ppermute | solution.py:228
  39.6 1.1 aggregate.5.refs_1_
  40.7 3.0 %collective-permute-done.8.refs_2_ = bf16[256,384]{1,0:T(8,128)(2,1)S(1)} collective-permute-done((bf16[256,384]{1,0:T(8,128)(2,1)S(1)}, bf16[256,384]{1,0:T(8,128)(2,1)S(1)}, u32[]{:S(2)}, u32[]{:S(2)}) %collective-permute-start.8) | collective-permute-done | bytes 196640 | tf_op jit(solution)/shard_map/spread_features/ppermute | solution.py:228
  44.2 0.7 aggregate.7
  45.0 16.1 %all_to_all.20.recv = bf16[8,2,64,384]{3,2,1,0:T(8,128)(2,1)S(1)} all-to-all(bf16[8,2,64,384]{3,2,1,0:T(8,128)(2,1)S(1)} %aggregate.7), channel_id=1, replica_groups=mesh['y'=4,'zh'=4,'core'=2,'x'=4,'zl'=2] {'x','zl'}, dimensions={0} | all-to-all | bytes 1572864 | tf_op jit(solution)/shard_map/sum_over_rep/all_to_all | solution.py:279
  61.2 1.9 %collective-permute-start.11 = (bf16[2,64,384]{2,1,0:T(8,128)(2,1)S(1)}, bf16[2,64,384]{2,1,0:T(8,128)(2,1)S(1)}, u32[]{:S(2)}, u32[]{:S(2)}) collective-permute-start(bf16[2,64,384]{2,1,0:T(8,128)(2,1)S(1)} %sum_over_rep.1.mine), channel_id=1, source_target_pairs={{0,8},{8,0},{1,9},{9,1},{2,10},{10,2},{3,11},{11,3},{4,12},{12,4},... | collective-permute-start | bytes 294920 | tf_op jit(solution)/shard_map/sum_over_rep/ppermute | solution.py:281
  63.1 0.9 collective-permute-done.11.other
  64.1 1.1 layer.1
  65.1 15.6 %all_to_all.21.recv = bf16[16,56,384]{2,1,0:T(8,128)(2,1)S(1)} all-to-all(bf16[16,56,384]{2,1,0:T(8,128)(2,1)S(1)} %get-tuple-element.30), channel_id=1, replica_groups=mesh['y'=4,'zh'=4,'core'=2,'x'=4,'zl'=2] {'x','y'}, dimensions={0} | all-to-all | bytes 1376256 | tf_op jit(solution)/shard_map/sum_over_plane/all_to_all | solution.py:290
  80.9 0.6 collective-permute-start.12
  81.5 2.3 %collective-permute-done.12.two = bf16[56,384]{1,0:T(8,128)(2,1)S(1)} collective-permute-done((bf16[56,384]{1,0:T(8,128)(2,1)S(1)}, bf16[56,384]{1,0:T(8,128)(2,1)S(1)}, u32[]{:S(2)}, u32[]{:S(2)}) %collective-permute-start.12) | collective-permute-done | bytes 43040 | tf_op jit(solution)/shard_map/sum_over_z/ppermute | solution.py:293
  83.9 0.9 collective-permute-start.13
  84.8 2.7 %collective-permute-start.14 = (bf16[56,384]{1,0:T(8,128)(2,1)S(1)}, bf16[56,384]{1,0:T(8,128)(2,1)S(1)}, u32[]{:S(2)}, u32[]{:S(2)}) collective-permute-start(bf16[56,384]{1,0:T(8,128)(2,1)S(1)} %sum_over_z.2.refs_0_), channel_id=1, source_target_pairs={{0,48},{16,0},{32,16},{48,32},{1,49},{17,1},{33,17},{49,33},{2,50}... | collective-permute-start | bytes 129032 | tf_op jit(solution)/shard_map/sum_over_z/ppermute | solution.py:295
  87.5 3.1 %collective-permute-start.15 = (bf16[56,384]{1,0:T(8,128)(2,1)S(1)}, bf16[56,384]{1,0:T(8,128)(2,1)S(1)}, u32[]{:S(2)}, u32[]{:S(2)}) collective-permute-start(bf16[56,384]{1,0:T(8,128)(2,1)S(1)} %sum_over_z.2.refs_0_), channel_id=1, source_target_pairs={{0,32},{16,48},{32,0},{48,16},{1,33},{17,49},{33,1},{49,17},{2,34}... | collective-permute-start | bytes 129032 | tf_op jit(solution)/shard_map/sum_over_z/ppermute | solution.py:295
  90.6 4.3 %collective-permute-done.15.refs_3_ = bf16[56,384]{1,0:T(8,128)(2,1)S(1)} collective-permute-done((bf16[56,384]{1,0:T(8,128)(2,1)S(1)}, bf16[56,384]{1,0:T(8,128)(2,1)S(1)}, u32[]{:S(2)}, u32[]{:S(2)}) %collective-permute-start.15) | collective-permute-done | bytes 43040 | tf_op jit(solution)/shard_map/sum_over_z/ppermute | solution.py:295
  95.0 13.2 %all_to_all.22.own = bf16[16,56,384]{2,1,0:T(8,128)(2,1)S(1)} all-to-all(bf16[16,56,384]{2,1,0:T(8,128)(2,1)S(1)} %sum_over_z.3), channel_id=1, replica_groups=mesh['y'=4,'zh'=4,'core'=2,'x'=4,'zl'=2] {'x','y'}, dimensions={0} | all-to-all | bytes 1376256 | tf_op jit(solution)/shard_map/gather_plane/all_to_all | solution.py:300
  108.2 5.3 %collective-permute-start.16 = (bf16[896,384]{1,0:T(8,128)(2,1)S(1)}, bf16[896,384]{1,0:T(8,128)(2,1)S(1)}, u32[]{:S(2)}, u32[]{:S(2)}) collective-permute-start(bf16[896,384]{1,0:T(8,128)(2,1)S(1)} %bitcast.2), channel_id=1, source_target_pairs={{0,8},{8,0},{1,9},{9,1},{2,10},{10,2},{3,11},{11,3},{4,12},{12,4},... | collective-permute-start | bytes 2064392 | tf_op jit(solution)/shard_map/gather_plane/ppermute | solution.py:301
  113.5 1.1 finish.2.begun
  114.6 0.7 collective-permute-done.16
  115.3 1.1 finish.3
  (30 shorter events, 1.0 us)
Async XLA Ops:
  0.6 1.1 copy-start.2
  1.8 17.0 %collective-permute-start.2 = (bf16[4,4,4,128,128]{4,3,2,1,0:T(8,128)(2,1)}, bf16[4,4,4,128,128]{4,3,2,1,0:T(8,128)(2,1)S(1)}, u32[]{:S(2)}, u32[]{:S(2)}) collective-permute-start(bf16[4,4,4,128,128]{4,3,2,1,0:T(8,128)(2,1)} %tiles), channel_id=1, source_target_pairs={{0,8},{8,0},{1,9},{9,1},{2,10},{10,2},{3,11},{11,3},{4,12},{12,4},... | collective-permute-start | bytes 6291464 | tf_op jit(solution)/shard_map/spread_tiles/ppermute | solution.py:259
  5.2 18.6 %collective-permute-start = (bf16[256,384]{1,0:T(8,128)(2,1)S(1)}, bf16[256,384]{1,0:T(8,128)(2,1)S(1)}, u32[]{:S(2)}, u32[]{:S(2)}) collective-permute-start(bf16[256,384]{1,0:T(8,128)(2,1)S(1)} %get-tuple-element.20), channel_id=1, source_target_pairs={{0,224},{1,152},{2,112},{3,40},{4,80},{5,8},{6,192},{7,184},{8,0},... | collective-permute-start | bytes 589832 | tf_op jit(solution)/shard_map/spread_features/ppermute | solution.py:256
  5.3 29.8 %collective-permute-start.3 = (bf16[256,384]{1,0:T(8,128)(2,1)S(1)}, bf16[256,384]{1,0:T(8,128)(2,1)S(1)}, u32[]{:S(2)}, u32[]{:S(2)}) collective-permute-start(bf16[256,384]{1,0:T(8,128)(2,1)S(1)} %get-tuple-element.26), channel_id=1, source_target_pairs={{0,224},{1,152},{2,112},{3,40},{4,80},{5,8},{6,192},{7,184},{8,0},... | collective-permute-start | bytes 589832 | tf_op jit(solution)/shard_map/spread_features/ppermute | solution.py:256
  13.9 4.9 %collective-permute-start.1 = (s32[4,4,4]{2,1,0:T(4,128)S(1)}, s32[4,4,4]{2,1,0:T(4,128)S(1)}, u32[]{:S(2)}, u32[]{:S(2)}) collective-permute-start(s32[4,4,4]{2,1,0:T(4,128)S(1)} %compare_select_fusion.picks), channel_id=1, source_target_pairs={{0,8},{8,0},{1,9},{9,1},{2,10},{10,2},{3,11},{11,3},{4,12},{12,4},... | collective-permute-start | bytes 776 | tf_op jit(solution)/shard_map/spread_tiles/ppermute | solution.py:259
  18.8 1.6 %copy-start = (bf16[4,4,4,128,128]{4,3,2,1,0:T(8,128)(2,1)S(1)}, bf16[4,4,4,128,128]{4,3,2,1,0:T(8,128)(2,1)}, u32[]{:S(2)}) copy-start(bf16[4,4,4,128,128]{4,3,2,1,0:T(8,128)(2,1)} %tiles) | copy-start | bytes 6291460
  20.4 16.1 %copy-start.3 = (bf16[64,768]{1,0:T(8,128)(2,1)S(1)}, bf16[64,768]{1,0:T(8,128)(2,1)}, u32[]{:S(2)}) copy-start(bf16[64,768]{1,0:T(8,128)(2,1)} %cot.1) | copy-start | bytes 294916
  23.8 11.2 %collective-permute-start.4 = (bf16[256,384]{1,0:T(8,128)(2,1)S(1)}, bf16[256,384]{1,0:T(8,128)(2,1)S(1)}, u32[]{:S(2)}, u32[]{:S(2)}) collective-permute-start(bf16[256,384]{1,0:T(8,128)(2,1)S(1)} %collective-permute-done.refs_1_), channel_id=1, source_target_pairs={{0,64},{64,128},{128,192},{192,0},{1,65},{65,129},{129,193},{193,1... | collective-permute-start | bytes 589832 | tf_op jit(solution)/shard_map/spread_features/ppermute | solution.py:228
  23.9 12.6 %collective-permute-start.5 = (bf16[256,384]{1,0:T(8,128)(2,1)S(1)}, bf16[256,384]{1,0:T(8,128)(2,1)S(1)}, u32[]{:S(2)}, u32[]{:S(2)}) collective-permute-start(bf16[256,384]{1,0:T(8,128)(2,1)S(1)} %collective-permute-done.refs_1_), channel_id=1, source_target_pairs={{0,192},{64,0},{128,64},{192,128},{1,193},{65,1},{129,65},{193,129... | collective-permute-start | bytes 589832 | tf_op jit(solution)/shard_map/spread_features/ppermute | solution.py:228
  26.6 13.1 %collective-permute-start.6 = (bf16[256,384]{1,0:T(8,128)(2,1)S(1)}, bf16[256,384]{1,0:T(8,128)(2,1)S(1)}, u32[]{:S(2)}, u32[]{:S(2)}) collective-permute-start(bf16[256,384]{1,0:T(8,128)(2,1)S(1)} %collective-permute-done.refs_1_), channel_id=1, source_target_pairs={{0,48},{16,0},{32,16},{48,32},{1,49},{17,1},{33,17},{49,33},{2,50}... | collective-permute-start | bytes 589832 | tf_op jit(solution)/shard_map/spread_features/ppermute | solution.py:228
  35.0 8.7 %collective-permute-start.8 = (bf16[256,384]{1,0:T(8,128)(2,1)S(1)}, bf16[256,384]{1,0:T(8,128)(2,1)S(1)}, u32[]{:S(2)}, u32[]{:S(2)}) collective-permute-start(bf16[256,384]{1,0:T(8,128)(2,1)S(1)} %collective-permute-done.3.refs_2_), channel_id=1, source_target_pairs={{0,16},{16,32},{32,48},{48,0},{1,17},{17,33},{33,49},{49,1},{2,18}... | collective-permute-start | bytes 589832 | tf_op jit(solution)/shard_map/spread_features/ppermute | solution.py:228
  35.0 9.2 %collective-permute-start.10 = (bf16[256,384]{1,0:T(8,128)(2,1)S(1)}, bf16[256,384]{1,0:T(8,128)(2,1)S(1)}, u32[]{:S(2)}, u32[]{:S(2)}) collective-permute-start(bf16[256,384]{1,0:T(8,128)(2,1)S(1)} %collective-permute-done.3.refs_2_), channel_id=1, source_target_pairs={{0,192},{64,0},{128,64},{192,128},{1,193},{65,1},{129,65},{193,129... | collective-permute-start | bytes 589832 | tf_op jit(solution)/shard_map/spread_features/ppermute | solution.py:228
  35.0 9.2 %collective-permute-start.9 = (bf16[256,384]{1,0:T(8,128)(2,1)S(1)}, bf16[256,384]{1,0:T(8,128)(2,1)S(1)}, u32[]{:S(2)}, u32[]{:S(2)}) collective-permute-start(bf16[256,384]{1,0:T(8,128)(2,1)S(1)} %collective-permute-done.3.refs_2_), channel_id=1, source_target_pairs={{0,64},{64,128},{128,192},{192,0},{1,65},{65,129},{129,193},{193,1... | collective-permute-start | bytes 589832 | tf_op jit(solution)/shard_map/spread_features/ppermute | solution.py:228
  36.5 4.2 %collective-permute-start.7 = (bf16[64,768]{1,0:T(8,128)(2,1)S(1)}, bf16[64,768]{1,0:T(8,128)(2,1)S(1)}, u32[]{:S(2)}, u32[]{:S(2)}) collective-permute-start(bf16[64,768]{1,0:T(8,128)(2,1)S(1)} %copy-done.3), channel_id=1, source_target_pairs={{0,8},{8,0},{1,9},{9,1},{2,10},{10,2},{3,11},{11,3},{4,12},{12,4},... | collective-permute-start | bytes 294920 | tf_op jit(solution)/shard_map/aggregate/ppermute | solution.py:274
  44.9 18.2 %copy-start.4 = (f32[768]{0:T(1024)S(1)}, f32[768]{0:T(1024)}, u32[]{:S(2)}) copy-start(f32[768]{0:T(1024)} %param.12) | copy-start | bytes 9220
  44.9 19.1 %copy-start.1 = (bf16[768,768]{1,0:T(8,128)(2,1)S(1)}, bf16[768,768]{1,0:T(8,128)(2,1)}, u32[]{:S(2)}) copy-start(bf16[768,768]{1,0:T(8,128)(2,1)} %weight.1) | copy-start | bytes 3538948
  61.2 2.9 %collective-permute-start.11 = (bf16[2,64,384]{2,1,0:T(8,128)(2,1)S(1)}, bf16[2,64,384]{2,1,0:T(8,128)(2,1)S(1)}, u32[]{:S(2)}, u32[]{:S(2)}) collective-permute-start(bf16[2,64,384]{2,1,0:T(8,128)(2,1)S(1)} %sum_over_rep.1.mine), channel_id=1, source_target_pairs={{0,8},{8,0},{1,9},{9,1},{2,10},{10,2},{3,11},{11,3},{4,12},{12,4},... | collective-permute-start | bytes 294920 | tf_op jit(solution)/shard_map/sum_over_rep/ppermute | solution.py:281
  80.9 3.0 %collective-permute-start.12 = (bf16[56,384]{1,0:T(8,128)(2,1)S(1)}, bf16[56,384]{1,0:T(8,128)(2,1)S(1)}, u32[]{:S(2)}, u32[]{:S(2)}) collective-permute-start(bf16[56,384]{1,0:T(8,128)(2,1)S(1)} %sum_over_plane.1.one), channel_id=1, source_target_pairs={{0,1},{1,0},{2,3},{3,2},{4,5},{5,4},{6,7},{7,6},{8,9},{9,8},{10,11... | collective-permute-start | bytes 129032 | tf_op jit(solution)/shard_map/sum_over_z/ppermute | solution.py:293
  83.9 6.7 %collective-permute-start.13 = (bf16[56,384]{1,0:T(8,128)(2,1)S(1)}, bf16[56,384]{1,0:T(8,128)(2,1)S(1)}, u32[]{:S(2)}, u32[]{:S(2)}) collective-permute-start(bf16[56,384]{1,0:T(8,128)(2,1)S(1)} %sum_over_z.2.refs_0_), channel_id=1, source_target_pairs={{0,16},{16,32},{32,48},{48,0},{1,17},{17,33},{33,49},{49,1},{2,18}... | collective-permute-start | bytes 129032 | tf_op jit(solution)/shard_map/sum_over_z/ppermute | solution.py:295
  84.8 5.8 %collective-permute-start.14 = (bf16[56,384]{1,0:T(8,128)(2,1)S(1)}, bf16[56,384]{1,0:T(8,128)(2,1)S(1)}, u32[]{:S(2)}, u32[]{:S(2)}) collective-permute-start(bf16[56,384]{1,0:T(8,128)(2,1)S(1)} %sum_over_z.2.refs_0_), channel_id=1, source_target_pairs={{0,48},{16,0},{32,16},{48,32},{1,49},{17,1},{33,17},{49,33},{2,50}... | collective-permute-start | bytes 129032 | tf_op jit(solution)/shard_map/sum_over_z/ppermute | solution.py:295
  87.5 7.4 %collective-permute-start.15 = (bf16[56,384]{1,0:T(8,128)(2,1)S(1)}, bf16[56,384]{1,0:T(8,128)(2,1)S(1)}, u32[]{:S(2)}, u32[]{:S(2)}) collective-permute-start(bf16[56,384]{1,0:T(8,128)(2,1)S(1)} %sum_over_z.2.refs_0_), channel_id=1, source_target_pairs={{0,32},{16,48},{32,0},{48,16},{1,33},{17,49},{33,1},{49,17},{2,34}... | collective-permute-start | bytes 129032 | tf_op jit(solution)/shard_map/sum_over_z/ppermute | solution.py:295
  108.2 7.1 %collective-permute-start.16 = (bf16[896,384]{1,0:T(8,128)(2,1)S(1)}, bf16[896,384]{1,0:T(8,128)(2,1)S(1)}, u32[]{:S(2)}, u32[]{:S(2)}) collective-permute-start(bf16[896,384]{1,0:T(8,128)(2,1)S(1)} %bitcast.2), channel_id=1, source_target_pairs={{0,8},{8,0},{1,9},{9,1},{2,10},{10,2},{3,11},{11,3},{4,12},{12,4},... | collective-permute-start | bytes 2064392 | tf_op jit(solution)/shard_map/gather_plane/ppermute | solution.py:301
